TPU v7x, 32 devices: a whole 2x2x4 slice. The times are simulated.
32 devices in a mesh: dp: 4 (over y, x), expert: 8 (over z, core).
Axes of the slice: x: 2, y: 2, z: 4, core: 2. Of those that a mesh axis runs over, the one named last changes fastest.
Arguments:
- tokens: bfloat16 [768, 7168], P(('dp', 'expert')), may hold values from -6 to 6
- grad_out: bfloat16 [768, 7168], P(('dp', 'expert')), may hold values from -6 to 6
- route_ids: int32 [768, 8], P(('dp', 'expert')), may hold values from 0 to 31, all different within a row; in each aligned block of 24 rows (0 to 23, 24 to 47, ...) at most 7 rows name the same one
- route_weight: bfloat16 [768, 8], P(('dp', 'expert')), may hold values from 0.049804688 to 1
- cluster_of: int32 [32], replicated, may hold values from 0 to 3, as said below
- gate_basis: bfloat16 [4, 512, 7168], P(None, 'expert', 'dp'), may hold values from -0.0625 to 0.0625
- up_basis: bfloat16 [4, 512, 7168], P(None, 'expert', 'dp'), may hold values from -0.0625 to 0.0625
- down_basis: bfloat16 [4, 512, 7168], P(None, 'expert', 'dp'), may hold values from -0.25 to 0.25
- gate_factor: bfloat16 [32, 512, 2048], P('expert', None, 'dp'), may hold values from -0.25 to 0.25
- up_factor: bfloat16 [32, 512, 2048], P('expert', None, 'dp'), may hold values from -0.25 to 0.25
- down_factor: bfloat16 [32, 2048, 512], P('expert', 'dp'), may hold values from -0.125 to 0.125
Outputs:
- grad_tokens: bfloat16 [768, 7168], P(('dp', 'expert'))
- grad_route: float32 [768, 8], P(('dp', 'expert'))
- grad_gate_basis: float32 [4, 512, 7168], P(None, 'expert', 'dp')
- grad_up_basis: float32 [4, 512, 7168], P(None, 'expert', 'dp')
- grad_down_basis: float32 [4, 512, 7168], P(None, 'expert', 'dp')
- grad_gate_factor: float32 [32, 512, 2048], P('expert', None, 'dp')
- grad_up_factor: float32 [32, 512, 2048], P('expert', None, 'dp')
- grad_down_factor: float32 [32, 2048, 512], P('expert', 'dp')
Inputs may be any that keep to these rules, and one draw needn't show every extreme that they name: `route_ids`: each token names 8 different experts. Among the 24 tokens of one block no expert is named more than 7 times, and in every draw some expert is named exactly 7 times in some block. `cluster_of`: never falls from one expert to the next; all 4 experts of each group of 4 consecutive experts share one cluster; every cluster holds 1 to 3 such groups, and one holds exactly 3.
All inputs are finite; a program needn't handle non-finite values.
Results may differ from a plain program's by a relative error of at most 0.013.
Values may be sent and summed in bfloat16 or wider, within the bound.
No kernel may reach another device: no remote copies, remote signals or barrier semaphores. Data moves between devices by JAX's collectives and lax.ppermute only.
A program may use at most 128 MiB of HBM per device.

v0:
```python
import jax
import jax.numpy as jnp
from jax import lax
from jax.experimental import pallas as pl
from jax.experimental.pallas import tpu as pltpu
from jax.sharding import Mesh
from jax.sharding import PartitionSpec as P

FL = jnp.float32
BF = jnp.bfloat16
VMEM = pltpu.VMEM


def mm(spec, a, b):
    return jnp.einsum(spec, a, b, preferred_element_type=FL)


def dot(a, b, a_dim, b_dim):
    return lax.dot_general(a, b, (((a_dim,), (b_dim,)), ((), ())), preferred_element_type=FL)


def after(value, first):
    mark = lax.slice(first, (0,) * first.ndim, (1,) * first.ndim).reshape(()).astype(FL) * 0.0
    return value + mark.astype(value.dtype)


def core_swap(value):
    return lax.ppermute(value, "core", [(0, 1), (1, 0)])


def in_order(pieces, me):
    bit = 1
    while bit < len(pieces):
        odd = (me & bit) != 0
        pieces = [
            jnp.where(odd, pieces[j ^ bit], pieces[j]) for j in range(len(pieces))
        ]
        bit *= 2
    return pieces


def trade(chunk_for, axis):
    n = lax.axis_size(axis)
    sent = [lax.ppermute(chunk_for(k), axis, [(i, i ^ k) for i in range(n)]) for k in range(1, n)]
    return [chunk_for(0)] + sent


def gather_z(share):
    n = lax.axis_size("ez")
    if n != 4:
        return trade(lambda k: share, "ez")
    far = lax.ppermute(share, "ez", [(0, 2), (2, 0), (1, 3), (3, 1)])
    near = lax.ppermute(share, "ez", [(0, 1), (1, 0), (2, 3), (3, 2)])
    inner = lax.ppermute(share, "ez", [(1, 2), (2, 1)])
    ends = lax.ppermute(far, "ez", [(2, 3), (1, 0)])
    return [share, near, far, inner, ends]


def scatter_z(share_of):
    n = lax.axis_size("ez")
    if n != 4:
        got = trade(lambda k: share_of(k).astype(BF), "ez")
        return share_of(0) + sum(piece.astype(FL) for piece in got[1:])
    third = share_of(3).astype(BF)
    ends = lax.ppermute(third, "ez", [(0, 1), (3, 2)])
    near = lax.ppermute(share_of(1).astype(BF), "ez", [(0, 1), (1, 0), (2, 3), (3, 2)])
    inner = lax.ppermute(third, "ez", [(1, 2), (2, 1)])
    second = (share_of(2) + ends.astype(FL)).astype(BF)
    far = lax.ppermute(second, "ez", [(0, 2), (2, 0), (1, 3), (3, 1)])
    return share_of(0) + near.astype(FL) + inner.astype(FL) + far.astype(FL)


def whole(array):
    return pl.BlockSpec(array.shape, lambda *_: (0,) * array.ndim, memory_space=VMEM)


def each(array):
    shape = (1,) + array.shape[1:]
    return pl.BlockSpec(shape, lambda j: (j,) + (0,) * (array.ndim - 1), memory_space=VMEM)


SCALAR = pl.BlockSpec(memory_space=pltpu.SMEM)
ANYWHERE = pl.BlockSpec(memory_space=pl.ANY)


def params(total):
    return pltpu.CompilerParams(vmem_limit_bytes=(8 + total * 15 // 1024) << 20)


def shaped(shape, kind):
    return jax.ShapeDtypeStruct(shape, kind)


def project(pieces, parts, z, n_z, first):
    share, width = pieces[0].shape
    half = n_z * share

    def kernel(z_ref, *refs):
        got, rest = refs[: len(pieces)], refs[len(pieces) :]
        bases, rest = rest[: len(parts)], rest[len(parts) :]
        cols, products = rest[1], rest[2:]
        me = z_ref[0]
        for k in range(n_z):
            at = pl.multiple_of((me ^ k) * share, 16)
            piece = got[k][...]
            if k == 3 and len(pieces) > n_z:
                middle = jnp.logical_or(me == 1, me == 2)
                piece = jnp.where(middle, piece, got[4][...])
            cols[pl.ds(at, share), :] = piece
        for base, product in zip(bases, products):
            product[...] = dot(base[...], cols[...], 1, 1).astype(BF)

    outs = [shaped((half, width), BF)] + [shaped((part.shape[0], half), BF) for part in parts]
    return pl.pallas_call(
        kernel,
        out_shape=outs,
        in_specs=[SCALAR]
        + [whole(piece) for piece in pieces]
        + [whole(part) for part in parts]
        + [ANYWHERE],
        out_specs=[whole(out) for out in outs],
        compiler_params=params(2 * half),
        cost_estimate=pl.CostEstimate(
            flops=2 * half * width * sum(part.shape[0] for part in parts),
            bytes_accessed=8 << 20,
            transcendentals=0,
        ),
        name="project",
    )(z.reshape(1), *pieces, *parts, first)


def make_picks(cell, weight, slots):
    local, _, total = cell.shape

    def kernel(cell_ref, weight_ref, pick_ref, heavy_ref, slot_ref):
        hit = cell_ref[0] == lax.broadcasted_iota(jnp.int32, (slots, total), 0)
        heavy = jnp.where(hit, weight_ref[0], 0.0)
        pick_ref[0] = jnp.where(hit, 1.0, 0.0).astype(BF)
        heavy_ref[0] = heavy.astype(BF)
        slot_ref[0] = jnp.sum(heavy, axis=1, keepdims=True)

    outs = [
        shaped((local, slots, total), BF),
        shaped((local, slots, total), BF),
        shaped((local, slots, 1), FL),
    ]
    return pl.pallas_call(
        kernel,
        grid=(local,),
        out_shape=outs,
        in_specs=[each(cell), each(weight)],
        out_specs=[each(out) for out in outs],
        compiler_params=params(total),
        cost_estimate=pl.CostEstimate(
            flops=6 * local * slots * total,
            bytes_accessed=4 * local * slots * total,
            transcendentals=0,
        ),
        name="make_picks",
    )(cell, weight)


def lay_out(pieces, target, me, count):
    n_dp = len(pieces)
    n_ex, rows, half = pieces[0].shape
    part = rows // count
    for k in range(n_dp):
        for e in range(n_ex):
            at = pl.multiple_of(((e // 2) * n_dp + (me ^ k)) * part, part)
            for b in range(count):
                piece = pieces[k][e, b * part : (b + 1) * part, :]
                target[b, pl.ds(at, part), (e % 2) * half : (e % 2 + 1) * half] = piece.astype(
                    target.dtype
                )


def rows_kind(part):
    return BF if part % 16 == 0 else FL


def hand_out(source, pieces, me, count):
    n_dp = len(pieces)
    n_ex, rows, half = pieces[0].shape
    part = rows // count
    for k in range(n_dp):
        for e in range(n_ex):
            at = pl.multiple_of(((e // 2) * n_dp + (me ^ k)) * part, part)
            for b in range(count):
                pieces[k][e, b * part : (b + 1) * part, :] = source[
                    b, pl.ds(at, part), (e % 2) * half : (e % 2 + 1) * half
                ].astype(BF)


def forward(pieces, pick, heavy, gate_factor, up_factor, down_factor, dp):
    n_dp = len(pieces)
    n_ex, rows, half = pieces[0].shape
    local, slots, total = pick.shape
    rank, hid = gate_factor.shape[1:]

    def kernel(dp_ref, *refs):
        got, refs = refs[:n_dp], refs[n_dp:]
        pick_ref, heavy_ref, gate_ref, up_ref, down_ref = refs[:5]
        hg_ref, hu_ref, hidden_ref, mixed_ref, act_ref, lift_ref = refs[5:11]
        sent = refs[11 : 11 + n_dp]
        rows_ref, total_ref = refs[11 + n_dp :]
        j = pl.program_id(0)
        me = dp_ref[0]

        @pl.when(j == 0)
        def _():
            lay_out(got, rows_ref, me, 2)
            total_ref[...] = jnp.zeros_like(total_ref)

        take = pick_ref[0]
        hg = dot(take, rows_ref[0].astype(BF), 1, 1).astype(BF)
        hu = dot(take, rows_ref[1].astype(BF), 1, 1).astype(BF)
        hg_ref[0] = hg
        hu_ref[0] = hu
        gate_pre = dot(hg, gate_ref[0], 1, 0)
        up_pre = dot(hu, up_ref[0], 1, 0)
        sig = 1.0 / (1.0 + jnp.exp(-gate_pre))
        act = gate_pre * sig
        act_ref[0] = act
        lift_ref[0] = up_pre * (sig * (1.0 + gate_pre * (1.0 - sig)))
        hidden = (act * up_pre).astype(BF)
        hidden_ref[0] = hidden
        mixed = dot(hidden, down_ref[0], 1, 0).astype(BF)
        mixed_ref[0] = mixed
        total_ref[0] += dot(mixed, heavy_ref[0], 0, 0)

        @pl.when(j == local - 1)
        def _():
            hand_out(total_ref, sent, me, 1)

    slot_shape = (local, slots, rank)
    hid_shape = (local, slots, hid)
    outs = [
        shaped(slot_shape, BF),
        shaped(slot_shape, BF),
        shaped(hid_shape, BF),
        shaped(slot_shape, BF),
        shaped(hid_shape, FL),
        shaped(hid_shape, FL),
    ]
    chunks = [shaped((n_ex, rows // 2, half), BF)] * n_dp
    got = pl.pallas_call(
        kernel,
        grid=(local,),
        out_shape=outs + chunks,
        in_specs=[SCALAR]
        + [whole(piece) for piece in pieces]
        + [each(x) for x in (pick, heavy, gate_factor, up_factor, down_factor)],
        out_specs=[each(out) for out in outs] + [whole(chunk) for chunk in chunks],
        scratch_shapes=[pltpu.VMEM((2, rank, total), rows_kind(rows // 2)), pltpu.VMEM((1, rank, total), FL)],
        compiler_params=params(total),
        cost_estimate=pl.CostEstimate(
            flops=local * slots * rank * (6 * total + 6 * hid),
            bytes_accessed=16 << 20,
            transcendentals=local * slots * hid,
        ),
        name="forward",
    )(dp.reshape(1), *pieces, pick, heavy, gate_factor, up_factor, down_factor)
    return got[:6], got[6:]


def backward(pieces, pick, weight, mixed, act, lift, gate_factor, up_factor, down_factor, dp):
    n_dp = len(pieces)
    n_ex, rows, half = pieces[0].shape
    local, slots, total = pick.shape
    rank, hid = gate_factor.shape[1:]

    def kernel(dp_ref, *refs):
        got, refs = refs[:n_dp], refs[n_dp:]
        pick_ref, weight_ref, mixed_ref, act_ref, lift_ref = refs[:5]
        gate_ref, up_ref, down_ref = refs[5:8]
        back_ref, gate_out, up_out, dots_ref = refs[8:12]
        sent = refs[12 : 12 + n_dp]
        rows_ref, total_ref = refs[12 + n_dp :]
        j = pl.program_id(0)
        me = dp_ref[0]

        @pl.when(j == 0)
        def _():
            lay_out(got, rows_ref, me, 1)
            total_ref[...] = jnp.zeros_like(total_ref)

        take = pick_ref[0]
        hd = dot(take, rows_ref[0].astype(BF), 1, 1)
        dots_ref[0] = jnp.sum(mixed_ref[0].astype(FL) * hd, axis=1, keepdims=True)
        back = (weight_ref[0] * hd).astype(BF)
        back_ref[0] = back
        grad_hidden = dot(back, down_ref[0], 1, 1)
        grad_gate = (grad_hidden * lift_ref[0]).astype(BF)
        grad_up = (grad_hidden * act_ref[0]).astype(BF)
        gate_out[0] = grad_gate
        up_out[0] = grad_up
        total_ref[0] += dot(dot(grad_gate, gate_ref[0], 1, 1).astype(BF), take, 0, 0)
        total_ref[1] += dot(dot(grad_up, up_ref[0], 1, 1).astype(BF), take, 0, 0)

        @pl.when(j == local - 1)
        def _():
            hand_out(total_ref, sent, me, 2)

    outs = [
        shaped((local, slots, rank), BF),
        shaped((local, slots, hid), BF),
        shaped((local, slots, hid), BF),
        shaped((local, slots, 1), FL),
    ]
    chunks = [shaped((n_ex, 2 * rows, half), BF)] * n_dp
    ins = (pick, weight, mixed, act, lift, gate_factor, up_factor, down_factor)
    got = pl.pallas_call(
        kernel,
        grid=(local,),
        out_shape=outs + chunks,
        in_specs=[SCALAR] + [whole(piece) for piece in pieces] + [each(x) for x in ins],
        out_specs=[each(out) for out in outs] + [whole(chunk) for chunk in chunks],
        scratch_shapes=[pltpu.VMEM((1, rank, total), rows_kind(rows)), pltpu.VMEM((2, rank, total), FL)],
        compiler_params=params(total),
        cost_estimate=pl.CostEstimate(
            flops=local * slots * rank * (6 * total + 6 * hid),
            bytes_accessed=16 << 20,
            transcendentals=0,
        ),
        name="backward",
    )(dp.reshape(1), *pieces, *ins)
    return got[:4], got[4:]


def factor_grads(hg, grad_gate, hu, grad_up, hidden, back, total):
    local, slots, rank = hg.shape
    hid = hidden.shape[2]

    def kernel(hg_ref, gate_ref, hu_ref, up_ref, hidden_ref, back_ref, out_g, out_u, out_d):
        out_g[0] = dot(hg_ref[0], gate_ref[0], 0, 0)
        out_u[0] = dot(hu_ref[0], up_ref[0], 0, 0)
        out_d[0] = dot(hidden_ref[0], back_ref[0], 0, 0)

    outs = [
        shaped((local, rank, hid), FL),
        shaped((local, rank, hid), FL),
        shaped((local, hid, rank), FL),
    ]
    ins = (hg, grad_gate, hu, grad_up, hidden, back)
    return pl.pallas_call(
        kernel,
        grid=(local,),
        out_shape=outs,
        in_specs=[each(x) for x in ins],
        out_specs=[each(out) for out in outs],
        compiler_params=params(total),
        cost_estimate=pl.CostEstimate(
            flops=6 * local * slots * rank * hid,
            bytes_accessed=18 << 20,
            transcendentals=0,
        ),
        name="factor_grads",
    )(*ins)


def body(
    tokens,
    grad_out,
    route_ids,
    route_weight,
    cluster_of,
    gate_basis,
    up_basis,
    down_basis,
    gate_factor,
    up_factor,
    down_factor,
):
    n_dp = lax.axis_size("dp")
    n_z = lax.axis_size("ez")
    n_ex = n_z * 2
    dp = lax.axis_index("dp")
    z = lax.axis_index("ez")
    core = lax.axis_index("core")
    me_e = z * 2 + core
    tok_rows = tokens.shape[0]
    top = route_ids.shape[1]
    local = gate_factor.shape[0]
    experts = local * n_ex
    capacity = max(2, 5 * tok_rows * top // (4 * experts))
    blocks = n_dp * n_ex
    total = blocks * tok_rows
    half = total // 2
    share = n_dp * tok_rows
    slots = blocks * capacity
    clusters, rank_own, width = gate_basis.shape
    parts_core = n_dp // 2
    rank_part = rank_own // parts_core

    def own_columns(rows):
        pieces = trade(
            lambda k: lax.dynamic_slice_in_dim(rows, (dp ^ k) * width, width, 1), "dp"
        )
        return jnp.concatenate(in_order(pieces, dp), axis=0)

    x_share = own_columns(tokens)
    x_pieces = gather_z(x_share)
    dy_share = own_columns(after(grad_out, x_share))
    dy_pieces = gather_z(after(dy_share, x_pieces[3]))

    def chip_rows(bases):
        own = after(jnp.stack(bases, axis=1), x_share)
        other = core_swap(own)
        count = len(bases)
        own = own.reshape(clusters, count, parts_core, rank_part, width)
        other = other.reshape(clusters, count, parts_core, rank_part, width)
        result = []
        for k in range(n_dp):
            part = dp ^ k
            at = part % parts_core
            mine = lax.dynamic_index_in_dim(own, at, 2, False)
            theirs = lax.dynamic_index_in_dim(other, at, 2, False)
            rows = jnp.where(part // parts_core == core, mine, theirs)
            result.append(rows.reshape(clusters * count * rank_part, width))
        return result

    rows_in = chip_rows([gate_basis, up_basis])
    rows_out = chip_rows([down_basis])

    routing = jnp.concatenate([route_ids.astype(FL), route_weight.astype(FL)], axis=1)
    routing = after(routing, x_share)
    routing = jnp.broadcast_to(routing[None], (blocks, tok_rows, 2 * top))
    routing = lax.all_to_all(routing, ("dp", "ez", "core"), split_axis=0, concat_axis=0, tiled=True)
    routing = after(routing, x_pieces[2])
    routing = routing.reshape(n_dp, n_z, 2, tok_rows, 2 * top).transpose(2, 1, 0, 3, 4)
    routing = routing.reshape(blocks, tok_rows, 2 * top)
    ids = routing[:, :, :top].astype(jnp.int32)
    weights = routing[:, :, top:]
    own_ids = me_e * local + jnp.arange(local, dtype=jnp.int32)
    hit = ids[None] == own_ids[:, None, None, None]
    named = jnp.any(hit, axis=3)
    weight_of = jnp.sum(jnp.where(hit, weights[None], 0.0), axis=3)
    order = jnp.cumsum(named.astype(jnp.int32), axis=2) - 1
    cell = jnp.arange(blocks, dtype=jnp.int32)[None, :, None] * capacity + order
    cell = jnp.where(named, cell, -1).reshape(local, 1, total)
    pick, heavy, slot_weight = make_picks(cell, weight_of.reshape(local, 1, total), slots)

    group_cluster = cluster_of.reshape(n_ex, local)[:, 0]

    def sum_parts(got):
        return sum(piece.astype(FL) for piece in got).astype(BF)

    def to_group(mine):
        mine = mine.reshape(clusters, -1, half)
        send = mine.at[group_cluster].get(mode="promise_in_bounds")
        return lax.all_to_all(send, ("ez", "core"), split_axis=0, concat_axis=0, tiled=True)

    x_half, *terms = project(x_pieces, rows_in, z, n_z, x_share)
    mine_in = sum_parts(trade(lambda k: terms[k], "dp"))
    got_in = to_group(mine_in)
    dy_half, *terms_out = project(dy_pieces, rows_out, z, n_z, mine_in)
    mine_out = sum_parts(trade(lambda k: terms_out[k], "dp"))
    got_out = to_group(after(mine_out, got_in))
    h_pieces = trade(lambda k: got_in, "dp")
    (hg, hu, hidden, mixed, act, lift), mixed_chunks = forward(
        h_pieces, pick, heavy, gate_factor, up_factor, down_factor, dp
    )
    d_pieces = trade(lambda k: got_out, "dp")
    (back, grad_gate, grad_up, dots), in_chunks = backward(
        d_pieces, pick, slot_weight, mixed, act, lift, gate_factor, up_factor, down_factor, dp
    )

    owner = group_cluster[None, :] == jnp.arange(clusters, dtype=jnp.int32)[:, None]

    def from_groups(mine):
        got = lax.all_to_all(mine, ("ez", "core"), split_axis=0, concat_axis=0, tiled=True)
        return jnp.sum(
            jnp.where(owner[:, :, None, None], got.astype(FL)[None], 0.0), axis=1
        ).astype(BF).reshape(-1, half)

    mixed_mine = sum_parts(trade(lambda k: mixed_chunks[k], "dp"))
    in_mine = sum_parts(trade(lambda k: in_chunks[k], "dp"))
    in_sum = from_groups(in_mine)
    mixed_sum = after(from_groups(mixed_mine), in_mine)
    in_parts = trade(lambda k: in_sum, "dp")
    mixed_parts = trade(lambda k: mixed_sum, "dp")
    grad_gate_factor, grad_up_factor, grad_down_factor = factor_grads(
        hg, grad_gate, hu, grad_up, hidden, back, total
    )

    grad_x = sum(mm("rt,rf->tf", part, rows) for part, rows in zip(in_parts, rows_in))
    shares = grad_x.reshape(n_z, share, width)
    mine = scatter_z(lambda k: lax.dynamic_index_in_dim(shares, z ^ k, 0, False)).astype(BF)
    pieces = trade(
        lambda k: lax.dynamic_slice_in_dim(mine, (dp ^ k) * tok_rows, tok_rows, 0), "dp"
    )
    grad_tokens = jnp.concatenate(in_order(pieces, dp), axis=1)

    def both_cores(value, axis):
        other = core_swap(value)
        first = core == 0
        return jnp.concatenate(
            [jnp.where(first, value, other), jnp.where(first, other, value)], axis=axis
        )

    x_all = both_cores(x_half, 0)
    dy_all = both_cores(dy_half, 0)

    def own_ranks(parts, count):
        stack = jnp.stack(in_order(parts, dp))
        stack = stack.reshape(2, parts_core, clusters, count, rank_part, half)
        keep = jnp.where(core == 0, stack[0], stack[1])
        give = jnp.where(core == 0, stack[1], stack[0])
        other = core_swap(give)
        first = core == 0
        rows = jnp.stack([jnp.where(first, keep, other), jnp.where(first, other, keep)])
        rows = rows.transpose(3, 2, 1, 4, 0, 5)
        return rows.reshape(count, clusters * rank_own, total)

    shape = (clusters, rank_own, width)
    (sum_mixed,) = own_ranks(mixed_parts, 1)
    sum_gate, sum_up = own_ranks(in_parts, 2)
    grad_down_basis = mm("rt,tf->rf", sum_mixed, dy_all).reshape(shape)
    grad_gate_basis = mm("rt,tf->rf", sum_gate, x_all).reshape(shape)
    grad_up_basis = mm("rt,tf->rf", sum_up, x_all).reshape(shape)

    placed = cell == jnp.arange(slots, dtype=jnp.int32)[None, :, None]
    scores = jnp.sum(jnp.where(placed, after(dots, in_mine), 0.0), axis=1)
    scores = scores.reshape(local, 2, n_z, n_dp, tok_rows).transpose(3, 2, 1, 0, 4)
    scores = scores.reshape(blocks, local, tok_rows)
    returned = lax.all_to_all(
        scores, ("dp", "ez", "core"), split_axis=0, concat_axis=0, tiled=True
    )
    by_expert = jnp.sum(returned.reshape(n_dp, experts, tok_rows), axis=0)
    chosen = route_ids[:, :, None] == jnp.arange(experts, dtype=jnp.int32)[None, None, :]
    grad_route = jnp.sum(jnp.where(chosen, by_expert.T[:, None, :], 0.0), axis=2)
    return (
        grad_tokens,
        grad_route,
        grad_gate_basis,
        grad_up_basis,
        grad_down_basis,
        grad_gate_factor,
        grad_up_factor,
        grad_down_factor,
    )


def solution(mesh):
    n_dp, n_ex = mesh.shape["dp"], mesh.shape["expert"]
    split = Mesh(mesh.devices.reshape(n_dp, n_ex // 2, 2), ("dp", "ez", "core"))
    ex = ("ez", "core")
    rows = P(("dp", "ez", "core"), None)
    basis = P(None, ex, "dp")
    in_specs = (
        rows,
        rows,
        rows,
        rows,
        P(),
        basis,
        basis,
        basis,
        P(ex, None, "dp"),
        P(ex, None, "dp"),
        P(ex, "dp", None),
    )
    out_specs = (
        rows,
        rows,
        basis,
        basis,
        basis,
        P(ex, None, "dp"),
        P(ex, None, "dp"),
        P(ex, "dp", None),
    )
    return jax.shard_map(body, mesh=split, in_specs=in_specs, out_specs=out_specs, check_vma=False)
```

profile of v0, /device:TPU:0, one launch (start us, length us, event | category | flops | bytes accessed | tf_op | source)
XLA Modules:
  0.0 293.8 jit_solution(12351029280606251040)
XLA Ops:
  25.6 7.3 %all-to-all-start.2 = ((f32[32,1,384]{2,1,0:T(1,128)}), f32[32,1,384]{2,1,0:T(1,128)}, u32[]{:S(2)}, u32[]{:S(2)}) async-start(f32[32,1,384]{2,1,0:T(1,128)} %reshape.464), calls=%async_computation.2 | async-start | bytes 98304 | tf_op jit(solution)/shard_map/all_to_all | solution.py:428
  45.6 18.4 %collective-permute-done.13.refs_2_ = bf16[96,1792]{1,0:T(8,128)(2,1)} collective-permute-done((bf16[96,1792]{1,0:T(8,128)(2,1)S(1)}, bf16[96,1792]{1,0:T(8,128)(2,1)}, u32[]{:S(2)}, u32[]{:S(2)}) %collective-permute-start.13) | collective-permute-done | bytes 344096 | tf_op jit(solution)/shard_map/ppermute | solution.py:52
  69.1 6.1 %collective-permute-done.14.refs_4_ = bf16[96,1792]{1,0:T(8,128)(2,1)S(1)} collective-permute-done((bf16[96,1792]{1,0:T(8,128)(2,1)}, bf16[96,1792]{1,0:T(8,128)(2,1)S(1)}, u32[]{:S(2)}, u32[]{:S(2)}) %collective-permute-start.14) | collective-permute-done | bytes 344096 | tf_op jit(solution)/shard_map/ppermute | solution.py:55
  75.3 3.9 %project.2 = (bf16[384,1792]{1,0:T(8,128)(2,1)S(1)}, bf16[256,384]{1,0:T(8,128)(2,1)S(1)}, bf16[256,384]{1,0:T(8,128)(2,1)}, bf16[256,384]{1,0:T(8,128)(2,1)}, bf16[256,384]{1,0:T(8,128)(2,1)}) custom-call(s32[1]{0:T(128)} %bitcast.1.z_ref, bf16[96,1792]{1,0:T(8,128)(2,1)S(1)} %pad_maximum_fusion.3.refs_0_.refs_9_, ...), custom_call_target="tpu_custom_call" | custom-call | flops 1409286144 | bytes 8388608 | tf_op jit(solution)/shard_map/project/pallas_call | solution.py:114
  94.0 10.5 %all-to-all-start = ((bf16[8,64,384]{2,1,0:T(8,128)(2,1)}), bf16[8,64,384]{2,1,0:T(8,128)(2,1)}, u32[]{:S(2)}, u32[]{:S(2)}) async-start(bf16[8,64,384]{2,1,0:T(8,128)(2,1)} %gather_fusion), calls=%async_computation | async-start | bytes 786432 | tf_op jit(solution)/shard_map/all_to_all | solution.py:451
  109.3 3.7 %project.3 = (bf16[384,1792]{1,0:T(8,128)(2,1)S(1)}, bf16[128,384]{1,0:T(8,128)(2,1)S(1)}, bf16[128,384]{1,0:T(8,128)(2,1)S(1)}, bf16[128,384]{1,0:T(8,128)(2,1)}, bf16[128,384]{1,0:T(8,128)(2,1)}) custom-call(s32[1]{0:T(128)} %bitcast.1.z_ref, bf16[96,1792]{1,0:T(8,128)(2,1)S(1)} %maximum_add_fusion.1.refs_0_, ...), custom_call_target="tpu_custom_call" | custom-call | flops 704643072 | bytes 8388608 | tf_op jit(solution)/shard_map/project/pallas_call | solution.py:114
  123.5 5.1 %all-to-all-start.1 = ((bf16[8,32,384]{2,1,0:T(8,128)(2,1)}), bf16[8,32,384]{2,1,0:T(8,128)(2,1)S(1)}, u32[]{:S(2)}, u32[]{:S(2)}) async-start(bf16[8,32,384]{2,1,0:T(8,128)(2,1)} %gather_fusion.1), calls=%async_computation.1 | async-start | bytes 393216 | tf_op jit(solution)/shard_map/all_to_all | solution.py:451
  136.9 3.9 %collective-permute-done.25.refs_1_ = bf16[8,64,384]{2,1,0:T(8,128)(2,1)} collective-permute-done((bf16[8,64,384]{2,1,0:T(8,128)(2,1)}, bf16[8,64,384]{2,1,0:T(8,128)(2,1)}, u32[]{:S(2)}, u32[]{:S(2)}) %collective-permute-start.25) | collective-permute-done | bytes 393248 | tf_op jit(solution)/shard_map/ppermute | solution.py:44
  142.3 7.8 %collective-permute-done.26.refs_2_ = bf16[8,64,384]{2,1,0:T(8,128)(2,1)} collective-permute-done((bf16[8,64,384]{2,1,0:T(8,128)(2,1)}, bf16[8,64,384]{2,1,0:T(8,128)(2,1)}, u32[]{:S(2)}, u32[]{:S(2)}) %collective-permute-start.26) | collective-permute-done | bytes 393248 | tf_op jit(solution)/shard_map/ppermute | solution.py:44
  159.1 8.2 %forward.1 = (bf16[4,224,512]{2,1,0:T(8,128)(2,1)S(1)}, bf16[4,224,512]{2,1,0:T(8,128)(2,1)S(1)}, bf16[4,224,512]{2,1,0:T(8,128)(2,1)S(1)}, bf16[4,224,512]{2,1,...) custom-call(s32[1]{0:T(128)} %bitcast.dp_ref, ...), custom_call_target="tpu_custom_call" | custom-call | flops 3523215360 | bytes 16777216 | tf_op jit(solution)/shard_map/forward/pallas_call | solution.py:246
  170.0 3.1 %broadcast_select_fusion.3 = (bf16[384,1792]{1,0:T(8,128)(2,1)}, bf16[384,1792]{1,0:T(8,128)(2,1)}) fusion(bf16[384,1792]{1,0:T(8,128)(2,1)S(1)} %copy-done.9, bf16[384,1792]{1,0:T(8,128)(2,1)} %collective-permute-done.42, pred[]{:T(512)S(6)} %eq.110), kind=kLoop, calls=%fused_computation.22 | loop fusion | flops 1376256 | bytes 5505025 | tf_op jit(solution)/shard_map/jit(_where)/select_n | solution.py:498
  174.3 9.1 %backward.1 = (bf16[4,224,512]{2,1,0:T(8,128)(2,1)S(1)}, bf16[4,224,512]{2,1,0:T(8,128)(2,1)S(1)}, bf16[4,224,512]{2,1,0:T(8,128)(2,1)S(1)}, f32[4,224,1]{2,1,0:...) custom-call(s32[1]{0:T(128)} %bitcast.dp_ref, ...), custom_call_target="tpu_custom_call" | custom-call | flops 3523215360 | bytes 16777216 | tf_op jit(solution)/shard_map/backward/pallas_call | solution.py:312
  185.7 5.2 %factor_grads.1 = (f32[4,512,512]{2,1,0:T(8,128)}, f32[4,512,512]{2,1,0:T(8,128)}, f32[4,512,512]{2,1,0:T(8,128)}) custom-call(bf16[4,224,512]{2,1,0:T(8,128)(2,1)S(1)} %get-tuple-element.67.hg_ref, bf16[4,224,512]{2,1,0:T(8,128)(2,1)S(1)} %get-tuple-element.68.gate_ref, bf16[4,224,512]{2,1,0:T(8,128)(2,1)S(1)} %get-tuple-element.69.hu_ref, ...), custom_call_target="tpu_custom_call" | custom-call | flops 1409286144 | bytes 18874368 | tf_op jit(solution)/shard_map/factor_grads/pallas_call | solution.py:345
  193.0 5.3 %all-to-all-start.5 = ((bf16[8,32,384]{2,1,0:T(8,128)(2,1)}), bf16[8,32,384]{2,1,0:T(8,128)(2,1)S(1)}, u32[]{:S(2)}, u32[]{:S(2)}) async-start(bf16[8,32,384]{2,1,0:T(8,128)(2,1)} %add_convert_fusion.1), calls=%async_computation.5 | async-start | bytes 393216 | tf_op jit(solution)/shard_map/all_to_all | solution.py:471
  198.3 3.5 %broadcast_select_fusion.1 = (bf16[384,1792]{1,0:T(8,128)(2,1)}, bf16[384,1792]{1,0:T(8,128)(2,1)}) fusion(bf16[384,1792]{1,0:T(8,128)(2,1)} %copy-done.10, bf16[384,1792]{1,0:T(8,128)(2,1)} %collective-permute-done.50, pred[]{:T(512)S(6)} %eq.110), kind=kLoop, calls=%fused_computation.20 | loop fusion | flops 1376256 | bytes 5505025 | tf_op jit(solution)/shard_map/jit(_where)/select_n | solution.py:498
  201.8 4.8 %all-to-all-done.5 = bf16[8,32,384]{2,1,0:T(8,128)(2,1)S(1)} async-done(((bf16[8,32,384]{2,1,0:T(8,128)(2,1)}), bf16[8,32,384]{2,1,0:T(8,128)(2,1)S(1)}, u32[]{:S(2)}, u32[]{:S(2)}) %all-to-all-start.5) | async-done | bytes 196640 | tf_op jit(solution)/shard_map/all_to_all | solution.py:471
  220.9 5.4 %all-to-all-done.4 = f32[32,4,24]{2,1,0:T(4,128)S(1)} async-done(((f32[32,4,24]{2,1,0:T(4,128)}), f32[32,4,24]{2,1,0:T(4,128)S(1)}, u32[]{:S(2)}, u32[]{:S(2)}) %all-to-all-start.4) | async-done | bytes 12320 | tf_op jit(solution)/shard_map/all_to_all | solution.py:526
  227.0 3.7 %all-to-all-start.3 = ((bf16[8,64,384]{2,1,0:T(8,128)(2,1)}), bf16[8,64,384]{2,1,0:T(8,128)(2,1)S(1)}, u32[]{:S(2)}, u32[]{:S(2)}) async-start(bf16[8,64,384]{2,1,0:T(8,128)(2,1)} %add_convert_fusion), calls=%async_computation.3 | async-start | bytes 786432 | tf_op jit(solution)/shard_map/all_to_all | solution.py:471
  236.2 4.0 %fusion.1 = f32[4,64,1792]{2,1,0:T(8,128)} fusion(bf16[4,64,768]{2,1,0:T(8,128)(2,1)} %dot_general.35, bf16[384,1792]{1,0:T(8,128)(2,1)} %get-tuple-element.95, bf16[384,1792]{1,0:T(8,128)(2,1)} %get-tuple-element.94), kind=kOutput, calls=%fused_computation.8 | convolution fusion | flops 710148096 | bytes 4980736 | tf_op jit(solution)/shard_map/rt,tf->rf/dot_general | solution.py:15
  247.5 6.7 %collective-permute-done.31 = bf16[256,384]{1,0:T(8,128)(2,1)S(1)} collective-permute-done((bf16[256,384]{1,0:T(8,128)(2,1)S(1)}, bf16[256,384]{1,0:T(8,128)(2,1)S(1)}, u32[]{:S(2)}, u32[]{:S(2)}) %collective-permute-start.31) | collective-permute-done | bytes 196640 | tf_op jit(solution)/shard_map/ppermute | solution.py:44
  261.7 5.6 %collective-permute-done.36 = bf16[96,1792]{1,0:T(8,128)(2,1)S(1)} collective-permute-done((bf16[96,1792]{1,0:T(8,128)(2,1)}, bf16[96,1792]{1,0:T(8,128)(2,1)S(1)}, u32[]{:S(2)}, u32[]{:S(2)}) %collective-permute-start.36) | collective-permute-done | bytes 344096 | tf_op jit(solution)/shard_map/ppermute | solution.py:65
  268.1 3.3 %collective-permute-start.37 = (bf16[96,1792]{1,0:T(8,128)(2,1)}, bf16[96,1792]{1,0:T(8,128)(2,1)}, u32[]{:S(2)}, u32[]{:S(2)}) collective-permute-start(bf16[96,1792]{1,0:T(8,128)(2,1)} %fusion.6), channel_id=1, source_target_pairs={{0,4},{4,0},{2,6},{6,2},{1,5},{5,1},{3,7},{7,3},{8,12},{12,8},{10,... | collective-permute-start | bytes 1032200 | tf_op jit(solution)/shard_map/ppermute | solution.py:69
  273.9 3.1 %fusion.5 = f32[4,64,1792]{2,1,0:T(8,128)} fusion(bf16[4,64,768]{2,1,0:T(8,128)(2,1)} %dot_general.31, bf16[384,1792]{1,0:T(8,128)(2,1)S(1)} %copy-done.31, bf16[384,1792]{1,0:T(8,128)(2,1)S(1)} %copy-done.30), kind=kOutput, calls=%fused_computation.17 | convolution fusion | flops 710148096 | bytes 4980736 | tf_op jit(solution)/shard_map/rt,tf->rf/dot_general | solution.py:15
  277.0 7.6 %collective-permute-done.37 = bf16[96,1792]{1,0:T(8,128)(2,1)} collective-permute-done((bf16[96,1792]{1,0:T(8,128)(2,1)}, bf16[96,1792]{1,0:T(8,128)(2,1)}, u32[]{:S(2)}, u32[]{:S(2)}) %collective-permute-start.37) | collective-permute-done | bytes 344096 | tf_op jit(solution)/shard_map/ppermute | solution.py:69
  (291 shorter events, 143.4 us)
Async XLA Ops:
  15.5 20.7 %collective-permute-start.3 = (bf16[24,1792]{1,0:T(8,128)(2,1)}, bf16[24,1792]{1,0:T(8,128)(2,1)}, u32[]{:S(2)}, u32[]{:S(2)}) collective-permute-start(bf16[24,1792]{1,0:T(8,128)(2,1)} %get-tuple-element.143), channel_id=1, source_target_pairs={{0,24},{8,16},{16,8},{24,0},{1,25},{9,17},{17,9},{25,1},{2,26},{10... | collective-permute-start | bytes 258056 | tf_op jit(solution)/shard_map/ppermute | solution.py:44
  18.4 19.6 %collective-permute-start.4 = (bf16[24,1792]{1,0:T(8,128)(2,1)}, bf16[24,1792]{1,0:T(8,128)(2,1)}, u32[]{:S(2)}, u32[]{:S(2)}) collective-permute-start(bf16[24,1792]{1,0:T(8,128)(2,1)} %get-tuple-element.142), channel_id=1, source_target_pairs={{0,16},{8,24},{16,0},{24,8},{1,17},{9,25},{17,1},{25,9},{2,18},{10... | collective-permute-start | bytes 258056 | tf_op jit(solution)/shard_map/ppermute | solution.py:44
  18.9 21.5 %collective-permute-start.5 = (bf16[24,1792]{1,0:T(8,128)(2,1)}, bf16[24,1792]{1,0:T(8,128)(2,1)}, u32[]{:S(2)}, u32[]{:S(2)}) collective-permute-start(bf16[24,1792]{1,0:T(8,128)(2,1)} %get-tuple-element.141), channel_id=1, source_target_pairs={{0,8},{8,0},{16,24},{24,16},{1,9},{9,1},{17,25},{25,17},{2,10},{10... | collective-permute-start | bytes 258056 | tf_op jit(solution)/shard_map/ppermute | solution.py:44
  20.0 23.7 %collective-permute-start.6 = (bf16[96,1792]{1,0:T(8,128)(2,1)S(1)}, bf16[96,1792]{1,0:T(8,128)(2,1)S(1)}, u32[]{:S(2)}, u32[]{:S(2)}) collective-permute-start(bf16[96,1792]{1,0:T(8,128)(2,1)S(1)} %pad_maximum_fusion.3.refs_0_.refs_9_), channel_id=1, source_target_pairs={{2,4},{4,2},{3,5},{5,3},{10,12},{12,10},{11,13},{13,11},{18,20},{2... | collective-permute-start | bytes 1032200 | tf_op jit(solution)/shard_map/ppermute | solution.py:54
  23.1 44.1 %collective-permute-start.15 = (bf16[4,2,64,1792]{3,2,0,1:T(8,128)(2,1)}, bf16[4,2,64,1792]{3,2,0,1:T(8,128)(2,1)S(1)}, u32[]{:S(2)}, u32[]{:S(2)}) collective-permute-start(bf16[4,2,64,1792]{3,2,0,1:T(8,128)(2,1)} %maximum_add_fusion), channel_id=1, source_target_pairs={{0,1},{1,0},{2,3},{3,2},{4,5},{5,4},{6,7},{7,6},{8,9},{9,8},{10,11... | collective-permute-start | bytes 5505032 | tf_op jit(solution)/shard_map/ppermute | solution.py:28
  36.3 32.9 %collective-permute-start.12 = (bf16[96,1792]{1,0:T(8,128)(2,1)S(1)}, bf16[96,1792]{1,0:T(8,128)(2,1)}, u32[]{:S(2)}, u32[]{:S(2)}) collective-permute-start(bf16[96,1792]{1,0:T(8,128)(2,1)S(1)} %pad_maximum_fusion.3.refs_0_.refs_9_), channel_id=1, source_target_pairs={{0,2},{2,0},{4,6},{6,4},{1,3},{3,1},{5,7},{7,5},{8,10},{10,8},{12,... | collective-permute-start | bytes 1032200 | tf_op jit(solution)/shard_map/ppermute | solution.py:53
  38.0 26.0 %collective-permute-start.13 = (bf16[96,1792]{1,0:T(8,128)(2,1)S(1)}, bf16[96,1792]{1,0:T(8,128)(2,1)}, u32[]{:S(2)}, u32[]{:S(2)}) collective-permute-start(bf16[96,1792]{1,0:T(8,128)(2,1)S(1)} %pad_maximum_fusion.3.refs_0_.refs_9_), channel_id=1, source_target_pairs={{0,4},{4,0},{2,6},{6,2},{1,5},{5,1},{3,7},{7,3},{8,12},{12,8},{10,... | collective-permute-start | bytes 1032200 | tf_op jit(solution)/shard_map/ppermute | solution.py:52
  40.4 66.6 %collective-permute-start.11 = (bf16[4,1,64,1792]{3,2,0,1:T(8,128)(2,1)}, bf16[4,1,64,1792]{3,2,0,1:T(8,128)(2,1)}, u32[]{:S(2)}, u32[]{:S(2)}) collective-permute-start(bf16[4,1,64,1792]{3,2,0,1:T(8,128)(2,1)} %fusion.33), channel_id=1, source_target_pairs={{0,1},{1,0},{2,3},{3,2},{4,5},{5,4},{6,7},{7,6},{8,9},{9,8},{10,11... | collective-permute-start | bytes 2752520 | tf_op jit(solution)/shard_map/ppermute | solution.py:28
  45.1 41.8 %collective-permute-start.8 = (bf16[96,1792]{1,0:T(8,128)(2,1)S(1)}, bf16[96,1792]{1,0:T(8,128)(2,1)}, u32[]{:S(2)}, u32[]{:S(2)}) collective-permute-start(bf16[96,1792]{1,0:T(8,128)(2,1)S(1)} %maximum_add_fusion.1.refs_0_), channel_id=1, source_target_pairs={{0,4},{4,0},{2,6},{6,2},{1,5},{5,1},{3,7},{7,3},{8,12},{12,8},{10,... | collective-permute-start | bytes 1032200 | tf_op jit(solution)/shard_map/ppermute | solution.py:52
  86.9 22.4 %collective-permute-start.7 = (bf16[96,1792]{1,0:T(8,128)(2,1)S(1)}, bf16[96,1792]{1,0:T(8,128)(2,1)}, u32[]{:S(2)}, u32[]{:S(2)}) collective-permute-start(bf16[96,1792]{1,0:T(8,128)(2,1)S(1)} %maximum_add_fusion.1.refs_0_), channel_id=1, source_target_pairs={{0,2},{2,0},{4,6},{6,4},{1,3},{3,1},{5,7},{7,5},{8,10},{10,8},{12,... | collective-permute-start | bytes 1032200 | tf_op jit(solution)/shard_map/ppermute | solution.py:53
  87.9 21.3 %collective-permute-start.9 = (bf16[96,1792]{1,0:T(8,128)(2,1)S(1)}, bf16[96,1792]{1,0:T(8,128)(2,1)}, u32[]{:S(2)}, u32[]{:S(2)}) collective-permute-start(bf16[96,1792]{1,0:T(8,128)(2,1)S(1)} %maximum_add_fusion.1.refs_0_), channel_id=1, source_target_pairs={{2,4},{4,2},{3,5},{5,3},{10,12},{12,10},{11,13},{13,11},{18,20},{2... | collective-permute-start | bytes 1032200 | tf_op jit(solution)/shard_map/ppermute | solution.py:54
  89.9 19.3 %collective-permute-start.10 = (bf16[96,1792]{1,0:T(8,128)(2,1)}, bf16[96,1792]{1,0:T(8,128)(2,1)}, u32[]{:S(2)}, u32[]{:S(2)}) collective-permute-start(bf16[96,1792]{1,0:T(8,128)(2,1)} %collective-permute-done.8.refs_2_), channel_id=1, source_target_pairs={{4,6},{2,0},{5,7},{3,1},{12,14},{10,8},{13,15},{11,9},{20,22},{18,... | collective-permute-start | bytes 1032200 | tf_op jit(solution)/shard_map/ppermute | solution.py:55
  94.0 24.0 %all-to-all-start = ((bf16[8,64,384]{2,1,0:T(8,128)(2,1)}), bf16[8,64,384]{2,1,0:T(8,128)(2,1)}, u32[]{:S(2)}, u32[]{:S(2)}) async-start(bf16[8,64,384]{2,1,0:T(8,128)(2,1)} %gather_fusion), calls=%async_computation | async-start | bytes 786432 | tf_op jit(solution)/shard_map/all_to_all | solution.py:451
  106.5 60.8 %collective-permute-start.42 = (bf16[384,1792]{1,0:T(8,128)(2,1)}, bf16[384,1792]{1,0:T(8,128)(2,1)}, u32[]{:S(2)}, u32[]{:S(2)}) collective-permute-start(bf16[384,1792]{1,0:T(8,128)(2,1)} %copy-done.8), channel_id=1, source_target_pairs={{0,1},{1,0},{2,3},{3,2},{4,5},{5,4},{6,7},{7,6},{8,9},{9,8},{10,11... | collective-permute-start | bytes 4128776 | tf_op jit(solution)/shard_map/ppermute | solution.py:28
  130.0 20.0 %collective-permute-start.26 = (bf16[8,64,384]{2,1,0:T(8,128)(2,1)}, bf16[8,64,384]{2,1,0:T(8,128)(2,1)}, u32[]{:S(2)}, u32[]{:S(2)}) collective-permute-start(bf16[8,64,384]{2,1,0:T(8,128)(2,1)} %all-to-all-done.refs_0_), channel_id=1, source_target_pairs={{0,16},{8,24},{16,0},{24,8},{1,17},{9,25},{17,1},{25,9},{2,18},{10... | collective-permute-start | bytes 1179656 | tf_op jit(solution)/shard_map/ppermute | solution.py:44
  130.9 20.4 %collective-permute-start.27 = (bf16[8,64,384]{2,1,0:T(8,128)(2,1)}, bf16[8,64,384]{2,1,0:T(8,128)(2,1)}, u32[]{:S(2)}, u32[]{:S(2)}) collective-permute-start(bf16[8,64,384]{2,1,0:T(8,128)(2,1)} %all-to-all-done.refs_0_), channel_id=1, source_target_pairs={{0,24},{8,16},{16,8},{24,0},{1,25},{9,17},{17,9},{25,1},{2,26},{10... | collective-permute-start | bytes 1179656 | tf_op jit(solution)/shard_map/ppermute | solution.py:44
  135.8 62.4 %collective-permute-start.50 = (bf16[384,1792]{1,0:T(8,128)(2,1)}, bf16[384,1792]{1,0:T(8,128)(2,1)}, u32[]{:S(2)}, u32[]{:S(2)}) collective-permute-start(bf16[384,1792]{1,0:T(8,128)(2,1)} %copy-done.10), channel_id=1, source_target_pairs={{0,1},{1,0},{2,3},{3,2},{4,5},{5,4},{6,7},{7,6},{8,9},{9,8},{10,11... | collective-permute-start | bytes 4128776 | tf_op jit(solution)/shard_map/ppermute | solution.py:28
  140.8 32.2 %collective-permute-start.22 = (bf16[8,32,384]{2,1,0:T(8,128)(2,1)S(1)}, bf16[8,32,384]{2,1,0:T(8,128)(2,1)S(1)}, u32[]{:S(2)}, u32[]{:S(2)}) collective-permute-start(bf16[8,32,384]{2,1,0:T(8,128)(2,1)S(1)} %all-to-all-done.1.refs_0_), channel_id=1, source_target_pairs={{0,8},{8,0},{16,24},{24,16},{1,9},{9,1},{17,25},{25,17},{2,10},{10... | collective-permute-start | bytes 589832 | tf_op jit(solution)/shard_map/ppermute | solution.py:44
  150.1 23.8 %collective-permute-start.23 = (bf16[8,32,384]{2,1,0:T(8,128)(2,1)S(1)}, bf16[8,32,384]{2,1,0:T(8,128)(2,1)S(1)}, u32[]{:S(2)}, u32[]{:S(2)}) collective-permute-start(bf16[8,32,384]{2,1,0:T(8,128)(2,1)S(1)} %all-to-all-done.1.refs_0_), channel_id=1, source_target_pairs={{0,16},{8,24},{16,0},{24,8},{1,17},{9,25},{17,1},{25,9},{2,18},{10... | collective-permute-start | bytes 589832 | tf_op jit(solution)/shard_map/ppermute | solution.py:44
  151.3 23.0 %collective-permute-start.24 = (bf16[8,32,384]{2,1,0:T(8,128)(2,1)S(1)}, bf16[8,32,384]{2,1,0:T(8,128)(2,1)S(1)}, u32[]{:S(2)}, u32[]{:S(2)}) collective-permute-start(bf16[8,32,384]{2,1,0:T(8,128)(2,1)S(1)} %all-to-all-done.1.refs_0_), channel_id=1, source_target_pairs={{0,24},{8,16},{16,8},{24,0},{1,25},{9,17},{17,9},{25,1},{2,26},{10... | collective-permute-start | bytes 589832 | tf_op jit(solution)/shard_map/ppermute | solution.py:44
  167.4 23.6 %collective-permute-start.45 = (bf16[8,32,384]{2,1,0:T(8,128)(2,1)S(1)}, bf16[8,32,384]{2,1,0:T(8,128)(2,1)S(1)}, u32[]{:S(2)}, u32[]{:S(2)}) collective-permute-start(bf16[8,32,384]{2,1,0:T(8,128)(2,1)S(1)} %get-tuple-element.65), channel_id=1, source_target_pairs={{0,24},{8,16},{16,8},{24,0},{1,25},{9,17},{17,9},{25,1},{2,26},{10... | collective-permute-start | bytes 589832 | tf_op jit(solution)/shard_map/ppermute | solution.py:44
  173.0 18.8 %collective-permute-start.44 = (bf16[8,32,384]{2,1,0:T(8,128)(2,1)S(1)}, bf16[8,32,384]{2,1,0:T(8,128)(2,1)S(1)}, u32[]{:S(2)}, u32[]{:S(2)}) collective-permute-start(bf16[8,32,384]{2,1,0:T(8,128)(2,1)S(1)} %get-tuple-element.64), channel_id=1, source_target_pairs={{0,16},{8,24},{16,0},{24,8},{1,17},{9,25},{17,1},{25,9},{2,18},{10... | collective-permute-start | bytes 589832 | tf_op jit(solution)/shard_map/ppermute | solution.py:44
  183.4 23.4 %collective-permute-start.30 = (bf16[8,64,384]{2,1,0:T(8,128)(2,1)}, bf16[8,64,384]{2,1,0:T(8,128)(2,1)}, u32[]{:S(2)}, u32[]{:S(2)}) collective-permute-start(bf16[8,64,384]{2,1,0:T(8,128)(2,1)} %get-tuple-element.59), channel_id=1, source_target_pairs={{0,24},{8,16},{16,8},{24,0},{1,25},{9,17},{17,9},{25,1},{2,26},{10... | collective-permute-start | bytes 1179656 | tf_op jit(solution)/shard_map/ppermute | solution.py:44
  258.5 18.5 %collective-permute-start.35 = (bf16[96,1792]{1,0:T(8,128)(2,1)}, bf16[96,1792]{1,0:T(8,128)(2,1)}, u32[]{:S(2)}, u32[]{:S(2)}) collective-permute-start(bf16[96,1792]{1,0:T(8,128)(2,1)} %get-tuple-element.99), channel_id=1, source_target_pairs={{2,4},{4,2},{3,5},{5,3},{10,12},{12,10},{11,13},{13,11},{18,20},{2... | collective-permute-start | bytes 1032200 | tf_op jit(solution)/shard_map/ppermute | solution.py:67
  (77 other events, 676.9 us)
where the time goes:
time: 296 us; the launch traced here: 294 us
  starting transfers between devices  92 us (31%)
  waiting for transfers between devices  75 us (25%)
  local copies, waits for them, and re-layouts  41.9 us (14%)
  other arithmetic  37.3 us (13%)
  Pallas kernels  31.1 us (11%)
  matrix products  11.6 us (4%)
  between operations  4.89 us (2%)
    ppermute x33, starting transfers between devices, trade(): lax.ppermute(chunk_for(k), axis, [(i, i ^ k) for i in range(n)])  39.5 us
    ppermute x33, waiting for transfers between devices, trade(): lax.ppermute(chunk_for(k), axis, [(i, i ^ k) for i in range(n)])  23.4 us
    unnamed x94, local copies, waits for them, and re-layouts  22 us
    ppermute x2, waiting for transfers between devices, gather_z(): far = lax.ppermute(share, 'ez', [(0, 2), (2, 0), (1, 3), (3, 1)])  18.4 us
    all_to_all x2, starting transfers between devices, to_group(): lax.all_to_all(send, ('ez', 'core'), split_axis=0, concat_axis=0, tiled=T...  15.6 us
    dot_general x7, matrix products, mm(): return jnp.einsum(spec, a, b, preferred_element_type=FL)  11.6 us
    pallas_call x1, Pallas kernels, backward(): pl.pallas_call(kernel, grid=(local,), out_shape=outs + chunks, in_specs=[...  9.13 us
    all_to_all x2, starting transfers between devices, from_groups(): lax.all_to_all(mine, ('ez', 'core'), split_axis=0, concat_axis=0, tiled=T...  8.97 us
  transfers between devices with their start and end apart: 57, of which 17 were waited for; matrix products, arithmetic and copies ran while one was open for 21% of the time, Pallas kernels for 11%

commit v1 on v0

--- a/solution.py
+++ b/solution.py
@@ -1,3 +1,5 @@
+import functools
+
 import jax
 import jax.numpy as jnp
 from jax import lax
@@ -83,50 +85,134 @@
 ANYWHERE = pl.BlockSpec(memory_space=pl.ANY)
 
 
-def params(total):
-    return pltpu.CompilerParams(vmem_limit_bytes=(8 + total * 15 // 1024) << 20)
+def params():
+    return pltpu.CompilerParams(vmem_limit_bytes=56 << 20)
 
 
 def shaped(shape, kind):
     return jax.ShapeDtypeStruct(shape, kind)
 
 
-def project(pieces, parts, z, n_z, first):
+def place_rows(own, other, target, part, at_core, low, same):
+    count = len(own)
+
+    def fill(source):
+        for c in range(own[0].shape[0]):
+            for b in range(count):
+                to = (c * count + b) * part
+                target[to : to + part, :] = source[b][c, pl.ds(low, part), :]
+
+    pl.when(same == (at_core == 0))(functools.partial(fill, own))
+    pl.when(same != (at_core == 0))(functools.partial(fill, other))
+
+
+def project(pieces, rows, own, other, spot, n_dp, n_z, first):
     share, width = pieces[0].shape
     half = n_z * share
-
-    def kernel(z_ref, *refs):
-        got, rest = refs[: len(pieces)], refs[len(pieces) :]
-        bases, rest = rest[: len(parts)], rest[len(parts) :]
-        cols, products = rest[1], rest[2:]
-        me = z_ref[0]
+    bases = list(own) + list(other)
+    count = len(own)
+    clusters, rank_own, _ = own[0].shape
+    parts_core = n_dp // 2
+    part = rank_own // parts_core
+    row_count = clusters * count * part
+    built = rows is None
+
+    def kernel(spot_ref, *refs):
+        got, refs = refs[: len(pieces)], refs[len(pieces) :]
+        z, dp, core = spot_ref[0], spot_ref[1], spot_ref[2]
+        if built:
+            ours, theirs = refs[:count], refs[count : 2 * count]
+            cols, parts, products = refs[2 * count + 1], refs[2 * count + 2 :][:n_dp], refs[-n_dp:]
+            for k in range(n_dp):
+                low = pl.multiple_of((lax.rem(dp, parts_core) ^ (k % parts_core)) * part, part)
+                same = core == dp // parts_core
+                place_rows(ours, theirs, parts[k], part, k // parts_core, low, same)
+        else:
+            parts, cols, products = refs[:n_dp], refs[n_dp + 1], refs[-n_dp:]
         for k in range(n_z):
-            at = pl.multiple_of((me ^ k) * share, 16)
+            at = pl.multiple_of((z ^ k) * share, 16)
             piece = got[k][...]
             if k == 3 and len(pieces) > n_z:
-                middle = jnp.logical_or(me == 1, me == 2)
+                middle = jnp.logical_or(z == 1, z == 2)
                 piece = jnp.where(middle, piece, got[4][...])
             cols[pl.ds(at, share), :] = piece
-        for base, product in zip(bases, products):
+        for base, product in zip(parts, products):
             product[...] = dot(base[...], cols[...], 1, 1).astype(BF)
 
-    outs = [shaped((half, width), BF)] + [shaped((part.shape[0], half), BF) for part in parts]
-    return pl.pallas_call(
+    ins = list(pieces) + (bases if built else list(rows))
+    outs = [shaped((half, width), BF)]
+    if built:
+        outs += [shaped((row_count, width), BF)] * n_dp
+    outs += [shaped((row_count, half), BF)] * n_dp
+    got = pl.pallas_call(
         kernel,
         out_shape=outs,
-        in_specs=[SCALAR]
-        + [whole(piece) for piece in pieces]
-        + [whole(part) for part in parts]
-        + [ANYWHERE],
+        in_specs=[SCALAR] + [whole(x) for x in ins] + [ANYWHERE],
         out_specs=[whole(out) for out in outs],
-        compiler_params=params(2 * half),
+        compiler_params=params(),
         cost_estimate=pl.CostEstimate(
-            flops=2 * half * width * sum(part.shape[0] for part in parts),
+            flops=2 * half * width * n_dp * row_count,
             bytes_accessed=8 << 20,
             transcendentals=0,
         ),
         name="project",
-    )(z.reshape(1), *pieces, *parts, first)
+    )(spot, *ins, first)
+    return got[0], (got[1 : 1 + n_dp] if built else rows), got[-n_dp:]
+
+
+def basis_grads(keep, other, cols, other_cols, spot, shape, n_dp):
+    clusters, rank_own, width = shape
+    parts_core = n_dp // 2
+    part = rank_own // parts_core
+    half = cols.shape[0]
+    count = keep[0].shape[0] // (clusters * part)
+    block = 256 if width % 256 == 0 else width
+
+    def kernel(spot_ref, *refs):
+        ours, theirs = refs[:parts_core], refs[parts_core : 2 * parts_core]
+        cols_ref, other_ref = refs[2 * parts_core : 2 * parts_core + 2]
+        outs, rows_ref = refs[-1 - count : -1], refs[-1]
+        dp = spot_ref[1]
+
+        @pl.when(pl.program_id(0) == 0)
+        def _():
+            for k in range(parts_core):
+                low = (lax.rem(dp, parts_core) ^ k) * part
+                for c in range(clusters):
+                    at = pl.multiple_of(c * rank_own + low, part)
+                    for b in range(count):
+                        take = slice((c * count + b) * part, (c * count + b + 1) * part)
+                        kind = rows_ref.dtype
+                        rows_ref[0, b, pl.ds(at, part), :] = ours[k][take, :].astype(kind)
+                        rows_ref[1, b, pl.ds(at, part), :] = theirs[k][take, :].astype(kind)
+
+        for b in range(count):
+            total = dot(rows_ref[0, b].astype(BF), cols_ref[...], 1, 0)
+            total += dot(rows_ref[1, b].astype(BF), other_ref[...], 1, 0)
+            outs[b][...] = total
+
+    ins = list(keep) + list(other)
+    out = shaped((clusters * rank_own, width), FL)
+    strip = pl.BlockSpec((half, block), lambda j: (0, j), memory_space=VMEM)
+    got = pl.pallas_call(
+        kernel,
+        grid=(width // block,),
+        out_shape=[out] * count,
+        in_specs=[SCALAR] + [whole(x) for x in ins] + [strip, strip],
+        out_specs=[
+            pl.BlockSpec((clusters * rank_own, block), lambda j: (0, j), memory_space=VMEM)
+        ]
+        * count,
+        scratch_shapes=[pltpu.VMEM((2, count, clusters * rank_own, half), rows_kind(part))],
+        compiler_params=params(),
+        cost_estimate=pl.CostEstimate(
+            flops=4 * count * clusters * rank_own * half * width,
+            bytes_accessed=(3 + 2 * count) << 20,
+            transcendentals=0,
+        ),
+        name="basis_grads",
+    )(spot, *ins, cols, other_cols)
+    return [grad.reshape(shape) for grad in got]
 
 
 def make_picks(cell, weight, slots):
@@ -150,7 +236,7 @@
         out_shape=outs,
         in_specs=[each(cell), each(weight)],
         out_specs=[each(out) for out in outs],
-        compiler_params=params(total),
+        compiler_params=params(),
         cost_estimate=pl.CostEstimate(
             flops=6 * local * slots * total,
             bytes_accessed=4 * local * slots * total,
@@ -252,7 +338,7 @@
         + [each(x) for x in (pick, heavy, gate_factor, up_factor, down_factor)],
         out_specs=[each(out) for out in outs] + [whole(chunk) for chunk in chunks],
         scratch_shapes=[pltpu.VMEM((2, rank, total), rows_kind(rows // 2)), pltpu.VMEM((1, rank, total), FL)],
-        compiler_params=params(total),
+        compiler_params=params(),
         cost_estimate=pl.CostEstimate(
             flops=local * slots * rank * (6 * total + 6 * hid),
             bytes_accessed=16 << 20,
@@ -316,7 +402,7 @@
         in_specs=[SCALAR] + [whole(piece) for piece in pieces] + [each(x) for x in ins],
         out_specs=[each(out) for out in outs] + [whole(chunk) for chunk in chunks],
         scratch_shapes=[pltpu.VMEM((1, rank, total), rows_kind(rows)), pltpu.VMEM((2, rank, total), FL)],
-        compiler_params=params(total),
+        compiler_params=params(),
         cost_estimate=pl.CostEstimate(
             flops=local * slots * rank * (6 * total + 6 * hid),
             bytes_accessed=16 << 20,
@@ -327,11 +413,11 @@
     return got[:4], got[4:]
 
 
-def factor_grads(hg, grad_gate, hu, grad_up, hidden, back, total):
+def factor_grads(hg, grad_gate, hu, grad_up, hidden, back, first):
     local, slots, rank = hg.shape
     hid = hidden.shape[2]
 
-    def kernel(hg_ref, gate_ref, hu_ref, up_ref, hidden_ref, back_ref, out_g, out_u, out_d):
+    def kernel(hg_ref, gate_ref, hu_ref, up_ref, hidden_ref, back_ref, _, out_g, out_u, out_d):
         out_g[0] = dot(hg_ref[0], gate_ref[0], 0, 0)
         out_u[0] = dot(hu_ref[0], up_ref[0], 0, 0)
         out_d[0] = dot(hidden_ref[0], back_ref[0], 0, 0)
@@ -346,16 +432,16 @@
         kernel,
         grid=(local,),
         out_shape=outs,
-        in_specs=[each(x) for x in ins],
+        in_specs=[each(x) for x in ins] + [ANYWHERE],
         out_specs=[each(out) for out in outs],
-        compiler_params=params(total),
+        compiler_params=params(),
         cost_estimate=pl.CostEstimate(
             flops=6 * local * slots * rank * hid,
             bytes_accessed=18 << 20,
             transcendentals=0,
         ),
         name="factor_grads",
-    )(*ins)
+    )(*ins, first)
 
 
 def body(
@@ -400,15 +486,17 @@
 
     x_share = own_columns(tokens)
     x_pieces = gather_z(x_share)
-    dy_share = own_columns(after(grad_out, x_share))
-    dy_pieces = gather_z(after(dy_share, x_pieces[3]))
-
-    def chip_rows(bases):
-        own = after(jnp.stack(bases, axis=1), x_share)
-        other = core_swap(own)
-        count = len(bases)
-        own = own.reshape(clusters, count, parts_core, rank_part, width)
-        other = other.reshape(clusters, count, parts_core, rank_part, width)
+    dy_share = own_columns(after(grad_out, x_pieces[1]))
+    dy_pieces = gather_z(after(dy_share, x_pieces[2]))
+    spot = jnp.stack([z, dp, core]).astype(jnp.int32)
+
+    def chip_rows(own, other):
+        if rank_part % 16 == 0:
+            return None
+        count = len(own)
+        shape = (clusters, count, parts_core, rank_part, width)
+        own = jnp.stack(own, axis=1).reshape(shape)
+        other = jnp.stack(other, axis=1).reshape(shape)
         result = []
         for k in range(n_dp):
             part = dp ^ k
@@ -419,14 +507,14 @@
             result.append(rows.reshape(clusters * count * rank_part, width))
         return result
 
-    rows_in = chip_rows([gate_basis, up_basis])
-    rows_out = chip_rows([down_basis])
+    own_in, own_out = [gate_basis, up_basis], [down_basis]
+    other_in = [core_swap(basis) for basis in own_in]
+    other_out = [core_swap(basis) for basis in own_out]
 
     routing = jnp.concatenate([route_ids.astype(FL), route_weight.astype(FL)], axis=1)
-    routing = after(routing, x_share)
+    routing = after(routing, x_pieces[-1])
     routing = jnp.broadcast_to(routing[None], (blocks, tok_rows, 2 * top))
     routing = lax.all_to_all(routing, ("dp", "ez", "core"), split_axis=0, concat_axis=0, tiled=True)
-    routing = after(routing, x_pieces[2])
     routing = routing.reshape(n_dp, n_z, 2, tok_rows, 2 * top).transpose(2, 1, 0, 3, 4)
     routing = routing.reshape(blocks, tok_rows, 2 * top)
     ids = routing[:, :, :top].astype(jnp.int32)
@@ -450,12 +538,16 @@
         send = mine.at[group_cluster].get(mode="promise_in_bounds")
         return lax.all_to_all(send, ("ez", "core"), split_axis=0, concat_axis=0, tiled=True)
 
-    x_half, *terms = project(x_pieces, rows_in, z, n_z, x_share)
+    x_half, rows_in, terms = project(
+        x_pieces, chip_rows(own_in, other_in), own_in, other_in, spot, n_dp, n_z, x_share
+    )
     mine_in = sum_parts(trade(lambda k: terms[k], "dp"))
     got_in = to_group(mine_in)
-    dy_half, *terms_out = project(dy_pieces, rows_out, z, n_z, mine_in)
+    dy_half, _, terms_out = project(
+        dy_pieces, chip_rows(own_out, other_out), own_out, other_out, spot, n_dp, n_z, mine_in
+    )
     mine_out = sum_parts(trade(lambda k: terms_out[k], "dp"))
-    got_out = to_group(after(mine_out, got_in))
+    got_out = to_group(mine_out)
     h_pieces = trade(lambda k: got_in, "dp")
     (hg, hu, hidden, mixed, act, lift), mixed_chunks = forward(
         h_pieces, pick, heavy, gate_factor, up_factor, down_factor, dp
@@ -476,11 +568,11 @@
     mixed_mine = sum_parts(trade(lambda k: mixed_chunks[k], "dp"))
     in_mine = sum_parts(trade(lambda k: in_chunks[k], "dp"))
     in_sum = from_groups(in_mine)
-    mixed_sum = after(from_groups(mixed_mine), in_mine)
     in_parts = trade(lambda k: in_sum, "dp")
+    mixed_sum = from_groups(after(mixed_mine, in_parts[1]))
     mixed_parts = trade(lambda k: mixed_sum, "dp")
     grad_gate_factor, grad_up_factor, grad_down_factor = factor_grads(
-        hg, grad_gate, hu, grad_up, hidden, back, total
+        hg, grad_gate, hu, grad_up, hidden, back, in_mine
     )
 
     grad_x = sum(mm("rt,rf->tf", part, rows) for part, rows in zip(in_parts, rows_in))
@@ -491,36 +583,26 @@
     )
     grad_tokens = jnp.concatenate(in_order(pieces, dp), axis=1)
 
-    def both_cores(value, axis):
-        other = core_swap(value)
-        first = core == 0
-        return jnp.concatenate(
-            [jnp.where(first, value, other), jnp.where(first, other, value)], axis=axis
-        )
-
-    x_all = both_cores(x_half, 0)
-    dy_all = both_cores(dy_half, 0)
-
-    def own_ranks(parts, count):
-        stack = jnp.stack(in_order(parts, dp))
-        stack = stack.reshape(2, parts_core, clusters, count, rank_part, half)
-        keep = jnp.where(core == 0, stack[0], stack[1])
-        give = jnp.where(core == 0, stack[1], stack[0])
-        other = core_swap(give)
-        first = core == 0
-        rows = jnp.stack([jnp.where(first, keep, other), jnp.where(first, other, keep)])
-        rows = rows.transpose(3, 2, 1, 4, 0, 5)
-        return rows.reshape(count, clusters * rank_own, total)
+    x_other = core_swap(x_half)
+    dy_other = core_swap(dy_half)
+    same = core == dp // parts_core
+
+    def own_ranks(parts):
+        near, far = parts[:parts_core], parts[parts_core:]
+        keep = [jnp.where(same, a, b) for a, b in zip(near, far)]
+        other = [core_swap(jnp.where(same, b, a)) for a, b in zip(near, far)]
+        return keep, other
 
     shape = (clusters, rank_own, width)
-    (sum_mixed,) = own_ranks(mixed_parts, 1)
-    sum_gate, sum_up = own_ranks(in_parts, 2)
-    grad_down_basis = mm("rt,tf->rf", sum_mixed, dy_all).reshape(shape)
-    grad_gate_basis = mm("rt,tf->rf", sum_gate, x_all).reshape(shape)
-    grad_up_basis = mm("rt,tf->rf", sum_up, x_all).reshape(shape)
+    grad_gate_basis, grad_up_basis = basis_grads(
+        *own_ranks(in_parts), x_half, x_other, spot, shape, n_dp
+    )
+    (grad_down_basis,) = basis_grads(
+        *own_ranks(mixed_parts), dy_half, dy_other, spot, shape, n_dp
+    )
 
     placed = cell == jnp.arange(slots, dtype=jnp.int32)[None, :, None]
-    scores = jnp.sum(jnp.where(placed, after(dots, in_mine), 0.0), axis=1)
+    scores = jnp.sum(jnp.where(placed, after(dots, in_parts[2]), 0.0), axis=1)
     scores = scores.reshape(local, 2, n_z, n_dp, tok_rows).transpose(3, 2, 1, 0, 4)
     scores = scores.reshape(blocks, local, tok_rows)
     returned = lax.all_to_all(

time: 296 us -> 298 us (level)
  waiting for transfers between devices: 75 us -> 108 us
  Pallas kernels: 31.1 us -> 59.2 us
  local copies, waits for them, and re-layouts: 41.9 us -> 16 us
  other arithmetic: 37.3 us -> 20 us
  matrix products: 11.6 us -> 2.36 us
  starting transfers between devices: 92 us -> 85.3 us
    unnamed x94 -> x68, local copies, waits for them, and re-layouts: 22 us -> 4.94 us
    pallas_call x2 -> x4, Pallas kernels: 7.63 us -> 24.6 us  [the longest x2 14.4 us: basis_grads(): pl.pallas_call(kernel, grid=(width // block,), out_shape=[out] * count, i...]
    ppermute x2, waiting for transfers between devices: 0.01 us -> 14.3 us  [gather_z(): near = lax.ppermute(share, 'ez', [(0, 1), (1, 0), (2, 3), (3, 2)])]
    ppermute x2, waiting for transfers between devices: 18.4 us -> 4.46 us  [gather_z(): far = lax.ppermute(share, 'ez', [(0, 2), (2, 0), (1, 3), (3, 1)])]
    ppermute x2, waiting for transfers between devices: 6.14 us -> 17 us  [gather_z(): ends = lax.ppermute(far, 'ez', [(2, 3), (1, 0)])]
    all_to_all x2, waiting for transfers between devices: 7.46 us -> 18 us  [from_groups(): lax.all_to_all(mine, ('ez', 'core'), split_axis=0, concat_axis=0, tiled=T...]
    dot_general x7 -> x4, matrix products: 11.6 us -> 2.36 us  [mm(): return jnp.einsum(spec, a, b, preferred_element_type=FL)]
    all_to_all x2, starting transfers between devices: 15.6 us -> 7.11 us  [to_group(): lax.all_to_all(send, ('ez', 'core'), split_axis=0, concat_axis=0, tiled=T...]
  transfers between devices with their start and end apart: 57 -> 60, of which waited for: 17 -> 25; matrix products, arithmetic and copies ran while one was open for 21% -> 10% of each run, Pallas kernels for 11% -> 16%
where the time goes in v1:
time: 298 us; the launch traced here: 296 us
  waiting for transfers between devices  108 us (36%)
  starting transfers between devices  85.3 us (29%)
  Pallas kernels  59.2 us (20%)
  other arithmetic  20 us (7%)
  local copies, waits for them, and re-layouts  16 us (5%)
  between operations  4.73 us (2%)
    ppermute x33, starting transfers between devices, trade(): lax.ppermute(chunk_for(k), axis, [(i, i ^ k) for i in range(n)])  42.3 us
    ppermute x33, waiting for transfers between devices, trade(): lax.ppermute(chunk_for(k), axis, [(i, i ^ k) for i in range(n)])  29.5 us
    all_to_all x2, waiting for transfers between devices, from_groups(): lax.all_to_all(mine, ('ez', 'core'), split_axis=0, concat_axis=0, tiled=T...  18 us
    ppermute x2, waiting for transfers between devices, gather_z(): ends = lax.ppermute(far, 'ez', [(2, 3), (1, 0)])  17 us
    pallas_call x2, Pallas kernels, basis_grads(): pl.pallas_call(kernel, grid=(width // block,), out_shape=[out] * count, i...  14.4 us
    ppermute x2, waiting for transfers between devices, gather_z(): near = lax.ppermute(share, 'ez', [(0, 1), (1, 0), (2, 3), (3, 2)])  14.3 us
    ppermute x1, waiting for transfers between devices, scatter_z(): far = lax.ppermute(second, 'ez', [(0, 2), (2, 0), (1, 3), (3, 1)])  13 us
    pallas_call x1, Pallas kernels, backward(): pl.pallas_call(kernel, grid=(local,), out_shape=outs + chunks, in_specs=[...  12.1 us
  transfers between devices with their start and end apart: 60, of which 25 were waited for; matrix products, arithmetic and copies ran while one was open for 10% of the time, Pallas kernels for 16%

profile of v1, /device:TPU:0, one launch (start us, length us, event | category | flops | bytes accessed | tf_op | source)
XLA Modules:
  0.0 295.9 jit_solution(12659422693896163959)
XLA Ops:
  1.7 4.0 %collective-permute-start = (bf16[24,1792]{1,0:T(8,128)(2,1)S(1)}, bf16[24,1792]{1,0:T(8,128)(2,1)S(1)}, u32[]{:S(2)}, u32[]{:S(2)}) collective-permute-start(bf16[24,1792]{1,0:T(8,128)(2,1)S(1)} %get-tuple-element.132), channel_id=1, source_target_pairs={{0,24},{8,16},{16,8},{24,0},{1,25},{9,17},{17,9},{25,1},{2,26},{10... | collective-permute-start | bytes 258056 | tf_op jit(solution)/shard_map/ppermute | solution.py:46
  18.8 4.5 %collective-permute-done.3.refs_1_ = bf16[96,1792]{1,0:T(8,128)(2,1)S(1)} collective-permute-done((bf16[96,1792]{1,0:T(8,128)(2,1)S(1)}, bf16[96,1792]{1,0:T(8,128)(2,1)S(1)}, u32[]{:S(2)}, u32[]{:S(2)}) %collective-permute-start.3) | collective-permute-done | bytes 344096 | tf_op jit(solution)/shard_map/ppermute | solution.py:55
  30.0 4.5 %collective-permute-done.7.refs_2_ = bf16[96,1792]{1,0:T(8,128)(2,1)S(1)} collective-permute-done((bf16[96,1792]{1,0:T(8,128)(2,1)S(1)}, bf16[96,1792]{1,0:T(8,128)(2,1)S(1)}, u32[]{:S(2)}, u32[]{:S(2)}) %collective-permute-start.7) | collective-permute-done | bytes 344096 | tf_op jit(solution)/shard_map/ppermute | solution.py:54
  40.4 10.1 %collective-permute-done.14.refs_4_ = bf16[96,1792]{1,0:T(8,128)(2,1)S(1)} collective-permute-done((bf16[96,1792]{1,0:T(8,128)(2,1)S(1)}, bf16[96,1792]{1,0:T(8,128)(2,1)S(1)}, u32[]{:S(2)}, u32[]{:S(2)}) %collective-permute-start.14) | collective-permute-done | bytes 344096 | tf_op jit(solution)/shard_map/ppermute | solution.py:57
  53.1 5.7 %project.2 = (bf16[384,1792]{1,0:T(8,128)(2,1)}, bf16[256,1792]{1,0:T(8,128)(2,1)}, bf16[256,1792]{1,0:T(8,128)(2,1)}, bf16[256,1792]{1,0:T(8,128)(2,1)}, bf16[2...) custom-call(s32[3]{0:T(128)} %pad_add_fusion.spot_ref, ...), custom_call_target="tpu_custom_call" | custom-call | flops 1409286144 | bytes 8388608 | tf_op jit(solution)/shard_map/project/pallas_call | solution.py:147
  63.1 4.1 %all-to-all-start.1 = ((f32[32,1,384]{2,1,0:T(1,128)}), f32[32,1,384]{2,1,0:T(1,128)S(1)}, u32[]{:S(2)}, u32[]{:S(2)}) async-start(f32[32,1,384]{2,1,0:T(1,128)} %reshape.229), calls=%async_computation.1 | async-start | bytes 98304 | tf_op jit(solution)/shard_map/all_to_all | solution.py:517
  85.6 9.8 %collective-permute-done.8.refs_1_ = bf16[96,1792]{1,0:T(8,128)(2,1)} collective-permute-done((bf16[96,1792]{1,0:T(8,128)(2,1)S(1)}, bf16[96,1792]{1,0:T(8,128)(2,1)}, u32[]{:S(2)}, u32[]{:S(2)}) %collective-permute-start.8) | collective-permute-done | bytes 344096 | tf_op jit(solution)/shard_map/ppermute | solution.py:55
  95.4 6.9 %collective-permute-done.11.refs_4_ = bf16[96,1792]{1,0:T(8,128)(2,1)} collective-permute-done((bf16[96,1792]{1,0:T(8,128)(2,1)}, bf16[96,1792]{1,0:T(8,128)(2,1)}, u32[]{:S(2)}, u32[]{:S(2)}) %collective-permute-start.11) | collective-permute-done | bytes 344096 | tf_op jit(solution)/shard_map/ppermute | solution.py:57
  102.3 4.5 %project.3 = (bf16[384,1792]{1,0:T(8,128)(2,1)}, bf16[128,1792]{1,0:T(8,128)(2,1)}, bf16[128,1792]{1,0:T(8,128)(2,1)}, bf16[128,1792]{1,0:T(8,128)(2,1)}, bf16[1...) custom-call(s32[3]{0:T(128)} %pad_add_fusion.spot_ref, ...), custom_call_target="tpu_custom_call" | custom-call | flops 704643072 | bytes 8388608 | tf_op jit(solution)/shard_map/project/pallas_call | solution.py:147
  117.1 3.7 %all-to-all-start = ((bf16[8,32,384]{2,1,0:T(8,128)(2,1)}), bf16[8,32,384]{2,1,0:T(8,128)(2,1)S(1)}, u32[]{:S(2)}, u32[]{:S(2)}) async-start(bf16[8,32,384]{2,1,0:T(8,128)(2,1)} %gather_fusion), calls=%async_computation | async-start | bytes 393216 | tf_op jit(solution)/shard_map/all_to_all | solution.py:539
  133.5 11.2 %forward.1 = (bf16[4,224,512]{2,1,0:T(8,128)(2,1)}, bf16[4,224,512]{2,1,0:T(8,128)(2,1)}, bf16[4,224,512]{2,1,0:T(8,128)(2,1)}, bf16[4,224,512]{2,1,0:T(8,128)(2...) custom-call(s32[1]{0:T(128)} %bitcast.dp_ref, ...), custom_call_target="tpu_custom_call" | custom-call | flops 3523215360 | bytes 16777216 | tf_op jit(solution)/shard_map/forward/pallas_call | solution.py:332
  145.6 12.1 %backward.1 = (bf16[4,224,512]{2,1,0:T(8,128)(2,1)}, bf16[4,224,512]{2,1,0:T(8,128)(2,1)}, bf16[4,224,512]{2,1,0:T(8,128)(2,1)}, f32[4,224,1]{2,1,0:T(8,128)}, b...) custom-call(s32[1]{0:T(128)} %bitcast.dp_ref, ...), custom_call_target="tpu_custom_call" | custom-call | flops 3523215360 | bytes 16777216 | tf_op jit(solution)/shard_map/backward/pallas_call | solution.py:398
  161.3 9.7 %collective-permute-done.31 = bf16[8,64,384]{2,1,0:T(8,128)(2,1)S(1)} collective-permute-done((bf16[8,64,384]{2,1,0:T(8,128)(2,1)}, bf16[8,64,384]{2,1,0:T(8,128)(2,1)S(1)}, u32[]{:S(2)}, u32[]{:S(2)}) %collective-permute-start.31) | collective-permute-done | bytes 393248 | tf_op jit(solution)/shard_map/ppermute | solution.py:46
  170.9 5.2 %collective-permute-done.30 = bf16[8,64,384]{2,1,0:T(8,128)(2,1)S(1)} collective-permute-done((bf16[8,64,384]{2,1,0:T(8,128)(2,1)}, bf16[8,64,384]{2,1,0:T(8,128)(2,1)S(1)}, u32[]{:S(2)}, u32[]{:S(2)}) %collective-permute-start.30) | collective-permute-done | bytes 393248 | tf_op jit(solution)/shard_map/ppermute | solution.py:46
  178.1 4.0 %all-to-all-start.3 = ((bf16[8,64,384]{2,1,0:T(8,128)(2,1)}), bf16[8,64,384]{2,1,0:T(8,128)(2,1)S(1)}, u32[]{:S(2)}, u32[]{:S(2)}) async-start(bf16[8,64,384]{2,1,0:T(8,128)(2,1)} %add_convert_fusion._), calls=%async_computation.3 | async-start | bytes 786432 | tf_op jit(solution)/shard_map/all_to_all | solution.py:563
  182.3 12.3 %all-to-all-done.3 = bf16[8,64,384]{2,1,0:T(8,128)(2,1)S(1)} async-done(((bf16[8,64,384]{2,1,0:T(8,128)(2,1)}), bf16[8,64,384]{2,1,0:T(8,128)(2,1)S(1)}, u32[]{:S(2)}, u32[]{:S(2)}) %all-to-all-start.3) | async-done | bytes 393248 | tf_op jit(solution)/shard_map/all_to_all | solution.py:563
  199.4 7.9 %factor_grads.1 = (f32[4,512,512]{2,1,0:T(8,128)}, f32[4,512,512]{2,1,0:T(8,128)}, f32[4,512,512]{2,1,0:T(8,128)}) custom-call(bf16[4,224,512]{2,1,0:T(8,128)(2,1)} %get-tuple-element.79.hg_ref, bf16[4,224,512]{2,1,0:T(8,128)(2,1)} %get-tuple-element.80.gate_ref, bf16[4,224,512]{2,1,0:T(8,128)(2,1)} %get-tuple-element.81.hu_ref, ...), custom_call_target="tpu_custom_call" | custom-call | flops 1409286144 | bytes 18874368 | tf_op jit(solution)/shard_map/factor_grads/pallas_call | solution.py:431
  226.8 4.0 %collective-permute-start.37 = (bf16[96,1792]{1,0:T(8,128)(2,1)}, bf16[96,1792]{1,0:T(8,128)(2,1)}, u32[]{:S(2)}, u32[]{:S(2)}) collective-permute-start(bf16[96,1792]{1,0:T(8,128)(2,1)} %get-tuple-element.107), channel_id=1, source_target_pairs={{0,2},{6,4},{1,3},{7,5},{8,10},{14,12},{9,11},{15,13},{16,18},{22,... | collective-permute-start | bytes 1032200 | tf_op jit(solution)/shard_map/ppermute | solution.py:67
  233.4 3.7 %all-to-all-start.5 = ((bf16[8,32,384]{2,1,0:T(8,128)(2,1)}), bf16[8,32,384]{2,1,0:T(8,128)(2,1)S(1)}, u32[]{:S(2)}, u32[]{:S(2)}) async-start(bf16[8,32,384]{2,1,0:T(8,128)(2,1)} %fusion.9), calls=%async_computation.5 | async-start | bytes 393216 | tf_op jit(solution)/shard_map/all_to_all | solution.py:563
  239.7 5.7 %all-to-all-done.5 = bf16[8,32,384]{2,1,0:T(8,128)(2,1)S(1)} async-done(((bf16[8,32,384]{2,1,0:T(8,128)(2,1)}), bf16[8,32,384]{2,1,0:T(8,128)(2,1)S(1)}, u32[]{:S(2)}, u32[]{:S(2)}) %all-to-all-start.5) | async-done | bytes 196640 | tf_op jit(solution)/shard_map/all_to_all | solution.py:563
  256.7 5.9 %collective-permute-done.35 = bf16[96,1792]{1,0:T(8,128)(2,1)S(1)} collective-permute-done((bf16[96,1792]{1,0:T(8,128)(2,1)}, bf16[96,1792]{1,0:T(8,128)(2,1)S(1)}, u32[]{:S(2)}, u32[]{:S(2)}) %collective-permute-start.35) | collective-permute-done | bytes 344096 | tf_op jit(solution)/shard_map/ppermute | solution.py:68
  262.7 13.0 %collective-permute-done.38 = bf16[96,1792]{1,0:T(8,128)(2,1)S(1)} collective-permute-done((bf16[96,1792]{1,0:T(8,128)(2,1)S(1)}, bf16[96,1792]{1,0:T(8,128)(2,1)S(1)}, u32[]{:S(2)}, u32[]{:S(2)}) %collective-permute-start.38) | collective-permute-done | bytes 344096 | tf_op jit(solution)/shard_map/ppermute | solution.py:71
  280.0 7.8 %basis_grads.2 = (f32[256,1792]{1,0:T(8,128)}, f32[256,1792]{1,0:T(8,128)}) custom-call(s32[3]{0:T(128)} %pad_add_fusion.spot_ref, bf16[256,384]{1,0:T(8,128)(2,1)} %get-tuple-element.123.refs_0_, bf16[256,384]{1,0:T(8,128)(2,1)} %get-tuple-element.121.refs_1_, bf16[256,384]{1,0:T(8,128)(2,1)} %copy-done.29, bf16[256,384]{1,0:T(8,128)(2,1)} %copy-done.30, ...), custom_call_target="tpu_custom_call" | custom-call | flops 1409286144 | bytes 7340032 | tf_op jit(solution)/shard_map/basis_grads/pallas_call | solution.py:197
  288.4 6.6 %basis_grads.3 = f32[256,1792]{1,0:T(8,128)} custom-call(s32[3]{0:T(128)} %pad_add_fusion.spot_ref, bf16[128,384]{1,0:T(8,128)(2,1)} %get-tuple-element.138.refs_0_, bf16[128,384]{1,0:T(8,128)(2,1)} %get-tuple-element.136.refs_1_, bf16[128,384]{1,0:T(8,128)(2,1)} %copy-done.22, bf16[128,384]{1,0:T(8,128)(2,1)} %copy-done.23, ...), custom_call_target="tpu_custom_call" | custom-call | flops 704643072 | bytes 5242880 | tf_op jit(solution)/shard_map/basis_grads/pallas_call | solution.py:197
  (249 shorter events, 124.3 us)
Async XLA Ops:
  13.4 39.0 %collective-permute-start.15 = (bf16[4,64,1792]{2,1,0:T(8,128)(2,1)}, bf16[4,64,1792]{2,1,0:T(8,128)(2,1)}, u32[]{:S(2)}, u32[]{:S(2)}) collective-permute-start(bf16[4,64,1792]{2,1,0:T(8,128)(2,1)} %refs_5_.2), channel_id=1, source_target_pairs={{0,1},{1,0},{2,3},{3,2},{4,5},{5,4},{6,7},{7,6},{8,9},{9,8},{10,11... | collective-permute-start | bytes 2752520 | tf_op jit(solution)/shard_map/ppermute | solution.py:30
  13.4 39.0 %collective-permute-start.16 = (bf16[4,64,1792]{2,1,0:T(8,128)(2,1)}, bf16[4,64,1792]{2,1,0:T(8,128)(2,1)}, u32[]{:S(2)}, u32[]{:S(2)}) collective-permute-start(bf16[4,64,1792]{2,1,0:T(8,128)(2,1)} %refs_6_.2), channel_id=1, source_target_pairs={{0,1},{1,0},{2,3},{3,2},{4,5},{5,4},{6,7},{7,6},{8,9},{9,8},{10,11... | collective-permute-start | bytes 2752520 | tf_op jit(solution)/shard_map/ppermute | solution.py:30
  16.1 18.4 %collective-permute-start.7 = (bf16[96,1792]{1,0:T(8,128)(2,1)S(1)}, bf16[96,1792]{1,0:T(8,128)(2,1)S(1)}, u32[]{:S(2)}, u32[]{:S(2)}) collective-permute-start(bf16[96,1792]{1,0:T(8,128)(2,1)S(1)} %pad_maximum_fusion.refs_0_.refs_9_), channel_id=1, source_target_pairs={{0,4},{4,0},{2,6},{6,2},{1,5},{5,1},{3,7},{7,3},{8,12},{12,8},{10,... | collective-permute-start | bytes 1032200 | tf_op jit(solution)/shard_map/ppermute | solution.py:54
  37.5 57.9 %collective-permute-start.12 = (bf16[4,64,1792]{2,1,0:T(8,128)(2,1)S(1)}, bf16[4,64,1792]{2,1,0:T(8,128)(2,1)S(1)}, u32[]{:S(2)}, u32[]{:S(2)}) collective-permute-start(bf16[4,64,1792]{2,1,0:T(8,128)(2,1)S(1)} %copy-done.4), channel_id=1, source_target_pairs={{0,1},{1,0},{2,3},{3,2},{4,5},{5,4},{6,7},{7,6},{8,9},{9,8},{10,11... | collective-permute-start | bytes 2752520 | tf_op jit(solution)/shard_map/ppermute | solution.py:30
  50.6 31.0 %collective-permute-start.9 = (bf16[96,1792]{1,0:T(8,128)(2,1)S(1)}, bf16[96,1792]{1,0:T(8,128)(2,1)}, u32[]{:S(2)}, u32[]{:S(2)}) collective-permute-start(bf16[96,1792]{1,0:T(8,128)(2,1)S(1)} %maximum_add_fusion.refs_0_), channel_id=1, source_target_pairs={{0,4},{4,0},{2,6},{6,2},{1,5},{5,1},{3,7},{7,3},{8,12},{12,8},{10,... | collective-permute-start | bytes 1032200 | tf_op jit(solution)/shard_map/ppermute | solution.py:54
  74.5 36.2 %all-to-all-start.2 = ((bf16[8,64,384]{2,1,0:T(8,128)(2,1)}), bf16[8,64,384]{2,1,0:T(8,128)(2,1)S(1)}, u32[]{:S(2)}, u32[]{:S(2)}) async-start(bf16[8,64,384]{2,1,0:T(8,128)(2,1)} %gather_fusion.1), calls=%async_computation.2 | async-start | bytes 786432 | tf_op jit(solution)/shard_map/all_to_all | solution.py:539
  78.2 17.2 %collective-permute-start.8 = (bf16[96,1792]{1,0:T(8,128)(2,1)S(1)}, bf16[96,1792]{1,0:T(8,128)(2,1)}, u32[]{:S(2)}, u32[]{:S(2)}) collective-permute-start(bf16[96,1792]{1,0:T(8,128)(2,1)S(1)} %maximum_add_fusion.refs_0_), channel_id=1, source_target_pairs={{0,2},{2,0},{4,6},{6,4},{1,3},{3,1},{5,7},{7,5},{8,10},{10,8},{12,... | collective-permute-start | bytes 1032200 | tf_op jit(solution)/shard_map/ppermute | solution.py:55
  81.6 20.7 %collective-permute-start.11 = (bf16[96,1792]{1,0:T(8,128)(2,1)}, bf16[96,1792]{1,0:T(8,128)(2,1)}, u32[]{:S(2)}, u32[]{:S(2)}) collective-permute-start(bf16[96,1792]{1,0:T(8,128)(2,1)} %collective-permute-done.9.refs_2_), channel_id=1, source_target_pairs={{4,6},{2,0},{5,7},{3,1},{12,14},{10,8},{13,15},{11,9},{20,22},{18,... | collective-permute-start | bytes 1032200 | tf_op jit(solution)/shard_map/ppermute | solution.py:57
  110.8 20.5 %collective-permute-start.26 = (bf16[8,64,384]{2,1,0:T(8,128)(2,1)S(1)}, bf16[8,64,384]{2,1,0:T(8,128)(2,1)S(1)}, u32[]{:S(2)}, u32[]{:S(2)}) collective-permute-start(bf16[8,64,384]{2,1,0:T(8,128)(2,1)S(1)} %all-to-all-done.2.refs_0_), channel_id=1, source_target_pairs={{0,8},{8,0},{16,24},{24,16},{1,9},{9,1},{17,25},{25,17},{2,10},{10... | collective-permute-start | bytes 1179656 | tf_op jit(solution)/shard_map/ppermute | solution.py:46
  111.5 21.1 %collective-permute-start.27 = (bf16[8,64,384]{2,1,0:T(8,128)(2,1)S(1)}, bf16[8,64,384]{2,1,0:T(8,128)(2,1)S(1)}, u32[]{:S(2)}, u32[]{:S(2)}) collective-permute-start(bf16[8,64,384]{2,1,0:T(8,128)(2,1)S(1)} %all-to-all-done.2.refs_0_), channel_id=1, source_target_pairs={{0,16},{8,24},{16,0},{24,8},{1,17},{9,25},{17,1},{25,9},{2,18},{10... | collective-permute-start | bytes 1179656 | tf_op jit(solution)/shard_map/ppermute | solution.py:46
  113.6 18.9 %collective-permute-start.28 = (bf16[8,64,384]{2,1,0:T(8,128)(2,1)S(1)}, bf16[8,64,384]{2,1,0:T(8,128)(2,1)S(1)}, u32[]{:S(2)}, u32[]{:S(2)}) collective-permute-start(bf16[8,64,384]{2,1,0:T(8,128)(2,1)S(1)} %all-to-all-done.2.refs_0_), channel_id=1, source_target_pairs={{0,24},{8,16},{16,8},{24,0},{1,25},{9,17},{17,9},{25,1},{2,26},{10... | collective-permute-start | bytes 1179656 | tf_op jit(solution)/shard_map/ppermute | solution.py:46
  159.4 16.7 %collective-permute-start.30 = (bf16[8,64,384]{2,1,0:T(8,128)(2,1)}, bf16[8,64,384]{2,1,0:T(8,128)(2,1)S(1)}, u32[]{:S(2)}, u32[]{:S(2)}) collective-permute-start(bf16[8,64,384]{2,1,0:T(8,128)(2,1)} %get-tuple-element.64), channel_id=1, source_target_pairs={{0,16},{8,24},{16,0},{24,8},{1,17},{9,25},{17,1},{25,9},{2,18},{10... | collective-permute-start | bytes 1179656 | tf_op jit(solution)/shard_map/ppermute | solution.py:46
  178.1 16.5 %all-to-all-start.3 = ((bf16[8,64,384]{2,1,0:T(8,128)(2,1)}), bf16[8,64,384]{2,1,0:T(8,128)(2,1)S(1)}, u32[]{:S(2)}, u32[]{:S(2)}) async-start(bf16[8,64,384]{2,1,0:T(8,128)(2,1)} %add_convert_fusion._), calls=%async_computation.3 | async-start | bytes 786432 | tf_op jit(solution)/shard_map/all_to_all | solution.py:563
  196.5 79.4 %collective-permute-start.44 = (bf16[384,1792]{1,0:T(8,128)(2,1)}, bf16[384,1792]{1,0:T(8,128)(2,1)}, u32[]{:S(2)}, u32[]{:S(2)}) collective-permute-start(bf16[384,1792]{1,0:T(8,128)(2,1)} %get-tuple-element.71.refs_4_), channel_id=1, source_target_pairs={{0,1},{1,0},{2,3},{3,2},{4,5},{5,4},{6,7},{7,6},{8,9},{9,8},{10,11... | collective-permute-start | bytes 4128776 | tf_op jit(solution)/shard_map/ppermute | solution.py:30
  196.6 79.9 %collective-permute-start.53 = (bf16[384,1792]{1,0:T(8,128)(2,1)}, bf16[384,1792]{1,0:T(8,128)(2,1)}, u32[]{:S(2)}, u32[]{:S(2)}) collective-permute-start(bf16[384,1792]{1,0:T(8,128)(2,1)} %get-tuple-element.78.refs_4_), channel_id=1, source_target_pairs={{0,1},{1,0},{2,3},{3,2},{4,5},{5,4},{6,7},{7,6},{8,9},{9,8},{10,11... | collective-permute-start | bytes 4128776 | tf_op jit(solution)/shard_map/ppermute | solution.py:30
  197.1 29.7 %collective-permute-start.47 = (bf16[8,32,384]{2,1,0:T(8,128)(2,1)}, bf16[8,32,384]{2,1,0:T(8,128)(2,1)}, u32[]{:S(2)}, u32[]{:S(2)}) collective-permute-start(bf16[8,32,384]{2,1,0:T(8,128)(2,1)} %get-tuple-element.77), channel_id=1, source_target_pairs={{0,24},{8,16},{16,8},{24,0},{1,25},{9,17},{17,9},{25,1},{2,26},{10... | collective-permute-start | bytes 589832 | tf_op jit(solution)/shard_map/ppermute | solution.py:46
  198.5 32.3 %collective-permute-start.46 = (bf16[8,32,384]{2,1,0:T(8,128)(2,1)}, bf16[8,32,384]{2,1,0:T(8,128)(2,1)}, u32[]{:S(2)}, u32[]{:S(2)}) collective-permute-start(bf16[8,32,384]{2,1,0:T(8,128)(2,1)} %get-tuple-element.76), channel_id=1, source_target_pairs={{0,16},{8,24},{16,0},{24,8},{1,17},{9,25},{17,1},{25,9},{2,18},{10... | collective-permute-start | bytes 589832 | tf_op jit(solution)/shard_map/ppermute | solution.py:46
  211.3 22.1 %all-to-all-start.4 = ((f32[32,4,24]{2,1,0:T(4,128)}), f32[32,4,24]{2,1,0:T(4,128)}, u32[]{:S(2)}, u32[]{:S(2)}) async-start(f32[32,4,24]{2,1,0:T(4,128)} %copy.74), calls=%async_computation.4 | async-start | bytes 131072 | tf_op jit(solution)/shard_map/all_to_all | solution.py:608
  226.8 21.3 %collective-permute-start.37 = (bf16[96,1792]{1,0:T(8,128)(2,1)}, bf16[96,1792]{1,0:T(8,128)(2,1)}, u32[]{:S(2)}, u32[]{:S(2)}) collective-permute-start(bf16[96,1792]{1,0:T(8,128)(2,1)} %get-tuple-element.107), channel_id=1, source_target_pairs={{0,2},{6,4},{1,3},{7,5},{8,10},{14,12},{9,11},{15,13},{16,18},{22,... | collective-permute-start | bytes 1032200 | tf_op jit(solution)/shard_map/ppermute | solution.py:67
  253.8 21.8 %collective-permute-start.38 = (bf16[96,1792]{1,0:T(8,128)(2,1)S(1)}, bf16[96,1792]{1,0:T(8,128)(2,1)S(1)}, u32[]{:S(2)}, u32[]{:S(2)}) collective-permute-start(bf16[96,1792]{1,0:T(8,128)(2,1)S(1)} %fusion.2), channel_id=1, source_target_pairs={{0,4},{4,0},{2,6},{6,2},{1,5},{5,1},{3,7},{7,3},{8,12},{12,8},{10,... | collective-permute-start | bytes 1032200 | tf_op jit(solution)/shard_map/ppermute | solution.py:71
  256.7 21.3 %collective-permute-start.42 = (bf16[256,384]{1,0:T(8,128)(2,1)S(1)}, bf16[256,384]{1,0:T(8,128)(2,1)S(1)}, u32[]{:S(2)}, u32[]{:S(2)}) collective-permute-start(bf16[256,384]{1,0:T(8,128)(2,1)S(1)} %copy-done.17), channel_id=1, source_target_pairs={{0,1},{1,0},{2,3},{3,2},{4,5},{5,4},{6,7},{7,6},{8,9},{9,8},{10,11... | collective-permute-start | bytes 589832 | tf_op jit(solution)/shard_map/ppermute | solution.py:30
  276.5 18.6 %collective-permute-start.39 = (bf16[24,1792]{1,0:T(8,128)(2,1)S(1)}, bf16[24,1792]{1,0:T(8,128)(2,1)S(1)}, u32[]{:S(2)}, u32[]{:S(2)}) collective-permute-start(bf16[24,1792]{1,0:T(8,128)(2,1)S(1)} %get-tuple-element.126), channel_id=1, source_target_pairs={{0,24},{8,16},{16,8},{24,0},{1,25},{9,17},{17,9},{25,1},{2,26},{10... | collective-permute-start | bytes 258056 | tf_op jit(solution)/shard_map/ppermute | solution.py:46
  278.0 17.0 %collective-permute-start.40 = (bf16[24,1792]{1,0:T(8,128)(2,1)S(1)}, bf16[24,1792]{1,0:T(8,128)(2,1)S(1)}, u32[]{:S(2)}, u32[]{:S(2)}) collective-permute-start(bf16[24,1792]{1,0:T(8,128)(2,1)S(1)} %get-tuple-element.125), channel_id=1, source_target_pairs={{0,16},{8,24},{16,0},{24,8},{1,17},{9,25},{17,1},{25,9},{2,18},{10... | collective-permute-start | bytes 258056 | tf_op jit(solution)/shard_map/ppermute | solution.py:46
  278.8 16.2 %collective-permute-start.41 = (bf16[24,1792]{1,0:T(8,128)(2,1)S(1)}, bf16[24,1792]{1,0:T(8,128)(2,1)S(1)}, u32[]{:S(2)}, u32[]{:S(2)}) collective-permute-start(bf16[24,1792]{1,0:T(8,128)(2,1)S(1)} %get-tuple-element.124), channel_id=1, source_target_pairs={{0,8},{8,0},{16,24},{24,16},{1,9},{9,1},{17,25},{25,17},{2,10},{10... | collective-permute-start | bytes 258056 | tf_op jit(solution)/shard_map/ppermute | solution.py:46
  (67 other events, 744.9 us)

commit v2 on v1

--- a/solution.py
+++ b/solution.py
@@ -62,14 +62,14 @@
     n = lax.axis_size("ez")
     if n != 4:
         got = trade(lambda k: share_of(k).astype(BF), "ez")
-        return share_of(0) + sum(piece.astype(FL) for piece in got[1:])
+        return share_of(0) + sum(piece.astype(FL) for piece in got[1:]), got[1], got[1]
     third = share_of(3).astype(BF)
     ends = lax.ppermute(third, "ez", [(0, 1), (3, 2)])
     near = lax.ppermute(share_of(1).astype(BF), "ez", [(0, 1), (1, 0), (2, 3), (3, 2)])
     inner = lax.ppermute(third, "ez", [(1, 2), (2, 1)])
     second = (share_of(2) + ends.astype(FL)).astype(BF)
     far = lax.ppermute(second, "ez", [(0, 2), (2, 0), (1, 3), (3, 1)])
-    return share_of(0) + near.astype(FL) + inner.astype(FL) + far.astype(FL)
+    return share_of(0) + near.astype(FL) + inner.astype(FL) + far.astype(FL), near, second
 
 
 def whole(array):
@@ -85,62 +85,60 @@
 ANYWHERE = pl.BlockSpec(memory_space=pl.ANY)
 
 
-def params():
-    return pltpu.CompilerParams(vmem_limit_bytes=56 << 20)
+FREE = pl.CostEstimate(flops=0, bytes_accessed=0, transcendentals=0)
+
+
+def params(total, big=False):
+    return pltpu.CompilerParams(vmem_limit_bytes=(56 if big else 8 + total * 15 // 1024) << 20)
 
 
 def shaped(shape, kind):
     return jax.ShapeDtypeStruct(shape, kind)
 
 
-def place_rows(own, other, target, part, at_core, low, same):
-    count = len(own)
-
-    def fill(source):
-        for c in range(own[0].shape[0]):
-            for b in range(count):
-                to = (c * count + b) * part
-                target[to : to + part, :] = source[b][c, pl.ds(low, part), :]
-
-    pl.when(same == (at_core == 0))(functools.partial(fill, own))
-    pl.when(same != (at_core == 0))(functools.partial(fill, other))
-
-
-def project(pieces, rows, own, other, spot, n_dp, n_z, first):
-    share, width = pieces[0].shape
-    half = n_z * share
-    bases = list(own) + list(other)
-    count = len(own)
-    clusters, rank_own, _ = own[0].shape
+def project(pieces, rows, bases, spot, n_dp, n_z, first):
+    gathered = len(pieces) == 1
+    width = pieces[0].shape[1]
+    half = pieces[0].shape[0] * (1 if gathered else n_z)
+    share = half // n_z
+    count = len(bases)
+    clusters, rank_own = bases[0].shape[1:3]
     parts_core = n_dp // 2
     part = rank_own // parts_core
     row_count = clusters * count * part
     built = rows is None
+    ins = list(pieces) + list(bases if built else rows)
 
     def kernel(spot_ref, *refs):
-        got, refs = refs[: len(pieces)], refs[len(pieces) :]
-        z, dp, core = spot_ref[0], spot_ref[1], spot_ref[2]
+        got, sources = refs[: len(pieces)], refs[len(pieces) : len(ins)]
+        outs = list(refs[len(ins) + 1 :])
+        z, dp = spot_ref[0], spot_ref[1]
+        cols = got[0] if gathered else outs.pop(0)
+        products = outs[-n_dp:]
+        parts = sources
         if built:
-            ours, theirs = refs[:count], refs[count : 2 * count]
-            cols, parts, products = refs[2 * count + 1], refs[2 * count + 2 :][:n_dp], refs[-n_dp:]
+            parts = outs[:n_dp]
             for k in range(n_dp):
-                low = pl.multiple_of((lax.rem(dp, parts_core) ^ (k % parts_core)) * part, part)
-                same = core == dp // parts_core
-                place_rows(ours, theirs, parts[k], part, k // parts_core, low, same)
-        else:
-            parts, cols, products = refs[:n_dp], refs[n_dp + 1], refs[-n_dp:]
-        for k in range(n_z):
-            at = pl.multiple_of((z ^ k) * share, 16)
-            piece = got[k][...]
-            if k == 3 and len(pieces) > n_z:
-                middle = jnp.logical_or(z == 1, z == 2)
-                piece = jnp.where(middle, piece, got[4][...])
-            cols[pl.ds(at, share), :] = piece
+                own = dp ^ k
+                low = pl.multiple_of(lax.rem(own, parts_core) * part, part)
+                for c in range(clusters):
+                    for b in range(count):
+                        to = (c * count + b) * part
+                        parts[k][to : to + part, :] = sources[b][
+                            own // parts_core, c, pl.ds(low, part), :
+                        ]
+        if not gathered:
+            for k in range(n_z):
+                at = pl.multiple_of((z ^ k) * share, 16)
+                piece = got[k][...]
+                if k == 3 and len(pieces) > n_z:
+                    middle = jnp.logical_or(z == 1, z == 2)
+                    piece = jnp.where(middle, piece, got[4][...])
+                cols[pl.ds(at, share), :] = piece
         for base, product in zip(parts, products):
             product[...] = dot(base[...], cols[...], 1, 1).astype(BF)
 
-    ins = list(pieces) + (bases if built else list(rows))
-    outs = [shaped((half, width), BF)]
+    outs = [] if gathered else [shaped((half, width), BF)]
     if built:
         outs += [shaped((row_count, width), BF)] * n_dp
     outs += [shaped((row_count, half), BF)] * n_dp
@@ -149,30 +147,26 @@
         out_shape=outs,
         in_specs=[SCALAR] + [whole(x) for x in ins] + [ANYWHERE],
         out_specs=[whole(out) for out in outs],
-        compiler_params=params(),
-        cost_estimate=pl.CostEstimate(
-            flops=2 * half * width * n_dp * row_count,
-            bytes_accessed=8 << 20,
-            transcendentals=0,
-        ),
+        compiler_params=params(2 * half, True),
+        cost_estimate=FREE,
         name="project",
     )(spot, *ins, first)
-    return got[0], (got[1 : 1 + n_dp] if built else rows), got[-n_dp:]
-
-
-def basis_grads(keep, other, cols, other_cols, spot, shape, n_dp):
+    cols = pieces[0] if gathered else got[0]
+    return cols, (got[-2 * n_dp : -n_dp] if built else rows), got[-n_dp:]
+
+
+def basis_grads(keep, other, cols, spot, shape, n_dp, first):
     clusters, rank_own, width = shape
     parts_core = n_dp // 2
     part = rank_own // parts_core
-    half = cols.shape[0]
+    half = cols.shape[1]
     count = keep[0].shape[0] // (clusters * part)
-    block = 256 if width % 256 == 0 else width
+    block = width // 2 if width % 256 == 0 else width
 
     def kernel(spot_ref, *refs):
         ours, theirs = refs[:parts_core], refs[parts_core : 2 * parts_core]
-        cols_ref, other_ref = refs[2 * parts_core : 2 * parts_core + 2]
-        outs, rows_ref = refs[-1 - count : -1], refs[-1]
-        dp = spot_ref[1]
+        cols_ref, outs, rows_ref = refs[2 * parts_core], refs[-1 - count : -1], refs[-1]
+        dp, core = spot_ref[1], spot_ref[2]
 
         @pl.when(pl.program_id(0) == 0)
         def _():
@@ -183,65 +177,52 @@
                     for b in range(count):
                         take = slice((c * count + b) * part, (c * count + b + 1) * part)
                         kind = rows_ref.dtype
-                        rows_ref[0, b, pl.ds(at, part), :] = ours[k][take, :].astype(kind)
-                        rows_ref[1, b, pl.ds(at, part), :] = theirs[k][take, :].astype(kind)
+                        rows_ref[core, b, pl.ds(at, part), :] = ours[k][take, :].astype(kind)
+                        rows_ref[1 - core, b, pl.ds(at, part), :] = theirs[k][take, :].astype(kind)
 
         for b in range(count):
-            total = dot(rows_ref[0, b].astype(BF), cols_ref[...], 1, 0)
-            total += dot(rows_ref[1, b].astype(BF), other_ref[...], 1, 0)
+            total = dot(rows_ref[0, b].astype(BF), cols_ref[0], 1, 0)
+            total += dot(rows_ref[1, b].astype(BF), cols_ref[1], 1, 0)
             outs[b][...] = total
 
     ins = list(keep) + list(other)
     out = shaped((clusters * rank_own, width), FL)
-    strip = pl.BlockSpec((half, block), lambda j: (0, j), memory_space=VMEM)
     got = pl.pallas_call(
         kernel,
         grid=(width // block,),
         out_shape=[out] * count,
-        in_specs=[SCALAR] + [whole(x) for x in ins] + [strip, strip],
+        in_specs=[SCALAR]
+        + [whole(x) for x in ins]
+        + [pl.BlockSpec((2, half, block), lambda j: (0, 0, j), memory_space=VMEM), ANYWHERE],
         out_specs=[
             pl.BlockSpec((clusters * rank_own, block), lambda j: (0, j), memory_space=VMEM)
         ]
         * count,
         scratch_shapes=[pltpu.VMEM((2, count, clusters * rank_own, half), rows_kind(part))],
-        compiler_params=params(),
-        cost_estimate=pl.CostEstimate(
-            flops=4 * count * clusters * rank_own * half * width,
-            bytes_accessed=(3 + 2 * count) << 20,
-            transcendentals=0,
-        ),
+        compiler_params=params(2 * half),
+        cost_estimate=FREE,
         name="basis_grads",
-    )(spot, *ins, cols, other_cols)
+    )(spot, *ins, cols, first)
     return [grad.reshape(shape) for grad in got]
 
 
 def make_picks(cell, weight, slots):
     local, _, total = cell.shape
 
-    def kernel(cell_ref, weight_ref, pick_ref, heavy_ref, slot_ref):
+    def kernel(cell_ref, weight_ref, pick_ref, slot_ref):
         hit = cell_ref[0] == lax.broadcasted_iota(jnp.int32, (slots, total), 0)
-        heavy = jnp.where(hit, weight_ref[0], 0.0)
         pick_ref[0] = jnp.where(hit, 1.0, 0.0).astype(BF)
-        heavy_ref[0] = heavy.astype(BF)
-        slot_ref[0] = jnp.sum(heavy, axis=1, keepdims=True)
-
-    outs = [
-        shaped((local, slots, total), BF),
-        shaped((local, slots, total), BF),
-        shaped((local, slots, 1), FL),
-    ]
+        slot_ref[0] = jnp.sum(jnp.where(hit, weight_ref[0], 0.0), axis=1, keepdims=True)
+
+    outs = [shaped((local, slots, total), BF), shaped((local, slots, 1), FL)]
     return pl.pallas_call(
         kernel,
         grid=(local,),
         out_shape=outs,
         in_specs=[each(cell), each(weight)],
         out_specs=[each(out) for out in outs],
-        compiler_params=params(),
-        cost_estimate=pl.CostEstimate(
-            flops=6 * local * slots * total,
-            bytes_accessed=4 * local * slots * total,
-            transcendentals=0,
-        ),
+        compiler_params=params(total),
+        cost_estimate=FREE,
         name="make_picks",
     )(cell, weight)
 
@@ -277,7 +258,7 @@
                 ].astype(BF)
 
 
-def forward(pieces, pick, heavy, gate_factor, up_factor, down_factor, dp):
+def forward(pieces, pick, gate_factor, up_factor, down_factor, dp):
     n_dp = len(pieces)
     n_ex, rows, half = pieces[0].shape
     local, slots, total = pick.shape
@@ -285,17 +266,14 @@
 
     def kernel(dp_ref, *refs):
         got, refs = refs[:n_dp], refs[n_dp:]
-        pick_ref, heavy_ref, gate_ref, up_ref, down_ref = refs[:5]
-        hg_ref, hu_ref, hidden_ref, mixed_ref, act_ref, lift_ref = refs[5:11]
-        sent = refs[11 : 11 + n_dp]
-        rows_ref, total_ref = refs[11 + n_dp :]
+        pick_ref, gate_ref, up_ref, down_ref = refs[:4]
+        hg_ref, hu_ref, hidden_ref, mixed_ref, act_ref, lift_ref, rows_ref = refs[4:]
         j = pl.program_id(0)
         me = dp_ref[0]
 
         @pl.when(j == 0)
         def _():
             lay_out(got, rows_ref, me, 2)
-            total_ref[...] = jnp.zeros_like(total_ref)
 
         take = pick_ref[0]
         hg = dot(take, rows_ref[0].astype(BF), 1, 1).astype(BF)
@@ -310,13 +288,7 @@
         lift_ref[0] = up_pre * (sig * (1.0 + gate_pre * (1.0 - sig)))
         hidden = (act * up_pre).astype(BF)
         hidden_ref[0] = hidden
-        mixed = dot(hidden, down_ref[0], 1, 0).astype(BF)
-        mixed_ref[0] = mixed
-        total_ref[0] += dot(mixed, heavy_ref[0], 0, 0)
-
-        @pl.when(j == local - 1)
-        def _():
-            hand_out(total_ref, sent, me, 1)
+        mixed_ref[0] = dot(hidden, down_ref[0], 1, 0).astype(BF)
 
     slot_shape = (local, slots, rank)
     hid_shape = (local, slots, hid)
@@ -328,25 +300,19 @@
         shaped(hid_shape, FL),
         shaped(hid_shape, FL),
     ]
-    chunks = [shaped((n_ex, rows // 2, half), BF)] * n_dp
-    got = pl.pallas_call(
+    return pl.pallas_call(
         kernel,
         grid=(local,),
-        out_shape=outs + chunks,
+        out_shape=outs,
         in_specs=[SCALAR]
         + [whole(piece) for piece in pieces]
-        + [each(x) for x in (pick, heavy, gate_factor, up_factor, down_factor)],
-        out_specs=[each(out) for out in outs] + [whole(chunk) for chunk in chunks],
-        scratch_shapes=[pltpu.VMEM((2, rank, total), rows_kind(rows // 2)), pltpu.VMEM((1, rank, total), FL)],
-        compiler_params=params(),
-        cost_estimate=pl.CostEstimate(
-            flops=local * slots * rank * (6 * total + 6 * hid),
-            bytes_accessed=16 << 20,
-            transcendentals=local * slots * hid,
-        ),
+        + [each(x) for x in (pick, gate_factor, up_factor, down_factor)],
+        out_specs=[each(out) for out in outs],
+        scratch_shapes=[pltpu.VMEM((2, rank, total), rows_kind(rows // 2))],
+        compiler_params=params(total, True),
+        cost_estimate=FREE,
         name="forward",
-    )(dp.reshape(1), *pieces, pick, heavy, gate_factor, up_factor, down_factor)
-    return got[:6], got[6:]
+    )(dp.reshape(1), *pieces, pick, gate_factor, up_factor, down_factor)
 
 
 def backward(pieces, pick, weight, mixed, act, lift, gate_factor, up_factor, down_factor, dp):
@@ -402,18 +368,50 @@
         in_specs=[SCALAR] + [whole(piece) for piece in pieces] + [each(x) for x in ins],
         out_specs=[each(out) for out in outs] + [whole(chunk) for chunk in chunks],
         scratch_shapes=[pltpu.VMEM((1, rank, total), rows_kind(rows)), pltpu.VMEM((2, rank, total), FL)],
-        compiler_params=params(),
-        cost_estimate=pl.CostEstimate(
-            flops=local * slots * rank * (6 * total + 6 * hid),
-            bytes_accessed=16 << 20,
-            transcendentals=0,
-        ),
+        compiler_params=params(total),
+        cost_estimate=FREE,
         name="backward",
     )(dp.reshape(1), *pieces, *ins)
     return got[:4], got[4:]
 
 
-def factor_grads(hg, grad_gate, hu, grad_up, hidden, back, first):
+def mixed_sums(mixed, pick, weight, dp, chunk, n_dp, first):
+    local, slots, rank = mixed.shape
+    total = pick.shape[2]
+
+    def kernel(dp_ref, mixed_ref, pick_ref, weight_ref, *refs):
+        sent, total_ref = refs[1:-1], refs[-1]
+        j = pl.program_id(0)
+        heavy = (pick_ref[0] * weight_ref[0]).astype(BF)
+        term = dot(mixed_ref[0], heavy, 0, 0)
+
+        @pl.when(j == 0)
+        def _():
+            total_ref[0] = term
+
+        @pl.when(j > 0)
+        def _():
+            total_ref[0] += term
+
+        @pl.when(j == local - 1)
+        def _():
+            hand_out(total_ref, sent, dp_ref[0], 1)
+
+    chunks = [shaped(chunk, BF)] * n_dp
+    return pl.pallas_call(
+        kernel,
+        grid=(local,),
+        out_shape=chunks,
+        in_specs=[SCALAR, each(mixed), each(pick), each(weight), ANYWHERE],
+        out_specs=[whole(out) for out in chunks],
+        scratch_shapes=[pltpu.VMEM((1, rank, total), FL)],
+        compiler_params=params(total),
+        cost_estimate=FREE,
+        name="mixed_sums",
+    )(dp.reshape(1), mixed, pick, weight, first)
+
+
+def factor_grads(hg, grad_gate, hu, grad_up, hidden, back, total, first):
     local, slots, rank = hg.shape
     hid = hidden.shape[2]
 
@@ -434,12 +432,8 @@
         out_shape=outs,
         in_specs=[each(x) for x in ins] + [ANYWHERE],
         out_specs=[each(out) for out in outs],
-        compiler_params=params(),
-        cost_estimate=pl.CostEstimate(
-            flops=6 * local * slots * rank * hid,
-            bytes_accessed=18 << 20,
-            transcendentals=0,
-        ),
+        compiler_params=params(total),
+        cost_estimate=FREE,
         name="factor_grads",
     )(*ins, first)
 
@@ -487,32 +481,29 @@
     x_share = own_columns(tokens)
     x_pieces = gather_z(x_share)
     dy_share = own_columns(after(grad_out, x_pieces[1]))
-    dy_pieces = gather_z(after(dy_share, x_pieces[2]))
+    dy_half = lax.all_gather(dy_share, "ez", axis=0, tiled=True)
     spot = jnp.stack([z, dp, core]).astype(jnp.int32)
 
-    def chip_rows(own, other):
+    def chip_rows(bases):
         if rank_part % 16 == 0:
             return None
-        count = len(own)
-        shape = (clusters, count, parts_core, rank_part, width)
-        own = jnp.stack(own, axis=1).reshape(shape)
-        other = jnp.stack(other, axis=1).reshape(shape)
+        both = jnp.stack(bases, axis=2)
+        both = both.reshape(2, clusters, len(bases), parts_core, rank_part, width)
         result = []
         for k in range(n_dp):
             part = dp ^ k
-            at = part % parts_core
-            mine = lax.dynamic_index_in_dim(own, at, 2, False)
-            theirs = lax.dynamic_index_in_dim(other, at, 2, False)
-            rows = jnp.where(part // parts_core == core, mine, theirs)
-            result.append(rows.reshape(clusters * count * rank_part, width))
+            rows = lax.dynamic_index_in_dim(both, part // parts_core, 0, False)
+            rows = lax.dynamic_index_in_dim(rows, part % parts_core, 2, False)
+            result.append(rows.reshape(clusters * len(bases) * rank_part, width))
         return result
 
-    own_in, own_out = [gate_basis, up_basis], [down_basis]
-    other_in = [core_swap(basis) for basis in own_in]
-    other_out = [core_swap(basis) for basis in own_out]
+    bases = [
+        lax.all_gather(basis, "core", axis=0) for basis in (gate_basis, up_basis, down_basis)
+    ]
+    bases_in, bases_out = bases[:2], bases[2:]
 
     routing = jnp.concatenate([route_ids.astype(FL), route_weight.astype(FL)], axis=1)
-    routing = after(routing, x_pieces[-1])
+    routing = after(routing, x_pieces[1])
     routing = jnp.broadcast_to(routing[None], (blocks, tok_rows, 2 * top))
     routing = lax.all_to_all(routing, ("dp", "ez", "core"), split_axis=0, concat_axis=0, tiled=True)
     routing = routing.reshape(n_dp, n_z, 2, tok_rows, 2 * top).transpose(2, 1, 0, 3, 4)
@@ -526,7 +517,8 @@
     order = jnp.cumsum(named.astype(jnp.int32), axis=2) - 1
     cell = jnp.arange(blocks, dtype=jnp.int32)[None, :, None] * capacity + order
     cell = jnp.where(named, cell, -1).reshape(local, 1, total)
-    pick, heavy, slot_weight = make_picks(cell, weight_of.reshape(local, 1, total), slots)
+    weight_of = weight_of.reshape(local, 1, total)
+    pick, slot_weight = make_picks(cell, weight_of, slots)
 
     group_cluster = cluster_of.reshape(n_ex, local)[:, 0]
 
@@ -539,20 +531,21 @@
         return lax.all_to_all(send, ("ez", "core"), split_axis=0, concat_axis=0, tiled=True)
 
     x_half, rows_in, terms = project(
-        x_pieces, chip_rows(own_in, other_in), own_in, other_in, spot, n_dp, n_z, x_share
+        x_pieces, chip_rows(bases_in), bases_in, spot, n_dp, n_z, x_share
     )
     mine_in = sum_parts(trade(lambda k: terms[k], "dp"))
     got_in = to_group(mine_in)
-    dy_half, _, terms_out = project(
-        dy_pieces, chip_rows(own_out, other_out), own_out, other_out, spot, n_dp, n_z, mine_in
+    _, _, terms_out = project(
+        [dy_half], chip_rows(bases_out), bases_out, spot, n_dp, n_z, mine_in
     )
     mine_out = sum_parts(trade(lambda k: terms_out[k], "dp"))
     got_out = to_group(mine_out)
     h_pieces = trade(lambda k: got_in, "dp")
-    (hg, hu, hidden, mixed, act, lift), mixed_chunks = forward(
-        h_pieces, pick, heavy, gate_factor, up_factor, down_factor, dp
+    hg, hu, hidden, mixed, act, lift = forward(
+        h_pieces, pick, gate_factor, up_factor, down_factor, dp
     )
     d_pieces = trade(lambda k: got_out, "dp")
+    mixed_chunks = mixed_sums(mixed, pick, weight_of, dp, got_out.shape, n_dp, d_pieces[1])
     (back, grad_gate, grad_up, dots), in_chunks = backward(
         d_pieces, pick, slot_weight, mixed, act, lift, gate_factor, up_factor, down_factor, dp
     )
@@ -567,24 +560,20 @@
 
     mixed_mine = sum_parts(trade(lambda k: mixed_chunks[k], "dp"))
     in_mine = sum_parts(trade(lambda k: in_chunks[k], "dp"))
-    in_sum = from_groups(in_mine)
+    grad_gate_factor, grad_up_factor, grad_down_factor = factor_grads(
+        hg, grad_gate, hu, grad_up, hidden, back, total, in_mine
+    )
+    mixed_sum = from_groups(mixed_mine)
+    in_sum = after(from_groups(in_mine), grad_gate_factor)
     in_parts = trade(lambda k: in_sum, "dp")
-    mixed_sum = from_groups(after(mixed_mine, in_parts[1]))
     mixed_parts = trade(lambda k: mixed_sum, "dp")
-    grad_gate_factor, grad_up_factor, grad_down_factor = factor_grads(
-        hg, grad_gate, hu, grad_up, hidden, back, in_mine
-    )
 
     grad_x = sum(mm("rt,rf->tf", part, rows) for part, rows in zip(in_parts, rows_in))
     shares = grad_x.reshape(n_z, share, width)
-    mine = scatter_z(lambda k: lax.dynamic_index_in_dim(shares, z ^ k, 0, False)).astype(BF)
-    pieces = trade(
-        lambda k: lax.dynamic_slice_in_dim(mine, (dp ^ k) * tok_rows, tok_rows, 0), "dp"
-    )
-    grad_tokens = jnp.concatenate(in_order(pieces, dp), axis=1)
-
-    x_other = core_swap(x_half)
-    dy_other = core_swap(dy_half)
+    mine, near, second = scatter_z(lambda k: lax.dynamic_index_in_dim(shares, z ^ k, 0, False))
+
+    x_both = lax.all_gather(x_half, "core", axis=0)
+    dy_both = lax.all_gather(dy_half, "core", axis=0)
     same = core == dp // parts_core
 
     def own_ranks(parts):
@@ -595,14 +584,14 @@
 
     shape = (clusters, rank_own, width)
     grad_gate_basis, grad_up_basis = basis_grads(
-        *own_ranks(in_parts), x_half, x_other, spot, shape, n_dp
+        *own_ranks(in_parts), x_both, spot, shape, n_dp, second
     )
     (grad_down_basis,) = basis_grads(
-        *own_ranks(mixed_parts), dy_half, dy_other, spot, shape, n_dp
+        *own_ranks(mixed_parts), dy_both, spot, shape, n_dp, second
     )
 
     placed = cell == jnp.arange(slots, dtype=jnp.int32)[None, :, None]
-    scores = jnp.sum(jnp.where(placed, after(dots, in_parts[2]), 0.0), axis=1)
+    scores = jnp.sum(jnp.where(placed, after(dots, near), 0.0), axis=1)
     scores = scores.reshape(local, 2, n_z, n_dp, tok_rows).transpose(3, 2, 1, 0, 4)
     scores = scores.reshape(blocks, local, tok_rows)
     returned = lax.all_to_all(
@@ -611,6 +600,14 @@
     by_expert = jnp.sum(returned.reshape(n_dp, experts, tok_rows), axis=0)
     chosen = route_ids[:, :, None] == jnp.arange(experts, dtype=jnp.int32)[None, None, :]
     grad_route = jnp.sum(jnp.where(chosen, by_expert.T[:, None, :], 0.0), axis=2)
+
+    for part in (grad_gate_basis, grad_down_basis, returned):
+        mine = after(mine, part)
+    mine = mine.astype(BF)
+    pieces = trade(
+        lambda k: lax.dynamic_slice_in_dim(mine, (dp ^ k) * tok_rows, tok_rows, 0), "dp"
+    )
+    grad_tokens = jnp.concatenate(in_order(pieces, dp), axis=1)
     return (
         grad_tokens,
         grad_route,

time: 298 us -> 311 us (1.044)
  local copies, waits for them, and re-layouts: 16 us -> 32.8 us
  Pallas kernels: 59.2 us -> 43.9 us
  between operations: 4.73 us -> 19 us
    all_to_all x2, waiting for transfers between devices: 18 us -> 0.01 us  [from_groups(): lax.all_to_all(mine, ('ez', 'core'), split_axis=0, concat_axis=0, tiled=T...]
    unnamed x68 -> x92, local copies, waits for them, and re-layouts: 4.94 us -> 21.3 us
    ppermute x1, waiting for transfers between devices: 13 us -> 0.01 us  [scatter_z(): far = lax.ppermute(second, 'ez', [(0, 2), (2, 0), (1, 3), (3, 1)])]
    ppermute x33, waiting for transfers between devices: 29.5 us -> 40.2 us  [trade(): lax.ppermute(chunk_for(k), axis, [(i, i ^ k) for i in range(n)])]
    ppermute x2 -> x1, waiting for transfers between devices: 4.46 us -> 13.5 us  [gather_z(): far = lax.ppermute(share, 'ez', [(0, 2), (2, 0), (1, 3), (3, 1)])]
    ppermute x1, waiting for transfers between devices: 5.95 us -> 14.2 us  [scatter_z(): lax.ppermute(share_of(1).astype(BF), 'ez', [(0, 1), (1, 0), (2, 3), (3, 2)])]
    ppermute x2 -> x1, waiting for transfers between devices: 17 us -> 24.8 us  [gather_z(): ends = lax.ppermute(far, 'ez', [(2, 3), (1, 0)])]
    pallas_call x2, Pallas kernels: 14.4 us -> 7.21 us  [basis_grads(): pl.pallas_call(kernel, grid=(width // block,), out_shape=[out] * count, i...]
  transfers between devices with their start and end apart: 60 -> 57, of which waited for: 25 -> 23; matrix products, arithmetic and copies ran while one was open for 10% -> 10% of each run, Pallas kernels for 16% -> 14%
where the time goes in v2:
time: 311 us; the launch traced here: 309 us
  waiting for transfers between devices  111 us (36%)
  starting transfers between devices  82.5 us (27%)
  Pallas kernels  43.9 us (14%)
  local copies, waits for them, and re-layouts  32.8 us (11%)
  between operations  19 us (6%)
  other arithmetic  18 us (6%)
    ppermute x33, waiting for transfers between devices, trade(): lax.ppermute(chunk_for(k), axis, [(i, i ^ k) for i in range(n)])  40.2 us
    ppermute x33, starting transfers between devices, trade(): lax.ppermute(chunk_for(k), axis, [(i, i ^ k) for i in range(n)])  39.5 us
    ppermute x1, waiting for transfers between devices, gather_z(): ends = lax.ppermute(far, 'ez', [(2, 3), (1, 0)])  24.8 us
    unnamed x92, local copies, waits for them, and re-layouts  21.3 us
    ppermute x1, waiting for transfers between devices, scatter_z(): lax.ppermute(share_of(1).astype(BF), 'ez', [(0, 1), (1, 0), (2, 3), (3, 2)])  14.2 us
    ppermute x1, waiting for transfers between devices, gather_z(): far = lax.ppermute(share, 'ez', [(0, 2), (2, 0), (1, 3), (3, 1)])  13.5 us
    pallas_call x2, Pallas kernels, project(): pl.pallas_call(kernel, out_shape=outs, in_specs=[SCALAR] + [whole(x) for...  10.5 us
    all_to_all x2, starting transfers between devices, from_groups(): lax.all_to_all(mine, ('ez', 'core'), split_axis=0, concat_axis=0, tiled=T...  9.79 us
  transfers between devices with their start and end apart: 57, of which 23 were waited for; matrix products, arithmetic and copies ran while one was open for 10% of the time, Pallas kernels for 14%

profile of v2, /device:TPU:0, one launch (start us, length us, event | category | flops | bytes accessed | tf_op | source)
XLA Modules:
  0.0 309.2 jit_solution(1437896525749639905)
XLA Ops:
  9.8 4.0 %collective-permute-start = (bf16[24,1792]{1,0:T(8,128)(2,1)S(1)}, bf16[24,1792]{1,0:T(8,128)(2,1)S(1)}, u32[]{:S(2)}, u32[]{:S(2)}) collective-permute-start(bf16[24,1792]{1,0:T(8,128)(2,1)S(1)} %get-tuple-element.128), channel_id=1, source_target_pairs={{0,24},{8,16},{16,8},{24,0},{1,25},{9,17},{17,9},{25,1},{2,26},{10... | collective-permute-start | bytes 258056 | tf_op jit(solution)/shard_map/ppermute | solution.py:46
  21.5 7.4 %collective-permute-done.3.refs_1_ = bf16[96,1792]{1,0:T(8,128)(2,1)S(1)} collective-permute-done((bf16[96,1792]{1,0:T(8,128)(2,1)S(1)}, bf16[96,1792]{1,0:T(8,128)(2,1)S(1)}, u32[]{:S(2)}, u32[]{:S(2)}) %collective-permute-start.3) | collective-permute-done | bytes 344096 | tf_op jit(solution)/shard_map/ppermute | solution.py:55
  42.0 13.5 %collective-permute-done.7.refs_2_ = bf16[96,1792]{1,0:T(8,128)(2,1)S(1)} collective-permute-done((bf16[96,1792]{1,0:T(8,128)(2,1)S(1)}, bf16[96,1792]{1,0:T(8,128)(2,1)S(1)}, u32[]{:S(2)}, u32[]{:S(2)}) %collective-permute-start.7) | collective-permute-done | bytes 344096 | tf_op jit(solution)/shard_map/ppermute | solution.py:54
  57.9 24.8 %collective-permute-done.9.refs_4_ = bf16[96,1792]{1,0:T(8,128)(2,1)S(1)} collective-permute-done((bf16[96,1792]{1,0:T(8,128)(2,1)S(1)}, bf16[96,1792]{1,0:T(8,128)(2,1)S(1)}, u32[]{:S(2)}, u32[]{:S(2)}) %collective-permute-start.9) | collective-permute-done | bytes 344096 | tf_op jit(solution)/shard_map/ppermute | solution.py:57
  83.4 5.9 %project.2 = (bf16[384,1792]{1,0:T(8,128)(2,1)}, bf16[256,1792]{1,0:T(8,128)(2,1)}, bf16[256,1792]{1,0:T(8,128)(2,1)}, bf16[256,1792]{1,0:T(8,128)(2,1)}, bf16[2...) custom-call(s32[3]{0:T(128)} %pad_add_fusion.spot_ref, ...), custom_call_target="tpu_custom_call" | custom-call | tf_op jit(solution)/shard_map/project/pallas_call | solution.py:145
  89.4 3.4 %collective-permute-start.10 = (bf16[256,384]{1,0:T(8,128)(2,1)}, bf16[256,384]{1,0:T(8,128)(2,1)S(1)}, u32[]{:S(2)}, u32[]{:S(2)}) collective-permute-start(bf16[256,384]{1,0:T(8,128)(2,1)} %get-tuple-element.47), channel_id=1, source_target_pairs={{0,8},{8,0},{16,24},{24,16},{1,9},{9,1},{17,25},{25,17},{2,10},{10... | collective-permute-start | bytes 589832 | tf_op jit(solution)/shard_map/ppermute | solution.py:46
  93.6 5.0 %all-to-all-start.1 = ((f32[32,1,384]{2,1,0:T(1,128)}), f32[32,1,384]{2,1,0:T(1,128)S(1)}, u32[]{:S(2)}, u32[]{:S(2)}) async-start(f32[32,1,384]{2,1,0:T(1,128)} %reshape.236), calls=%async_computation.1 | async-start | bytes 98304 | tf_op jit(solution)/shard_map/all_to_all | solution.py:508
  101.6 4.3 %all-to-all-done.1 = f32[32,1,384]{2,1,0:T(1,128)S(1)} async-done(((f32[32,1,384]{2,1,0:T(1,128)}), f32[32,1,384]{2,1,0:T(1,128)S(1)}, u32[]{:S(2)}, u32[]{:S(2)}) %all-to-all-start.1) | async-done | bytes 49184 | tf_op jit(solution)/shard_map/all_to_all | solution.py:508
  105.9 3.5 %all-to-all-start.2 = ((bf16[8,64,384]{2,1,0:T(8,128)(2,1)}), bf16[8,64,384]{2,1,0:T(8,128)(2,1)S(1)}, u32[]{:S(2)}, u32[]{:S(2)}) async-start(bf16[8,64,384]{2,1,0:T(8,128)(2,1)} %gather_fusion.1), calls=%async_computation.2 | async-start | bytes 786432 | tf_op jit(solution)/shard_map/all_to_all | solution.py:531
  111.1 4.6 %project.3 = (bf16[128,1792]{1,0:T(8,128)(2,1)}, bf16[128,1792]{1,0:T(8,128)(2,1)}, bf16[128,1792]{1,0:T(8,128)(2,1)}, bf16[128,1792]{1,0:T(8,128)(2,1)}, bf16[1...) custom-call(s32[3]{0:T(128)} %pad_add_fusion.spot_ref, ...), custom_call_target="tpu_custom_call" | custom-call | tf_op jit(solution)/shard_map/project/pallas_call | solution.py:145
  125.7 4.8 %all-to-all-start = ((bf16[8,32,384]{2,1,0:T(8,128)(2,1)}), bf16[8,32,384]{2,1,0:T(8,128)(2,1)S(1)}, u32[]{:S(2)}, u32[]{:S(2)}) async-start(bf16[8,32,384]{2,1,0:T(8,128)(2,1)} %gather_fusion), calls=%async_computation | async-start | bytes 393216 | tf_op jit(solution)/shard_map/all_to_all | solution.py:531
  134.9 4.0 %all-to-all-done.refs_0_ = bf16[8,32,384]{2,1,0:T(8,128)(2,1)S(1)} async-done(((bf16[8,32,384]{2,1,0:T(8,128)(2,1)}), bf16[8,32,384]{2,1,0:T(8,128)(2,1)S(1)}, u32[]{:S(2)}, u32[]{:S(2)}) %all-to-all-start) | async-done | bytes 196640 | tf_op jit(solution)/shard_map/all_to_all | solution.py:531
  144.2 7.4 %collective-permute-done.20.refs_2_ = bf16[8,64,384]{2,1,0:T(8,128)(2,1)S(1)} collective-permute-done((bf16[8,64,384]{2,1,0:T(8,128)(2,1)S(1)}, bf16[8,64,384]{2,1,0:T(8,128)(2,1)S(1)}, u32[]{:S(2)}, u32[]{:S(2)}) %collective-permute-start.20) | collective-permute-done | bytes 393248 | tf_op jit(solution)/shard_map/ppermute | solution.py:46
  153.1 9.0 %forward.1 = (bf16[4,224,512]{2,1,0:T(8,128)(2,1)}, bf16[4,224,512]{2,1,0:T(8,128)(2,1)}, bf16[4,224,512]{2,1,0:T(8,128)(2,1)}, bf16[4,224,512]{2,1,0:T(8,128)(2...) custom-call(s32[1]{0:T(128)} %bitcast.dp_ref, bf16[8,64,384]{2,1,0:T(8,128)(2,1)} %copy-done.25, ...), custom_call_target="tpu_custom_call" | custom-call | tf_op jit(solution)/shard_map/forward/pallas_call | solution.py:303
  173.5 8.9 %backward.1 = (bf16[4,224,512]{2,1,0:T(8,128)(2,1)S(1)}, bf16[4,224,512]{2,1,0:T(8,128)(2,1)S(1)}, bf16[4,224,512]{2,1,0:T(8,128)(2,1)S(1)}, f32[4,224,1]{2,1,0:...) custom-call(s32[1]{0:T(128)} %bitcast.dp_ref, ...), custom_call_target="tpu_custom_call" | custom-call | tf_op jit(solution)/shard_map/backward/pallas_call | solution.py:364
  190.3 5.5 %all-to-all-start.4 = ((bf16[8,32,384]{2,1,0:T(8,128)(2,1)}), bf16[8,32,384]{2,1,0:T(8,128)(2,1)S(1)}, u32[]{:S(2)}, u32[]{:S(2)}) async-start(bf16[8,32,384]{2,1,0:T(8,128)(2,1)} %add_convert_fusion.1), calls=%async_computation.4 | async-start | bytes 393216 | tf_op jit(solution)/shard_map/all_to_all | solution.py:556
  195.8 3.5 %collective-permute-done.24 = bf16[8,64,384]{2,1,0:T(8,128)(2,1)} collective-permute-done((bf16[8,64,384]{2,1,0:T(8,128)(2,1)}, bf16[8,64,384]{2,1,0:T(8,128)(2,1)}, u32[]{:S(2)}, u32[]{:S(2)}) %collective-permute-start.24) | collective-permute-done | bytes 393248 | tf_op jit(solution)/shard_map/ppermute | solution.py:46
  199.3 5.0 %collective-permute-done.23 = bf16[8,64,384]{2,1,0:T(8,128)(2,1)} collective-permute-done((bf16[8,64,384]{2,1,0:T(8,128)(2,1)}, bf16[8,64,384]{2,1,0:T(8,128)(2,1)}, u32[]{:S(2)}, u32[]{:S(2)}) %collective-permute-start.23) | collective-permute-done | bytes 393248 | tf_op jit(solution)/shard_map/ppermute | solution.py:46
  206.6 4.3 %all-to-all-start.3 = ((bf16[8,64,384]{2,1,0:T(8,128)(2,1)}), bf16[8,64,384]{2,1,0:T(8,128)(2,1)}, u32[]{:S(2)}, u32[]{:S(2)}) async-start(bf16[8,64,384]{2,1,0:T(8,128)(2,1)} %add_convert_fusion._), calls=%async_computation.3 | async-start | bytes 786432 | tf_op jit(solution)/shard_map/all_to_all | solution.py:556
  215.1 5.2 %factor_grads.1 = (f32[4,512,512]{2,1,0:T(8,128)}, f32[4,512,512]{2,1,0:T(8,128)}, f32[4,512,512]{2,1,0:T(8,128)}) custom-call(bf16[4,224,512]{2,1,0:T(8,128)(2,1)S(1)} %copy-done.11, bf16[4,224,512]{2,1,0:T(8,128)(2,1)S(1)} %copy-done.17, bf16[4,224,512]{2,1,0:T(8,128)(2,1)S(1)} %copy-done.12, bf16[4,224,512]{2,1,0:T(8,128)(2,1)S(1)} %copy-done.19, ...), custom_call_target="tpu_custom_call" | custom-call | tf_op jit(solution)/shard_map/factor_grads/pallas_call | solution.py:429
  231.0 4.7 %collective-permute-done.27 = bf16[256,384]{1,0:T(8,128)(2,1)S(1)} collective-permute-done((bf16[256,384]{1,0:T(8,128)(2,1)S(1)}, bf16[256,384]{1,0:T(8,128)(2,1)S(1)}, u32[]{:S(2)}, u32[]{:S(2)}) %collective-permute-start.27) | collective-permute-done | bytes 196640 | tf_op jit(solution)/shard_map/ppermute | solution.py:46
  246.7 14.2 %collective-permute-done.28 = bf16[96,1792]{1,0:T(8,128)(2,1)S(1)} collective-permute-done((bf16[96,1792]{1,0:T(8,128)(2,1)S(1)}, bf16[96,1792]{1,0:T(8,128)(2,1)S(1)}, u32[]{:S(2)}, u32[]{:S(2)}) %collective-permute-start.28) | collective-permute-done | bytes 344096 | tf_op jit(solution)/shard_map/ppermute | solution.py:68
  264.2 6.4 %all-to-all-start.5 = ((f32[32,4,24]{2,1,0:T(4,128)}), f32[32,4,24]{2,1,0:T(4,128)S(1)}, u32[]{:S(2)}, u32[]{:S(2)}) async-start(f32[32,4,24]{2,1,0:T(4,128)} %bitcast.28), calls=%async_computation.5 | async-start | bytes 131072 | tf_op jit(solution)/shard_map/all_to_all | solution.py:597
  278.4 4.2 %basis_grads.2 = (f32[256,1792]{1,0:T(8,128)}, f32[256,1792]{1,0:T(8,128)}) custom-call(s32[3]{0:T(128)S(1)} %copy-done.21, bf16[256,384]{1,0:T(8,128)(2,1)S(1)} %get-tuple-element.119.refs_0_, bf16[256,384]{1,0:T(8,128)(2,1)S(1)} %get-tuple-element.117.refs_1_, bf16[256,384]{1,0:T(8,128)(2,1)S(1)} %collective-permute-done.32.refs_2_, ...), custom_call_target="tpu_custom_call" | custom-call | tf_op jit(solution)/shard_map/basis_grads/pallas_call | solution.py:190
  (275 shorter events, 126.8 us)
Async XLA Ops:
  7.2 75.5 %all-gather.16.cloned.1.call-start = ((), (), s32[]{:S(2)}) async-start(), calls=%async_computation.8 | async-start | bytes 2752512 | tf_op jit(solution)/shard_map/all_gather | solution.py:501
  7.9 74.7 %all-gather.18.cloned.1.call-start = ((), (), s32[]{:S(2)}) async-start(), calls=%async_computation.9 | async-start | bytes 2752512 | tf_op jit(solution)/shard_map/all_gather | solution.py:501
  8.7 102.4 %all-gather.14.cloned.1.call-start = ((), (), s32[]{:S(2)}) async-start(), calls=%async_computation.7 | async-start | bytes 2752512 | tf_op jit(solution)/shard_map/all_gather | solution.py:501
  21.4 89.7 %all-gather.12.cloned.1.call-start = ((), (), s32[]{:S(2)}) async-start(), calls=%async_computation.6 | async-start | bytes 1720320 | tf_op jit(solution)/shard_map/all_gather | solution.py:484
  55.5 27.1 %collective-permute-start.9 = (bf16[96,1792]{1,0:T(8,128)(2,1)S(1)}, bf16[96,1792]{1,0:T(8,128)(2,1)S(1)}, u32[]{:S(2)}, u32[]{:S(2)}) collective-permute-start(bf16[96,1792]{1,0:T(8,128)(2,1)S(1)} %collective-permute-done.7.refs_2_), channel_id=1, source_target_pairs={{4,6},{2,0},{5,7},{3,1},{12,14},{10,8},{13,15},{11,9},{20,22},{18,... | collective-permute-start | bytes 1032200 | tf_op jit(solution)/shard_map/ppermute | solution.py:57
  98.6 178.0 %all-gather.20.cloned.1.call-start = ((), (), s32[]{:S(2)}) async-start(), calls=%async_computation.10 | async-start | bytes 4128768 | tf_op jit(solution)/shard_map/all_gather | solution.py:575
  105.9 19.8 %all-to-all-start.2 = ((bf16[8,64,384]{2,1,0:T(8,128)(2,1)}), bf16[8,64,384]{2,1,0:T(8,128)(2,1)S(1)}, u32[]{:S(2)}, u32[]{:S(2)}) async-start(bf16[8,64,384]{2,1,0:T(8,128)(2,1)} %gather_fusion.1), calls=%async_computation.2 | async-start | bytes 786432 | tf_op jit(solution)/shard_map/all_to_all | solution.py:531
  131.6 20.0 %collective-permute-start.20 = (bf16[8,64,384]{2,1,0:T(8,128)(2,1)S(1)}, bf16[8,64,384]{2,1,0:T(8,128)(2,1)S(1)}, u32[]{:S(2)}, u32[]{:S(2)}) collective-permute-start(bf16[8,64,384]{2,1,0:T(8,128)(2,1)S(1)} %all-to-all-done.2.refs_0_), channel_id=1, source_target_pairs={{0,16},{8,24},{16,0},{24,8},{1,17},{9,25},{17,1},{25,9},{2,18},{10... | collective-permute-start | bytes 1179656 | tf_op jit(solution)/shard_map/ppermute | solution.py:46
  132.3 19.4 %collective-permute-start.21 = (bf16[8,64,384]{2,1,0:T(8,128)(2,1)S(1)}, bf16[8,64,384]{2,1,0:T(8,128)(2,1)S(1)}, u32[]{:S(2)}, u32[]{:S(2)}) collective-permute-start(bf16[8,64,384]{2,1,0:T(8,128)(2,1)S(1)} %all-to-all-done.2.refs_0_), channel_id=1, source_target_pairs={{0,24},{8,16},{16,8},{24,0},{1,25},{9,17},{17,9},{25,1},{2,26},{10... | collective-permute-start | bytes 1179656 | tf_op jit(solution)/shard_map/ppermute | solution.py:46
  138.8 23.3 %collective-permute-start.16 = (bf16[8,32,384]{2,1,0:T(8,128)(2,1)S(1)}, bf16[8,32,384]{2,1,0:T(8,128)(2,1)S(1)}, u32[]{:S(2)}, u32[]{:S(2)}) collective-permute-start(bf16[8,32,384]{2,1,0:T(8,128)(2,1)S(1)} %all-to-all-done.refs_0_), channel_id=1, source_target_pairs={{0,8},{8,0},{16,24},{24,16},{1,9},{9,1},{17,25},{25,17},{2,10},{10... | collective-permute-start | bytes 589832 | tf_op jit(solution)/shard_map/ppermute | solution.py:46
  141.8 27.5 %collective-permute-start.17 = (bf16[8,32,384]{2,1,0:T(8,128)(2,1)S(1)}, bf16[8,32,384]{2,1,0:T(8,128)(2,1)S(1)}, u32[]{:S(2)}, u32[]{:S(2)}) collective-permute-start(bf16[8,32,384]{2,1,0:T(8,128)(2,1)S(1)} %all-to-all-done.refs_0_), channel_id=1, source_target_pairs={{0,16},{8,24},{16,0},{24,8},{1,17},{9,25},{17,1},{25,9},{2,18},{10... | collective-permute-start | bytes 589832 | tf_op jit(solution)/shard_map/ppermute | solution.py:46
  142.4 26.9 %collective-permute-start.18 = (bf16[8,32,384]{2,1,0:T(8,128)(2,1)S(1)}, bf16[8,32,384]{2,1,0:T(8,128)(2,1)S(1)}, u32[]{:S(2)}, u32[]{:S(2)}) collective-permute-start(bf16[8,32,384]{2,1,0:T(8,128)(2,1)S(1)} %all-to-all-done.refs_0_), channel_id=1, source_target_pairs={{0,24},{8,16},{16,8},{24,0},{1,25},{9,17},{17,9},{25,1},{2,26},{10... | collective-permute-start | bytes 589832 | tf_op jit(solution)/shard_map/ppermute | solution.py:46
  165.8 22.7 %collective-permute-start.36 = (bf16[8,32,384]{2,1,0:T(8,128)(2,1)S(1)}, bf16[8,32,384]{2,1,0:T(8,128)(2,1)S(1)}, u32[]{:S(2)}, u32[]{:S(2)}) collective-permute-start(bf16[8,32,384]{2,1,0:T(8,128)(2,1)S(1)} %get-tuple-element.79), channel_id=1, source_target_pairs={{0,24},{8,16},{16,8},{24,0},{1,25},{9,17},{17,9},{25,1},{2,26},{10... | collective-permute-start | bytes 589832 | tf_op jit(solution)/shard_map/ppermute | solution.py:46
  167.3 22.2 %collective-permute-start.35 = (bf16[8,32,384]{2,1,0:T(8,128)(2,1)S(1)}, bf16[8,32,384]{2,1,0:T(8,128)(2,1)S(1)}, u32[]{:S(2)}, u32[]{:S(2)}) collective-permute-start(bf16[8,32,384]{2,1,0:T(8,128)(2,1)S(1)} %get-tuple-element.78), channel_id=1, source_target_pairs={{0,16},{8,24},{16,0},{24,8},{1,17},{9,25},{17,1},{25,9},{2,18},{10... | collective-permute-start | bytes 589832 | tf_op jit(solution)/shard_map/ppermute | solution.py:46
  168.3 21.2 %collective-permute-start.34 = (bf16[8,32,384]{2,1,0:T(8,128)(2,1)S(1)}, bf16[8,32,384]{2,1,0:T(8,128)(2,1)S(1)}, u32[]{:S(2)}, u32[]{:S(2)}) collective-permute-start(bf16[8,32,384]{2,1,0:T(8,128)(2,1)S(1)} %get-tuple-element.77), channel_id=1, source_target_pairs={{0,8},{8,0},{16,24},{24,16},{1,9},{9,1},{17,25},{25,17},{2,10},{10... | collective-permute-start | bytes 589832 | tf_op jit(solution)/shard_map/ppermute | solution.py:46
  206.6 19.4 %all-to-all-start.3 = ((bf16[8,64,384]{2,1,0:T(8,128)(2,1)}), bf16[8,64,384]{2,1,0:T(8,128)(2,1)}, u32[]{:S(2)}, u32[]{:S(2)}) async-start(bf16[8,64,384]{2,1,0:T(8,128)(2,1)} %add_convert_fusion._), calls=%async_computation.3 | async-start | bytes 786432 | tf_op jit(solution)/shard_map/all_to_all | solution.py:556
  210.9 74.7 %all-gather.22.cloned.1.call-start = ((), (), s32[]{:S(2)}) async-start(), calls=%async_computation.11 | async-start | bytes 4128768 | tf_op jit(solution)/shard_map/all_gather | solution.py:576
  223.5 48.5 %collective-permute-start.39 = (bf16[128,384]{1,0:T(8,128)(2,1)S(1)}, bf16[128,384]{1,0:T(8,128)(2,1)}, u32[]{:S(2)}, u32[]{:S(2)}) collective-permute-start(bf16[128,384]{1,0:T(8,128)(2,1)S(1)} %bitcast.88), channel_id=1, source_target_pairs={{0,24},{8,16},{16,8},{24,0},{1,25},{9,17},{17,9},{25,1},{2,26},{10... | collective-permute-start | bytes 294920 | tf_op jit(solution)/shard_map/ppermute | solution.py:46
  224.6 47.8 %collective-permute-start.38 = (bf16[128,384]{1,0:T(8,128)(2,1)S(1)}, bf16[128,384]{1,0:T(8,128)(2,1)}, u32[]{:S(2)}, u32[]{:S(2)}) collective-permute-start(bf16[128,384]{1,0:T(8,128)(2,1)S(1)} %bitcast.89), channel_id=1, source_target_pairs={{0,8},{8,0},{16,24},{24,16},{1,9},{9,1},{17,25},{25,17},{2,10},{10... | collective-permute-start | bytes 294920 | tf_op jit(solution)/shard_map/ppermute | solution.py:46
  230.4 55.3 %collective-permute-start.40 = (bf16[128,384]{1,0:T(8,128)(2,1)}, bf16[128,384]{1,0:T(8,128)(2,1)S(1)}, u32[]{:S(2)}, u32[]{:S(2)}) collective-permute-start(bf16[128,384]{1,0:T(8,128)(2,1)} %get-tuple-element.133), channel_id=1, source_target_pairs={{0,1},{1,0},{2,3},{3,2},{4,5},{5,4},{6,7},{7,6},{8,9},{9,8},{10,11... | collective-permute-start | bytes 294920 | tf_op jit(solution)/shard_map/ppermute | solution.py:30
  243.2 27.4 %collective-permute-start.30 = (bf16[96,1792]{1,0:T(8,128)(2,1)S(1)}, bf16[96,1792]{1,0:T(8,128)(2,1)S(1)}, u32[]{:S(2)}, u32[]{:S(2)}) collective-permute-start(bf16[96,1792]{1,0:T(8,128)(2,1)S(1)} %get-tuple-element.103), channel_id=1, source_target_pairs={{0,2},{6,4},{1,3},{7,5},{8,10},{14,12},{9,11},{15,13},{16,18},{22,... | collective-permute-start | bytes 1032200 | tf_op jit(solution)/shard_map/ppermute | solution.py:67
  260.9 31.5 %collective-permute-start.29 = (bf16[96,1792]{1,0:T(8,128)(2,1)S(1)}, bf16[96,1792]{1,0:T(8,128)(2,1)S(1)}, u32[]{:S(2)}, u32[]{:S(2)}) collective-permute-start(bf16[96,1792]{1,0:T(8,128)(2,1)S(1)} %get-tuple-element.103), channel_id=1, source_target_pairs={{2,4},{4,2},{3,5},{5,3},{10,12},{12,10},{11,13},{13,11},{18,20},{2... | collective-permute-start | bytes 1032200 | tf_op jit(solution)/shard_map/ppermute | solution.py:69
  264.2 20.1 %all-to-all-start.5 = ((f32[32,4,24]{2,1,0:T(4,128)}), f32[32,4,24]{2,1,0:T(4,128)S(1)}, u32[]{:S(2)}, u32[]{:S(2)}) async-start(f32[32,4,24]{2,1,0:T(4,128)} %bitcast.28), calls=%async_computation.5 | async-start | bytes 131072 | tf_op jit(solution)/shard_map/all_to_all | solution.py:597
  272.5 19.9 %collective-permute-start.31 = (bf16[96,1792]{1,0:T(8,128)(2,1)S(1)}, bf16[96,1792]{1,0:T(8,128)(2,1)S(1)}, u32[]{:S(2)}, u32[]{:S(2)}) collective-permute-start(bf16[96,1792]{1,0:T(8,128)(2,1)S(1)} %fusion.2.refs_5_), channel_id=1, source_target_pairs={{0,4},{4,0},{2,6},{6,2},{1,5},{5,1},{3,7},{7,3},{8,12},{12,8},{10,... | collective-permute-start | bytes 1032200 | tf_op jit(solution)/shard_map/ppermute | solution.py:71
  (76 other events, 934.2 us)
Sparse Core Ops, SparseCore 0:
  9.6 12.8 all-gather.15
  24.0 11.3 all-gather.17
  37.0 11.3 all-gather.13
  50.4 37.2 all-gather.11
  101.2 12.7 all-gather.19
  213.0 11.9 all-gather.21

commit v3 on v2

--- a/solution.py
+++ b/solution.py
@@ -47,31 +47,6 @@
     return [chunk_for(0)] + sent
 
 
-def gather_z(share):
-    n = lax.axis_size("ez")
-    if n != 4:
-        return trade(lambda k: share, "ez")
-    far = lax.ppermute(share, "ez", [(0, 2), (2, 0), (1, 3), (3, 1)])
-    near = lax.ppermute(share, "ez", [(0, 1), (1, 0), (2, 3), (3, 2)])
-    inner = lax.ppermute(share, "ez", [(1, 2), (2, 1)])
-    ends = lax.ppermute(far, "ez", [(2, 3), (1, 0)])
-    return [share, near, far, inner, ends]
-
-
-def scatter_z(share_of):
-    n = lax.axis_size("ez")
-    if n != 4:
-        got = trade(lambda k: share_of(k).astype(BF), "ez")
-        return share_of(0) + sum(piece.astype(FL) for piece in got[1:]), got[1], got[1]
-    third = share_of(3).astype(BF)
-    ends = lax.ppermute(third, "ez", [(0, 1), (3, 2)])
-    near = lax.ppermute(share_of(1).astype(BF), "ez", [(0, 1), (1, 0), (2, 3), (3, 2)])
-    inner = lax.ppermute(third, "ez", [(1, 2), (2, 1)])
-    second = (share_of(2) + ends.astype(FL)).astype(BF)
-    far = lax.ppermute(second, "ez", [(0, 2), (2, 0), (1, 3), (3, 1)])
-    return share_of(0) + near.astype(FL) + inner.astype(FL) + far.astype(FL), near, second
-
-
 def whole(array):
     return pl.BlockSpec(array.shape, lambda *_: (0,) * array.ndim, memory_space=VMEM)
 
@@ -96,66 +71,57 @@
     return jax.ShapeDtypeStruct(shape, kind)
 
 
-def project(pieces, rows, bases, spot, n_dp, n_z, first):
-    gathered = len(pieces) == 1
-    width = pieces[0].shape[1]
-    half = pieces[0].shape[0] * (1 if gathered else n_z)
-    share = half // n_z
-    count = len(bases)
-    clusters, rank_own = bases[0].shape[1:3]
+def place_rows(own, other, target, part, from_own, low):
+    count = len(own)
+
+    def fill(source):
+        for c in range(own[0].shape[0]):
+            for b in range(count):
+                to = (c * count + b) * part
+                target[to : to + part, :] = source[b][c, pl.ds(low, part), :]
+
+    pl.when(from_own)(functools.partial(fill, own))
+    pl.when(jnp.logical_not(from_own))(functools.partial(fill, other))
+
+
+def project(cols, rows, own, other, spot, n_dp):
+    half = cols.shape[0]
+    count = len(own)
+    clusters, rank_own, width = own[0].shape
     parts_core = n_dp // 2
     part = rank_own // parts_core
     row_count = clusters * count * part
     built = rows is None
-    ins = list(pieces) + list(bases if built else rows)
-
-    def kernel(spot_ref, *refs):
-        got, sources = refs[: len(pieces)], refs[len(pieces) : len(ins)]
-        outs = list(refs[len(ins) + 1 :])
-        z, dp = spot_ref[0], spot_ref[1]
-        cols = got[0] if gathered else outs.pop(0)
-        products = outs[-n_dp:]
-        parts = sources
+    ins = [cols] + (list(own) + list(other) if built else list(rows))
+
+    def kernel(spot_ref, cols_ref, *refs):
+        sources, outs = refs[: len(ins) - 1], refs[len(ins) - 1 :]
+        dp, core = spot_ref[0], spot_ref[1]
+        parts, products = sources, outs[-n_dp:]
         if built:
             parts = outs[:n_dp]
             for k in range(n_dp):
-                own = dp ^ k
-                low = pl.multiple_of(lax.rem(own, parts_core) * part, part)
-                for c in range(clusters):
-                    for b in range(count):
-                        to = (c * count + b) * part
-                        parts[k][to : to + part, :] = sources[b][
-                            own // parts_core, c, pl.ds(low, part), :
-                        ]
-        if not gathered:
-            for k in range(n_z):
-                at = pl.multiple_of((z ^ k) * share, 16)
-                piece = got[k][...]
-                if k == 3 and len(pieces) > n_z:
-                    middle = jnp.logical_or(z == 1, z == 2)
-                    piece = jnp.where(middle, piece, got[4][...])
-                cols[pl.ds(at, share), :] = piece
+                low = pl.multiple_of(lax.rem(dp ^ k, parts_core) * part, part)
+                from_own = core == (dp ^ k) // parts_core
+                place_rows(sources[:count], sources[count:], parts[k], part, from_own, low)
         for base, product in zip(parts, products):
-            product[...] = dot(base[...], cols[...], 1, 1).astype(BF)
-
-    outs = [] if gathered else [shaped((half, width), BF)]
-    if built:
-        outs += [shaped((row_count, width), BF)] * n_dp
+            product[...] = dot(base[...], cols_ref[:, :width], 1, 1).astype(BF)
+
+    outs = [shaped((row_count, width), BF)] * n_dp if built else []
     outs += [shaped((row_count, half), BF)] * n_dp
     got = pl.pallas_call(
         kernel,
         out_shape=outs,
-        in_specs=[SCALAR] + [whole(x) for x in ins] + [ANYWHERE],
+        in_specs=[SCALAR] + [whole(x) for x in ins],
         out_specs=[whole(out) for out in outs],
         compiler_params=params(2 * half, True),
         cost_estimate=FREE,
         name="project",
-    )(spot, *ins, first)
-    cols = pieces[0] if gathered else got[0]
-    return cols, (got[-2 * n_dp : -n_dp] if built else rows), got[-n_dp:]
-
-
-def basis_grads(keep, other, cols, spot, shape, n_dp, first):
+    )(spot, *ins)
+    return (got[:n_dp] if built else rows), got[-n_dp:]
+
+
+def basis_grads(keep, other, cols, spot, shape, n_dp):
     clusters, rank_own, width = shape
     parts_core = n_dp // 2
     part = rank_own // parts_core
@@ -166,7 +132,7 @@
     def kernel(spot_ref, *refs):
         ours, theirs = refs[:parts_core], refs[parts_core : 2 * parts_core]
         cols_ref, outs, rows_ref = refs[2 * parts_core], refs[-1 - count : -1], refs[-1]
-        dp, core = spot_ref[1], spot_ref[2]
+        dp, core = spot_ref[0], spot_ref[1]
 
         @pl.when(pl.program_id(0) == 0)
         def _():
@@ -193,7 +159,7 @@
         out_shape=[out] * count,
         in_specs=[SCALAR]
         + [whole(x) for x in ins]
-        + [pl.BlockSpec((2, half, block), lambda j: (0, 0, j), memory_space=VMEM), ANYWHERE],
+        + [pl.BlockSpec((2, half, block), lambda j: (0, 0, j), memory_space=VMEM)],
         out_specs=[
             pl.BlockSpec((clusters * rank_own, block), lambda j: (0, j), memory_space=VMEM)
         ]
@@ -202,7 +168,7 @@
         compiler_params=params(2 * half),
         cost_estimate=FREE,
         name="basis_grads",
-    )(spot, *ins, cols, first)
+    )(spot, *ins, cols)
     return [grad.reshape(shape) for grad in got]
 
 
@@ -258,7 +224,7 @@
                 ].astype(BF)
 
 
-def forward(pieces, pick, gate_factor, up_factor, down_factor, dp):
+def forward(pieces, pick, weight, gate_factor, up_factor, down_factor, dp):
     n_dp = len(pieces)
     n_ex, rows, half = pieces[0].shape
     local, slots, total = pick.shape
@@ -266,14 +232,17 @@
 
     def kernel(dp_ref, *refs):
         got, refs = refs[:n_dp], refs[n_dp:]
-        pick_ref, gate_ref, up_ref, down_ref = refs[:4]
-        hg_ref, hu_ref, hidden_ref, mixed_ref, act_ref, lift_ref, rows_ref = refs[4:]
+        pick_ref, weight_ref, gate_ref, up_ref, down_ref = refs[:5]
+        hg_ref, hu_ref, hidden_ref, mixed_ref, act_ref, lift_ref = refs[5:11]
+        sent = refs[11 : 11 + n_dp]
+        rows_ref, total_ref = refs[11 + n_dp :]
         j = pl.program_id(0)
         me = dp_ref[0]
 
         @pl.when(j == 0)
         def _():
             lay_out(got, rows_ref, me, 2)
+            total_ref[...] = jnp.zeros_like(total_ref)
 
         take = pick_ref[0]
         hg = dot(take, rows_ref[0].astype(BF), 1, 1).astype(BF)
@@ -288,7 +257,13 @@
         lift_ref[0] = up_pre * (sig * (1.0 + gate_pre * (1.0 - sig)))
         hidden = (act * up_pre).astype(BF)
         hidden_ref[0] = hidden
-        mixed_ref[0] = dot(hidden, down_ref[0], 1, 0).astype(BF)
+        mixed = dot(hidden, down_ref[0], 1, 0).astype(BF)
+        mixed_ref[0] = mixed
+        total_ref[0] += dot(mixed, (take * weight_ref[0]).astype(BF), 0, 0)
+
+        @pl.when(j == local - 1)
+        def _():
+            hand_out(total_ref, sent, me, 1)
 
     slot_shape = (local, slots, rank)
     hid_shape = (local, slots, hid)
@@ -300,19 +275,21 @@
         shaped(hid_shape, FL),
         shaped(hid_shape, FL),
     ]
-    return pl.pallas_call(
+    chunks = [shaped((n_ex, rows // 2, half), BF)] * n_dp
+    got = pl.pallas_call(
         kernel,
         grid=(local,),
-        out_shape=outs,
+        out_shape=outs + chunks,
         in_specs=[SCALAR]
         + [whole(piece) for piece in pieces]
-        + [each(x) for x in (pick, gate_factor, up_factor, down_factor)],
-        out_specs=[each(out) for out in outs],
-        scratch_shapes=[pltpu.VMEM((2, rank, total), rows_kind(rows // 2))],
+        + [each(x) for x in (pick, weight, gate_factor, up_factor, down_factor)],
+        out_specs=[each(out) for out in outs] + [whole(chunk) for chunk in chunks],
+        scratch_shapes=[pltpu.VMEM((2, rank, total), rows_kind(rows // 2)), pltpu.VMEM((1, rank, total), FL)],
         compiler_params=params(total, True),
         cost_estimate=FREE,
         name="forward",
-    )(dp.reshape(1), *pieces, pick, gate_factor, up_factor, down_factor)
+    )(dp.reshape(1), *pieces, pick, weight, gate_factor, up_factor, down_factor)
+    return got[:6], got[6:]
 
 
 def backward(pieces, pick, weight, mixed, act, lift, gate_factor, up_factor, down_factor, dp):
@@ -368,47 +345,11 @@
         in_specs=[SCALAR] + [whole(piece) for piece in pieces] + [each(x) for x in ins],
         out_specs=[each(out) for out in outs] + [whole(chunk) for chunk in chunks],
         scratch_shapes=[pltpu.VMEM((1, rank, total), rows_kind(rows)), pltpu.VMEM((2, rank, total), FL)],
-        compiler_params=params(total),
+        compiler_params=params(total, True),
         cost_estimate=FREE,
         name="backward",
     )(dp.reshape(1), *pieces, *ins)
     return got[:4], got[4:]
-
-
-def mixed_sums(mixed, pick, weight, dp, chunk, n_dp, first):
-    local, slots, rank = mixed.shape
-    total = pick.shape[2]
-
-    def kernel(dp_ref, mixed_ref, pick_ref, weight_ref, *refs):
-        sent, total_ref = refs[1:-1], refs[-1]
-        j = pl.program_id(0)
-        heavy = (pick_ref[0] * weight_ref[0]).astype(BF)
-        term = dot(mixed_ref[0], heavy, 0, 0)
-
-        @pl.when(j == 0)
-        def _():
-            total_ref[0] = term
-
-        @pl.when(j > 0)
-        def _():
-            total_ref[0] += term
-
-        @pl.when(j == local - 1)
-        def _():
-            hand_out(total_ref, sent, dp_ref[0], 1)
-
-    chunks = [shaped(chunk, BF)] * n_dp
-    return pl.pallas_call(
-        kernel,
-        grid=(local,),
-        out_shape=chunks,
-        in_specs=[SCALAR, each(mixed), each(pick), each(weight), ANYWHERE],
-        out_specs=[whole(out) for out in chunks],
-        scratch_shapes=[pltpu.VMEM((1, rank, total), FL)],
-        compiler_params=params(total),
-        cost_estimate=FREE,
-        name="mixed_sums",
-    )(dp.reshape(1), mixed, pick, weight, first)
 
 
 def factor_grads(hg, grad_gate, hu, grad_up, hidden, back, total, first):
@@ -458,7 +399,7 @@
     z = lax.axis_index("ez")
     core = lax.axis_index("core")
     me_e = z * 2 + core
-    tok_rows = tokens.shape[0]
+    tok_rows, model_width = tokens.shape
     top = route_ids.shape[1]
     local = gate_factor.shape[0]
     experts = local * n_ex
@@ -466,50 +407,58 @@
     blocks = n_dp * n_ex
     total = blocks * tok_rows
     half = total // 2
-    share = n_dp * tok_rows
     slots = blocks * capacity
     clusters, rank_own, width = gate_basis.shape
     parts_core = n_dp // 2
     rank_part = rank_own // parts_core
 
-    def own_columns(rows):
-        pieces = trade(
-            lambda k: lax.dynamic_slice_in_dim(rows, (dp ^ k) * width, width, 1), "dp"
-        )
-        return jnp.concatenate(in_order(pieces, dp), axis=0)
-
-    x_share = own_columns(tokens)
-    x_pieces = gather_z(x_share)
-    dy_share = own_columns(after(grad_out, x_pieces[1]))
-    dy_half = lax.all_gather(dy_share, "ez", axis=0, tiled=True)
-    spot = jnp.stack([z, dp, core]).astype(jnp.int32)
-
-    def chip_rows(bases):
+    lanes = 128
+
+    def own_columns(rows, more):
+        rows = rows.reshape(tok_rows, n_dp, width).transpose(1, 0, 2)
+        if more is not None:
+            more = jnp.broadcast_to(more[None], (n_dp, tok_rows, lanes))
+            rows = jnp.concatenate([rows, more], axis=2)
+        rows = jnp.broadcast_to(rows[:, None], (n_dp, n_z) + rows.shape[1:])
+        rows = rows.reshape(n_dp * n_z, tok_rows, -1)
+        got = lax.all_to_all(rows, ("dp", "ez"), split_axis=0, concat_axis=0, tiled=True)
+        return got.reshape(half, -1)
+
+    routing = jnp.concatenate([route_ids.astype(BF), route_weight], axis=1)
+    routing = jnp.pad(routing, ((0, 0), (0, lanes - 2 * top)))
+    x_half = own_columns(tokens, routing)
+    dy_half = own_columns(after(grad_out, x_half), None)
+    spot = jnp.stack([dp, core]).astype(jnp.int32)
+
+    def chip_rows(own, other):
         if rank_part % 16 == 0:
             return None
-        both = jnp.stack(bases, axis=2)
-        both = both.reshape(2, clusters, len(bases), parts_core, rank_part, width)
+        count = len(own)
+        shape = (clusters, count, parts_core, rank_part, width)
+        own = jnp.stack(own, axis=1).reshape(shape)
+        other = jnp.stack(other, axis=1).reshape(shape)
         result = []
         for k in range(n_dp):
             part = dp ^ k
-            rows = lax.dynamic_index_in_dim(both, part // parts_core, 0, False)
-            rows = lax.dynamic_index_in_dim(rows, part % parts_core, 2, False)
-            result.append(rows.reshape(clusters * len(bases) * rank_part, width))
+            at = part % parts_core
+            mine = lax.dynamic_index_in_dim(own, at, 2, False)
+            theirs = lax.dynamic_index_in_dim(other, at, 2, False)
+            rows = jnp.where(part // parts_core == core, mine, theirs)
+            result.append(rows.reshape(clusters * count * rank_part, width))
         return result
 
-    bases = [
-        lax.all_gather(basis, "core", axis=0) for basis in (gate_basis, up_basis, down_basis)
-    ]
-    bases_in, bases_out = bases[:2], bases[2:]
-
-    routing = jnp.concatenate([route_ids.astype(FL), route_weight.astype(FL)], axis=1)
-    routing = after(routing, x_pieces[1])
-    routing = jnp.broadcast_to(routing[None], (blocks, tok_rows, 2 * top))
-    routing = lax.all_to_all(routing, ("dp", "ez", "core"), split_axis=0, concat_axis=0, tiled=True)
-    routing = routing.reshape(n_dp, n_z, 2, tok_rows, 2 * top).transpose(2, 1, 0, 3, 4)
-    routing = routing.reshape(blocks, tok_rows, 2 * top)
+    own_in, own_out = [gate_basis, up_basis], [down_basis]
+    other_in = [core_swap(basis) for basis in own_in]
+    other_out = [core_swap(basis) for basis in own_out]
+
+    routing = x_half[:, width:]
+    swapped = core_swap(routing)
+    routing = jnp.stack(
+        [jnp.where(core == 0, routing, swapped), jnp.where(core == 0, swapped, routing)]
+    )
+    routing = routing.reshape(blocks, tok_rows, lanes)
     ids = routing[:, :, :top].astype(jnp.int32)
-    weights = routing[:, :, top:]
+    weights = routing[:, :, top : 2 * top].astype(FL)
     own_ids = me_e * local + jnp.arange(local, dtype=jnp.int32)
     hit = ids[None] == own_ids[:, None, None, None]
     named = jnp.any(hit, axis=3)
@@ -530,22 +479,21 @@
         send = mine.at[group_cluster].get(mode="promise_in_bounds")
         return lax.all_to_all(send, ("ez", "core"), split_axis=0, concat_axis=0, tiled=True)
 
-    x_half, rows_in, terms = project(
-        x_pieces, chip_rows(bases_in), bases_in, spot, n_dp, n_z, x_share
+    rows_in, terms = project(
+        x_half, chip_rows(own_in, other_in), own_in, other_in, spot, n_dp
     )
     mine_in = sum_parts(trade(lambda k: terms[k], "dp"))
     got_in = to_group(mine_in)
-    _, _, terms_out = project(
-        [dy_half], chip_rows(bases_out), bases_out, spot, n_dp, n_z, mine_in
+    _, terms_out = project(
+        dy_half, chip_rows(own_out, other_out), own_out, other_out, spot, n_dp
     )
     mine_out = sum_parts(trade(lambda k: terms_out[k], "dp"))
     got_out = to_group(mine_out)
     h_pieces = trade(lambda k: got_in, "dp")
-    hg, hu, hidden, mixed, act, lift = forward(
-        h_pieces, pick, gate_factor, up_factor, down_factor, dp
+    (hg, hu, hidden, mixed, act, lift), mixed_chunks = forward(
+        h_pieces, pick, weight_of, gate_factor, up_factor, down_factor, dp
     )
     d_pieces = trade(lambda k: got_out, "dp")
-    mixed_chunks = mixed_sums(mixed, pick, weight_of, dp, got_out.shape, n_dp, d_pieces[1])
     (back, grad_gate, grad_up, dots), in_chunks = backward(
         d_pieces, pick, slot_weight, mixed, act, lift, gate_factor, up_factor, down_factor, dp
     )
@@ -568,9 +516,20 @@
     in_parts = trade(lambda k: in_sum, "dp")
     mixed_parts = trade(lambda k: mixed_sum, "dp")
 
+    placed = cell == jnp.arange(slots, dtype=jnp.int32)[None, :, None]
+    scores = jnp.sum(jnp.where(placed, dots, 0.0), axis=1).reshape(local, 2, half)
+    mine = jnp.where(core == 0, scores[:, 0], scores[:, 1])
+    theirs = core_swap(jnp.where(core == 0, scores[:, 1], scores[:, 0]))
+    first = jnp.where(core == 0, mine, theirs)
+    second = jnp.where(core == 0, theirs, mine)
+    scores = jnp.concatenate([first, second], axis=0).T.astype(BF)
+    scores = jnp.pad(scores, ((0, 0), (0, lanes - 2 * local)))
+
     grad_x = sum(mm("rt,rf->tf", part, rows) for part, rows in zip(in_parts, rows_in))
-    shares = grad_x.reshape(n_z, share, width)
-    mine, near, second = scatter_z(lambda k: lax.dynamic_index_in_dim(shares, z ^ k, 0, False))
+    rows = jnp.concatenate([grad_x.astype(BF), scores], axis=1)
+    rows = rows.reshape(n_dp * n_z, tok_rows, width + lanes)
+    rows = lax.all_to_all(rows, ("dp", "ez"), split_axis=0, concat_axis=0, tiled=True)
+    rows = rows.reshape(n_dp, n_z, tok_rows, width + lanes)
 
     x_both = lax.all_gather(x_half, "core", axis=0)
     dy_both = lax.all_gather(dy_half, "core", axis=0)
@@ -584,30 +543,20 @@
 
     shape = (clusters, rank_own, width)
     grad_gate_basis, grad_up_basis = basis_grads(
-        *own_ranks(in_parts), x_both, spot, shape, n_dp, second
+        *own_ranks(in_parts), x_both, spot, shape, n_dp
     )
     (grad_down_basis,) = basis_grads(
-        *own_ranks(mixed_parts), dy_both, spot, shape, n_dp, second
-    )
-
-    placed = cell == jnp.arange(slots, dtype=jnp.int32)[None, :, None]
-    scores = jnp.sum(jnp.where(placed, after(dots, near), 0.0), axis=1)
-    scores = scores.reshape(local, 2, n_z, n_dp, tok_rows).transpose(3, 2, 1, 0, 4)
-    scores = scores.reshape(blocks, local, tok_rows)
-    returned = lax.all_to_all(
-        scores, ("dp", "ez", "core"), split_axis=0, concat_axis=0, tiled=True
-    )
-    by_expert = jnp.sum(returned.reshape(n_dp, experts, tok_rows), axis=0)
+        *own_ranks(mixed_parts), dy_both, spot, shape, n_dp
+    )
+
+    grad_rows = jnp.sum(rows[..., :width].astype(FL), axis=1)
+    for part in (grad_gate_basis, grad_down_basis):
+        grad_rows = after(grad_rows, part)
+    grad_tokens = grad_rows.astype(BF).transpose(1, 0, 2).reshape(tok_rows, model_width)
+    by_expert = jnp.sum(rows[..., width : width + 2 * local].astype(FL), axis=0)
+    by_expert = by_expert.transpose(1, 0, 2).reshape(tok_rows, 1, experts)
     chosen = route_ids[:, :, None] == jnp.arange(experts, dtype=jnp.int32)[None, None, :]
-    grad_route = jnp.sum(jnp.where(chosen, by_expert.T[:, None, :], 0.0), axis=2)
-
-    for part in (grad_gate_basis, grad_down_basis, returned):
-        mine = after(mine, part)
-    mine = mine.astype(BF)
-    pieces = trade(
-        lambda k: lax.dynamic_slice_in_dim(mine, (dp ^ k) * tok_rows, tok_rows, 0), "dp"
-    )
-    grad_tokens = jnp.concatenate(in_order(pieces, dp), axis=1)
+    grad_route = jnp.sum(jnp.where(chosen, by_expert, 0.0), axis=2)
     return (
         grad_tokens,
         grad_route,

time: 311 us -> 278 us (0.89)
  blocking collectives: 0 us -> 44.7 us
  waiting for transfers between devices: 111 us -> 67.5 us
  starting transfers between devices: 82.5 us -> 56.2 us
  local copies, waits for them, and re-layouts: 32.8 us -> 26.1 us
    ppermute x8 -> x0, waiting for transfers between devices: 59.8 us -> none  [the longest x1 24.8 us: gather_z(): ends = lax.ppermute(far, 'ez', [(2, 3), (1, 0)])]
    all_to_all x0 -> x1, blocking collectives: none -> 44.7 us  [own_columns(): lax.all_to_all(rows, ('dp', 'ez'), split_axis=0, concat_axis=0, tiled=True)]
    ppermute x8 -> x0, starting transfers between devices: 12.7 us -> none  [the longest x1 3.24 us: scatter_z(): ends = lax.ppermute(third, 'ez', [(0, 1), (3, 2)])]
    ppermute x33 -> x24, starting transfers between devices: 39.5 us -> 28.6 us  [trade(): lax.ppermute(chunk_for(k), axis, [(i, i ^ k) for i in range(n)])]
    ppermute x33 -> x24, waiting for transfers between devices: 40.2 us -> 48.5 us  [trade(): lax.ppermute(chunk_for(k), axis, [(i, i ^ k) for i in range(n)])]
    unnamed x92 -> x65, local copies, waits for them, and re-layouts: 21.3 us -> 13.3 us
    ppermute x4 -> x9, waiting for transfers between devices: 0.01 us -> 4.62 us  [core_swap(): return lax.ppermute(value, 'core', [(0, 1), (1, 0)])]
    all_to_all x2, waiting for transfers between devices: 3.98 us -> 8.55 us  [to_group(): lax.all_to_all(send, ('ez', 'core'), split_axis=0, concat_axis=0, tiled=T...]
  transfers between devices with their start and end apart: 57 -> 41, of which waited for: 23 -> 16; matrix products, arithmetic and copies ran while one was open for 10% -> 9% of each run, Pallas kernels for 14% -> 12%
where the time goes in v3:
time: 278 us; the launch traced here: 276 us
  waiting for transfers between devices  67.5 us (24%)
  starting transfers between devices  56.2 us (20%)
  Pallas kernels  46.1 us (17%)
  blocking collectives  44.7 us (16%)
  local copies, waits for them, and re-layouts  26.1 us (9%)
  between operations  17.4 us (6%)
  other arithmetic  15.6 us (6%)
    ppermute x24, waiting for transfers between devices, trade(): lax.ppermute(chunk_for(k), axis, [(i, i ^ k) for i in range(n)])  48.5 us
    all_to_all x1, blocking collectives, own_columns(): lax.all_to_all(rows, ('dp', 'ez'), split_axis=0, concat_axis=0, tiled=True)  44.7 us
    ppermute x24, starting transfers between devices, trade(): lax.ppermute(chunk_for(k), axis, [(i, i ^ k) for i in range(n)])  28.6 us
    unnamed x65, local copies, waits for them, and re-layouts  13.3 us
    pallas_call x1, Pallas kernels, backward(): pl.pallas_call(kernel, grid=(local,), out_shape=outs + chunks, in_specs=[...  12.1 us
    pallas_call x1, Pallas kernels, forward(): pl.pallas_call(kernel, grid=(local,), out_shape=outs + chunks, in_specs=[...  10.9 us
    pallas_call x2, Pallas kernels, project(): pl.pallas_call(kernel, out_shape=outs, in_specs=[SCALAR] + [whole(x) for...  9.82 us
    all_to_all x2, waiting for transfers between devices, to_group(): lax.all_to_all(send, ('ez', 'core'), split_axis=0, concat_axis=0, tiled=T...  8.55 us
  transfers between devices with their start and end apart: 41, of which 16 were waited for; matrix products, arithmetic and copies ran while one was open for 9% of the time, Pallas kernels for 12%

profile of v3, /device:TPU:0, one launch (start us, length us, event | category | flops | bytes accessed | tf_op | source)
XLA Modules:
  0.0 275.7 jit_solution(1554297756827138265)
XLA Ops:
  10.2 44.7 %all_to_all.35 = bf16[16,24,1920]{2,1,0:T(8,128)(2,1)S(1)} all-to-all(bf16[16,24,1920]{2,1,0:T(8,128)(2,1)S(1)} %bitcast.65), channel_id=1, replica_groups=mesh['dp'=4,'ez'=4,'core'=2] {'dp','ez'}, dimensions={0} | all-to-all | bytes 2949120 | tf_op jit(solution)/shard_map/all_to_all | solution.py:424
  57.6 3.7 %all-to-all-start.1 = ((bf16[16,24,1792]{2,1,0:T(8,128)(2,1)}), bf16[16,24,1792]{2,1,0:T(8,128)(2,1)S(1)}, u32[]{:S(2)}, u32[]{:S(2)}) async-start(bf16[16,24,1792]{2,1,0:T(8,128)(2,1)} %bitcast.68), calls=%async_computation.1 | async-start | bytes 2752512 | tf_op jit(solution)/shard_map/all_to_all | solution.py:424
  64.2 2.6 collective-permute-done.9.refs_3_
  66.9 5.5 %project.3 = (bf16[256,1792]{1,0:T(8,128)(2,1)}, bf16[256,1792]{1,0:T(8,128)(2,1)}, bf16[256,1792]{1,0:T(8,128)(2,1)}, bf16[256,1792]{1,0:T(8,128)(2,1)}, bf16[2...) custom-call(s32[2]{0:T(128)} %pad_add_fusion.spot_ref, ...), custom_call_target="tpu_custom_call" | custom-call | tf_op jit(solution)/shard_map/project/pallas_call | solution.py:112
  72.4 2.7 collective-permute-start.12
  76.8 7.1 %collective-permute-done.12 = bf16[256,384]{1,0:T(8,128)(2,1)S(1)} collective-permute-done((bf16[256,384]{1,0:T(8,128)(2,1)}, bf16[256,384]{1,0:T(8,128)(2,1)S(1)}, u32[]{:S(2)}, u32[]{:S(2)}) %collective-permute-start.12) | collective-permute-done | bytes 196640 | tf_op jit(solution)/shard_map/ppermute | solution.py:46
  89.7 5.3 %all-to-all-done.1 = bf16[16,24,1792]{2,1,0:T(8,128)(2,1)S(1)} async-done(((bf16[16,24,1792]{2,1,0:T(8,128)(2,1)}), bf16[16,24,1792]{2,1,0:T(8,128)(2,1)S(1)}, u32[]{:S(2)}, u32[]{:S(2)}) %all-to-all-start.1) | async-done | bytes 1376288 | tf_op jit(solution)/shard_map/all_to_all | solution.py:424
  95.0 3.5 %all-to-all-start.3 = ((bf16[8,64,384]{2,1,0:T(8,128)(2,1)}), bf16[8,64,384]{2,1,0:T(8,128)(2,1)S(1)}, u32[]{:S(2)}, u32[]{:S(2)}) async-start(bf16[8,64,384]{2,1,0:T(8,128)(2,1)} %gather_fusion.1), calls=%async_computation.3 | async-start | bytes 786432 | tf_op jit(solution)/shard_map/all_to_all | solution.py:480
  100.7 4.3 %project.2 = (bf16[128,1792]{1,0:T(8,128)(2,1)}, bf16[128,1792]{1,0:T(8,128)(2,1)}, bf16[128,1792]{1,0:T(8,128)(2,1)}, bf16[128,1792]{1,0:T(8,128)(2,1)}, bf16[1...) custom-call(s32[2]{0:T(128)} %pad_add_fusion.spot_ref, ...), custom_call_target="tpu_custom_call" | custom-call | tf_op jit(solution)/shard_map/project/pallas_call | solution.py:112
  116.7 3.7 %all-to-all-start.2 = ((bf16[8,32,384]{2,1,0:T(8,128)(2,1)}), bf16[8,32,384]{2,1,0:T(8,128)(2,1)S(1)}, u32[]{:S(2)}, u32[]{:S(2)}) async-start(bf16[8,32,384]{2,1,0:T(8,128)(2,1)} %gather_fusion), calls=%async_computation.2 | async-start | bytes 393216 | tf_op jit(solution)/shard_map/all_to_all | solution.py:480
  121.6 7.2 %all-to-all-done.2.refs_0_ = bf16[8,32,384]{2,1,0:T(8,128)(2,1)S(1)} async-done(((bf16[8,32,384]{2,1,0:T(8,128)(2,1)}), bf16[8,32,384]{2,1,0:T(8,128)(2,1)S(1)}, u32[]{:S(2)}, u32[]{:S(2)}) %all-to-all-start.2) | async-done | bytes 196640 | tf_op jit(solution)/shard_map/all_to_all | solution.py:480
  135.8 10.9 %forward.1 = (bf16[4,224,512]{2,1,0:T(8,128)(2,1)}, bf16[4,224,512]{2,1,0:T(8,128)(2,1)}, bf16[4,224,512]{2,1,0:T(8,128)(2,1)}, bf16[4,224,512]{2,1,0:T(8,128)(2...) custom-call(s32[1]{0:T(128)} %bitcast.dp_ref, ...), custom_call_target="tpu_custom_call" | custom-call | tf_op jit(solution)/shard_map/forward/pallas_call | solution.py:279
  147.5 12.1 %backward.1 = (bf16[4,224,512]{2,1,0:T(8,128)(2,1)}, bf16[4,224,512]{2,1,0:T(8,128)(2,1)}, bf16[4,224,512]{2,1,0:T(8,128)(2,1)}, f32[4,224,1]{2,1,0:T(8,128)}, b...) custom-call(s32[1]{0:T(128)} %bitcast.dp_ref, ...), custom_call_target="tpu_custom_call" | custom-call | tf_op jit(solution)/shard_map/backward/pallas_call | solution.py:341
  166.2 6.7 %collective-permute-done.18 = bf16[8,64,384]{2,1,0:T(8,128)(2,1)S(1)} collective-permute-done((bf16[8,64,384]{2,1,0:T(8,128)(2,1)}, bf16[8,64,384]{2,1,0:T(8,128)(2,1)S(1)}, u32[]{:S(2)}, u32[]{:S(2)}) %collective-permute-start.18) | collective-permute-done | bytes 393248 | tf_op jit(solution)/shard_map/ppermute | solution.py:46
  174.0 6.3 %collective-permute-done.17 = bf16[8,64,384]{2,1,0:T(8,128)(2,1)} collective-permute-done((bf16[8,64,384]{2,1,0:T(8,128)(2,1)}, bf16[8,64,384]{2,1,0:T(8,128)(2,1)}, u32[]{:S(2)}, u32[]{:S(2)}) %collective-permute-start.17) | collective-permute-done | bytes 393248 | tf_op jit(solution)/shard_map/ppermute | solution.py:46
  183.4 3.5 %all-to-all-start.4 = ((bf16[8,64,384]{2,1,0:T(8,128)(2,1)}), bf16[8,64,384]{2,1,0:T(8,128)(2,1)S(1)}, u32[]{:S(2)}, u32[]{:S(2)}) async-start(bf16[8,64,384]{2,1,0:T(8,128)(2,1)} %add_convert_fusion._), calls=%async_computation.4 | async-start | bytes 786432 | tf_op jit(solution)/shard_map/all_to_all | solution.py:504
  194.7 5.2 %factor_grads.1 = (f32[4,512,512]{2,1,0:T(8,128)}, f32[4,512,512]{2,1,0:T(8,128)}, f32[4,512,512]{2,1,0:T(8,128)}) custom-call(bf16[4,224,512]{2,1,0:T(8,128)(2,1)S(1)} %copy-done.3, bf16[4,224,512]{2,1,0:T(8,128)(2,1)S(1)} %copy-done.7, bf16[4,224,512]{2,1,0:T(8,128)(2,1)S(1)} %copy-done.4, bf16[4,224,512]{2,1,0:T(8,128)(2,1)S(1)} %copy-done.8, ...), custom_call_target="tpu_custom_call" | custom-call | tf_op jit(solution)/shard_map/factor_grads/pallas_call | solution.py:370
  201.9 4.8 %all-to-all-start.6 = ((bf16[8,32,384]{2,1,0:T(8,128)(2,1)}), bf16[8,32,384]{2,1,0:T(8,128)(2,1)S(1)}, u32[]{:S(2)}, u32[]{:S(2)}) async-start(bf16[8,32,384]{2,1,0:T(8,128)(2,1)} %add_convert_fusion.2), calls=%async_computation.6 | async-start | bytes 393216 | tf_op jit(solution)/shard_map/all_to_all | solution.py:504
  211.0 4.9 %collective-permute-done.21 = bf16[256,384]{1,0:T(8,128)(2,1)S(1)} collective-permute-done((bf16[256,384]{1,0:T(8,128)(2,1)S(1)}, bf16[256,384]{1,0:T(8,128)(2,1)S(1)}, u32[]{:S(2)}, u32[]{:S(2)}) %collective-permute-start.21) | collective-permute-done | bytes 196640 | tf_op jit(solution)/shard_map/ppermute | solution.py:46
  216.5 3.2 %collective-permute-done.20 = bf16[256,384]{1,0:T(8,128)(2,1)S(1)} collective-permute-done((bf16[256,384]{1,0:T(8,128)(2,1)S(1)}, bf16[256,384]{1,0:T(8,128)(2,1)S(1)}, u32[]{:S(2)}, u32[]{:S(2)}) %collective-permute-start.20) | collective-permute-done | bytes 196640 | tf_op jit(solution)/shard_map/ppermute | solution.py:46
  223.3 5.6 %all-to-all-start.5 = ((bf16[16,24,1920]{2,1,0:T(8,128)(2,1)}), bf16[16,24,1920]{2,1,0:T(8,128)(2,1)S(1)}, u32[]{:S(2)}, u32[]{:S(2)}) async-start(bf16[16,24,1920]{2,1,0:T(8,128)(2,1)} %bitcast.21), calls=%async_computation.5 | async-start | bytes 2949120 | tf_op jit(solution)/shard_map/all_to_all | solution.py:531
  233.5 15.9 %collective-permute-done.28 = bf16[128,384]{1,0:T(8,128)(2,1)S(1)} collective-permute-done((bf16[128,384]{1,0:T(8,128)(2,1)S(1)}, bf16[128,384]{1,0:T(8,128)(2,1)S(1)}, u32[]{:S(2)}, u32[]{:S(2)}) %collective-permute-start.28) | collective-permute-done | bytes 98336 | tf_op jit(solution)/shard_map/ppermute | solution.py:46
  254.1 4.2 %basis_grads.2 = (f32[256,1792]{1,0:T(8,128)}, f32[256,1792]{1,0:T(8,128)}) custom-call(s32[2]{0:T(128)S(1)} %copy-done.11, bf16[256,384]{1,0:T(8,128)(2,1)S(1)} %get-tuple-element.105.refs_0_, bf16[256,384]{1,0:T(8,128)(2,1)S(1)} %get-tuple-element.103.refs_1_, bf16[256,384]{1,0:T(8,128)(2,1)S(1)} %collective-permute-done.23.refs_2_, ...), custom_call_target="tpu_custom_call" | custom-call | tf_op jit(solution)/shard_map/basis_grads/pallas_call | solution.py:156
  262.0 3.0 %basis_grads.3 = f32[256,1792]{1,0:T(8,128)} custom-call(s32[2]{0:T(128)S(1)} %copy-done.11, bf16[128,384]{1,0:T(8,128)(2,1)S(1)} %get-tuple-element.109.refs_0_, bf16[128,384]{1,0:T(8,128)(2,1)S(1)} %get-tuple-element.107.refs_1_, bf16[128,384]{1,0:T(8,128)(2,1)S(1)} %collective-permute-done.31.refs_2_, ...), custom_call_target="tpu_custom_call" | custom-call | tf_op jit(solution)/shard_map/basis_grads/pallas_call | solution.py:156
  (213 shorter events, 81.6 us)
Async XLA Ops:
  57.6 37.4 %all-to-all-start.1 = ((bf16[16,24,1792]{2,1,0:T(8,128)(2,1)}), bf16[16,24,1792]{2,1,0:T(8,128)(2,1)S(1)}, u32[]{:S(2)}, u32[]{:S(2)}) async-start(bf16[16,24,1792]{2,1,0:T(8,128)(2,1)} %bitcast.68), calls=%async_computation.1 | async-start | bytes 2752512 | tf_op jit(solution)/shard_map/all_to_all | solution.py:424
  61.9 37.8 %collective-permute-start = (bf16[4,64,1792]{2,1,0:T(8,128)(2,1)}, bf16[4,64,1792]{2,1,0:T(8,128)(2,1)S(1)}, u32[]{:S(2)}, u32[]{:S(2)}) collective-permute-start(bf16[4,64,1792]{2,1,0:T(8,128)(2,1)} %refs_0_.2), channel_id=1, source_target_pairs={{0,1},{1,0},{2,3},{3,2},{4,5},{5,4},{6,7},{7,6},{8,9},{9,8},{10,11... | collective-permute-start | bytes 2752520 | tf_op jit(solution)/shard_map/ppermute | solution.py:30
  76.8 21.7 %collective-permute-start.7 = (bf16[384,128]{1,0:T(8,128)(2,1)S(1)}, bf16[384,128]{1,0:T(8,128)(2,1)S(1)}, u32[]{:S(2)}, u32[]{:S(2)}) collective-permute-start(bf16[384,128]{1,0:T(8,128)(2,1)S(1)} %slice.55), channel_id=1, source_target_pairs={{0,1},{1,0},{2,3},{3,2},{4,5},{5,4},{6,7},{7,6},{8,9},{9,8},{10,11... | collective-permute-start | bytes 294920 | tf_op jit(solution)/shard_map/ppermute | solution.py:30
  95.0 15.9 %all-to-all-start.3 = ((bf16[8,64,384]{2,1,0:T(8,128)(2,1)}), bf16[8,64,384]{2,1,0:T(8,128)(2,1)S(1)}, u32[]{:S(2)}, u32[]{:S(2)}) async-start(bf16[8,64,384]{2,1,0:T(8,128)(2,1)} %gather_fusion.1), calls=%async_computation.3 | async-start | bytes 786432 | tf_op jit(solution)/shard_map/all_to_all | solution.py:480
  111.0 19.9 %collective-permute-start.13 = (bf16[8,64,384]{2,1,0:T(8,128)(2,1)S(1)}, bf16[8,64,384]{2,1,0:T(8,128)(2,1)S(1)}, u32[]{:S(2)}, u32[]{:S(2)}) collective-permute-start(bf16[8,64,384]{2,1,0:T(8,128)(2,1)S(1)} %all-to-all-done.3.refs_0_), channel_id=1, source_target_pairs={{0,8},{8,0},{16,24},{24,16},{1,9},{9,1},{17,25},{25,17},{2,10},{10... | collective-permute-start | bytes 1179656 | tf_op jit(solution)/shard_map/ppermute | solution.py:46
  111.7 23.1 %collective-permute-start.14 = (bf16[8,64,384]{2,1,0:T(8,128)(2,1)S(1)}, bf16[8,64,384]{2,1,0:T(8,128)(2,1)S(1)}, u32[]{:S(2)}, u32[]{:S(2)}) collective-permute-start(bf16[8,64,384]{2,1,0:T(8,128)(2,1)S(1)} %all-to-all-done.3.refs_0_), channel_id=1, source_target_pairs={{0,16},{8,24},{16,0},{24,8},{1,17},{9,25},{17,1},{25,9},{2,18},{10... | collective-permute-start | bytes 1179656 | tf_op jit(solution)/shard_map/ppermute | solution.py:46
  112.6 22.2 %collective-permute-start.15 = (bf16[8,64,384]{2,1,0:T(8,128)(2,1)S(1)}, bf16[8,64,384]{2,1,0:T(8,128)(2,1)S(1)}, u32[]{:S(2)}, u32[]{:S(2)}) collective-permute-start(bf16[8,64,384]{2,1,0:T(8,128)(2,1)S(1)} %all-to-all-done.3.refs_0_), channel_id=1, source_target_pairs={{0,24},{8,16},{16,8},{24,0},{1,25},{9,17},{17,9},{25,1},{2,26},{10... | collective-permute-start | bytes 1179656 | tf_op jit(solution)/shard_map/ppermute | solution.py:46
  120.4 131.1 %all-gather.3.cloned.1.call-start = ((), (), s32[]{:S(2)}) async-start(), calls=%async_computation.7 | async-start | bytes 4423680 | tf_op jit(solution)/shard_map/all_gather | solution.py:534
  128.7 17.9 %collective-permute-start.4 = (bf16[8,32,384]{2,1,0:T(8,128)(2,1)S(1)}, bf16[8,32,384]{2,1,0:T(8,128)(2,1)S(1)}, u32[]{:S(2)}, u32[]{:S(2)}) collective-permute-start(bf16[8,32,384]{2,1,0:T(8,128)(2,1)S(1)} %all-to-all-done.2.refs_0_), channel_id=1, source_target_pairs={{0,8},{8,0},{16,24},{24,16},{1,9},{9,1},{17,25},{25,17},{2,10},{10... | collective-permute-start | bytes 589832 | tf_op jit(solution)/shard_map/ppermute | solution.py:46
  129.9 16.8 %collective-permute-start.5 = (bf16[8,32,384]{2,1,0:T(8,128)(2,1)S(1)}, bf16[8,32,384]{2,1,0:T(8,128)(2,1)S(1)}, u32[]{:S(2)}, u32[]{:S(2)}) collective-permute-start(bf16[8,32,384]{2,1,0:T(8,128)(2,1)S(1)} %all-to-all-done.2.refs_0_), channel_id=1, source_target_pairs={{0,16},{8,24},{16,0},{24,8},{1,17},{9,25},{17,1},{25,9},{2,18},{10... | collective-permute-start | bytes 589832 | tf_op jit(solution)/shard_map/ppermute | solution.py:46
  130.9 15.8 %collective-permute-start.6 = (bf16[8,32,384]{2,1,0:T(8,128)(2,1)S(1)}, bf16[8,32,384]{2,1,0:T(8,128)(2,1)S(1)}, u32[]{:S(2)}, u32[]{:S(2)}) collective-permute-start(bf16[8,32,384]{2,1,0:T(8,128)(2,1)S(1)} %all-to-all-done.2.refs_0_), channel_id=1, source_target_pairs={{0,24},{8,16},{16,8},{24,0},{1,25},{9,17},{17,9},{25,1},{2,26},{10... | collective-permute-start | bytes 589832 | tf_op jit(solution)/shard_map/ppermute | solution.py:46
  161.3 19.1 %collective-permute-start.17 = (bf16[8,64,384]{2,1,0:T(8,128)(2,1)}, bf16[8,64,384]{2,1,0:T(8,128)(2,1)}, u32[]{:S(2)}, u32[]{:S(2)}) collective-permute-start(bf16[8,64,384]{2,1,0:T(8,128)(2,1)} %get-tuple-element.60), channel_id=1, source_target_pairs={{0,16},{8,24},{16,0},{24,8},{1,17},{9,25},{17,1},{25,9},{2,18},{10... | collective-permute-start | bytes 1179656 | tf_op jit(solution)/shard_map/ppermute | solution.py:46
  162.3 18.9 %collective-permute-start.16 = (bf16[8,64,384]{2,1,0:T(8,128)(2,1)}, bf16[8,64,384]{2,1,0:T(8,128)(2,1)}, u32[]{:S(2)}, u32[]{:S(2)}) collective-permute-start(bf16[8,64,384]{2,1,0:T(8,128)(2,1)} %get-tuple-element.59), channel_id=1, source_target_pairs={{0,8},{8,0},{16,24},{24,16},{1,9},{9,1},{17,25},{25,17},{2,10},{10... | collective-permute-start | bytes 1179656 | tf_op jit(solution)/shard_map/ppermute | solution.py:46
  163.5 23.4 %collective-permute-start.27 = (bf16[8,32,384]{2,1,0:T(8,128)(2,1)}, bf16[8,32,384]{2,1,0:T(8,128)(2,1)}, u32[]{:S(2)}, u32[]{:S(2)}) collective-permute-start(bf16[8,32,384]{2,1,0:T(8,128)(2,1)} %get-tuple-element.78), channel_id=1, source_target_pairs={{0,24},{8,16},{16,8},{24,0},{1,25},{9,17},{17,9},{25,1},{2,26},{10... | collective-permute-start | bytes 589832 | tf_op jit(solution)/shard_map/ppermute | solution.py:46
  165.1 21.8 %collective-permute-start.26 = (bf16[8,32,384]{2,1,0:T(8,128)(2,1)}, bf16[8,32,384]{2,1,0:T(8,128)(2,1)}, u32[]{:S(2)}, u32[]{:S(2)}) collective-permute-start(bf16[8,32,384]{2,1,0:T(8,128)(2,1)} %get-tuple-element.77), channel_id=1, source_target_pairs={{0,16},{8,24},{16,0},{24,8},{1,17},{9,25},{17,1},{25,9},{2,18},{10... | collective-permute-start | bytes 589832 | tf_op jit(solution)/shard_map/ppermute | solution.py:46
  172.9 14.1 %collective-permute-start.25 = (bf16[8,32,384]{2,1,0:T(8,128)(2,1)}, bf16[8,32,384]{2,1,0:T(8,128)(2,1)}, u32[]{:S(2)}, u32[]{:S(2)}) collective-permute-start(bf16[8,32,384]{2,1,0:T(8,128)(2,1)} %get-tuple-element.76), channel_id=1, source_target_pairs={{0,8},{8,0},{16,24},{24,16},{1,9},{9,1},{17,25},{25,17},{2,10},{10... | collective-permute-start | bytes 589832 | tf_op jit(solution)/shard_map/ppermute | solution.py:46
  183.4 18.5 %all-to-all-start.4 = ((bf16[8,64,384]{2,1,0:T(8,128)(2,1)}), bf16[8,64,384]{2,1,0:T(8,128)(2,1)S(1)}, u32[]{:S(2)}, u32[]{:S(2)}) async-start(bf16[8,64,384]{2,1,0:T(8,128)(2,1)} %add_convert_fusion._), calls=%async_computation.4 | async-start | bytes 786432 | tf_op jit(solution)/shard_map/all_to_all | solution.py:504
  190.7 17.9 %collective-permute-start.22 = (bf16[4,384]{1,0:T(4,128)(2,1)S(1)}, bf16[4,384]{1,0:T(4,128)(2,1)S(1)}, u32[]{:S(2)}, u32[]{:S(2)}) collective-permute-start(bf16[4,384]{1,0:T(4,128)(2,1)S(1)} %select_bitcast_fusion.2), channel_id=1, source_target_pairs={{0,1},{1,0},{2,3},{3,2},{4,5},{5,4},{6,7},{7,6},{8,9},{9,8},{10,11... | collective-permute-start | bytes 9224 | tf_op jit(solution)/shard_map/ppermute | solution.py:30
  201.9 21.4 %all-to-all-start.6 = ((bf16[8,32,384]{2,1,0:T(8,128)(2,1)}), bf16[8,32,384]{2,1,0:T(8,128)(2,1)S(1)}, u32[]{:S(2)}, u32[]{:S(2)}) async-start(bf16[8,32,384]{2,1,0:T(8,128)(2,1)} %add_convert_fusion.2), calls=%async_computation.6 | async-start | bytes 393216 | tf_op jit(solution)/shard_map/all_to_all | solution.py:504
  223.3 43.6 %all-to-all-start.5 = ((bf16[16,24,1920]{2,1,0:T(8,128)(2,1)}), bf16[16,24,1920]{2,1,0:T(8,128)(2,1)S(1)}, u32[]{:S(2)}, u32[]{:S(2)}) async-start(bf16[16,24,1920]{2,1,0:T(8,128)(2,1)} %bitcast.21), calls=%async_computation.5 | async-start | bytes 2949120 | tf_op jit(solution)/shard_map/all_to_all | solution.py:531
  228.9 31.2 %all-gather.5.cloned.1.call-start = ((), (), s32[]{:S(2)}) async-start(), calls=%async_computation.8 | async-start | bytes 4128768 | tf_op jit(solution)/shard_map/all_gather | solution.py:535
  229.9 19.5 %collective-permute-start.28 = (bf16[128,384]{1,0:T(8,128)(2,1)S(1)}, bf16[128,384]{1,0:T(8,128)(2,1)S(1)}, u32[]{:S(2)}, u32[]{:S(2)}) collective-permute-start(bf16[128,384]{1,0:T(8,128)(2,1)S(1)} %bitcast.81), channel_id=1, source_target_pairs={{0,16},{8,24},{16,0},{24,8},{1,17},{9,25},{17,1},{25,9},{2,18},{10... | collective-permute-start | bytes 294920 | tf_op jit(solution)/shard_map/ppermute | solution.py:46
  231.9 18.9 %collective-permute-start.30 = (bf16[128,384]{1,0:T(8,128)(2,1)S(1)}, bf16[128,384]{1,0:T(8,128)(2,1)S(1)}, u32[]{:S(2)}, u32[]{:S(2)}) collective-permute-start(bf16[128,384]{1,0:T(8,128)(2,1)S(1)} %bitcast.82), channel_id=1, source_target_pairs={{0,24},{8,16},{16,8},{24,0},{1,25},{9,17},{17,9},{25,1},{2,26},{10... | collective-permute-start | bytes 294920 | tf_op jit(solution)/shard_map/ppermute | solution.py:46
  233.4 17.5 %collective-permute-start.29 = (bf16[128,384]{1,0:T(8,128)(2,1)S(1)}, bf16[128,384]{1,0:T(8,128)(2,1)S(1)}, u32[]{:S(2)}, u32[]{:S(2)}) collective-permute-start(bf16[128,384]{1,0:T(8,128)(2,1)S(1)} %bitcast.83), channel_id=1, source_target_pairs={{0,8},{8,0},{16,24},{24,16},{1,9},{9,1},{17,25},{25,17},{2,10},{10... | collective-permute-start | bytes 294920 | tf_op jit(solution)/shard_map/ppermute | solution.py:46
  (47 other events, 439.3 us)
Sparse Core Ops, SparseCore 0:
  163.4 9.8 all-gather.2
  231.3 12.8 all-gather.4

commit v4 on v3

--- a/solution.py
+++ b/solution.py
@@ -121,18 +121,19 @@
     return (got[:n_dp] if built else rows), got[-n_dp:]
 
 
-def basis_grads(keep, other, cols, spot, shape, n_dp):
+def basis_grads(keep, other, cols, other_cols, spot, shape, n_dp):
     clusters, rank_own, width = shape
     parts_core = n_dp // 2
     part = rank_own // parts_core
-    half = cols.shape[1]
+    half = cols.shape[0]
     count = keep[0].shape[0] // (clusters * part)
     block = width // 2 if width % 256 == 0 else width
 
     def kernel(spot_ref, *refs):
         ours, theirs = refs[:parts_core], refs[parts_core : 2 * parts_core]
-        cols_ref, outs, rows_ref = refs[2 * parts_core], refs[-1 - count : -1], refs[-1]
-        dp, core = spot_ref[0], spot_ref[1]
+        cols_ref, other_ref = refs[2 * parts_core : 2 * parts_core + 2]
+        outs, rows_ref = refs[-1 - count : -1], refs[-1]
+        dp = spot_ref[0]
 
         @pl.when(pl.program_id(0) == 0)
         def _():
@@ -143,12 +144,12 @@
                     for b in range(count):
                         take = slice((c * count + b) * part, (c * count + b + 1) * part)
                         kind = rows_ref.dtype
-                        rows_ref[core, b, pl.ds(at, part), :] = ours[k][take, :].astype(kind)
-                        rows_ref[1 - core, b, pl.ds(at, part), :] = theirs[k][take, :].astype(kind)
+                        rows_ref[0, b, pl.ds(at, part), :] = ours[k][take, :].astype(kind)
+                        rows_ref[1, b, pl.ds(at, part), :] = theirs[k][take, :].astype(kind)
 
         for b in range(count):
-            total = dot(rows_ref[0, b].astype(BF), cols_ref[0], 1, 0)
-            total += dot(rows_ref[1, b].astype(BF), cols_ref[1], 1, 0)
+            total = dot(rows_ref[0, b].astype(BF), cols_ref[...], 1, 0)
+            total += dot(rows_ref[1, b].astype(BF), other_ref[...], 1, 0)
             outs[b][...] = total
 
     ins = list(keep) + list(other)
@@ -159,7 +160,7 @@
         out_shape=[out] * count,
         in_specs=[SCALAR]
         + [whole(x) for x in ins]
-        + [pl.BlockSpec((2, half, block), lambda j: (0, 0, j), memory_space=VMEM)],
+        + [pl.BlockSpec((half, block), lambda j: (0, j), memory_space=VMEM)] * 2,
         out_specs=[
             pl.BlockSpec((clusters * rank_own, block), lambda j: (0, j), memory_space=VMEM)
         ]
@@ -168,7 +169,7 @@
         compiler_params=params(2 * half),
         cost_estimate=FREE,
         name="basis_grads",
-    )(spot, *ins, cols)
+    )(spot, *ins, cols, other_cols)
     return [grad.reshape(shape) for grad in got]
 
 
@@ -224,7 +225,7 @@
                 ].astype(BF)
 
 
-def forward(pieces, pick, weight, gate_factor, up_factor, down_factor, dp):
+def forward(pieces, pick, gate_factor, up_factor, down_factor, dp):
     n_dp = len(pieces)
     n_ex, rows, half = pieces[0].shape
     local, slots, total = pick.shape
@@ -232,17 +233,14 @@
 
     def kernel(dp_ref, *refs):
         got, refs = refs[:n_dp], refs[n_dp:]
-        pick_ref, weight_ref, gate_ref, up_ref, down_ref = refs[:5]
-        hg_ref, hu_ref, hidden_ref, mixed_ref, act_ref, lift_ref = refs[5:11]
-        sent = refs[11 : 11 + n_dp]
-        rows_ref, total_ref = refs[11 + n_dp :]
+        pick_ref, gate_ref, up_ref, down_ref = refs[:4]
+        hg_ref, hu_ref, hidden_ref, mixed_ref, act_ref, lift_ref, rows_ref = refs[4:]
         j = pl.program_id(0)
         me = dp_ref[0]
 
         @pl.when(j == 0)
         def _():
             lay_out(got, rows_ref, me, 2)
-            total_ref[...] = jnp.zeros_like(total_ref)
 
         take = pick_ref[0]
         hg = dot(take, rows_ref[0].astype(BF), 1, 1).astype(BF)
@@ -257,13 +255,7 @@
         lift_ref[0] = up_pre * (sig * (1.0 + gate_pre * (1.0 - sig)))
         hidden = (act * up_pre).astype(BF)
         hidden_ref[0] = hidden
-        mixed = dot(hidden, down_ref[0], 1, 0).astype(BF)
-        mixed_ref[0] = mixed
-        total_ref[0] += dot(mixed, (take * weight_ref[0]).astype(BF), 0, 0)
-
-        @pl.when(j == local - 1)
-        def _():
-            hand_out(total_ref, sent, me, 1)
+        mixed_ref[0] = dot(hidden, down_ref[0], 1, 0).astype(BF)
 
     slot_shape = (local, slots, rank)
     hid_shape = (local, slots, hid)
@@ -275,21 +267,19 @@
         shaped(hid_shape, FL),
         shaped(hid_shape, FL),
     ]
-    chunks = [shaped((n_ex, rows // 2, half), BF)] * n_dp
-    got = pl.pallas_call(
+    return pl.pallas_call(
         kernel,
         grid=(local,),
-        out_shape=outs + chunks,
+        out_shape=outs,
         in_specs=[SCALAR]
         + [whole(piece) for piece in pieces]
-        + [each(x) for x in (pick, weight, gate_factor, up_factor, down_factor)],
-        out_specs=[each(out) for out in outs] + [whole(chunk) for chunk in chunks],
-        scratch_shapes=[pltpu.VMEM((2, rank, total), rows_kind(rows // 2)), pltpu.VMEM((1, rank, total), FL)],
+        + [each(x) for x in (pick, gate_factor, up_factor, down_factor)],
+        out_specs=[each(out) for out in outs],
+        scratch_shapes=[pltpu.VMEM((2, rank, total), rows_kind(rows // 2))],
         compiler_params=params(total, True),
         cost_estimate=FREE,
         name="forward",
-    )(dp.reshape(1), *pieces, pick, weight, gate_factor, up_factor, down_factor)
-    return got[:6], got[6:]
+    )(dp.reshape(1), *pieces, pick, gate_factor, up_factor, down_factor)
 
 
 def backward(pieces, pick, weight, mixed, act, lift, gate_factor, up_factor, down_factor, dp):
@@ -350,6 +340,42 @@
         name="backward",
     )(dp.reshape(1), *pieces, *ins)
     return got[:4], got[4:]
+
+
+def mixed_sums(mixed, pick, weight, dp, chunk, n_dp, first):
+    local, slots, rank = mixed.shape
+    total = pick.shape[2]
+
+    def kernel(dp_ref, mixed_ref, pick_ref, weight_ref, *refs):
+        sent, total_ref = refs[1:-1], refs[-1]
+        j = pl.program_id(0)
+        heavy = (pick_ref[0] * weight_ref[0]).astype(BF)
+        term = dot(mixed_ref[0], heavy, 0, 0)
+
+        @pl.when(j == 0)
+        def _():
+            total_ref[0] = term
+
+        @pl.when(j > 0)
+        def _():
+            total_ref[0] += term
+
+        @pl.when(j == local - 1)
+        def _():
+            hand_out(total_ref, sent, dp_ref[0], 1)
+
+    chunks = [shaped(chunk, BF)] * n_dp
+    return pl.pallas_call(
+        kernel,
+        grid=(local,),
+        out_shape=chunks,
+        in_specs=[SCALAR, each(mixed), each(pick), each(weight), ANYWHERE],
+        out_specs=[whole(out) for out in chunks],
+        scratch_shapes=[pltpu.VMEM((1, rank, total), FL)],
+        compiler_params=params(total),
+        cost_estimate=FREE,
+        name="mixed_sums",
+    )(dp.reshape(1), mixed, pick, weight, first)
 
 
 def factor_grads(hg, grad_gate, hu, grad_up, hidden, back, total, first):
@@ -490,31 +516,39 @@
     mine_out = sum_parts(trade(lambda k: terms_out[k], "dp"))
     got_out = to_group(mine_out)
     h_pieces = trade(lambda k: got_in, "dp")
-    (hg, hu, hidden, mixed, act, lift), mixed_chunks = forward(
-        h_pieces, pick, weight_of, gate_factor, up_factor, down_factor, dp
+    hg, hu, hidden, mixed, act, lift = forward(
+        h_pieces, pick, gate_factor, up_factor, down_factor, dp
     )
     d_pieces = trade(lambda k: got_out, "dp")
     (back, grad_gate, grad_up, dots), in_chunks = backward(
         d_pieces, pick, slot_weight, mixed, act, lift, gate_factor, up_factor, down_factor, dp
     )
 
-    owner = group_cluster[None, :] == jnp.arange(clusters, dtype=jnp.int32)[:, None]
-
-    def from_groups(mine):
-        got = lax.all_to_all(mine, ("ez", "core"), split_axis=0, concat_axis=0, tiled=True)
-        return jnp.sum(
-            jnp.where(owner[:, :, None, None], got.astype(FL)[None], 0.0), axis=1
-        ).astype(BF).reshape(-1, half)
-
+    numbers = jnp.arange(clusters, dtype=jnp.int32)[:, None]
+
+    def by_cluster(got, groups):
+        owner = (groups[None, :] == numbers)[:, :, None, None]
+        summed = jnp.sum(jnp.where(owner, got.astype(FL)[None], 0.0), axis=1)
+        return summed.astype(BF).reshape(-1, half)
+
+    in_mine = sum_parts(trade(lambda k: in_chunks[k], "dp"))
+    mixed_chunks = mixed_sums(mixed, pick, weight_of, dp, got_out.shape, n_dp, in_mine)
     mixed_mine = sum_parts(trade(lambda k: mixed_chunks[k], "dp"))
-    in_mine = sum_parts(trade(lambda k: in_chunks[k], "dp"))
+    got = lax.all_to_all(in_mine, ("ez", "core"), split_axis=0, concat_axis=0, tiled=True)
+    in_sum = after(by_cluster(got, group_cluster), mixed_mine)
+    in_parts = trade(lambda k: in_sum, "dp")
+
+    mixed_mine = after(mixed_mine, in_parts[-1])
+    got = [lax.dynamic_index_in_dim(mixed_mine, me_e, 0, False)]
+    for k in range(1, n_ex):
+        piece = lax.dynamic_index_in_dim(mixed_mine, me_e ^ k, 0, False)
+        got.append(lax.ppermute(piece, ("ez", "core"), [(i, i ^ k) for i in range(n_ex)]))
+    partners = group_cluster[me_e ^ jnp.arange(n_ex, dtype=jnp.int32)]
+    mixed_sum = by_cluster(jnp.stack(got), partners)
+    mixed_parts = trade(lambda k: mixed_sum, "dp")
     grad_gate_factor, grad_up_factor, grad_down_factor = factor_grads(
-        hg, grad_gate, hu, grad_up, hidden, back, total, in_mine
-    )
-    mixed_sum = from_groups(mixed_mine)
-    in_sum = after(from_groups(in_mine), grad_gate_factor)
-    in_parts = trade(lambda k: in_sum, "dp")
-    mixed_parts = trade(lambda k: mixed_sum, "dp")
+        hg, grad_gate, hu, grad_up, hidden, back, total, in_parts[-1]
+    )
 
     placed = cell == jnp.arange(slots, dtype=jnp.int32)[None, :, None]
     scores = jnp.sum(jnp.where(placed, dots, 0.0), axis=1).reshape(local, 2, half)
@@ -531,8 +565,8 @@
     rows = lax.all_to_all(rows, ("dp", "ez"), split_axis=0, concat_axis=0, tiled=True)
     rows = rows.reshape(n_dp, n_z, tok_rows, width + lanes)
 
-    x_both = lax.all_gather(x_half, "core", axis=0)
-    dy_both = lax.all_gather(dy_half, "core", axis=0)
+    x_other = core_swap(x_half)
+    dy_other = core_swap(dy_half)
     same = core == dp // parts_core
 
     def own_ranks(parts):
@@ -543,14 +577,14 @@
 
     shape = (clusters, rank_own, width)
     grad_gate_basis, grad_up_basis = basis_grads(
-        *own_ranks(in_parts), x_both, spot, shape, n_dp
+        *own_ranks(in_parts), x_half, x_other, spot, shape, n_dp
     )
     (grad_down_basis,) = basis_grads(
-        *own_ranks(mixed_parts), dy_both, spot, shape, n_dp
+        *own_ranks(mixed_parts), dy_half, dy_other, spot, shape, n_dp
     )
 
     grad_rows = jnp.sum(rows[..., :width].astype(FL), axis=1)
-    for part in (grad_gate_basis, grad_down_basis):
+    for part in (grad_gate_factor, grad_gate_basis, grad_down_basis):
         grad_rows = after(grad_rows, part)
     grad_tokens = grad_rows.astype(BF).transpose(1, 0, 2).reshape(tok_rows, model_width)
     by_expert = jnp.sum(rows[..., width : width + 2 * local].astype(FL), axis=0)

time: 278 us -> 324 us (1.17)
  waiting for transfers between devices: 67.5 us -> 93.5 us
  starting transfers between devices: 56.2 us -> 70.8 us
  local copies, waits for them, and re-layouts: 26.1 us -> 38.2 us
  between operations: 17.4 us -> 5.4 us
  other arithmetic: 15.6 us -> 19 us
    ppermute x0 -> x7, waiting for transfers between devices: none -> 29.4 us  [body(): lax.ppermute(piece, ('ez', 'core'), [(i, i ^ k) for i in range(n_ex)])]
    ppermute x0 -> x7, starting transfers between devices: none -> 11.4 us  [body(): lax.ppermute(piece, ('ez', 'core'), [(i, i ^ k) for i in range(n_ex)])]
    all_to_all x2, starting transfers between devices: 7.19 us -> 16.7 us  [to_group(): lax.all_to_all(send, ('ez', 'core'), split_axis=0, concat_axis=0, tiled=T...]
    unnamed x65 -> x97, local copies, waits for them, and re-layouts: 13.3 us -> 21.4 us
    all_to_all x2 -> x1, starting transfers between devices: 8.25 us -> 4.34 us  [body(): lax.all_to_all(in_mine, ('ez', 'core'), split_axis=0, concat_axis=0, tile...]
    ppermute x9 -> x11, waiting for transfers between devices: 4.62 us -> 1.16 us  [core_swap(): return lax.ppermute(value, 'core', [(0, 1), (1, 0)])]
    pallas_call x1 -> x2, Pallas kernels: 10.9 us -> 11.1 us  [the longest x1 8.86 us: forward(): pl.pallas_call(kernel, grid=(local,), out_shape=outs, in_specs=[SCALAR] +...]
  transfers between devices with their start and end apart: 41 -> 47, of which waited for: 16 -> 21; matrix products, arithmetic and copies ran while one was open for 9% -> 12% of each run, Pallas kernels for 12% -> 11%
where the time goes in v4:
time: 324 us; the launch traced here: 323 us
  waiting for transfers between devices  93.5 us (29%)
  starting transfers between devices  70.8 us (22%)
  Pallas kernels  47.6 us (15%)
  blocking collectives  44.7 us (14%)
  local copies, waits for them, and re-layouts  38.2 us (12%)
  other arithmetic  19 us (6%)
  between operations  5.4 us (2%)
  matrix products  3.52 us (1%)
    ppermute x24, waiting for transfers between devices, trade(): lax.ppermute(chunk_for(k), axis, [(i, i ^ k) for i in range(n)])  51.5 us
    all_to_all x1, blocking collectives, own_columns(): lax.all_to_all(rows, ('dp', 'ez'), split_axis=0, concat_axis=0, tiled=True)  44.7 us
    ppermute x7, waiting for transfers between devices, body(): lax.ppermute(piece, ('ez', 'core'), [(i, i ^ k) for i in range(n_ex)])  29.4 us
    ppermute x24, starting transfers between devices, trade(): lax.ppermute(chunk_for(k), axis, [(i, i ^ k) for i in range(n)])  26.9 us
    unnamed x97, local copies, waits for them, and re-layouts  21.4 us
    all_to_all x2, starting transfers between devices, to_group(): lax.all_to_all(send, ('ez', 'core'), split_axis=0, concat_axis=0, tiled=T...  16.7 us
    pallas_call x1, Pallas kernels, backward(): pl.pallas_call(kernel, grid=(local,), out_shape=outs + chunks, in_specs=[...  12.2 us
    ppermute x7, starting transfers between devices, body(): lax.ppermute(piece, ('ez', 'core'), [(i, i ^ k) for i in range(n_ex)])  11.4 us
  transfers between devices with their start and end apart: 47, of which 21 were waited for; matrix products, arithmetic and copies ran while one was open for 12% of the time, Pallas kernels for 11%

profile of v4, /device:TPU:0, one launch (start us, length us, event | category | flops | bytes accessed | tf_op | source)
XLA Modules:
  0.0 322.6 jit_solution(7730609827303092021)
XLA Ops:
  3.7 44.7 %all_to_all.30 = bf16[16,24,1920]{2,1,0:T(8,128)(2,1)S(1)} all-to-all(bf16[16,24,1920]{2,1,0:T(8,128)(2,1)S(1)} %bitcast.95), channel_id=1, replica_groups=mesh['dp'=4,'ez'=4,'core'=2] {'dp','ez'}, dimensions={0} | all-to-all | bytes 2949120 | tf_op jit(solution)/shard_map/all_to_all | solution.py:450
  51.1 3.7 %all-to-all-start.1 = ((bf16[16,24,1792]{2,1,0:T(8,128)(2,1)}), bf16[16,24,1792]{2,1,0:T(8,128)(2,1)S(1)}, u32[]{:S(2)}, u32[]{:S(2)}) async-start(bf16[16,24,1792]{2,1,0:T(8,128)(2,1)} %bitcast.97), calls=%async_computation.1 | async-start | bytes 2752512 | tf_op jit(solution)/shard_map/all_to_all | solution.py:450
  59.0 5.5 %project.3 = (bf16[256,1792]{1,0:T(8,128)(2,1)}, bf16[256,1792]{1,0:T(8,128)(2,1)}, bf16[256,1792]{1,0:T(8,128)(2,1)}, bf16[256,1792]{1,0:T(8,128)(2,1)}, bf16[2...) custom-call(s32[2]{0:T(128)} %pad_add_fusion.spot_ref, ...), custom_call_target="tpu_custom_call" | custom-call | tf_op jit(solution)/shard_map/project/pallas_call | solution.py:112
  68.1 7.2 %collective-permute-done.10 = bf16[256,384]{1,0:T(8,128)(2,1)S(1)} collective-permute-done((bf16[256,384]{1,0:T(8,128)(2,1)}, bf16[256,384]{1,0:T(8,128)(2,1)S(1)}, u32[]{:S(2)}, u32[]{:S(2)}) %collective-permute-start.10) | collective-permute-done | bytes 196640 | tf_op jit(solution)/shard_map/ppermute | solution.py:46
  75.3 5.4 %collective-permute-done.12 = bf16[256,384]{1,0:T(8,128)(2,1)S(1)} collective-permute-done((bf16[256,384]{1,0:T(8,128)(2,1)}, bf16[256,384]{1,0:T(8,128)(2,1)S(1)}, u32[]{:S(2)}, u32[]{:S(2)}) %collective-permute-start.12) | collective-permute-done | bytes 196640 | tf_op jit(solution)/shard_map/ppermute | solution.py:46
  83.1 5.4 %all-to-all-done.1 = bf16[16,24,1792]{2,1,0:T(8,128)(2,1)S(1)} async-done(((bf16[16,24,1792]{2,1,0:T(8,128)(2,1)}), bf16[16,24,1792]{2,1,0:T(8,128)(2,1)S(1)}, u32[]{:S(2)}, u32[]{:S(2)}) %all-to-all-start.1) | async-done | bytes 1376288 | tf_op jit(solution)/shard_map/all_to_all | solution.py:450
  95.3 4.3 %project.2 = (bf16[128,1792]{1,0:T(8,128)(2,1)}, bf16[128,1792]{1,0:T(8,128)(2,1)}, bf16[128,1792]{1,0:T(8,128)(2,1)}, bf16[128,1792]{1,0:T(8,128)(2,1)}, bf16[1...) custom-call(s32[2]{0:T(128)} %pad_add_fusion.spot_ref, ...), custom_call_target="tpu_custom_call" | custom-call | tf_op jit(solution)/shard_map/project/pallas_call | solution.py:112
  109.5 13.2 %all-to-all-start.2 = ((bf16[8,32,384]{2,1,0:T(8,128)(2,1)}), bf16[8,32,384]{2,1,0:T(8,128)(2,1)S(1)}, u32[]{:S(2)}, u32[]{:S(2)}) async-start(bf16[8,32,384]{2,1,0:T(8,128)(2,1)} %gather_fusion), calls=%async_computation.2 | async-start | bytes 393216 | tf_op jit(solution)/shard_map/all_to_all | solution.py:506
  125.6 5.4 %all-to-all-done.2.refs_0_ = bf16[8,32,384]{2,1,0:T(8,128)(2,1)S(1)} async-done(((bf16[8,32,384]{2,1,0:T(8,128)(2,1)}), bf16[8,32,384]{2,1,0:T(8,128)(2,1)S(1)}, u32[]{:S(2)}, u32[]{:S(2)}) %all-to-all-start.2) | async-done | bytes 196640 | tf_op jit(solution)/shard_map/all_to_all | solution.py:506
  138.1 8.9 %forward.1 = (bf16[4,224,512]{2,1,0:T(8,128)(2,1)}, bf16[4,224,512]{2,1,0:T(8,128)(2,1)}, bf16[4,224,512]{2,1,0:T(8,128)(2,1)}, bf16[4,224,512]{2,1,0:T(8,128)(2...) custom-call(s32[1]{0:T(128)} %bitcast.dp_ref, bf16[8,64,384]{2,1,0:T(8,128)(2,1)} %copy-done.18, ...), custom_call_target="tpu_custom_call" | custom-call | tf_op jit(solution)/shard_map/forward/pallas_call | solution.py:270
  147.8 12.2 %backward.1 = (bf16[4,224,512]{2,1,0:T(8,128)(2,1)}, bf16[4,224,512]{2,1,0:T(8,128)(2,1)}, bf16[4,224,512]{2,1,0:T(8,128)(2,1)}, f32[4,224,1]{2,1,0:T(8,128)}, b...) custom-call(s32[1]{0:T(128)} %bitcast.dp_ref, ...), custom_call_target="tpu_custom_call" | custom-call | tf_op jit(solution)/shard_map/backward/pallas_call | solution.py:331
  163.9 8.5 %collective-permute-done.16 = bf16[8,64,384]{2,1,0:T(8,128)(2,1)S(1)} collective-permute-done((bf16[8,64,384]{2,1,0:T(8,128)(2,1)}, bf16[8,64,384]{2,1,0:T(8,128)(2,1)S(1)}, u32[]{:S(2)}, u32[]{:S(2)}) %collective-permute-start.16) | collective-permute-done | bytes 393248 | tf_op jit(solution)/shard_map/ppermute | solution.py:46
  172.4 6.7 %collective-permute-done.17 = bf16[8,64,384]{2,1,0:T(8,128)(2,1)} collective-permute-done((bf16[8,64,384]{2,1,0:T(8,128)(2,1)}, bf16[8,64,384]{2,1,0:T(8,128)(2,1)}, u32[]{:S(2)}, u32[]{:S(2)}) %collective-permute-start.17) | collective-permute-done | bytes 393248 | tf_op jit(solution)/shard_map/ppermute | solution.py:46
  181.2 4.3 %all-to-all-start.4 = ((bf16[8,64,384]{2,1,0:T(8,128)(2,1)}), bf16[8,64,384]{2,1,0:T(8,128)(2,1)S(1)}, u32[]{:S(2)}, u32[]{:S(2)}) async-start(bf16[8,64,384]{2,1,0:T(8,128)(2,1)} %add_convert_fusion.refs_0_), calls=%async_computation.4 | async-start | bytes 786432 | tf_op jit(solution)/shard_map/all_to_all | solution.py:537
  196.3 4.3 %collective-permute-done.19 = bf16[8,32,384]{2,1,0:T(8,128)(2,1)S(1)} collective-permute-done((bf16[8,32,384]{2,1,0:T(8,128)(2,1)S(1)}, bf16[8,32,384]{2,1,0:T(8,128)(2,1)S(1)}, u32[]{:S(2)}, u32[]{:S(2)}) %collective-permute-start.19) | collective-permute-done | bytes 196640 | tf_op jit(solution)/shard_map/ppermute | solution.py:46
  210.1 5.0 %collective-permute-done.24._ = bf16[256,384]{1,0:T(8,128)(2,1)S(1)} collective-permute-done((bf16[256,384]{1,0:T(8,128)(2,1)S(1)}, bf16[256,384]{1,0:T(8,128)(2,1)S(1)}, u32[]{:S(2)}, u32[]{:S(2)}) %collective-permute-start.24) | collective-permute-done | bytes 196640 | tf_op jit(solution)/shard_map/ppermute | solution.py:46
  226.4 5.8 %all-to-all-start.5 = ((bf16[16,24,1920]{2,1,0:T(8,128)(2,1)}), bf16[16,24,1920]{2,1,0:T(8,128)(2,1)}, u32[]{:S(2)}, u32[]{:S(2)}) async-start(bf16[16,24,1920]{2,1,0:T(8,128)(2,1)} %bitcast.96), calls=%async_computation.5 | async-start | bytes 2949120 | tf_op jit(solution)/shard_map/all_to_all | solution.py:565
  236.2 22.1 %collective-permute-done.30 = bf16[32,384]{1,0:T(8,128)(2,1)S(1)} collective-permute-done((bf16[32,384]{1,0:T(8,128)(2,1)S(1)}, bf16[32,384]{1,0:T(8,128)(2,1)S(1)}, u32[]{:S(2)}, u32[]{:S(2)}) %collective-permute-start.30) | collective-permute-done | bytes 24608 | tf_op jit(solution)/shard_map/ppermute | solution.py:545
  261.8 3.6 %collective-permute-start.32 = (bf16[32,384]{1,0:T(8,128)(2,1)S(1)}, bf16[32,384]{1,0:T(8,128)(2,1)S(1)}, u32[]{:S(2)}, u32[]{:S(2)}) collective-permute-start(bf16[32,384]{1,0:T(8,128)(2,1)S(1)} %copy-done.37), channel_id=1, source_target_pairs={{0,4},{1,5},{2,6},{3,7},{4,0},{5,1},{6,2},{7,3},{8,12},{9,13},{10,... | collective-permute-start | bytes 73736 | tf_op jit(solution)/shard_map/ppermute | solution.py:545
  269.4 3.5 %collective-permute-done.33 = bf16[32,384]{1,0:T(8,128)(2,1)S(1)} collective-permute-done((bf16[32,384]{1,0:T(8,128)(2,1)S(1)}, bf16[32,384]{1,0:T(8,128)(2,1)S(1)}, u32[]{:S(2)}, u32[]{:S(2)}) %collective-permute-start.33) | collective-permute-done | bytes 24608 | tf_op jit(solution)/shard_map/ppermute | solution.py:545
  286.9 3.6 %collective-permute-done.36 = bf16[128,384]{1,0:T(8,128)(2,1)S(1)} collective-permute-done((bf16[128,384]{1,0:T(8,128)(2,1)S(1)}, bf16[128,384]{1,0:T(8,128)(2,1)S(1)}, u32[]{:S(2)}, u32[]{:S(2)}) %collective-permute-start.36) | collective-permute-done | bytes 98336 | tf_op jit(solution)/shard_map/ppermute | solution.py:46
  298.9 5.2 %factor_grads.1 = (f32[4,512,512]{2,1,0:T(8,128)}, f32[4,512,512]{2,1,0:T(8,128)}, f32[4,512,512]{2,1,0:T(8,128)}) custom-call(bf16[4,224,512]{2,1,0:T(8,128)(2,1)S(1)} %copy-done.7, bf16[4,224,512]{2,1,0:T(8,128)(2,1)S(1)} %copy-done.11, bf16[4,224,512]{2,1,0:T(8,128)(2,1)S(1)} %copy-done.8, bf16[4,224,512]{2,1,0:T(8,128)(2,1)S(1)} %copy-done.12, ...), custom_call_target="tpu_custom_call" | custom-call | tf_op jit(solution)/shard_map/factor_grads/pallas_call | solution.py:396
  306.0 4.8 %basis_grads.2 = (f32[256,1792]{1,0:T(8,128)}, f32[256,1792]{1,0:T(8,128)}) custom-call(s32[2]{0:T(128)S(1)} %copy-done.15, bf16[256,384]{1,0:T(8,128)(2,1)S(1)} %get-tuple-element.105.refs_0_, bf16[256,384]{1,0:T(8,128)(2,1)S(1)} %get-tuple-element.103.refs_1_, bf16[256,384]{1,0:T(8,128)(2,1)} %collective-permute-done.26.refs_2_, ...), custom_call_target="tpu_custom_call" | custom-call | tf_op jit(solution)/shard_map/basis_grads/pallas_call | solution.py:157
  312.8 3.6 %basis_grads.3 = f32[256,1792]{1,0:T(8,128)} custom-call(s32[2]{0:T(128)S(1)} %copy-done.15, bf16[128,384]{1,0:T(8,128)(2,1)S(1)} %copy-done.14, bf16[128,384]{1,0:T(8,128)(2,1)S(1)} %get-tuple-element.107.refs_1_, bf16[128,384]{1,0:T(8,128)(2,1)} %collective-permute-done.39.refs_2_, bf16[128,384]{1,0:T(8,128)(2,1)} %collective-permute-done.40.refs_3_, ...), custom_call_target="tpu_custom_call" | custom-call | tf_op jit(solution)/shard_map/basis_grads/pallas_call | solution.py:157
  (265 shorter events, 120.2 us)
Async XLA Ops:
  51.1 37.4 %all-to-all-start.1 = ((bf16[16,24,1792]{2,1,0:T(8,128)(2,1)}), bf16[16,24,1792]{2,1,0:T(8,128)(2,1)S(1)}, u32[]{:S(2)}, u32[]{:S(2)}) async-start(bf16[16,24,1792]{2,1,0:T(8,128)(2,1)} %bitcast.97), calls=%async_computation.1 | async-start | bytes 2752512 | tf_op jit(solution)/shard_map/all_to_all | solution.py:450
  55.4 39.9 %collective-permute-start = (bf16[4,64,1792]{2,1,0:T(8,128)(2,1)}, bf16[4,64,1792]{2,1,0:T(8,128)(2,1)}, u32[]{:S(2)}, u32[]{:S(2)}) collective-permute-start(bf16[4,64,1792]{2,1,0:T(8,128)(2,1)} %refs_0_.2), channel_id=1, source_target_pairs={{0,1},{1,0},{2,3},{3,2},{4,5},{5,4},{6,7},{7,6},{8,9},{9,8},{10,11... | collective-permute-start | bytes 2752520 | tf_op jit(solution)/shard_map/ppermute | solution.py:30
  68.1 23.9 %collective-permute-start.7 = (bf16[384,128]{1,0:T(8,128)(2,1)S(1)}, bf16[384,128]{1,0:T(8,128)(2,1)S(1)}, u32[]{:S(2)}, u32[]{:S(2)}) collective-permute-start(bf16[384,128]{1,0:T(8,128)(2,1)S(1)} %slice.65), channel_id=1, source_target_pairs={{0,1},{1,0},{2,3},{3,2},{4,5},{5,4},{6,7},{7,6},{8,9},{9,8},{10,11... | collective-permute-start | bytes 294920 | tf_op jit(solution)/shard_map/ppermute | solution.py:30
  88.5 15.9 %all-to-all-start.3 = ((bf16[8,64,384]{2,1,0:T(8,128)(2,1)}), bf16[8,64,384]{2,1,0:T(8,128)(2,1)S(1)}, u32[]{:S(2)}, u32[]{:S(2)}) async-start(bf16[8,64,384]{2,1,0:T(8,128)(2,1)} %gather_fusion.1), calls=%async_computation.3 | async-start | bytes 786432 | tf_op jit(solution)/shard_map/all_to_all | solution.py:506
  104.4 29.6 %collective-permute-start.15 = (bf16[8,64,384]{2,1,0:T(8,128)(2,1)S(1)}, bf16[8,64,384]{2,1,0:T(8,128)(2,1)S(1)}, u32[]{:S(2)}, u32[]{:S(2)}) collective-permute-start(bf16[8,64,384]{2,1,0:T(8,128)(2,1)S(1)} %all-to-all-done.3.refs_0_), channel_id=1, source_target_pairs={{0,24},{8,16},{16,8},{24,0},{1,25},{9,17},{17,9},{25,1},{2,26},{10... | collective-permute-start | bytes 1179656 | tf_op jit(solution)/shard_map/ppermute | solution.py:46
  109.5 21.6 %all-to-all-start.2 = ((bf16[8,32,384]{2,1,0:T(8,128)(2,1)}), bf16[8,32,384]{2,1,0:T(8,128)(2,1)S(1)}, u32[]{:S(2)}, u32[]{:S(2)}) async-start(bf16[8,32,384]{2,1,0:T(8,128)(2,1)} %gather_fusion), calls=%async_computation.2 | async-start | bytes 393216 | tf_op jit(solution)/shard_map/all_to_all | solution.py:506
  124.0 13.3 %collective-permute-start.14 = (bf16[8,64,384]{2,1,0:T(8,128)(2,1)S(1)}, bf16[8,64,384]{2,1,0:T(8,128)(2,1)S(1)}, u32[]{:S(2)}, u32[]{:S(2)}) collective-permute-start(bf16[8,64,384]{2,1,0:T(8,128)(2,1)S(1)} %all-to-all-done.3.refs_0_), channel_id=1, source_target_pairs={{0,16},{8,24},{16,0},{24,8},{1,17},{9,25},{17,1},{25,9},{2,18},{10... | collective-permute-start | bytes 1179656 | tf_op jit(solution)/shard_map/ppermute | solution.py:46
  124.0 13.2 %collective-permute-start.13 = (bf16[8,64,384]{2,1,0:T(8,128)(2,1)S(1)}, bf16[8,64,384]{2,1,0:T(8,128)(2,1)S(1)}, u32[]{:S(2)}, u32[]{:S(2)}) collective-permute-start(bf16[8,64,384]{2,1,0:T(8,128)(2,1)S(1)} %all-to-all-done.3.refs_0_), channel_id=1, source_target_pairs={{0,8},{8,0},{16,24},{24,16},{1,9},{9,1},{17,25},{25,17},{2,10},{10... | collective-permute-start | bytes 1179656 | tf_op jit(solution)/shard_map/ppermute | solution.py:46
  131.1 15.9 %collective-permute-start.6 = (bf16[8,32,384]{2,1,0:T(8,128)(2,1)S(1)}, bf16[8,32,384]{2,1,0:T(8,128)(2,1)S(1)}, u32[]{:S(2)}, u32[]{:S(2)}) collective-permute-start(bf16[8,32,384]{2,1,0:T(8,128)(2,1)S(1)} %all-to-all-done.2.refs_0_), channel_id=1, source_target_pairs={{0,24},{8,16},{16,8},{24,0},{1,25},{9,17},{17,9},{25,1},{2,26},{10... | collective-permute-start | bytes 589832 | tf_op jit(solution)/shard_map/ppermute | solution.py:46
  131.6 15.4 %collective-permute-start.5 = (bf16[8,32,384]{2,1,0:T(8,128)(2,1)S(1)}, bf16[8,32,384]{2,1,0:T(8,128)(2,1)S(1)}, u32[]{:S(2)}, u32[]{:S(2)}) collective-permute-start(bf16[8,32,384]{2,1,0:T(8,128)(2,1)S(1)} %all-to-all-done.2.refs_0_), channel_id=1, source_target_pairs={{0,16},{8,24},{16,0},{24,8},{1,17},{9,25},{17,1},{25,9},{2,18},{10... | collective-permute-start | bytes 589832 | tf_op jit(solution)/shard_map/ppermute | solution.py:46
  161.5 17.5 %collective-permute-start.17 = (bf16[8,64,384]{2,1,0:T(8,128)(2,1)}, bf16[8,64,384]{2,1,0:T(8,128)(2,1)}, u32[]{:S(2)}, u32[]{:S(2)}) collective-permute-start(bf16[8,64,384]{2,1,0:T(8,128)(2,1)} %get-tuple-element.60), channel_id=1, source_target_pairs={{0,16},{8,24},{16,0},{24,8},{1,17},{9,25},{17,1},{25,9},{2,18},{10... | collective-permute-start | bytes 1179656 | tf_op jit(solution)/shard_map/ppermute | solution.py:46
  162.1 16.9 %collective-permute-start.18 = (bf16[8,64,384]{2,1,0:T(8,128)(2,1)}, bf16[8,64,384]{2,1,0:T(8,128)(2,1)}, u32[]{:S(2)}, u32[]{:S(2)}) collective-permute-start(bf16[8,64,384]{2,1,0:T(8,128)(2,1)} %get-tuple-element.61), channel_id=1, source_target_pairs={{0,24},{8,16},{16,8},{24,0},{1,25},{9,17},{17,9},{25,1},{2,26},{10... | collective-permute-start | bytes 1179656 | tf_op jit(solution)/shard_map/ppermute | solution.py:46
  163.6 127.6 %collective-permute-start.28 = (bf16[384,1920]{1,0:T(8,128)(2,1)S(1)}, bf16[384,1920]{1,0:T(8,128)(2,1)}, u32[]{:S(2)}, u32[]{:S(2)}) collective-permute-start(bf16[384,1920]{1,0:T(8,128)(2,1)S(1)} %bitcast.90), channel_id=1, source_target_pairs={{0,1},{1,0},{2,3},{3,2},{4,5},{5,4},{6,7},{7,6},{8,9},{9,8},{10,11... | collective-permute-start | bytes 4423688 | tf_op jit(solution)/shard_map/ppermute | solution.py:30
  181.2 24.6 %all-to-all-start.4 = ((bf16[8,64,384]{2,1,0:T(8,128)(2,1)}), bf16[8,64,384]{2,1,0:T(8,128)(2,1)S(1)}, u32[]{:S(2)}, u32[]{:S(2)}) async-start(bf16[8,64,384]{2,1,0:T(8,128)(2,1)} %add_convert_fusion.refs_0_), calls=%async_computation.4 | async-start | bytes 786432 | tf_op jit(solution)/shard_map/all_to_all | solution.py:537
  185.6 127.1 %collective-permute-start.41 = (bf16[384,1792]{1,0:T(8,128)(2,1)S(1)}, bf16[384,1792]{1,0:T(8,128)(2,1)}, u32[]{:S(2)}, u32[]{:S(2)}) collective-permute-start(bf16[384,1792]{1,0:T(8,128)(2,1)S(1)} %bitcast.93), channel_id=1, source_target_pairs={{0,1},{1,0},{2,3},{3,2},{4,5},{5,4},{6,7},{7,6},{8,9},{9,8},{10,11... | collective-permute-start | bytes 4128776 | tf_op jit(solution)/shard_map/ppermute | solution.py:30
  209.1 14.2 %collective-permute-start.22 = (bf16[256,384]{1,0:T(8,128)(2,1)S(1)}, bf16[256,384]{1,0:T(8,128)(2,1)S(1)}, u32[]{:S(2)}, u32[]{:S(2)}) collective-permute-start(bf16[256,384]{1,0:T(8,128)(2,1)S(1)} %bitcast.104), channel_id=1, source_target_pairs={{0,8},{8,0},{16,24},{24,16},{1,9},{9,1},{17,25},{25,17},{2,10},{10... | collective-permute-start | bytes 589832 | tf_op jit(solution)/shard_map/ppermute | solution.py:46
  217.0 57.8 %collective-permute-start.35 = (bf16[32,384]{1,0:T(8,128)(2,1)}, bf16[32,384]{1,0:T(8,128)(2,1)}, u32[]{:S(2)}, u32[]{:S(2)}) collective-permute-start(bf16[32,384]{1,0:T(8,128)(2,1)} %get-tuple-element.110), channel_id=1, source_target_pairs={{0,7},{1,6},{2,5},{3,4},{4,3},{5,2},{6,1},{7,0},{8,15},{9,14},{10,... | collective-permute-start | bytes 73736 | tf_op jit(solution)/shard_map/ppermute | solution.py:545
  219.4 54.1 %collective-permute-start.34 = (bf16[32,384]{1,0:T(8,128)(2,1)}, bf16[32,384]{1,0:T(8,128)(2,1)}, u32[]{:S(2)}, u32[]{:S(2)}) collective-permute-start(bf16[32,384]{1,0:T(8,128)(2,1)} %get-tuple-element.111), channel_id=1, source_target_pairs={{0,6},{1,7},{2,4},{3,5},{4,2},{5,3},{6,0},{7,1},{8,14},{9,15},{10,... | collective-permute-start | bytes 73736 | tf_op jit(solution)/shard_map/ppermute | solution.py:545
  226.4 91.8 %all-to-all-start.5 = ((bf16[16,24,1920]{2,1,0:T(8,128)(2,1)}), bf16[16,24,1920]{2,1,0:T(8,128)(2,1)}, u32[]{:S(2)}, u32[]{:S(2)}) async-start(bf16[16,24,1920]{2,1,0:T(8,128)(2,1)} %bitcast.96), calls=%async_computation.5 | async-start | bytes 2949120 | tf_op jit(solution)/shard_map/all_to_all | solution.py:565
  233.0 25.3 %collective-permute-start.30 = (bf16[32,384]{1,0:T(8,128)(2,1)S(1)}, bf16[32,384]{1,0:T(8,128)(2,1)S(1)}, u32[]{:S(2)}, u32[]{:S(2)}) collective-permute-start(bf16[32,384]{1,0:T(8,128)(2,1)S(1)} %copy-done.39), channel_id=1, source_target_pairs={{0,2},{1,3},{2,0},{3,1},{4,6},{5,7},{6,4},{7,5},{8,10},{9,11},{10,... | collective-permute-start | bytes 73736 | tf_op jit(solution)/shard_map/ppermute | solution.py:545
  272.9 33.1 %collective-permute-start.27 = (bf16[256,384]{1,0:T(8,128)(2,1)}, bf16[256,384]{1,0:T(8,128)(2,1)}, u32[]{:S(2)}, u32[]{:S(2)}) collective-permute-start(bf16[256,384]{1,0:T(8,128)(2,1)} %get-tuple-element.102), channel_id=1, source_target_pairs={{0,1},{1,0},{2,3},{3,2},{4,5},{5,4},{6,7},{7,6},{8,9},{9,8},{10,11... | collective-permute-start | bytes 589832 | tf_op jit(solution)/shard_map/ppermute | solution.py:30
  282.6 23.4 %collective-permute-start.26 = (bf16[256,384]{1,0:T(8,128)(2,1)}, bf16[256,384]{1,0:T(8,128)(2,1)}, u32[]{:S(2)}, u32[]{:S(2)}) collective-permute-start(bf16[256,384]{1,0:T(8,128)(2,1)} %get-tuple-element.104), channel_id=1, source_target_pairs={{0,1},{1,0},{2,3},{3,2},{4,5},{5,4},{6,7},{7,6},{8,9},{9,8},{10,11... | collective-permute-start | bytes 589832 | tf_op jit(solution)/shard_map/ppermute | solution.py:30
  290.5 22.2 %collective-permute-start.40 = (bf16[128,384]{1,0:T(8,128)(2,1)}, bf16[128,384]{1,0:T(8,128)(2,1)}, u32[]{:S(2)}, u32[]{:S(2)}) collective-permute-start(bf16[128,384]{1,0:T(8,128)(2,1)} %get-tuple-element.106), channel_id=1, source_target_pairs={{0,1},{1,0},{2,3},{3,2},{4,5},{5,4},{6,7},{7,6},{8,9},{9,8},{10,11... | collective-permute-start | bytes 294920 | tf_op jit(solution)/shard_map/ppermute | solution.py:30
  291.2 21.5 %collective-permute-start.39 = (bf16[128,384]{1,0:T(8,128)(2,1)}, bf16[128,384]{1,0:T(8,128)(2,1)}, u32[]{:S(2)}, u32[]{:S(2)}) collective-permute-start(bf16[128,384]{1,0:T(8,128)(2,1)} %get-tuple-element.108), channel_id=1, source_target_pairs={{0,1},{1,0},{2,3},{3,2},{4,5},{5,4},{6,7},{7,6},{8,9},{9,8},{10,11... | collective-permute-start | bytes 294920 | tf_op jit(solution)/shard_map/ppermute | solution.py:30
  (66 other events, 707.1 us)

commit v5 on v3

--- a/solution.py
+++ b/solution.py
@@ -121,18 +121,19 @@
     return (got[:n_dp] if built else rows), got[-n_dp:]
 
 
-def basis_grads(keep, other, cols, spot, shape, n_dp):
+def basis_grads(keep, other, cols, other_cols, spot, shape, n_dp, first):
     clusters, rank_own, width = shape
     parts_core = n_dp // 2
     part = rank_own // parts_core
-    half = cols.shape[1]
+    half = cols.shape[0]
     count = keep[0].shape[0] // (clusters * part)
     block = width // 2 if width % 256 == 0 else width
 
     def kernel(spot_ref, *refs):
         ours, theirs = refs[:parts_core], refs[parts_core : 2 * parts_core]
-        cols_ref, outs, rows_ref = refs[2 * parts_core], refs[-1 - count : -1], refs[-1]
-        dp, core = spot_ref[0], spot_ref[1]
+        cols_ref, other_ref = refs[2 * parts_core : 2 * parts_core + 2]
+        outs, rows_ref = refs[-1 - count : -1], refs[-1]
+        dp = spot_ref[0]
 
         @pl.when(pl.program_id(0) == 0)
         def _():
@@ -143,12 +144,12 @@
                     for b in range(count):
                         take = slice((c * count + b) * part, (c * count + b + 1) * part)
                         kind = rows_ref.dtype
-                        rows_ref[core, b, pl.ds(at, part), :] = ours[k][take, :].astype(kind)
-                        rows_ref[1 - core, b, pl.ds(at, part), :] = theirs[k][take, :].astype(kind)
+                        rows_ref[0, b, pl.ds(at, part), :] = ours[k][take, :].astype(kind)
+                        rows_ref[1, b, pl.ds(at, part), :] = theirs[k][take, :].astype(kind)
 
         for b in range(count):
-            total = dot(rows_ref[0, b].astype(BF), cols_ref[0], 1, 0)
-            total += dot(rows_ref[1, b].astype(BF), cols_ref[1], 1, 0)
+            total = dot(rows_ref[0, b].astype(BF), cols_ref[...], 1, 0)
+            total += dot(rows_ref[1, b].astype(BF), other_ref[...], 1, 0)
             outs[b][...] = total
 
     ins = list(keep) + list(other)
@@ -159,7 +160,8 @@
         out_shape=[out] * count,
         in_specs=[SCALAR]
         + [whole(x) for x in ins]
-        + [pl.BlockSpec((2, half, block), lambda j: (0, 0, j), memory_space=VMEM)],
+        + [pl.BlockSpec((half, block), lambda j: (0, j), memory_space=VMEM)] * 2
+        + [ANYWHERE],
         out_specs=[
             pl.BlockSpec((clusters * rank_own, block), lambda j: (0, j), memory_space=VMEM)
         ]
@@ -168,7 +170,7 @@
         compiler_params=params(2 * half),
         cost_estimate=FREE,
         name="basis_grads",
-    )(spot, *ins, cols)
+    )(spot, *ins, cols, other_cols, first)
     return [grad.reshape(shape) for grad in got]
 
 
@@ -346,7 +348,11 @@
         out_specs=[each(out) for out in outs] + [whole(chunk) for chunk in chunks],
         scratch_shapes=[pltpu.VMEM((1, rank, total), rows_kind(rows)), pltpu.VMEM((2, rank, total), FL)],
         compiler_params=params(total, True),
-        cost_estimate=FREE,
+        cost_estimate=pl.CostEstimate(
+            flops=local * slots * rank * (6 * total + 6 * hid),
+            bytes_accessed=32 << 20,
+            transcendentals=0,
+        ),
         name="backward",
     )(dp.reshape(1), *pieces, *ins)
     return got[:4], got[4:]
@@ -488,8 +494,10 @@
         dy_half, chip_rows(own_out, other_out), own_out, other_out, spot, n_dp
     )
     mine_out = sum_parts(trade(lambda k: terms_out[k], "dp"))
+    h_pieces = trade(lambda k: got_in, "dp")
+    for piece in h_pieces[1:]:
+        mine_out = after(mine_out, piece)
     got_out = to_group(mine_out)
-    h_pieces = trade(lambda k: got_in, "dp")
     (hg, hu, hidden, mixed, act, lift), mixed_chunks = forward(
         h_pieces, pick, weight_of, gate_factor, up_factor, down_factor, dp
     )
@@ -498,23 +506,23 @@
         d_pieces, pick, slot_weight, mixed, act, lift, gate_factor, up_factor, down_factor, dp
     )
 
-    owner = group_cluster[None, :] == jnp.arange(clusters, dtype=jnp.int32)[:, None]
-
-    def from_groups(mine):
-        got = lax.all_to_all(mine, ("ez", "core"), split_axis=0, concat_axis=0, tiled=True)
-        return jnp.sum(
-            jnp.where(owner[:, :, None, None], got.astype(FL)[None], 0.0), axis=1
-        ).astype(BF).reshape(-1, half)
+    numbers = jnp.arange(clusters, dtype=jnp.int32)[:, None]
+
+    def by_cluster(got, groups):
+        owner = (groups[None, :] == numbers)[:, :, None, None]
+        summed = jnp.sum(jnp.where(owner, got.astype(FL)[None], 0.0), axis=1)
+        return summed.astype(BF).reshape(-1, half)
 
     mixed_mine = sum_parts(trade(lambda k: mixed_chunks[k], "dp"))
     in_mine = sum_parts(trade(lambda k: in_chunks[k], "dp"))
     grad_gate_factor, grad_up_factor, grad_down_factor = factor_grads(
         hg, grad_gate, hu, grad_up, hidden, back, total, in_mine
     )
-    mixed_sum = from_groups(mixed_mine)
-    in_sum = after(from_groups(in_mine), grad_gate_factor)
+    mine = jnp.concatenate([in_mine, mixed_mine], axis=1)
+    got = lax.all_to_all(mine, ("ez", "core"), split_axis=0, concat_axis=0, tiled=True)
+    in_sum = after(by_cluster(got[:, : 2 * rank_part], group_cluster), grad_gate_factor)
+    mixed_sum = by_cluster(got[:, 2 * rank_part :], group_cluster)
     in_parts = trade(lambda k: in_sum, "dp")
-    mixed_parts = trade(lambda k: mixed_sum, "dp")
 
     placed = cell == jnp.arange(slots, dtype=jnp.int32)[None, :, None]
     scores = jnp.sum(jnp.where(placed, dots, 0.0), axis=1).reshape(local, 2, half)
@@ -526,13 +534,12 @@
     scores = jnp.pad(scores, ((0, 0), (0, lanes - 2 * local)))
 
     grad_x = sum(mm("rt,rf->tf", part, rows) for part, rows in zip(in_parts, rows_in))
-    rows = jnp.concatenate([grad_x.astype(BF), scores], axis=1)
-    rows = rows.reshape(n_dp * n_z, tok_rows, width + lanes)
+    leaving = jnp.concatenate([grad_x.astype(BF), scores], axis=1)
+    rows = leaving.reshape(n_dp * n_z, tok_rows, width + lanes)
     rows = lax.all_to_all(rows, ("dp", "ez"), split_axis=0, concat_axis=0, tiled=True)
     rows = rows.reshape(n_dp, n_z, tok_rows, width + lanes)
-
-    x_both = lax.all_gather(x_half, "core", axis=0)
-    dy_both = lax.all_gather(dy_half, "core", axis=0)
+    x_other = core_swap(x_half)
+    dy_other = core_swap(dy_half)
     same = core == dp // parts_core
 
     def own_ranks(parts):
@@ -543,15 +550,16 @@
 
     shape = (clusters, rank_own, width)
     grad_gate_basis, grad_up_basis = basis_grads(
-        *own_ranks(in_parts), x_both, spot, shape, n_dp
-    )
+        *own_ranks(in_parts), x_half, x_other, spot, shape, n_dp, leaving
+    )
+    mixed_sum = after(mixed_sum, grad_gate_basis)
+    mixed_parts = trade(lambda k: mixed_sum, "dp")
     (grad_down_basis,) = basis_grads(
-        *own_ranks(mixed_parts), dy_both, spot, shape, n_dp
+        *own_ranks(mixed_parts), dy_half, dy_other, spot, shape, n_dp, leaving
     )
 
     grad_rows = jnp.sum(rows[..., :width].astype(FL), axis=1)
-    for part in (grad_gate_basis, grad_down_basis):
-        grad_rows = after(grad_rows, part)
+    grad_rows = after(grad_rows, grad_down_basis)
     grad_tokens = grad_rows.astype(BF).transpose(1, 0, 2).reshape(tok_rows, model_width)
     by_expert = jnp.sum(rows[..., width : width + 2 * local].astype(FL), axis=0)
     by_expert = by_expert.transpose(1, 0, 2).reshape(tok_rows, 1, experts)

time: 278 us -> 292 us (1.050)
  waiting for transfers between devices: 67.5 us -> 122 us
  blocking collectives: 44.7 us -> 0 us
  between operations: 17.4 us -> 5.98 us
  local copies, waits for them, and re-layouts: 26.1 us -> 32.6 us
  starting transfers between devices: 56.2 us -> 61 us
    all_to_all x1 -> x2, waiting for transfers between devices: 5.33 us -> 57.9 us  [own_columns(): lax.all_to_all(rows, ('dp', 'ez'), split_axis=0, concat_axis=0, tiled=True)]
    all_to_all x1 -> x0, blocking collectives: 44.7 us -> none  [own_columns(): lax.all_to_all(rows, ('dp', 'ez'), split_axis=0, concat_axis=0, tiled=True)]
    ppermute x24, waiting for transfers between devices: 48.5 us -> 30.9 us  [trade(): lax.ppermute(chunk_for(k), axis, [(i, i ^ k) for i in range(n)])]
    all_to_all x2, waiting for transfers between devices: 8.55 us -> 19.5 us  [to_group(): lax.all_to_all(send, ('ez', 'core'), split_axis=0, concat_axis=0, tiled=T...]
    all_to_all x1 -> x2, starting transfers between devices: 3.7 us -> 12 us  [own_columns(): lax.all_to_all(rows, ('dp', 'ez'), split_axis=0, concat_axis=0, tiled=True)]
    all_to_all x1, waiting for transfers between devices: 0.01 us -> 6.47 us  [body(): lax.all_to_all(rows, ('dp', 'ez'), split_axis=0, concat_axis=0, tiled=True)]
    all_to_all x2 -> x1, starting transfers between devices: 8.25 us -> 3.97 us  [body(): lax.all_to_all(mine, ('ez', 'core'), split_axis=0, concat_axis=0, tiled=T...]
    slice x4 -> x7, local copies, waits for them, and re-layouts: 4.21 us -> 8.33 us  [after(): lax.slice(first, (0,) * first.ndim, (1,) * first.ndim).reshape(())]
  transfers between devices with their start and end apart: 41 -> 41, of which waited for: 16 -> 20; matrix products, arithmetic and copies ran while one was open for 9% -> 8% of each run, Pallas kernels for 12% -> 14%
where the time goes in v5:
time: 292 us; the launch traced here: 290 us
  waiting for transfers between devices  122 us (42%)
  starting transfers between devices  61 us (21%)
  Pallas kernels  47 us (16%)
  local copies, waits for them, and re-layouts  32.6 us (11%)
  other arithmetic  17.8 us (6%)
  between operations  5.98 us (2%)
  matrix products  3.58 us (1%)
    all_to_all x2, waiting for transfers between devices, own_columns(): lax.all_to_all(rows, ('dp', 'ez'), split_axis=0, concat_axis=0, tiled=True)  57.9 us
    ppermute x24, waiting for transfers between devices, trade(): lax.ppermute(chunk_for(k), axis, [(i, i ^ k) for i in range(n)])  30.9 us
    ppermute x24, starting transfers between devices, trade(): lax.ppermute(chunk_for(k), axis, [(i, i ^ k) for i in range(n)])  29.3 us
    all_to_all x2, waiting for transfers between devices, to_group(): lax.all_to_all(send, ('ez', 'core'), split_axis=0, concat_axis=0, tiled=T...  19.5 us
    unnamed x85, local copies, waits for them, and re-layouts  14.1 us
    pallas_call x1, Pallas kernels, backward(): pl.pallas_call(kernel, grid=(local,), out_shape=outs + chunks, in_specs=[...  12.2 us
    all_to_all x2, starting transfers between devices, own_columns(): lax.all_to_all(rows, ('dp', 'ez'), split_axis=0, concat_axis=0, tiled=True)  12 us
    pallas_call x1, Pallas kernels, forward(): pl.pallas_call(kernel, grid=(local,), out_shape=outs + chunks, in_specs=[...  10.9 us
  transfers between devices with their start and end apart: 41, of which 20 were waited for; matrix products, arithmetic and copies ran while one was open for 8% of the time, Pallas kernels for 14%

profile of v5, /device:TPU:0, one launch (start us, length us, event | category | flops | bytes accessed | tf_op | source)
XLA Modules:
  0.0 290.2 jit_solution(8530379492442642154)
XLA Ops:
  4.8 8.3 %all-to-all-start = ((bf16[16,24,1920]{2,1,0:T(8,128)(2,1)}), bf16[16,24,1920]{2,1,0:T(8,128)(2,1)S(1)}, u32[]{:S(2)}, u32[]{:S(2)}) async-start(bf16[16,24,1920]{2,1,0:T(8,128)(2,1)} %bitcast.3), calls=%async_computation | async-start | bytes 2949120 | tf_op jit(solution)/shard_map/all_to_all | solution.py:430
  17.1 32.6 %all-to-all-done = bf16[16,24,1920]{2,1,0:T(8,128)(2,1)S(1)} async-done(((bf16[16,24,1920]{2,1,0:T(8,128)(2,1)}), bf16[16,24,1920]{2,1,0:T(8,128)(2,1)S(1)}, u32[]{:S(2)}, u32[]{:S(2)}) %all-to-all-start) | async-done | bytes 1474592 | tf_op jit(solution)/shard_map/all_to_all | solution.py:430
  50.9 5.5 %project.3 = (bf16[256,1792]{1,0:T(8,128)(2,1)}, bf16[256,1792]{1,0:T(8,128)(2,1)}, bf16[256,1792]{1,0:T(8,128)(2,1)}, bf16[256,1792]{1,0:T(8,128)(2,1)}, bf16[2...) custom-call(s32[2]{0:T(128)} %pad_add_fusion.spot_ref, ...), custom_call_target="tpu_custom_call" | custom-call | tf_op jit(solution)/shard_map/project/pallas_call | solution.py:112
  62.4 2.8 collective-permute-done.8
  69.0 3.6 %all-to-all-start.2 = ((bf16[8,64,384]{2,1,0:T(8,128)(2,1)}), bf16[8,64,384]{2,1,0:T(8,128)(2,1)S(1)}, u32[]{:S(2)}, u32[]{:S(2)}) async-start(bf16[8,64,384]{2,1,0:T(8,128)(2,1)} %gather_fusion), calls=%async_computation.2 | async-start | bytes 786432 | tf_op jit(solution)/shard_map/all_to_all | solution.py:486
  73.0 12.2 %all-to-all-done.2.refs_0_ = bf16[8,64,384]{2,1,0:T(8,128)(2,1)S(1)} async-done(((bf16[8,64,384]{2,1,0:T(8,128)(2,1)}), bf16[8,64,384]{2,1,0:T(8,128)(2,1)S(1)}, u32[]{:S(2)}, u32[]{:S(2)}) %all-to-all-start.2) | async-done | bytes 393248 | tf_op jit(solution)/shard_map/all_to_all | solution.py:486
  86.4 3.7 %all-to-all-start.1 = ((bf16[16,24,1792]{2,1,0:T(8,128)(2,1)}), bf16[16,24,1792]{2,1,0:T(8,128)(2,1)S(1)}, u32[]{:S(2)}, u32[]{:S(2)}) async-start(bf16[16,24,1792]{2,1,0:T(8,128)(2,1)} %bitcast.68), calls=%async_computation.1 | async-start | bytes 2752512 | tf_op jit(solution)/shard_map/all_to_all | solution.py:430
  91.6 2.7 collective-permute-start.11
  99.5 25.3 %all-to-all-done.1 = bf16[16,24,1792]{2,1,0:T(8,128)(2,1)S(1)} async-done(((bf16[16,24,1792]{2,1,0:T(8,128)(2,1)}), bf16[16,24,1792]{2,1,0:T(8,128)(2,1)S(1)}, u32[]{:S(2)}, u32[]{:S(2)}) %all-to-all-start.1) | async-done | bytes 1376288 | tf_op jit(solution)/shard_map/all_to_all | solution.py:430
  125.9 4.3 %project.2 = (bf16[128,1792]{1,0:T(8,128)(2,1)}, bf16[128,1792]{1,0:T(8,128)(2,1)}, bf16[128,1792]{1,0:T(8,128)(2,1)}, bf16[128,1792]{1,0:T(8,128)(2,1)}, bf16[1...) custom-call(s32[2]{0:T(128)} %pad_add_fusion.spot_ref, ...), custom_call_target="tpu_custom_call" | custom-call | tf_op jit(solution)/shard_map/project/pallas_call | solution.py:112
  142.9 3.6 %all-to-all-start.3 = ((bf16[8,32,384]{2,1,0:T(8,128)(2,1)}), bf16[8,32,384]{2,1,0:T(8,128)(2,1)S(1)}, u32[]{:S(2)}, u32[]{:S(2)}) async-start(bf16[8,32,384]{2,1,0:T(8,128)(2,1)} %gather_fusion.1), calls=%async_computation.3 | async-start | bytes 393216 | tf_op jit(solution)/shard_map/all_to_all | solution.py:486
  147.2 7.3 %all-to-all-done.3.refs_0_ = bf16[8,32,384]{2,1,0:T(8,128)(2,1)S(1)} async-done(((bf16[8,32,384]{2,1,0:T(8,128)(2,1)}), bf16[8,32,384]{2,1,0:T(8,128)(2,1)S(1)}, u32[]{:S(2)}, u32[]{:S(2)}) %all-to-all-start.3) | async-done | bytes 196640 | tf_op jit(solution)/shard_map/all_to_all | solution.py:486
  160.7 10.9 %forward.1 = (bf16[4,224,512]{2,1,0:T(8,128)(2,1)}, bf16[4,224,512]{2,1,0:T(8,128)(2,1)}, bf16[4,224,512]{2,1,0:T(8,128)(2,1)}, bf16[4,224,512]{2,1,0:T(8,128)(2...) custom-call(s32[1]{0:T(128)} %bitcast.dp_ref, ...), custom_call_target="tpu_custom_call" | custom-call | tf_op jit(solution)/shard_map/forward/pallas_call | solution.py:281
  176.0 12.2 %backward.1 = (bf16[4,224,512]{2,1,0:T(8,128)(2,1)}, bf16[4,224,512]{2,1,0:T(8,128)(2,1)}, bf16[4,224,512]{2,1,0:T(8,128)(2,1)}, f32[4,224,1]{2,1,0:T(8,128)}, b...) custom-call(s32[1]{0:T(128)} %bitcast.dp_ref, ...), custom_call_target="tpu_custom_call" | custom-call | flops 3523215360 | bytes 33554432 | tf_op jit(solution)/shard_map/backward/pallas_call | solution.py:343
  191.8 9.5 %collective-permute-done.18 = bf16[8,64,384]{2,1,0:T(8,128)(2,1)S(1)} collective-permute-done((bf16[8,64,384]{2,1,0:T(8,128)(2,1)}, bf16[8,64,384]{2,1,0:T(8,128)(2,1)S(1)}, u32[]{:S(2)}, u32[]{:S(2)}) %collective-permute-start.18) | collective-permute-done | bytes 393248 | tf_op jit(solution)/shard_map/ppermute | solution.py:46
  201.4 3.7 %collective-permute-done.17 = bf16[8,64,384]{2,1,0:T(8,128)(2,1)S(1)} collective-permute-done((bf16[8,64,384]{2,1,0:T(8,128)(2,1)}, bf16[8,64,384]{2,1,0:T(8,128)(2,1)S(1)}, u32[]{:S(2)}, u32[]{:S(2)}) %collective-permute-start.17) | collective-permute-done | bytes 393248 | tf_op jit(solution)/shard_map/ppermute | solution.py:46
  207.3 4.0 %all-to-all-start.4 = ((bf16[8,96,384]{2,1,0:T(8,128)(2,1)}), bf16[8,96,384]{2,1,0:T(8,128)(2,1)S(1)}, u32[]{:S(2)}, u32[]{:S(2)}) async-start(bf16[8,96,384]{2,1,0:T(8,128)(2,1)} %pad_maximum_fusion), calls=%async_computation.4 | async-start | bytes 1179648 | tf_op jit(solution)/shard_map/all_to_all | solution.py:522
  219.7 5.2 %factor_grads.1 = (f32[4,512,512]{2,1,0:T(8,128)}, f32[4,512,512]{2,1,0:T(8,128)}, f32[4,512,512]{2,1,0:T(8,128)}) custom-call(bf16[4,224,512]{2,1,0:T(8,128)(2,1)S(1)} %copy-done.5, bf16[4,224,512]{2,1,0:T(8,128)(2,1)S(1)} %copy-done.9, bf16[4,224,512]{2,1,0:T(8,128)(2,1)S(1)} %copy-done.6, bf16[4,224,512]{2,1,0:T(8,128)(2,1)S(1)} %copy-done.10, ...), custom_call_target="tpu_custom_call" | custom-call | tf_op jit(solution)/shard_map/factor_grads/pallas_call | solution.py:376
  232.3 5.0 %collective-permute-done.24 = bf16[256,384]{1,0:T(8,128)(2,1)S(1)} collective-permute-done((bf16[256,384]{1,0:T(8,128)(2,1)S(1)}, bf16[256,384]{1,0:T(8,128)(2,1)S(1)}, u32[]{:S(2)}, u32[]{:S(2)}) %collective-permute-start.24) | collective-permute-done | bytes 196640 | tf_op jit(solution)/shard_map/ppermute | solution.py:46
  243.8 5.2 %all-to-all-start.5 = ((bf16[16,24,1920]{2,1,0:T(8,128)(2,1)}), bf16[16,24,1920]{2,1,0:T(8,128)(2,1)}, u32[]{:S(2)}, u32[]{:S(2)}) async-start(bf16[16,24,1920]{2,1,0:T(8,128)(2,1)} %bitcast.24), calls=%async_computation.5 | async-start | bytes 2949120 | tf_op jit(solution)/shard_map/all_to_all | solution.py:539
  254.9 4.6 %basis_grads.2 = (f32[256,1792]{1,0:T(8,128)}, f32[256,1792]{1,0:T(8,128)}) custom-call(s32[2]{0:T(128)S(1)} %copy-done.13, bf16[256,384]{1,0:T(8,128)(2,1)S(1)} %get-tuple-element.105.refs_0_, bf16[256,384]{1,0:T(8,128)(2,1)S(1)} %get-tuple-element.103.refs_1_, bf16[256,384]{1,0:T(8,128)(2,1)S(1)} %collective-permute-done.26.refs_2_, ...), custom_call_target="tpu_custom_call" | custom-call | tf_op jit(solution)/shard_map/basis_grads/pallas_call | solution.py:157
  265.0 4.6 %collective-permute-done.29 = bf16[128,384]{1,0:T(8,128)(2,1)S(1)} collective-permute-done((bf16[128,384]{1,0:T(8,128)(2,1)S(1)}, bf16[128,384]{1,0:T(8,128)(2,1)S(1)}, u32[]{:S(2)}, u32[]{:S(2)}) %collective-permute-start.29) | collective-permute-done | bytes 98336 | tf_op jit(solution)/shard_map/ppermute | solution.py:46
  274.0 3.5 %basis_grads.3 = f32[256,1792]{1,0:T(8,128)} custom-call(s32[2]{0:T(128)S(1)} %copy-done.13, bf16[128,384]{1,0:T(8,128)(2,1)S(1)} %get-tuple-element.109.refs_0_, bf16[128,384]{1,0:T(8,128)(2,1)S(1)} %get-tuple-element.107.refs_1_, bf16[128,384]{1,0:T(8,128)(2,1)S(1)} %collective-permute-done.32.refs_2_, ...), custom_call_target="tpu_custom_call" | custom-call | tf_op jit(solution)/shard_map/basis_grads/pallas_call | solution.py:157
  279.4 6.5 %all-to-all-done.5 = bf16[16,24,1920]{2,1,0:T(8,128)(2,1)} async-done(((bf16[16,24,1920]{2,1,0:T(8,128)(2,1)}), bf16[16,24,1920]{2,1,0:T(8,128)(2,1)}, u32[]{:S(2)}, u32[]{:S(2)}) %all-to-all-start.5) | async-done | bytes 1474592 | tf_op jit(solution)/shard_map/all_to_all | solution.py:539
  (235 shorter events, 97.3 us)
Async XLA Ops:
  4.8 44.9 %all-to-all-start = ((bf16[16,24,1920]{2,1,0:T(8,128)(2,1)}), bf16[16,24,1920]{2,1,0:T(8,128)(2,1)S(1)}, u32[]{:S(2)}, u32[]{:S(2)}) async-start(bf16[16,24,1920]{2,1,0:T(8,128)(2,1)} %bitcast.3), calls=%async_computation | async-start | bytes 2949120 | tf_op jit(solution)/shard_map/all_to_all | solution.py:430
  56.9 9.7 %collective-permute-start.7 = (bf16[256,384]{1,0:T(8,128)(2,1)}, bf16[256,384]{1,0:T(8,128)(2,1)S(1)}, u32[]{:S(2)}, u32[]{:S(2)}) collective-permute-start(bf16[256,384]{1,0:T(8,128)(2,1)} %get-tuple-element.51), channel_id=1, source_target_pairs={{0,16},{8,24},{16,0},{24,8},{1,17},{9,25},{17,1},{25,9},{2,18},{10... | collective-permute-start | bytes 589832 | tf_op jit(solution)/shard_map/ppermute | solution.py:46
  69.0 16.2 %all-to-all-start.2 = ((bf16[8,64,384]{2,1,0:T(8,128)(2,1)}), bf16[8,64,384]{2,1,0:T(8,128)(2,1)S(1)}, u32[]{:S(2)}, u32[]{:S(2)}) async-start(bf16[8,64,384]{2,1,0:T(8,128)(2,1)} %gather_fusion), calls=%async_computation.2 | async-start | bytes 786432 | tf_op jit(solution)/shard_map/all_to_all | solution.py:486
  86.4 38.4 %all-to-all-start.1 = ((bf16[16,24,1792]{2,1,0:T(8,128)(2,1)}), bf16[16,24,1792]{2,1,0:T(8,128)(2,1)S(1)}, u32[]{:S(2)}, u32[]{:S(2)}) async-start(bf16[16,24,1792]{2,1,0:T(8,128)(2,1)} %bitcast.68), calls=%async_computation.1 | async-start | bytes 2752512 | tf_op jit(solution)/shard_map/all_to_all | solution.py:430
  91.6 39.8 %collective-permute-start.11 = (bf16[8,64,384]{2,1,0:T(8,128)(2,1)S(1)}, bf16[8,64,384]{2,1,0:T(8,128)(2,1)}, u32[]{:S(2)}, u32[]{:S(2)}) collective-permute-start(bf16[8,64,384]{2,1,0:T(8,128)(2,1)S(1)} %all-to-all-done.2.refs_0_), channel_id=1, source_target_pairs={{0,24},{8,16},{16,8},{24,0},{1,25},{9,17},{17,9},{25,1},{2,26},{10... | collective-permute-start | bytes 1179656 | tf_op jit(solution)/shard_map/ppermute | solution.py:46
  94.3 42.5 %collective-permute-start.10 = (bf16[8,64,384]{2,1,0:T(8,128)(2,1)S(1)}, bf16[8,64,384]{2,1,0:T(8,128)(2,1)}, u32[]{:S(2)}, u32[]{:S(2)}) collective-permute-start(bf16[8,64,384]{2,1,0:T(8,128)(2,1)S(1)} %all-to-all-done.2.refs_0_), channel_id=1, source_target_pairs={{0,16},{8,24},{16,0},{24,8},{1,17},{9,25},{17,1},{25,9},{2,18},{10... | collective-permute-start | bytes 1179656 | tf_op jit(solution)/shard_map/ppermute | solution.py:46
  94.9 43.8 %collective-permute-start.9 = (bf16[8,64,384]{2,1,0:T(8,128)(2,1)S(1)}, bf16[8,64,384]{2,1,0:T(8,128)(2,1)}, u32[]{:S(2)}, u32[]{:S(2)}) collective-permute-start(bf16[8,64,384]{2,1,0:T(8,128)(2,1)S(1)} %all-to-all-done.2.refs_0_), channel_id=1, source_target_pairs={{0,8},{8,0},{16,24},{24,16},{1,9},{9,1},{17,25},{25,17},{2,10},{10... | collective-permute-start | bytes 1179656 | tf_op jit(solution)/shard_map/ppermute | solution.py:46
  130.2 10.3 %collective-permute-start.3 = (bf16[128,384]{1,0:T(8,128)(2,1)}, bf16[128,384]{1,0:T(8,128)(2,1)S(1)}, u32[]{:S(2)}, u32[]{:S(2)}) collective-permute-start(bf16[128,384]{1,0:T(8,128)(2,1)} %get-tuple-element.48), channel_id=1, source_target_pairs={{0,24},{8,16},{16,8},{24,0},{1,25},{9,17},{17,9},{25,1},{2,26},{10... | collective-permute-start | bytes 294920 | tf_op jit(solution)/shard_map/ppermute | solution.py:46
  130.8 9.8 %collective-permute-start.2 = (bf16[128,384]{1,0:T(8,128)(2,1)}, bf16[128,384]{1,0:T(8,128)(2,1)S(1)}, u32[]{:S(2)}, u32[]{:S(2)}) collective-permute-start(bf16[128,384]{1,0:T(8,128)(2,1)} %get-tuple-element.47), channel_id=1, source_target_pairs={{0,16},{8,24},{16,0},{24,8},{1,17},{9,25},{17,1},{25,9},{2,18},{10... | collective-permute-start | bytes 294920 | tf_op jit(solution)/shard_map/ppermute | solution.py:46
  142.9 11.7 %all-to-all-start.3 = ((bf16[8,32,384]{2,1,0:T(8,128)(2,1)}), bf16[8,32,384]{2,1,0:T(8,128)(2,1)S(1)}, u32[]{:S(2)}, u32[]{:S(2)}) async-start(bf16[8,32,384]{2,1,0:T(8,128)(2,1)} %gather_fusion.1), calls=%async_computation.3 | async-start | bytes 393216 | tf_op jit(solution)/shard_map/all_to_all | solution.py:486
  154.6 18.6 %collective-permute-start.12 = (bf16[8,32,384]{2,1,0:T(8,128)(2,1)S(1)}, bf16[8,32,384]{2,1,0:T(8,128)(2,1)S(1)}, u32[]{:S(2)}, u32[]{:S(2)}) collective-permute-start(bf16[8,32,384]{2,1,0:T(8,128)(2,1)S(1)} %all-to-all-done.3.refs_0_), channel_id=1, source_target_pairs={{0,8},{8,0},{16,24},{24,16},{1,9},{9,1},{17,25},{25,17},{2,10},{10... | collective-permute-start | bytes 589832 | tf_op jit(solution)/shard_map/ppermute | solution.py:46
  154.6 20.6 %collective-permute-start.13 = (bf16[8,32,384]{2,1,0:T(8,128)(2,1)S(1)}, bf16[8,32,384]{2,1,0:T(8,128)(2,1)S(1)}, u32[]{:S(2)}, u32[]{:S(2)}) collective-permute-start(bf16[8,32,384]{2,1,0:T(8,128)(2,1)S(1)} %all-to-all-done.3.refs_0_), channel_id=1, source_target_pairs={{0,16},{8,24},{16,0},{24,8},{1,17},{9,25},{17,1},{25,9},{2,18},{10... | collective-permute-start | bytes 589832 | tf_op jit(solution)/shard_map/ppermute | solution.py:46
  155.7 19.5 %collective-permute-start.14 = (bf16[8,32,384]{2,1,0:T(8,128)(2,1)S(1)}, bf16[8,32,384]{2,1,0:T(8,128)(2,1)S(1)}, u32[]{:S(2)}, u32[]{:S(2)}) collective-permute-start(bf16[8,32,384]{2,1,0:T(8,128)(2,1)S(1)} %all-to-all-done.3.refs_0_), channel_id=1, source_target_pairs={{0,24},{8,16},{16,8},{24,0},{1,25},{9,17},{17,9},{25,1},{2,26},{10... | collective-permute-start | bytes 589832 | tf_op jit(solution)/shard_map/ppermute | solution.py:46
  171.6 18.1 %collective-permute-start.21 = (bf16[8,32,384]{2,1,0:T(8,128)(2,1)}, bf16[8,32,384]{2,1,0:T(8,128)(2,1)S(1)}, u32[]{:S(2)}, u32[]{:S(2)}) collective-permute-start(bf16[8,32,384]{2,1,0:T(8,128)(2,1)} %get-tuple-element.65), channel_id=1, source_target_pairs={{0,24},{8,16},{16,8},{24,0},{1,25},{9,17},{17,9},{25,1},{2,26},{10... | collective-permute-start | bytes 589832 | tf_op jit(solution)/shard_map/ppermute | solution.py:46
  172.2 19.5 %collective-permute-start.20 = (bf16[8,32,384]{2,1,0:T(8,128)(2,1)}, bf16[8,32,384]{2,1,0:T(8,128)(2,1)S(1)}, u32[]{:S(2)}, u32[]{:S(2)}) collective-permute-start(bf16[8,32,384]{2,1,0:T(8,128)(2,1)} %get-tuple-element.64), channel_id=1, source_target_pairs={{0,16},{8,24},{16,0},{24,8},{1,17},{9,25},{17,1},{25,9},{2,18},{10... | collective-permute-start | bytes 589832 | tf_op jit(solution)/shard_map/ppermute | solution.py:46
  173.1 18.6 %collective-permute-start.19 = (bf16[8,32,384]{2,1,0:T(8,128)(2,1)}, bf16[8,32,384]{2,1,0:T(8,128)(2,1)S(1)}, u32[]{:S(2)}, u32[]{:S(2)}) collective-permute-start(bf16[8,32,384]{2,1,0:T(8,128)(2,1)} %get-tuple-element.63), channel_id=1, source_target_pairs={{0,8},{8,0},{16,24},{24,16},{1,9},{9,1},{17,25},{25,17},{2,10},{10... | collective-permute-start | bytes 589832 | tf_op jit(solution)/shard_map/ppermute | solution.py:46
  188.1 13.2 %collective-permute-start.18 = (bf16[8,64,384]{2,1,0:T(8,128)(2,1)}, bf16[8,64,384]{2,1,0:T(8,128)(2,1)S(1)}, u32[]{:S(2)}, u32[]{:S(2)}) collective-permute-start(bf16[8,64,384]{2,1,0:T(8,128)(2,1)} %get-tuple-element.61), channel_id=1, source_target_pairs={{0,24},{8,16},{16,8},{24,0},{1,25},{9,17},{17,9},{25,1},{2,26},{10... | collective-permute-start | bytes 1179656 | tf_op jit(solution)/shard_map/ppermute | solution.py:46
  188.8 16.3 %collective-permute-start.17 = (bf16[8,64,384]{2,1,0:T(8,128)(2,1)}, bf16[8,64,384]{2,1,0:T(8,128)(2,1)S(1)}, u32[]{:S(2)}, u32[]{:S(2)}) collective-permute-start(bf16[8,64,384]{2,1,0:T(8,128)(2,1)} %get-tuple-element.60), channel_id=1, source_target_pairs={{0,16},{8,24},{16,0},{24,8},{1,17},{9,25},{17,1},{25,9},{2,18},{10... | collective-permute-start | bytes 1179656 | tf_op jit(solution)/shard_map/ppermute | solution.py:46
  189.7 15.3 %collective-permute-start.16 = (bf16[8,64,384]{2,1,0:T(8,128)(2,1)}, bf16[8,64,384]{2,1,0:T(8,128)(2,1)S(1)}, u32[]{:S(2)}, u32[]{:S(2)}) collective-permute-start(bf16[8,64,384]{2,1,0:T(8,128)(2,1)} %get-tuple-element.59), channel_id=1, source_target_pairs={{0,8},{8,0},{16,24},{24,16},{1,9},{9,1},{17,25},{25,17},{2,10},{10... | collective-permute-start | bytes 1179656 | tf_op jit(solution)/shard_map/ppermute | solution.py:46
  207.3 20.7 %all-to-all-start.4 = ((bf16[8,96,384]{2,1,0:T(8,128)(2,1)}), bf16[8,96,384]{2,1,0:T(8,128)(2,1)S(1)}, u32[]{:S(2)}, u32[]{:S(2)}) async-start(bf16[8,96,384]{2,1,0:T(8,128)(2,1)} %pad_maximum_fusion), calls=%async_computation.4 | async-start | bytes 1179648 | tf_op jit(solution)/shard_map/all_to_all | solution.py:522
  213.3 16.5 %collective-permute-start.25 = (bf16[4,384]{1,0:T(4,128)(2,1)S(1)}, bf16[4,384]{1,0:T(4,128)(2,1)S(1)}, u32[]{:S(2)}, u32[]{:S(2)}) collective-permute-start(bf16[4,384]{1,0:T(4,128)(2,1)S(1)} %select_bitcast_fusion.2), channel_id=1, source_target_pairs={{0,1},{1,0},{2,3},{3,2},{4,5},{5,4},{6,7},{7,6},{8,9},{9,8},{10,11... | collective-permute-start | bytes 9224 | tf_op jit(solution)/shard_map/ppermute | solution.py:30
  229.9 10.2 %collective-permute-start.23 = (bf16[256,384]{1,0:T(8,128)(2,1)S(1)}, bf16[256,384]{1,0:T(8,128)(2,1)S(1)}, u32[]{:S(2)}, u32[]{:S(2)}) collective-permute-start(bf16[256,384]{1,0:T(8,128)(2,1)S(1)} %bitcast.74), channel_id=1, source_target_pairs={{0,16},{8,24},{16,0},{24,8},{1,17},{9,25},{17,1},{25,9},{2,18},{10... | collective-permute-start | bytes 589832 | tf_op jit(solution)/shard_map/ppermute | solution.py:46
  243.8 42.1 %all-to-all-start.5 = ((bf16[16,24,1920]{2,1,0:T(8,128)(2,1)}), bf16[16,24,1920]{2,1,0:T(8,128)(2,1)}, u32[]{:S(2)}, u32[]{:S(2)}) async-start(bf16[16,24,1920]{2,1,0:T(8,128)(2,1)} %bitcast.24), calls=%async_computation.5 | async-start | bytes 2949120 | tf_op jit(solution)/shard_map/all_to_all | solution.py:539
  249.2 23.7 %collective-permute-start.34 = (bf16[384,1792]{1,0:T(8,128)(2,1)S(1)}, bf16[384,1792]{1,0:T(8,128)(2,1)}, u32[]{:S(2)}, u32[]{:S(2)}) collective-permute-start(bf16[384,1792]{1,0:T(8,128)(2,1)S(1)} %bitcast.66), channel_id=1, source_target_pairs={{0,1},{1,0},{2,3},{3,2},{4,5},{5,4},{6,7},{7,6},{8,9},{9,8},{10,11... | collective-permute-start | bytes 4128776 | tf_op jit(solution)/shard_map/ppermute | solution.py:30
  (57 other events, 454.1 us)

commit v6 on v5

--- a/solution.py
+++ b/solution.py
@@ -47,6 +47,31 @@
     return [chunk_for(0)] + sent
 
 
+def gather_z(share):
+    n = lax.axis_size("ez")
+    if n != 4:
+        return trade(lambda k: share, "ez")
+    far = lax.ppermute(share, "ez", [(0, 2), (2, 0), (1, 3), (3, 1)])
+    near = lax.ppermute(share, "ez", [(0, 1), (1, 0), (2, 3), (3, 2)])
+    inner = lax.ppermute(share, "ez", [(1, 2), (2, 1)])
+    ends = lax.ppermute(after(far, near), "ez", [(2, 3), (1, 0)])
+    return [share, near, far, inner, ends]
+
+
+def scatter_z(share_of):
+    n = lax.axis_size("ez")
+    if n != 4:
+        got = trade(lambda k: share_of(k).astype(BF), "ez")
+        return share_of(0) + sum(piece.astype(FL) for piece in got[1:]), got[1]
+    third = share_of(3).astype(BF)
+    ends = lax.ppermute(third, "ez", [(0, 1), (3, 2)])
+    near = lax.ppermute(share_of(1).astype(BF), "ez", [(0, 1), (1, 0), (2, 3), (3, 2)])
+    inner = lax.ppermute(third, "ez", [(1, 2), (2, 1)])
+    second = (share_of(2) + ends.astype(FL)).astype(BF)
+    far = lax.ppermute(second, "ez", [(0, 2), (2, 0), (1, 3), (3, 1)])
+    return share_of(0) + near.astype(FL) + inner.astype(FL) + far.astype(FL), second
+
+
 def whole(array):
     return pl.BlockSpec(array.shape, lambda *_: (0,) * array.ndim, memory_space=VMEM)
 
@@ -77,26 +102,31 @@
     def fill(source):
         for c in range(own[0].shape[0]):
             for b in range(count):
-                to = (c * count + b) * part
+                to = (b * own[0].shape[0] + c) * part
                 target[to : to + part, :] = source[b][c, pl.ds(low, part), :]
 
     pl.when(from_own)(functools.partial(fill, own))
     pl.when(jnp.logical_not(from_own))(functools.partial(fill, other))
 
 
-def project(cols, rows, own, other, spot, n_dp):
-    half = cols.shape[0]
+def project(pieces, rows, own, other, spot, n_dp, n_z, first):
+    gathered = len(pieces) == 1
+    share, lanes = pieces[0].shape
+    half = share * (1 if gathered else n_z)
     count = len(own)
     clusters, rank_own, width = own[0].shape
     parts_core = n_dp // 2
     part = rank_own // parts_core
     row_count = clusters * count * part
     built = rows is None
-    ins = [cols] + (list(own) + list(other) if built else list(rows))
-
-    def kernel(spot_ref, cols_ref, *refs):
-        sources, outs = refs[: len(ins) - 1], refs[len(ins) - 1 :]
-        dp, core = spot_ref[0], spot_ref[1]
+    given = list(own) + list(other) if built else list(rows)
+    ins = list(pieces) + given
+
+    def kernel(spot_ref, *refs):
+        got, sources = refs[: len(pieces)], refs[len(pieces) : len(ins)]
+        outs = list(refs[len(ins) + 1 :])
+        dp, core, z = spot_ref[0], spot_ref[1], spot_ref[2]
+        cols = got[0] if gathered else outs.pop(0)
         parts, products = sources, outs[-n_dp:]
         if built:
             parts = outs[:n_dp]
@@ -104,52 +134,95 @@
                 low = pl.multiple_of(lax.rem(dp ^ k, parts_core) * part, part)
                 from_own = core == (dp ^ k) // parts_core
                 place_rows(sources[:count], sources[count:], parts[k], part, from_own, low)
+        if not gathered:
+            for k in range(n_z):
+                at = pl.multiple_of((z ^ k) * share, 16)
+                piece = got[k][...]
+                if k == 3 and len(pieces) > n_z:
+                    middle = jnp.logical_or(z == 1, z == 2)
+                    piece = jnp.where(middle, piece, got[4][...])
+                cols[pl.ds(at, share), :] = piece
         for base, product in zip(parts, products):
-            product[...] = dot(base[...], cols_ref[:, :width], 1, 1).astype(BF)
-
-    outs = [shaped((row_count, width), BF)] * n_dp if built else []
+            product[...] = dot(base[...], cols[:, :width], 1, 1).astype(BF)
+
+    outs = [] if gathered else [shaped((half, lanes), BF)]
+    outs += [shaped((row_count, width), BF)] * n_dp if built else []
     outs += [shaped((row_count, half), BF)] * n_dp
     got = pl.pallas_call(
         kernel,
         out_shape=outs,
-        in_specs=[SCALAR] + [whole(x) for x in ins],
+        in_specs=[SCALAR] + [whole(x) for x in ins] + [ANYWHERE],
         out_specs=[whole(out) for out in outs],
         compiler_params=params(2 * half, True),
         cost_estimate=FREE,
         name="project",
-    )(spot, *ins)
-    return (got[:n_dp] if built else rows), got[-n_dp:]
-
-
-def basis_grads(keep, other, cols, other_cols, spot, shape, n_dp, first):
+    )(spot, *ins, first)
+    cols = pieces[0] if gathered else got[0]
+    return cols, (got[-2 * n_dp : -n_dp] if built else rows), got[-n_dp:]
+
+
+def sum_for_groups(pieces, groups, clusters, count, firsts):
+    rows, half = pieces[0].shape
+    part = rows // (clusters * count)
+    n_ex = groups.shape[0]
+
+    def kernel(groups_ref, *refs):
+        got, out_ref, sum_ref = refs[: len(pieces)], refs[-2], refs[-1]
+        for b in range(count):
+            for c in range(clusters):
+                take = slice((b * clusters + c) * part, (b * clusters + c + 1) * part)
+                total = got[0][take, :].astype(FL)
+                for piece in got[1:]:
+                    total += piece[take, :].astype(FL)
+                sum_ref[c, b] = total.astype(BF)
+        for e in range(n_ex):
+            for b in range(count):
+                out_ref[e, b * part : (b + 1) * part, :] = sum_ref[groups_ref[e], b]
+
+    out = shaped((n_ex, count * part, half), BF)
+    return pl.pallas_call(
+        kernel,
+        out_shape=out,
+        in_specs=[SCALAR] + [whole(x) for x in pieces] + [ANYWHERE] * len(firsts),
+        out_specs=whole(out),
+        scratch_shapes=[pltpu.VMEM((clusters, count, part, half), BF)],
+        compiler_params=params(2 * half),
+        cost_estimate=FREE,
+        name="sum_for_groups",
+    )(groups, *pieces, *firsts)
+
+
+def basis_grads(keep, other, x_cols, dy_cols, spot, shape, n_dp, first):
     clusters, rank_own, width = shape
     parts_core = n_dp // 2
     part = rank_own // parts_core
-    half = cols.shape[0]
-    count = keep[0].shape[0] // (clusters * part)
+    half = x_cols[0].shape[0]
+    count = 3
     block = width // 2 if width % 256 == 0 else width
 
     def kernel(spot_ref, *refs):
         ours, theirs = refs[:parts_core], refs[parts_core : 2 * parts_core]
-        cols_ref, other_ref = refs[2 * parts_core : 2 * parts_core + 2]
+        x_refs = refs[2 * parts_core : 2 * parts_core + 2]
+        dy_refs = refs[2 * parts_core + 2 : 2 * parts_core + 4]
         outs, rows_ref = refs[-1 - count : -1], refs[-1]
         dp = spot_ref[0]
 
         @pl.when(pl.program_id(0) == 0)
         def _():
+            kind = rows_ref.dtype
             for k in range(parts_core):
                 low = (lax.rem(dp, parts_core) ^ k) * part
                 for c in range(clusters):
                     at = pl.multiple_of(c * rank_own + low, part)
                     for b in range(count):
-                        take = slice((c * count + b) * part, (c * count + b + 1) * part)
-                        kind = rows_ref.dtype
+                        take = slice((b * clusters + c) * part, (b * clusters + c + 1) * part)
                         rows_ref[0, b, pl.ds(at, part), :] = ours[k][take, :].astype(kind)
                         rows_ref[1, b, pl.ds(at, part), :] = theirs[k][take, :].astype(kind)
 
         for b in range(count):
-            total = dot(rows_ref[0, b].astype(BF), cols_ref[...], 1, 0)
-            total += dot(rows_ref[1, b].astype(BF), other_ref[...], 1, 0)
+            cols = dy_refs if b == 2 else x_refs
+            total = dot(rows_ref[0, b].astype(BF), cols[0][...], 1, 0)
+            total += dot(rows_ref[1, b].astype(BF), cols[1][...], 1, 0)
             outs[b][...] = total
 
     ins = list(keep) + list(other)
@@ -160,17 +233,17 @@
         out_shape=[out] * count,
         in_specs=[SCALAR]
         + [whole(x) for x in ins]
-        + [pl.BlockSpec((half, block), lambda j: (0, j), memory_space=VMEM)] * 2
+        + [pl.BlockSpec((half, block), lambda j: (0, j), memory_space=VMEM)] * 4
         + [ANYWHERE],
         out_specs=[
             pl.BlockSpec((clusters * rank_own, block), lambda j: (0, j), memory_space=VMEM)
         ]
         * count,
         scratch_shapes=[pltpu.VMEM((2, count, clusters * rank_own, half), rows_kind(part))],
-        compiler_params=params(2 * half),
+        compiler_params=params(2 * half, True),
         cost_estimate=FREE,
         name="basis_grads",
-    )(spot, *ins, cols, other_cols, first)
+    )(spot, *ins, *x_cols, *dy_cols, first)
     return [grad.reshape(shape) for grad in got]
 
 
@@ -420,29 +493,32 @@
 
     lanes = 128
 
-    def own_columns(rows, more):
-        rows = rows.reshape(tok_rows, n_dp, width).transpose(1, 0, 2)
-        if more is not None:
-            more = jnp.broadcast_to(more[None], (n_dp, tok_rows, lanes))
-            rows = jnp.concatenate([rows, more], axis=2)
-        rows = jnp.broadcast_to(rows[:, None], (n_dp, n_z) + rows.shape[1:])
-        rows = rows.reshape(n_dp * n_z, tok_rows, -1)
-        got = lax.all_to_all(rows, ("dp", "ez"), split_axis=0, concat_axis=0, tiled=True)
-        return got.reshape(half, -1)
-
     routing = jnp.concatenate([route_ids.astype(BF), route_weight], axis=1)
     routing = jnp.pad(routing, ((0, 0), (0, lanes - 2 * top)))
-    x_half = own_columns(tokens, routing)
-    dy_half = own_columns(after(grad_out, x_half), None)
-    spot = jnp.stack([dp, core]).astype(jnp.int32)
+
+    def slice_for(k):
+        cols = lax.dynamic_slice_in_dim(tokens, (dp ^ k) * width, width, 1)
+        return jnp.concatenate([cols, routing], axis=1)
+
+    x_pieces = gather_z(jnp.concatenate(in_order(trade(slice_for, "dp"), dp), axis=0))
+    dy_cols = after(grad_out, x_pieces[-1]).reshape(tok_rows, n_dp, width).transpose(1, 0, 2)
+    dy_cols = jnp.broadcast_to(dy_cols[None], (n_z, n_dp, tok_rows, width))
+    dy_half = lax.all_to_all(
+        dy_cols.reshape(n_z * n_dp, tok_rows, width),
+        ("ez", "dp"),
+        split_axis=0,
+        concat_axis=0,
+        tiled=True,
+    ).reshape(half, width)
+    spot = jnp.stack([dp, core, z]).astype(jnp.int32)
 
     def chip_rows(own, other):
         if rank_part % 16 == 0:
             return None
         count = len(own)
-        shape = (clusters, count, parts_core, rank_part, width)
-        own = jnp.stack(own, axis=1).reshape(shape)
-        other = jnp.stack(other, axis=1).reshape(shape)
+        shape = (count, clusters, parts_core, rank_part, width)
+        own = jnp.stack(own).reshape(shape)
+        other = jnp.stack(other).reshape(shape)
         result = []
         for k in range(n_dp):
             part = dp ^ k
@@ -456,6 +532,10 @@
     own_in, own_out = [gate_basis, up_basis], [down_basis]
     other_in = [core_swap(basis) for basis in own_in]
     other_out = [core_swap(basis) for basis in own_out]
+
+    x_half, rows_in, terms = project(
+        x_pieces, chip_rows(own_in, other_in), own_in, other_in, spot, n_dp, n_z, route_ids
+    )
 
     routing = x_half[:, width:]
     swapped = core_swap(routing)
@@ -480,24 +560,21 @@
     def sum_parts(got):
         return sum(piece.astype(FL) for piece in got).astype(BF)
 
-    def to_group(mine):
-        mine = mine.reshape(clusters, -1, half)
-        send = mine.at[group_cluster].get(mode="promise_in_bounds")
-        return lax.all_to_all(send, ("ez", "core"), split_axis=0, concat_axis=0, tiled=True)
-
-    rows_in, terms = project(
-        x_half, chip_rows(own_in, other_in), own_in, other_in, spot, n_dp
-    )
-    mine_in = sum_parts(trade(lambda k: terms[k], "dp"))
-    got_in = to_group(mine_in)
-    _, terms_out = project(
-        dy_half, chip_rows(own_out, other_out), own_out, other_out, spot, n_dp
-    )
-    mine_out = sum_parts(trade(lambda k: terms_out[k], "dp"))
+    def spread(mine):
+        return lax.all_to_all(mine, ("ez", "core"), split_axis=0, concat_axis=0, tiled=True)
+
+    mine_in = sum_for_groups(
+        trade(lambda k: terms[k], "dp"), group_cluster, clusters, 2, [dy_half]
+    )
+    got_in = spread(mine_in)
     h_pieces = trade(lambda k: got_in, "dp")
-    for piece in h_pieces[1:]:
-        mine_out = after(mine_out, piece)
-    got_out = to_group(mine_out)
+    _, _, terms_out = project(
+        [dy_half], chip_rows(own_out, other_out), own_out, other_out, spot, n_dp, n_z, mine_in
+    )
+    mine_out = sum_for_groups(
+        trade(lambda k: terms_out[k], "dp"), group_cluster, clusters, 1, h_pieces[1:]
+    )
+    got_out = spread(mine_out)
     (hg, hu, hidden, mixed, act, lift), mixed_chunks = forward(
         h_pieces, pick, weight_of, gate_factor, up_factor, down_factor, dp
     )
@@ -505,24 +582,18 @@
     (back, grad_gate, grad_up, dots), in_chunks = backward(
         d_pieces, pick, slot_weight, mixed, act, lift, gate_factor, up_factor, down_factor, dp
     )
-
-    numbers = jnp.arange(clusters, dtype=jnp.int32)[:, None]
-
-    def by_cluster(got, groups):
-        owner = (groups[None, :] == numbers)[:, :, None, None]
-        summed = jnp.sum(jnp.where(owner, got.astype(FL)[None], 0.0), axis=1)
-        return summed.astype(BF).reshape(-1, half)
 
     mixed_mine = sum_parts(trade(lambda k: mixed_chunks[k], "dp"))
     in_mine = sum_parts(trade(lambda k: in_chunks[k], "dp"))
     grad_gate_factor, grad_up_factor, grad_down_factor = factor_grads(
         hg, grad_gate, hu, grad_up, hidden, back, total, in_mine
     )
-    mine = jnp.concatenate([in_mine, mixed_mine], axis=1)
-    got = lax.all_to_all(mine, ("ez", "core"), split_axis=0, concat_axis=0, tiled=True)
-    in_sum = after(by_cluster(got[:, : 2 * rank_part], group_cluster), grad_gate_factor)
-    mixed_sum = by_cluster(got[:, 2 * rank_part :], group_cluster)
-    in_parts = trade(lambda k: in_sum, "dp")
+    got = spread(jnp.concatenate([in_mine, mixed_mine], axis=1))
+    owner = group_cluster[:, None] == jnp.arange(clusters, dtype=jnp.int32)[None, :]
+    got = got.reshape(n_ex, 3, 1, rank_part, half).astype(FL)
+    sums = jnp.sum(jnp.where(owner[:, None, :, None, None], got, 0.0), axis=0)
+    sums = after(sums.astype(BF).reshape(-1, half), grad_gate_factor)
+    parts = trade(lambda k: sums, "dp")
 
     placed = cell == jnp.arange(slots, dtype=jnp.int32)[None, :, None]
     scores = jnp.sum(jnp.where(placed, dots, 0.0), axis=1).reshape(local, 2, half)
@@ -530,39 +601,38 @@
     theirs = core_swap(jnp.where(core == 0, scores[:, 1], scores[:, 0]))
     first = jnp.where(core == 0, mine, theirs)
     second = jnp.where(core == 0, theirs, mine)
-    scores = jnp.concatenate([first, second], axis=0).T.astype(BF)
-    scores = jnp.pad(scores, ((0, 0), (0, lanes - 2 * local)))
-
-    grad_x = sum(mm("rt,rf->tf", part, rows) for part, rows in zip(in_parts, rows_in))
-    leaving = jnp.concatenate([grad_x.astype(BF), scores], axis=1)
-    rows = leaving.reshape(n_dp * n_z, tok_rows, width + lanes)
-    rows = lax.all_to_all(rows, ("dp", "ez"), split_axis=0, concat_axis=0, tiled=True)
-    rows = rows.reshape(n_dp, n_z, tok_rows, width + lanes)
+    scores = jnp.concatenate([first, second], axis=0).T
+    lane = jnp.arange(lanes, dtype=jnp.int32) // (2 * local)
+    scores = jnp.where(lane == z, jnp.tile(scores, (1, lanes // (2 * local))), 0.0)
+
+    terms_in = 2 * clusters * rank_part
+    grad_x = sum(mm("rt,rf->tf", part[:terms_in], rows) for part, rows in zip(parts, rows_in))
+    leaving = jnp.concatenate([grad_x, scores], axis=1).reshape(n_z, -1, width + lanes)
+    mine, early = scatter_z(lambda k: lax.dynamic_index_in_dim(leaving, z ^ k, 0, False))
+
     x_other = core_swap(x_half)
     dy_other = core_swap(dy_half)
     same = core == dp // parts_core
-
-    def own_ranks(parts):
-        near, far = parts[:parts_core], parts[parts_core:]
-        keep = [jnp.where(same, a, b) for a, b in zip(near, far)]
-        other = [core_swap(jnp.where(same, b, a)) for a, b in zip(near, far)]
-        return keep, other
-
-    shape = (clusters, rank_own, width)
-    grad_gate_basis, grad_up_basis = basis_grads(
-        *own_ranks(in_parts), x_half, x_other, spot, shape, n_dp, leaving
-    )
-    mixed_sum = after(mixed_sum, grad_gate_basis)
-    mixed_parts = trade(lambda k: mixed_sum, "dp")
-    (grad_down_basis,) = basis_grads(
-        *own_ranks(mixed_parts), dy_half, dy_other, spot, shape, n_dp, leaving
-    )
-
-    grad_rows = jnp.sum(rows[..., :width].astype(FL), axis=1)
-    grad_rows = after(grad_rows, grad_down_basis)
-    grad_tokens = grad_rows.astype(BF).transpose(1, 0, 2).reshape(tok_rows, model_width)
-    by_expert = jnp.sum(rows[..., width : width + 2 * local].astype(FL), axis=0)
-    by_expert = by_expert.transpose(1, 0, 2).reshape(tok_rows, 1, experts)
+    near, far = parts[:parts_core], parts[parts_core:]
+    keep = [jnp.where(same, a, b) for a, b in zip(near, far)]
+    other = [core_swap(jnp.where(same, b, a)) for a, b in zip(near, far)]
+    grad_gate_basis, grad_up_basis, grad_down_basis = basis_grads(
+        keep,
+        other,
+        [x_half, x_other],
+        [dy_half, dy_other],
+        spot,
+        (clusters, rank_own, width),
+        n_dp,
+        early,
+    )
+
+    mine = after(mine, grad_gate_basis).astype(BF)
+    pieces = trade(
+        lambda k: lax.dynamic_slice_in_dim(mine, (dp ^ k) * tok_rows, tok_rows, 0), "dp"
+    )
+    grad_tokens = jnp.concatenate([x[:, :width] for x in in_order(pieces, dp)], axis=1)
+    by_expert = sum(x[:, width : width + experts].astype(FL) for x in pieces)[:, None, :]
     chosen = route_ids[:, :, None] == jnp.arange(experts, dtype=jnp.int32)[None, None, :]
     grad_route = jnp.sum(jnp.where(chosen, by_expert, 0.0), axis=2)
     return (

time: 292 us -> 309 us (1.058)
  starting transfers between devices: 61 us -> 95.3 us
  local copies, waits for them, and re-layouts: 32.6 us -> 25.2 us
  waiting for transfers between devices: 122 us -> 116 us
  other arithmetic: 17.8 us -> 14.4 us
    all_to_all x6 -> x4, waiting for transfers between devices: 85.1 us -> 16.3 us  [the longest x3 16.3 us: spread(): lax.all_to_all(mine, ('ez', 'core'), split_axis=0, concat_axis=0, tiled=T...]
    ppermute x24 -> x27, waiting for transfers between devices: 30.9 us -> 67.1 us  [trade(): lax.ppermute(chunk_for(k), axis, [(i, i ^ k) for i in range(n)])]
    ppermute x0 -> x8, waiting for transfers between devices: none -> 28.7 us  [the longest x1 13.4 us: gather_z(): near = lax.ppermute(share, 'ez', [(0, 1), (1, 0), (2, 3), (3, 2)])]
    ppermute x0 -> x8, starting transfers between devices: none -> 16.4 us  [the longest x1 4.31 us: scatter_z(): ends = lax.ppermute(third, 'ez', [(0, 1), (3, 2)])]
    all_to_all x6 -> x4, starting transfers between devices: 28.4 us -> 41.7 us  [the longest x3 36 us: spread(): lax.all_to_all(mine, ('ez', 'core'), split_axis=0, concat_axis=0, tiled=T...]
    ppermute x24 -> x27, starting transfers between devices: 29.3 us -> 34.5 us  [trade(): lax.ppermute(chunk_for(k), axis, [(i, i ^ k) for i in range(n)])]
    slice x7 -> x4, local copies, waits for them, and re-layouts: 8.33 us -> 3.47 us  [after(): lax.slice(first, (0,) * first.ndim, (1,) * first.ndim).reshape(())]
    unnamed x85 -> x86, local copies, waits for them, and re-layouts: 14.1 us -> 16 us
  transfers between devices with their start and end apart: 41 -> 48, of which waited for: 20 -> 29; matrix products, arithmetic and copies ran while one was open for 8% -> 6% of each run, Pallas kernels for 14% -> 15%
where the time goes in v6:
time: 309 us; the launch traced here: 308 us
  waiting for transfers between devices  116 us (38%)
  starting transfers between devices  95.3 us (31%)
  Pallas kernels  48.8 us (16%)
  local copies, waits for them, and re-layouts  25.2 us (8%)
  other arithmetic  14.4 us (5%)
  between operations  3.99 us (1%)
  matrix products  3.53 us (1%)
    ppermute x27, waiting for transfers between devices, trade(): lax.ppermute(chunk_for(k), axis, [(i, i ^ k) for i in range(n)])  67.1 us
    all_to_all x3, starting transfers between devices, spread(): lax.all_to_all(mine, ('ez', 'core'), split_axis=0, concat_axis=0, tiled=T...  36 us
    ppermute x27, starting transfers between devices, trade(): lax.ppermute(chunk_for(k), axis, [(i, i ^ k) for i in range(n)])  34.5 us
    all_to_all x3, waiting for transfers between devices, spread(): lax.all_to_all(mine, ('ez', 'core'), split_axis=0, concat_axis=0, tiled=T...  16.3 us
    unnamed x86, local copies, waits for them, and re-layouts  16 us
    ppermute x1, waiting for transfers between devices, gather_z(): near = lax.ppermute(share, 'ez', [(0, 1), (1, 0), (2, 3), (3, 2)])  13.4 us
    pallas_call x1, Pallas kernels, backward(): pl.pallas_call(kernel, grid=(local,), out_shape=outs + chunks, in_specs=[...  12.2 us
    pallas_call x1, Pallas kernels, forward(): pl.pallas_call(kernel, grid=(local,), out_shape=outs + chunks, in_specs=[...  10.9 us
  transfers between devices with their start and end apart: 48, of which 29 were waited for; matrix products, arithmetic and copies ran while one was open for 6% of the time, Pallas kernels for 15%

profile of v6, /device:TPU:0, one launch (start us, length us, event | category | flops | bytes accessed | tf_op | source)
XLA Modules:
  0.0 307.7 jit_solution(629609913463915905)
XLA Ops:
  3.4 4.0 %collective-permute-start = (bf16[24,1920]{1,0:T(8,128)(2,1)S(1)}, bf16[24,1920]{1,0:T(8,128)(2,1)S(1)}, u32[]{:S(2)}, u32[]{:S(2)}) collective-permute-start(bf16[24,1920]{1,0:T(8,128)(2,1)S(1)} %get-tuple-element.136), channel_id=1, source_target_pairs={{0,24},{8,16},{16,8},{24,0},{1,25},{9,17},{17,9},{25,1},{2,26},{10... | collective-permute-start | bytes 276488 | tf_op jit(solution)/shard_map/ppermute | solution.py:46
  16.8 13.4 %collective-permute-done.4.refs_1_ = bf16[96,1920]{1,0:T(8,128)(2,1)S(1)} collective-permute-done((bf16[96,1920]{1,0:T(8,128)(2,1)S(1)}, bf16[96,1920]{1,0:T(8,128)(2,1)S(1)}, u32[]{:S(2)}, u32[]{:S(2)}) %collective-permute-start.4) | collective-permute-done | bytes 368672 | tf_op jit(solution)/shard_map/ppermute | solution.py:55
  34.0 8.1 %collective-permute-done.5.refs_4_ = bf16[96,1920]{1,0:T(8,128)(2,1)S(1)} collective-permute-done((bf16[96,1920]{1,0:T(8,128)(2,1)S(1)}, bf16[96,1920]{1,0:T(8,128)(2,1)S(1)}, u32[]{:S(2)}, u32[]{:S(2)}) %collective-permute-start.5) | collective-permute-done | bytes 368672 | tf_op jit(solution)/shard_map/ppermute | solution.py:57
  44.9 5.8 %all-to-all-start = ((bf16[16,24,1792]{2,1,0:T(8,128)(2,1)}), bf16[16,24,1792]{2,1,0:T(8,128)(2,1)S(1)}, u32[]{:S(2)}, u32[]{:S(2)}) async-start(bf16[16,24,1792]{2,1,0:T(8,128)(2,1)} %bitcast.6), calls=%async_computation | async-start | bytes 2752512 | tf_op jit(solution)/shard_map/all_to_all | solution.py:506
  54.9 5.7 %project.2 = (bf16[384,1920]{1,0:T(8,128)(2,1)}, bf16[256,1792]{1,0:T(8,128)(2,1)}, bf16[256,1792]{1,0:T(8,128)(2,1)}, bf16[256,1792]{1,0:T(8,128)(2,1)}, bf16[2...) custom-call(s32[3]{0:T(128)} %pad_add_fusion.spot_ref, ...), custom_call_target="tpu_custom_call" | custom-call | tf_op jit(solution)/shard_map/project/pallas_call | solution.py:151
  64.3 8.3 %collective-permute-done.10.refs_1_ = bf16[256,384]{1,0:T(8,128)(2,1)S(1)} collective-permute-done((bf16[256,384]{1,0:T(8,128)(2,1)}, bf16[256,384]{1,0:T(8,128)(2,1)S(1)}, u32[]{:S(2)}, u32[]{:S(2)}) %collective-permute-start.10) | collective-permute-done | bytes 196640 | tf_op jit(solution)/shard_map/ppermute | solution.py:46
  72.6 7.5 %collective-permute-done.12.refs_3_ = bf16[256,384]{1,0:T(8,128)(2,1)S(1)} collective-permute-done((bf16[256,384]{1,0:T(8,128)(2,1)}, bf16[256,384]{1,0:T(8,128)(2,1)S(1)}, u32[]{:S(2)}, u32[]{:S(2)}) %collective-permute-start.12) | collective-permute-done | bytes 196640 | tf_op jit(solution)/shard_map/ppermute | solution.py:46
  82.6 28.5 %all-to-all-start.1 = ((bf16[8,64,384]{2,1,0:T(8,128)(2,1)}), bf16[8,64,384]{2,1,0:T(8,128)(2,1)S(1)}, u32[]{:S(2)}, u32[]{:S(2)}) async-start(bf16[8,64,384]{2,1,0:T(8,128)(2,1)} %sum_for_groups.2.refs_3_), calls=%async_computation.1 | async-start | bytes 786432 | tf_op jit(solution)/shard_map/all_to_all | solution.py:564
  114.6 9.1 %all-to-all-done.1.refs_0_ = bf16[8,64,384]{2,1,0:T(8,128)(2,1)S(1)} async-done(((bf16[8,64,384]{2,1,0:T(8,128)(2,1)}), bf16[8,64,384]{2,1,0:T(8,128)(2,1)S(1)}, u32[]{:S(2)}, u32[]{:S(2)}) %all-to-all-start.1) | async-done | bytes 393248 | tf_op jit(solution)/shard_map/all_to_all | solution.py:564
  127.2 4.3 %project.3 = (bf16[128,1792]{1,0:T(8,128)(2,1)}, bf16[128,1792]{1,0:T(8,128)(2,1)}, bf16[128,1792]{1,0:T(8,128)(2,1)}, bf16[128,1792]{1,0:T(8,128)(2,1)}, bf16[1...) custom-call(s32[3]{0:T(128)} %pad_add_fusion.spot_ref, ...), custom_call_target="tpu_custom_call" | custom-call | tf_op jit(solution)/shard_map/project/pallas_call | solution.py:151
  134.3 10.7 %collective-permute-done.13.refs_1_ = bf16[128,384]{1,0:T(8,128)(2,1)S(1)} collective-permute-done((bf16[128,384]{1,0:T(8,128)(2,1)}, bf16[128,384]{1,0:T(8,128)(2,1)S(1)}, u32[]{:S(2)}, u32[]{:S(2)}) %collective-permute-start.13) | collective-permute-done | bytes 98336 | tf_op jit(solution)/shard_map/ppermute | solution.py:46
  153.0 3.6 %all-to-all-start.2 = ((bf16[8,32,384]{2,1,0:T(8,128)(2,1)}), bf16[8,32,384]{2,1,0:T(8,128)(2,1)S(1)}, u32[]{:S(2)}, u32[]{:S(2)}) async-start(bf16[8,32,384]{2,1,0:T(8,128)(2,1)} %sum_for_groups.3), calls=%async_computation.2 | async-start | bytes 393216 | tf_op jit(solution)/shard_map/all_to_all | solution.py:564
  158.0 6.6 %all-to-all-done.2.refs_0_ = bf16[8,32,384]{2,1,0:T(8,128)(2,1)S(1)} async-done(((bf16[8,32,384]{2,1,0:T(8,128)(2,1)}), bf16[8,32,384]{2,1,0:T(8,128)(2,1)S(1)}, u32[]{:S(2)}, u32[]{:S(2)}) %all-to-all-start.2) | async-done | bytes 196640 | tf_op jit(solution)/shard_map/all_to_all | solution.py:564
  170.8 10.9 %forward.1 = (bf16[4,224,512]{2,1,0:T(8,128)(2,1)}, bf16[4,224,512]{2,1,0:T(8,128)(2,1)}, bf16[4,224,512]{2,1,0:T(8,128)(2,1)}, bf16[4,224,512]{2,1,0:T(8,128)(2...) custom-call(s32[1]{0:T(128)} %bitcast.dp_ref, ...), custom_call_target="tpu_custom_call" | custom-call | tf_op jit(solution)/shard_map/forward/pallas_call | solution.py:354
  186.0 12.2 %backward.1 = (bf16[4,224,512]{2,1,0:T(8,128)(2,1)}, bf16[4,224,512]{2,1,0:T(8,128)(2,1)}, bf16[4,224,512]{2,1,0:T(8,128)(2,1)}, f32[4,224,1]{2,1,0:T(8,128)}, b...) custom-call(s32[1]{0:T(128)} %bitcast.dp_ref, ...), custom_call_target="tpu_custom_call" | custom-call | flops 3523215360 | bytes 33554432 | tf_op jit(solution)/shard_map/backward/pallas_call | solution.py:416
  202.2 8.3 %collective-permute-done.23 = bf16[8,64,384]{2,1,0:T(8,128)(2,1)S(1)} collective-permute-done((bf16[8,64,384]{2,1,0:T(8,128)(2,1)}, bf16[8,64,384]{2,1,0:T(8,128)(2,1)S(1)}, u32[]{:S(2)}, u32[]{:S(2)}) %collective-permute-start.23) | collective-permute-done | bytes 393248 | tf_op jit(solution)/shard_map/ppermute | solution.py:46
  210.5 4.0 %collective-permute-done.24 = bf16[8,64,384]{2,1,0:T(8,128)(2,1)S(1)} collective-permute-done((bf16[8,64,384]{2,1,0:T(8,128)(2,1)}, bf16[8,64,384]{2,1,0:T(8,128)(2,1)S(1)}, u32[]{:S(2)}, u32[]{:S(2)}) %collective-permute-start.24) | collective-permute-done | bytes 393248 | tf_op jit(solution)/shard_map/ppermute | solution.py:46
  218.5 3.9 %all-to-all-start.3 = ((bf16[8,96,384]{2,1,0:T(8,128)(2,1)}), bf16[8,96,384]{2,1,0:T(8,128)(2,1)S(1)}, u32[]{:S(2)}, u32[]{:S(2)}) async-start(bf16[8,96,384]{2,1,0:T(8,128)(2,1)} %pad_maximum_fusion.1), calls=%async_computation.3 | async-start | bytes 1179648 | tf_op jit(solution)/shard_map/all_to_all | solution.py:564
  231.6 5.2 %factor_grads.1 = (f32[4,512,512]{2,1,0:T(8,128)}, f32[4,512,512]{2,1,0:T(8,128)}, f32[4,512,512]{2,1,0:T(8,128)}) custom-call(bf16[4,224,512]{2,1,0:T(8,128)(2,1)S(1)} %copy-done.6, bf16[4,224,512]{2,1,0:T(8,128)(2,1)S(1)} %copy-done.10, bf16[4,224,512]{2,1,0:T(8,128)(2,1)S(1)} %copy-done.7, bf16[4,224,512]{2,1,0:T(8,128)(2,1)S(1)} %copy-done.11, ...), custom_call_target="tpu_custom_call" | custom-call | tf_op jit(solution)/shard_map/factor_grads/pallas_call | solution.py:449
  243.7 6.1 %collective-permute-done.29 = bf16[384,384]{1,0:T(8,128)(2,1)S(1)} collective-permute-done((bf16[384,384]{1,0:T(8,128)(2,1)S(1)}, bf16[384,384]{1,0:T(8,128)(2,1)S(1)}, u32[]{:S(2)}, u32[]{:S(2)}) %collective-permute-start.29) | collective-permute-done | bytes 294944 | tf_op jit(solution)/shard_map/ppermute | solution.py:46
  251.6 6.0 %collective-permute-done.30 = bf16[384,384]{1,0:T(8,128)(2,1)S(1)} collective-permute-done((bf16[384,384]{1,0:T(8,128)(2,1)S(1)}, bf16[384,384]{1,0:T(8,128)(2,1)S(1)}, u32[]{:S(2)}, u32[]{:S(2)}) %collective-permute-start.30) | collective-permute-done | bytes 294944 | tf_op jit(solution)/shard_map/ppermute | solution.py:46
  262.6 4.3 %collective-permute-start.35 = (bf16[96,1920]{1,0:T(8,128)(2,1)S(1)}, bf16[96,1920]{1,0:T(8,128)(2,1)}, u32[]{:S(2)}, u32[]{:S(2)}) collective-permute-start(bf16[96,1920]{1,0:T(8,128)(2,1)S(1)} %get-tuple-element.103), channel_id=1, source_target_pairs={{0,2},{6,4},{1,3},{7,5},{8,10},{14,12},{9,11},{15,13},{16,18},{22,... | collective-permute-start | bytes 1105928 | tf_op jit(solution)/shard_map/ppermute | solution.py:67
  270.2 5.0 %collective-permute-done.35 = bf16[96,1920]{1,0:T(8,128)(2,1)} collective-permute-done((bf16[96,1920]{1,0:T(8,128)(2,1)S(1)}, bf16[96,1920]{1,0:T(8,128)(2,1)}, u32[]{:S(2)}, u32[]{:S(2)}) %collective-permute-start.35) | collective-permute-done | bytes 368672 | tf_op jit(solution)/shard_map/ppermute | solution.py:67
  283.6 7.0 %basis_grads.1 = (f32[256,1792]{1,0:T(8,128)}, f32[256,1792]{1,0:T(8,128)}, f32[256,1792]{1,0:T(8,128)}) custom-call(s32[3]{0:T(128)} %pad_add_fusion.spot_ref, bf16[384,384]{1,0:T(8,128)(2,1)} %get-tuple-element.109.refs_0_, bf16[384,384]{1,0:T(8,128)(2,1)} %get-tuple-element.107.refs_1_, bf16[384,384]{1,0:T(8,128)(2,1)} %copy-done.32, ...), custom_call_target="tpu_custom_call" | custom-call | tf_op jit(solution)/shard_map/basis_grads/pallas_call | solution.py:230
  (247 shorter events, 115.1 us)
Async XLA Ops:
  12.6 17.6 %collective-permute-start.4 = (bf16[96,1920]{1,0:T(8,128)(2,1)S(1)}, bf16[96,1920]{1,0:T(8,128)(2,1)S(1)}, u32[]{:S(2)}, u32[]{:S(2)}) collective-permute-start(bf16[96,1920]{1,0:T(8,128)(2,1)S(1)} %pad_maximum_fusion.2.refs_0_), channel_id=1, source_target_pairs={{0,2},{2,0},{4,6},{6,4},{1,3},{3,1},{5,7},{7,5},{8,10},{10,8},{12,... | collective-permute-start | bytes 1105928 | tf_op jit(solution)/shard_map/ppermute | solution.py:55
  14.2 18.5 %collective-permute-start.3 = (bf16[96,1920]{1,0:T(8,128)(2,1)S(1)}, bf16[96,1920]{1,0:T(8,128)(2,1)S(1)}, u32[]{:S(2)}, u32[]{:S(2)}) collective-permute-start(bf16[96,1920]{1,0:T(8,128)(2,1)S(1)} %pad_maximum_fusion.2.refs_0_), channel_id=1, source_target_pairs={{0,4},{4,0},{2,6},{6,2},{1,5},{5,1},{3,7},{7,3},{8,12},{12,8},{10,... | collective-permute-start | bytes 1105928 | tf_op jit(solution)/shard_map/ppermute | solution.py:54
  44.9 35.2 %all-to-all-start = ((bf16[16,24,1792]{2,1,0:T(8,128)(2,1)}), bf16[16,24,1792]{2,1,0:T(8,128)(2,1)S(1)}, u32[]{:S(2)}, u32[]{:S(2)}) async-start(bf16[16,24,1792]{2,1,0:T(8,128)(2,1)} %bitcast.6), calls=%async_computation | async-start | bytes 2752512 | tf_op jit(solution)/shard_map/all_to_all | solution.py:506
  64.0 16.1 %collective-permute-start.12 = (bf16[256,384]{1,0:T(8,128)(2,1)}, bf16[256,384]{1,0:T(8,128)(2,1)S(1)}, u32[]{:S(2)}, u32[]{:S(2)}) collective-permute-start(bf16[256,384]{1,0:T(8,128)(2,1)} %get-tuple-element.50), channel_id=1, source_target_pairs={{0,24},{8,16},{16,8},{24,0},{1,25},{9,17},{17,9},{25,1},{2,26},{10... | collective-permute-start | bytes 589832 | tf_op jit(solution)/shard_map/ppermute | solution.py:46
  64.1 63.1 %collective-permute-start.6 = (bf16[4,64,1792]{2,1,0:T(8,128)(2,1)}, bf16[4,64,1792]{2,1,0:T(8,128)(2,1)}, u32[]{:S(2)}, u32[]{:S(2)}) collective-permute-start(bf16[4,64,1792]{2,1,0:T(8,128)(2,1)} %refs_1_.1), channel_id=1, source_target_pairs={{0,1},{1,0},{2,3},{3,2},{4,5},{5,4},{6,7},{7,6},{8,9},{9,8},{10,11... | collective-permute-start | bytes 2752520 | tf_op jit(solution)/shard_map/ppermute | solution.py:30
  82.6 41.0 %all-to-all-start.1 = ((bf16[8,64,384]{2,1,0:T(8,128)(2,1)}), bf16[8,64,384]{2,1,0:T(8,128)(2,1)S(1)}, u32[]{:S(2)}, u32[]{:S(2)}) async-start(bf16[8,64,384]{2,1,0:T(8,128)(2,1)} %sum_for_groups.2.refs_3_), calls=%async_computation.1 | async-start | bytes 786432 | tf_op jit(solution)/shard_map/all_to_all | solution.py:564
  123.7 27.0 %collective-permute-start.16 = (bf16[8,64,384]{2,1,0:T(8,128)(2,1)S(1)}, bf16[8,64,384]{2,1,0:T(8,128)(2,1)S(1)}, u32[]{:S(2)}, u32[]{:S(2)}) collective-permute-start(bf16[8,64,384]{2,1,0:T(8,128)(2,1)S(1)} %all-to-all-done.1.refs_0_), channel_id=1, source_target_pairs={{0,8},{8,0},{16,24},{24,16},{1,9},{9,1},{17,25},{25,17},{2,10},{10... | collective-permute-start | bytes 1179656 | tf_op jit(solution)/shard_map/ppermute | solution.py:46
  125.1 25.5 %collective-permute-start.17 = (bf16[8,64,384]{2,1,0:T(8,128)(2,1)S(1)}, bf16[8,64,384]{2,1,0:T(8,128)(2,1)S(1)}, u32[]{:S(2)}, u32[]{:S(2)}) collective-permute-start(bf16[8,64,384]{2,1,0:T(8,128)(2,1)S(1)} %all-to-all-done.1.refs_0_), channel_id=1, source_target_pairs={{0,16},{8,24},{16,0},{24,8},{1,17},{9,25},{17,1},{25,9},{2,18},{10... | collective-permute-start | bytes 1179656 | tf_op jit(solution)/shard_map/ppermute | solution.py:46
  126.0 24.6 %collective-permute-start.18 = (bf16[8,64,384]{2,1,0:T(8,128)(2,1)S(1)}, bf16[8,64,384]{2,1,0:T(8,128)(2,1)S(1)}, u32[]{:S(2)}, u32[]{:S(2)}) collective-permute-start(bf16[8,64,384]{2,1,0:T(8,128)(2,1)S(1)} %all-to-all-done.1.refs_0_), channel_id=1, source_target_pairs={{0,24},{8,16},{16,8},{24,0},{1,25},{9,17},{17,9},{25,1},{2,26},{10... | collective-permute-start | bytes 1179656 | tf_op jit(solution)/shard_map/ppermute | solution.py:46
  164.6 19.5 %collective-permute-start.19 = (bf16[8,32,384]{2,1,0:T(8,128)(2,1)S(1)}, bf16[8,32,384]{2,1,0:T(8,128)(2,1)S(1)}, u32[]{:S(2)}, u32[]{:S(2)}) collective-permute-start(bf16[8,32,384]{2,1,0:T(8,128)(2,1)S(1)} %all-to-all-done.2.refs_0_), channel_id=1, source_target_pairs={{0,8},{8,0},{16,24},{24,16},{1,9},{9,1},{17,25},{25,17},{2,10},{10... | collective-permute-start | bytes 589832 | tf_op jit(solution)/shard_map/ppermute | solution.py:46
  166.1 19.2 %collective-permute-start.20 = (bf16[8,32,384]{2,1,0:T(8,128)(2,1)S(1)}, bf16[8,32,384]{2,1,0:T(8,128)(2,1)S(1)}, u32[]{:S(2)}, u32[]{:S(2)}) collective-permute-start(bf16[8,32,384]{2,1,0:T(8,128)(2,1)S(1)} %all-to-all-done.2.refs_0_), channel_id=1, source_target_pairs={{0,16},{8,24},{16,0},{24,8},{1,17},{9,25},{17,1},{25,9},{2,18},{10... | collective-permute-start | bytes 589832 | tf_op jit(solution)/shard_map/ppermute | solution.py:46
  167.0 18.3 %collective-permute-start.21 = (bf16[8,32,384]{2,1,0:T(8,128)(2,1)S(1)}, bf16[8,32,384]{2,1,0:T(8,128)(2,1)S(1)}, u32[]{:S(2)}, u32[]{:S(2)}) collective-permute-start(bf16[8,32,384]{2,1,0:T(8,128)(2,1)S(1)} %all-to-all-done.2.refs_0_), channel_id=1, source_target_pairs={{0,24},{8,16},{16,8},{24,0},{1,25},{9,17},{17,9},{25,1},{2,26},{10... | collective-permute-start | bytes 589832 | tf_op jit(solution)/shard_map/ppermute | solution.py:46
  181.7 18.9 %collective-permute-start.26 = (bf16[8,32,384]{2,1,0:T(8,128)(2,1)}, bf16[8,32,384]{2,1,0:T(8,128)(2,1)S(1)}, u32[]{:S(2)}, u32[]{:S(2)}) collective-permute-start(bf16[8,32,384]{2,1,0:T(8,128)(2,1)} %get-tuple-element.66), channel_id=1, source_target_pairs={{0,8},{8,0},{16,24},{24,16},{1,9},{9,1},{17,25},{25,17},{2,10},{10... | collective-permute-start | bytes 589832 | tf_op jit(solution)/shard_map/ppermute | solution.py:46
  183.2 18.8 %collective-permute-start.27 = (bf16[8,32,384]{2,1,0:T(8,128)(2,1)}, bf16[8,32,384]{2,1,0:T(8,128)(2,1)S(1)}, u32[]{:S(2)}, u32[]{:S(2)}) collective-permute-start(bf16[8,32,384]{2,1,0:T(8,128)(2,1)} %get-tuple-element.67), channel_id=1, source_target_pairs={{0,16},{8,24},{16,0},{24,8},{1,17},{9,25},{17,1},{25,9},{2,18},{10... | collective-permute-start | bytes 589832 | tf_op jit(solution)/shard_map/ppermute | solution.py:46
  184.1 17.9 %collective-permute-start.28 = (bf16[8,32,384]{2,1,0:T(8,128)(2,1)}, bf16[8,32,384]{2,1,0:T(8,128)(2,1)S(1)}, u32[]{:S(2)}, u32[]{:S(2)}) collective-permute-start(bf16[8,32,384]{2,1,0:T(8,128)(2,1)} %get-tuple-element.68), channel_id=1, source_target_pairs={{0,24},{8,16},{16,8},{24,0},{1,25},{9,17},{17,9},{25,1},{2,26},{10... | collective-permute-start | bytes 589832 | tf_op jit(solution)/shard_map/ppermute | solution.py:46
  199.7 14.9 %collective-permute-start.24 = (bf16[8,64,384]{2,1,0:T(8,128)(2,1)}, bf16[8,64,384]{2,1,0:T(8,128)(2,1)S(1)}, u32[]{:S(2)}, u32[]{:S(2)}) collective-permute-start(bf16[8,64,384]{2,1,0:T(8,128)(2,1)} %get-tuple-element.63), channel_id=1, source_target_pairs={{0,16},{8,24},{16,0},{24,8},{1,17},{9,25},{17,1},{25,9},{2,18},{10... | collective-permute-start | bytes 1179656 | tf_op jit(solution)/shard_map/ppermute | solution.py:46
  200.6 15.6 %collective-permute-start.25 = (bf16[8,64,384]{2,1,0:T(8,128)(2,1)}, bf16[8,64,384]{2,1,0:T(8,128)(2,1)}, u32[]{:S(2)}, u32[]{:S(2)}) collective-permute-start(bf16[8,64,384]{2,1,0:T(8,128)(2,1)} %get-tuple-element.64), channel_id=1, source_target_pairs={{0,24},{8,16},{16,8},{24,0},{1,25},{9,17},{17,9},{25,1},{2,26},{10... | collective-permute-start | bytes 1179656 | tf_op jit(solution)/shard_map/ppermute | solution.py:46
  218.5 20.7 %all-to-all-start.3 = ((bf16[8,96,384]{2,1,0:T(8,128)(2,1)}), bf16[8,96,384]{2,1,0:T(8,128)(2,1)S(1)}, u32[]{:S(2)}, u32[]{:S(2)}) async-start(bf16[8,96,384]{2,1,0:T(8,128)(2,1)} %pad_maximum_fusion.1), calls=%async_computation.3 | async-start | bytes 1179648 | tf_op jit(solution)/shard_map/all_to_all | solution.py:564
  224.8 56.1 %collective-permute-start.39 = (bf16[384,1920]{1,0:T(8,128)(2,1)}, bf16[384,1920]{1,0:T(8,128)(2,1)}, u32[]{:S(2)}, u32[]{:S(2)}) collective-permute-start(bf16[384,1920]{1,0:T(8,128)(2,1)} %get-tuple-element.55.refs_4_), channel_id=1, source_target_pairs={{0,1},{1,0},{2,3},{3,2},{4,5},{5,4},{6,7},{7,6},{8,9},{9,8},{10,11... | collective-permute-start | bytes 4423688 | tf_op jit(solution)/shard_map/ppermute | solution.py:30
  224.9 56.0 %collective-permute-start.40 = (bf16[384,1792]{1,0:T(8,128)(2,1)S(1)}, bf16[384,1792]{1,0:T(8,128)(2,1)}, u32[]{:S(2)}, u32[]{:S(2)}) collective-permute-start(bf16[384,1792]{1,0:T(8,128)(2,1)S(1)} %bitcast.62), channel_id=1, source_target_pairs={{0,1},{1,0},{2,3},{3,2},{4,5},{5,4},{6,7},{7,6},{8,9},{9,8},{10,11... | collective-permute-start | bytes 4128776 | tf_op jit(solution)/shard_map/ppermute | solution.py:30
  240.7 17.5 %collective-permute-start.31 = (bf16[384,384]{1,0:T(8,128)(2,1)S(1)}, bf16[384,384]{1,0:T(8,128)(2,1)S(1)}, u32[]{:S(2)}, u32[]{:S(2)}) collective-permute-start(bf16[384,384]{1,0:T(8,128)(2,1)S(1)} %bitcast.68), channel_id=1, source_target_pairs={{0,24},{8,16},{16,8},{24,0},{1,25},{9,17},{17,9},{25,1},{2,26},{10... | collective-permute-start | bytes 884744 | tf_op jit(solution)/shard_map/ppermute | solution.py:46
  266.9 25.5 %collective-permute-start.34 = (bf16[96,1920]{1,0:T(8,128)(2,1)S(1)}, bf16[96,1920]{1,0:T(8,128)(2,1)}, u32[]{:S(2)}, u32[]{:S(2)}) collective-permute-start(bf16[96,1920]{1,0:T(8,128)(2,1)S(1)} %get-tuple-element.103), channel_id=1, source_target_pairs={{2,4},{4,2},{3,5},{5,3},{10,12},{12,10},{11,13},{13,11},{18,20},{2... | collective-permute-start | bytes 1105928 | tf_op jit(solution)/shard_map/ppermute | solution.py:69
  268.4 24.1 %collective-permute-start.33 = (bf16[96,1920]{1,0:T(8,128)(2,1)}, bf16[96,1920]{1,0:T(8,128)(2,1)}, u32[]{:S(2)}, u32[]{:S(2)}) collective-permute-start(bf16[96,1920]{1,0:T(8,128)(2,1)} %get-tuple-element.102), channel_id=1, source_target_pairs={{0,2},{2,0},{4,6},{6,4},{1,3},{3,1},{5,7},{7,5},{8,10},{10,8},{12,... | collective-permute-start | bytes 1105928 | tf_op jit(solution)/shard_map/ppermute | solution.py:68
  276.5 16.8 %collective-permute-start.36 = (bf16[96,1920]{1,0:T(8,128)(2,1)S(1)}, bf16[96,1920]{1,0:T(8,128)(2,1)S(1)}, u32[]{:S(2)}, u32[]{:S(2)}) collective-permute-start(bf16[96,1920]{1,0:T(8,128)(2,1)S(1)} %fusion.2.refs_8_), channel_id=1, source_target_pairs={{0,4},{4,0},{2,6},{6,2},{1,5},{5,1},{3,7},{7,3},{8,12},{12,8},{10,... | collective-permute-start | bytes 1105928 | tf_op jit(solution)/shard_map/ppermute | solution.py:71
  (64 other events, 602.7 us)

commit v7 on v5

--- a/solution.py
+++ b/solution.py
@@ -84,7 +84,7 @@
     pl.when(jnp.logical_not(from_own))(functools.partial(fill, other))
 
 
-def project(cols, rows, own, other, spot, n_dp):
+def project(cols, at, rows, own, other, spot, n_dp):
     half = cols.shape[0]
     count = len(own)
     clusters, rank_own, width = own[0].shape
@@ -92,10 +92,10 @@
     part = rank_own // parts_core
     row_count = clusters * count * part
     built = rows is None
-    ins = [cols] + (list(own) + list(other) if built else list(rows))
+    given = list(own) + list(other) if built else list(rows)
 
     def kernel(spot_ref, cols_ref, *refs):
-        sources, outs = refs[: len(ins) - 1], refs[len(ins) - 1 :]
+        sources, outs = refs[: len(given)], refs[len(given) :]
         dp, core = spot_ref[0], spot_ref[1]
         parts, products = sources, outs[-n_dp:]
         if built:
@@ -105,29 +105,64 @@
                 from_own = core == (dp ^ k) // parts_core
                 place_rows(sources[:count], sources[count:], parts[k], part, from_own, low)
         for base, product in zip(parts, products):
-            product[...] = dot(base[...], cols_ref[:, :width], 1, 1).astype(BF)
+            product[...] = dot(base[...], cols_ref[...], 1, 1).astype(BF)
 
     outs = [shaped((row_count, width), BF)] * n_dp if built else []
     outs += [shaped((row_count, half), BF)] * n_dp
     got = pl.pallas_call(
         kernel,
+        grid=(1,),
         out_shape=outs,
-        in_specs=[SCALAR] + [whole(x) for x in ins],
+        in_specs=[SCALAR, pl.BlockSpec((half, width), lambda _: (0, at), memory_space=VMEM)]
+        + [whole(x) for x in given],
         out_specs=[whole(out) for out in outs],
         compiler_params=params(2 * half, True),
         cost_estimate=FREE,
         name="project",
-    )(spot, *ins)
+    )(spot, cols, *given)
     return (got[:n_dp] if built else rows), got[-n_dp:]
 
 
-def basis_grads(keep, other, cols, other_cols, spot, shape, n_dp, first):
+def sum_for_groups(pieces, groups, clusters, count, firsts):
+    rows, half = pieces[0].shape
+    part = rows // (clusters * count)
+    n_ex = groups.shape[0]
+
+    def kernel(groups_ref, *refs):
+        got, out_ref, sum_ref = refs[: len(pieces)], refs[-2], refs[-1]
+        for b in range(count):
+            for c in range(clusters):
+                take = slice((c * count + b) * part, (c * count + b + 1) * part)
+                total = got[0][take, :].astype(FL)
+                for piece in got[1:]:
+                    total += piece[take, :].astype(FL)
+                sum_ref[c, b] = total.astype(BF)
+        for e in range(n_ex):
+            for b in range(count):
+                out_ref[e, b * part : (b + 1) * part, :] = sum_ref[groups_ref[e], b]
+
+    out = shaped((n_ex, count * part, half), BF)
+    return pl.pallas_call(
+        kernel,
+        out_shape=out,
+        in_specs=[SCALAR] + [whole(x) for x in pieces] + [ANYWHERE] * len(firsts),
+        out_specs=whole(out),
+        scratch_shapes=[pltpu.VMEM((clusters, count, part, half), BF)],
+        compiler_params=params(2 * half),
+        cost_estimate=FREE,
+        name="sum_for_groups",
+    )(groups, *pieces, *firsts)
+
+
+def basis_grads(keep, other, cols, other_cols, at, spot, shape, n_dp, first):
     clusters, rank_own, width = shape
     parts_core = n_dp // 2
     part = rank_own // parts_core
     half = cols.shape[0]
     count = keep[0].shape[0] // (clusters * part)
     block = width // 2 if width % 256 == 0 else width
+
+    skip = at * (width // block)
 
     def kernel(spot_ref, *refs):
         ours, theirs = refs[:parts_core], refs[parts_core : 2 * parts_core]
@@ -160,7 +195,7 @@
         out_shape=[out] * count,
         in_specs=[SCALAR]
         + [whole(x) for x in ins]
-        + [pl.BlockSpec((half, block), lambda j: (0, j), memory_space=VMEM)] * 2
+        + [pl.BlockSpec((half, block), lambda j: (0, skip + j), memory_space=VMEM)] * 2
         + [ANYWHERE],
         out_specs=[
             pl.BlockSpec((clusters * rank_own, block), lambda j: (0, j), memory_space=VMEM)
@@ -420,20 +455,22 @@
 
     lanes = 128
 
-    def own_columns(rows, more):
-        rows = rows.reshape(tok_rows, n_dp, width).transpose(1, 0, 2)
-        if more is not None:
-            more = jnp.broadcast_to(more[None], (n_dp, tok_rows, lanes))
-            rows = jnp.concatenate([rows, more], axis=2)
-        rows = jnp.broadcast_to(rows[:, None], (n_dp, n_z) + rows.shape[1:])
-        rows = rows.reshape(n_dp * n_z, tok_rows, -1)
-        got = lax.all_to_all(rows, ("dp", "ez"), split_axis=0, concat_axis=0, tiled=True)
-        return got.reshape(half, -1)
-
     routing = jnp.concatenate([route_ids.astype(BF), route_weight], axis=1)
     routing = jnp.pad(routing, ((0, 0), (0, lanes - 2 * top)))
-    x_half = own_columns(tokens, routing)
-    dy_half = own_columns(after(grad_out, x_half), None)
+    leaving = [
+        grad_out.reshape(tok_rows, n_dp, width),
+        tokens.reshape(tok_rows, n_dp, width),
+        jnp.broadcast_to(routing[:, None], (tok_rows, n_dp, lanes)),
+    ]
+    leaving = jnp.concatenate(leaving, axis=2).transpose(1, 0, 2)
+    leaving = jnp.broadcast_to(leaving[:, None], (n_dp, n_z) + leaving.shape[1:])
+    cols = lax.all_to_all(
+        leaving.reshape(n_dp * n_z, tok_rows, -1),
+        ("dp", "ez"),
+        split_axis=0,
+        concat_axis=0,
+        tiled=True,
+    ).reshape(half, 2 * width + lanes)
     spot = jnp.stack([dp, core]).astype(jnp.int32)
 
     def chip_rows(own, other):
@@ -457,7 +494,7 @@
     other_in = [core_swap(basis) for basis in own_in]
     other_out = [core_swap(basis) for basis in own_out]
 
-    routing = x_half[:, width:]
+    routing = cols[:, 2 * width :]
     swapped = core_swap(routing)
     routing = jnp.stack(
         [jnp.where(core == 0, routing, swapped), jnp.where(core == 0, swapped, routing)]
@@ -480,24 +517,22 @@
     def sum_parts(got):
         return sum(piece.astype(FL) for piece in got).astype(BF)
 
-    def to_group(mine):
-        mine = mine.reshape(clusters, -1, half)
-        send = mine.at[group_cluster].get(mode="promise_in_bounds")
-        return lax.all_to_all(send, ("ez", "core"), split_axis=0, concat_axis=0, tiled=True)
+    def spread(mine):
+        return lax.all_to_all(mine, ("ez", "core"), split_axis=0, concat_axis=0, tiled=True)
 
     rows_in, terms = project(
-        x_half, chip_rows(own_in, other_in), own_in, other_in, spot, n_dp
-    )
-    mine_in = sum_parts(trade(lambda k: terms[k], "dp"))
-    got_in = to_group(mine_in)
+        cols, 1, chip_rows(own_in, other_in), own_in, other_in, spot, n_dp
+    )
     _, terms_out = project(
-        dy_half, chip_rows(own_out, other_out), own_out, other_out, spot, n_dp
-    )
-    mine_out = sum_parts(trade(lambda k: terms_out[k], "dp"))
+        cols, 0, chip_rows(own_out, other_out), own_out, other_out, spot, n_dp
+    )
+    mine_in = sum_for_groups(trade(lambda k: terms[k], "dp"), group_cluster, clusters, 2, terms_out[:1])
+    got_in = spread(mine_in)
     h_pieces = trade(lambda k: got_in, "dp")
-    for piece in h_pieces[1:]:
-        mine_out = after(mine_out, piece)
-    got_out = to_group(mine_out)
+    mine_out = sum_for_groups(
+        trade(lambda k: terms_out[k], "dp"), group_cluster, clusters, 1, h_pieces[1:]
+    )
+    got_out = spread(mine_out)
     (hg, hu, hidden, mixed, act, lift), mixed_chunks = forward(
         h_pieces, pick, weight_of, gate_factor, up_factor, down_factor, dp
     )
@@ -519,7 +554,7 @@
         hg, grad_gate, hu, grad_up, hidden, back, total, in_mine
     )
     mine = jnp.concatenate([in_mine, mixed_mine], axis=1)
-    got = lax.all_to_all(mine, ("ez", "core"), split_axis=0, concat_axis=0, tiled=True)
+    got = spread(mine)
     in_sum = after(by_cluster(got[:, : 2 * rank_part], group_cluster), grad_gate_factor)
     mixed_sum = by_cluster(got[:, 2 * rank_part :], group_cluster)
     in_parts = trade(lambda k: in_sum, "dp")
@@ -538,8 +573,7 @@
     rows = leaving.reshape(n_dp * n_z, tok_rows, width + lanes)
     rows = lax.all_to_all(rows, ("dp", "ez"), split_axis=0, concat_axis=0, tiled=True)
     rows = rows.reshape(n_dp, n_z, tok_rows, width + lanes)
-    x_other = core_swap(x_half)
-    dy_other = core_swap(dy_half)
+    other_cols = core_swap(cols)
     same = core == dp // parts_core
 
     def own_ranks(parts):
@@ -550,12 +584,12 @@
 
     shape = (clusters, rank_own, width)
     grad_gate_basis, grad_up_basis = basis_grads(
-        *own_ranks(in_parts), x_half, x_other, spot, shape, n_dp, leaving
+        *own_ranks(in_parts), cols, other_cols, 1, spot, shape, n_dp, leaving
     )
     mixed_sum = after(mixed_sum, grad_gate_basis)
     mixed_parts = trade(lambda k: mixed_sum, "dp")
     (grad_down_basis,) = basis_grads(
-        *own_ranks(mixed_parts), dy_half, dy_other, spot, shape, n_dp, leaving
+        *own_ranks(mixed_parts), cols, other_cols, 0, spot, shape, n_dp, leaving
     )
 
     grad_rows = jnp.sum(rows[..., :width].astype(FL), axis=1)

time: 292 us -> 298 us (1.021)
  other arithmetic: 17.8 us -> 25.6 us
  Pallas kernels: 47 us -> 50.7 us
  starting transfers between devices: 61 us -> 57.7 us
    ppermute x24, waiting for transfers between devices: 30.9 us -> 39.4 us  [trade(): lax.ppermute(chunk_for(k), axis, [(i, i ^ k) for i in range(n)])]
    all_to_all x5 -> x4, waiting for transfers between devices: 78.7 us -> 70.6 us  [the longest x1 62.2 us: body(): lax.all_to_all(leaving.reshape(n_dp * n_z, tok_rows, -1), ('dp', 'ez'), s...]
    slice x7 -> x3, local copies, waits for them, and re-layouts: 8.33 us -> 3.59 us  [after(): lax.slice(first, (0,) * first.ndim, (1,) * first.ndim).reshape(())]
    unnamed x85 -> x73, local copies, waits for them, and re-layouts: 14.1 us -> 18.4 us
    pallas_call x2 -> x4, Pallas kernels: 9.83 us -> 13.4 us  [the longest x2 9.94 us: project(): pl.pallas_call(kernel, grid=(1,), out_shape=outs, in_specs=[SCALAR, pl.Bl...]
    all_to_all x5 -> x4, starting transfers between devices: 23.2 us -> 20.8 us  [the longest x3 12.4 us: spread(): lax.all_to_all(mine, ('ez', 'core'), split_axis=0, concat_axis=0, tiled=T...]
    ppermute x11 -> x10, waiting for transfers between devices: 6.21 us -> 4.16 us  [core_swap(): return lax.ppermute(value, 'core', [(0, 1), (1, 0)])]
  transfers between devices with their start and end apart: 41 -> 39, of which waited for: 20 -> 17; matrix products, arithmetic and copies ran while one was open for 8% -> 13% of each run, Pallas kernels for 14% -> 16%
where the time goes in v7:
time: 298 us; the launch traced here: 296 us
  waiting for transfers between devices  120 us (40%)
  starting transfers between devices  57.7 us (19%)
  Pallas kernels  50.7 us (17%)
  local copies, waits for them, and re-layouts  34.9 us (12%)
  other arithmetic  25.6 us (9%)
  matrix products  3.51 us (1%)
  between operations  3.21 us (1%)
    all_to_all x1, waiting for transfers between devices, body(): lax.all_to_all(leaving.reshape(n_dp * n_z, tok_rows, -1), ('dp', 'ez'), s...  62.2 us
    ppermute x24, waiting for transfers between devices, trade(): lax.ppermute(chunk_for(k), axis, [(i, i ^ k) for i in range(n)])  39.4 us
    ppermute x24, starting transfers between devices, trade(): lax.ppermute(chunk_for(k), axis, [(i, i ^ k) for i in range(n)])  28.6 us
    unnamed x73, local copies, waits for them, and re-layouts  18.4 us
    all_to_all x3, starting transfers between devices, spread(): lax.all_to_all(mine, ('ez', 'core'), split_axis=0, concat_axis=0, tiled=T...  12.4 us
    pallas_call x1, Pallas kernels, backward(): pl.pallas_call(kernel, grid=(local,), out_shape=outs + chunks, in_specs=[...  12.2 us
    pallas_call x1, Pallas kernels, forward(): pl.pallas_call(kernel, grid=(local,), out_shape=outs + chunks, in_specs=[...  10.9 us
    pallas_call x2, Pallas kernels, project(): pl.pallas_call(kernel, grid=(1,), out_shape=outs, in_specs=[SCALAR, pl.Bl...  9.94 us
  transfers between devices with their start and end apart: 39, of which 17 were waited for; matrix products, arithmetic and copies ran while one was open for 13% of the time, Pallas kernels for 16%

profile of v7, /device:TPU:0, one launch (start us, length us, event | category | flops | bytes accessed | tf_op | source)
XLA Modules:
  0.0 296.0 jit_solution(14975114274327371072)
XLA Ops:
  6.8 8.3 %all-to-all-start = ((bf16[16,24,3712]{2,1,0:T(8,128)(2,1)}), bf16[16,24,3712]{2,1,0:T(8,128)(2,1)S(1)}, u32[]{:S(2)}, u32[]{:S(2)}) async-start(bf16[16,24,3712]{2,1,0:T(8,128)(2,1)} %bitcast.59), calls=%async_computation | async-start | bytes 5701632 | tf_op jit(solution)/shard_map/all_to_all | solution.py:467
  19.3 62.2 %all-to-all-done = bf16[16,24,3712]{2,1,0:T(8,128)(2,1)S(1)} async-done(((bf16[16,24,3712]{2,1,0:T(8,128)(2,1)}), bf16[16,24,3712]{2,1,0:T(8,128)(2,1)S(1)}, u32[]{:S(2)}, u32[]{:S(2)}) %all-to-all-start) | async-done | bytes 2850848 | tf_op jit(solution)/shard_map/all_to_all | solution.py:467
  83.0 5.5 %project.3 = (bf16[256,1792]{1,0:T(8,128)(2,1)}, bf16[256,1792]{1,0:T(8,128)(2,1)}, bf16[256,1792]{1,0:T(8,128)(2,1)}, bf16[256,1792]{1,0:T(8,128)(2,1)}, bf16[2...) custom-call(s32[2]{0:T(128)} %pad_add_fusion.spot_ref, ...), custom_call_target="tpu_custom_call" | custom-call | tf_op jit(solution)/shard_map/project/pallas_call | solution.py:112
  89.4 2.7 collective-permute-start.8
  92.2 4.5 %project.2 = (bf16[128,1792]{1,0:T(8,128)(2,1)}, bf16[128,1792]{1,0:T(8,128)(2,1)}, bf16[128,1792]{1,0:T(8,128)(2,1)}, bf16[128,1792]{1,0:T(8,128)(2,1)}, bf16[1...) custom-call(s32[2]{0:T(128)} %pad_add_fusion.spot_ref, ...), custom_call_target="tpu_custom_call" | custom-call | tf_op jit(solution)/shard_map/project/pallas_call | solution.py:112
  96.7 2.3 collective-permute-done.8.refs_3_
  101.8 4.1 %all-to-all-start.1 = ((bf16[8,64,384]{2,1,0:T(8,128)(2,1)}), bf16[8,64,384]{2,1,0:T(8,128)(2,1)}, u32[]{:S(2)}, u32[]{:S(2)}) async-start(bf16[8,64,384]{2,1,0:T(8,128)(2,1)} %sum_for_groups.2), calls=%async_computation.1 | async-start | bytes 786432 | tf_op jit(solution)/shard_map/all_to_all | solution.py:521
  110.4 8.0 %all-to-all-done.1.refs_0_ = bf16[8,64,384]{2,1,0:T(8,128)(2,1)} async-done(((bf16[8,64,384]{2,1,0:T(8,128)(2,1)}), bf16[8,64,384]{2,1,0:T(8,128)(2,1)}, u32[]{:S(2)}, u32[]{:S(2)}) %all-to-all-start.1) | async-done | bytes 393248 | tf_op jit(solution)/shard_map/all_to_all | solution.py:521
  132.4 3.0 %reduce_window_sum.11 = s32[4,32,24]{2,1,0:T(8,128)} reduce-window(s32[4,32,24]{2,1,0:T(8,128)} %copy.75, s32[]{:T(128)} %constant.38.clone.1), window={size=1x1x24 pad=0_0x0_0x23_0}, to_apply=%region_1.2 | reduce-window | flops 70656 | bytes 24580 | tf_op jit(solution)/shard_map/jit(cumsum)/reduce_window_sum | solution.py:509
  135.4 5.5 %collective-permute-done.3.refs_3_ = bf16[128,384]{1,0:T(8,128)(2,1)} collective-permute-done((bf16[128,384]{1,0:T(8,128)(2,1)}, bf16[128,384]{1,0:T(8,128)(2,1)}, u32[]{:S(2)}, u32[]{:S(2)}) %collective-permute-start.3) | collective-permute-done | bytes 98336 | tf_op jit(solution)/shard_map/ppermute | solution.py:46
  142.9 3.6 %all-to-all-start.2 = ((bf16[8,32,384]{2,1,0:T(8,128)(2,1)}), bf16[8,32,384]{2,1,0:T(8,128)(2,1)S(1)}, u32[]{:S(2)}, u32[]{:S(2)}) async-start(bf16[8,32,384]{2,1,0:T(8,128)(2,1)} %sum_for_groups.3), calls=%async_computation.2 | async-start | bytes 393216 | tf_op jit(solution)/shard_map/all_to_all | solution.py:521
  161.3 10.9 %forward.1 = (bf16[4,224,512]{2,1,0:T(8,128)(2,1)}, bf16[4,224,512]{2,1,0:T(8,128)(2,1)}, bf16[4,224,512]{2,1,0:T(8,128)(2,1)}, bf16[4,224,512]{2,1,0:T(8,128)(2...) custom-call(s32[1]{0:T(128)} %bitcast.dp_ref, ...), custom_call_target="tpu_custom_call" | custom-call | tf_op jit(solution)/shard_map/forward/pallas_call | solution.py:316
  176.6 12.2 %backward.1 = (bf16[4,224,512]{2,1,0:T(8,128)(2,1)}, bf16[4,224,512]{2,1,0:T(8,128)(2,1)}, bf16[4,224,512]{2,1,0:T(8,128)(2,1)}, f32[4,224,1]{2,1,0:T(8,128)}, b...) custom-call(s32[1]{0:T(128)} %bitcast.dp_ref, ...), custom_call_target="tpu_custom_call" | custom-call | flops 3523215360 | bytes 33554432 | tf_op jit(solution)/shard_map/backward/pallas_call | solution.py:378
  192.5 9.5 %collective-permute-done.18 = bf16[8,64,384]{2,1,0:T(8,128)(2,1)S(1)} collective-permute-done((bf16[8,64,384]{2,1,0:T(8,128)(2,1)}, bf16[8,64,384]{2,1,0:T(8,128)(2,1)S(1)}, u32[]{:S(2)}, u32[]{:S(2)}) %collective-permute-start.18) | collective-permute-done | bytes 393248 | tf_op jit(solution)/shard_map/ppermute | solution.py:46
  202.0 5.6 %collective-permute-done.17 = bf16[8,64,384]{2,1,0:T(8,128)(2,1)S(1)} collective-permute-done((bf16[8,64,384]{2,1,0:T(8,128)(2,1)}, bf16[8,64,384]{2,1,0:T(8,128)(2,1)S(1)}, u32[]{:S(2)}, u32[]{:S(2)}) %collective-permute-start.17) | collective-permute-done | bytes 393248 | tf_op jit(solution)/shard_map/ppermute | solution.py:46
  209.7 4.8 %all-to-all-start.3 = ((bf16[8,96,384]{2,1,0:T(8,128)(2,1)}), bf16[8,96,384]{2,1,0:T(8,128)(2,1)}, u32[]{:S(2)}, u32[]{:S(2)}) async-start(bf16[8,96,384]{2,1,0:T(8,128)(2,1)} %pad_maximum_fusion), calls=%async_computation.3 | async-start | bytes 1179648 | tf_op jit(solution)/shard_map/all_to_all | solution.py:521
  224.2 5.2 %factor_grads.1 = (f32[4,512,512]{2,1,0:T(8,128)}, f32[4,512,512]{2,1,0:T(8,128)}, f32[4,512,512]{2,1,0:T(8,128)}) custom-call(bf16[4,224,512]{2,1,0:T(8,128)(2,1)S(1)} %copy-done.6, bf16[4,224,512]{2,1,0:T(8,128)(2,1)S(1)} %copy-done.10, bf16[4,224,512]{2,1,0:T(8,128)(2,1)S(1)} %copy-done.7, bf16[4,224,512]{2,1,0:T(8,128)(2,1)S(1)} %copy-done.11, ...), custom_call_target="tpu_custom_call" | custom-call | tf_op jit(solution)/shard_map/factor_grads/pallas_call | solution.py:411
  236.6 4.9 %collective-permute-done.24 = bf16[256,384]{1,0:T(8,128)(2,1)S(1)} collective-permute-done((bf16[256,384]{1,0:T(8,128)(2,1)S(1)}, bf16[256,384]{1,0:T(8,128)(2,1)S(1)}, u32[]{:S(2)}, u32[]{:S(2)}) %collective-permute-start.24) | collective-permute-done | bytes 196640 | tf_op jit(solution)/shard_map/ppermute | solution.py:46
  243.3 2.0 collective-permute-done.23
  248.9 5.9 %all-to-all-start.4 = ((bf16[16,24,1920]{2,1,0:T(8,128)(2,1)}), bf16[16,24,1920]{2,1,0:T(8,128)(2,1)}, u32[]{:S(2)}, u32[]{:S(2)}) async-start(bf16[16,24,1920]{2,1,0:T(8,128)(2,1)} %bitcast.58), calls=%async_computation.4 | async-start | bytes 2949120 | tf_op jit(solution)/shard_map/all_to_all | solution.py:574
  257.8 4.6 %basis_grads.2 = (f32[256,1792]{1,0:T(8,128)}, f32[256,1792]{1,0:T(8,128)}) custom-call(s32[2]{0:T(128)S(1)} %copy-done.17, bf16[256,384]{1,0:T(8,128)(2,1)S(1)} %get-tuple-element.103.refs_0_, bf16[256,384]{1,0:T(8,128)(2,1)S(1)} %get-tuple-element.101.refs_1_, bf16[256,384]{1,0:T(8,128)(2,1)S(1)} %collective-permute-done.26.refs_2_, ...), custom_call_target="tpu_custom_call" | custom-call | tf_op jit(solution)/shard_map/basis_grads/pallas_call | solution.py:192
  267.9 7.6 %collective-permute-done.29 = bf16[128,384]{1,0:T(8,128)(2,1)S(1)} collective-permute-done((bf16[128,384]{1,0:T(8,128)(2,1)S(1)}, bf16[128,384]{1,0:T(8,128)(2,1)S(1)}, u32[]{:S(2)}, u32[]{:S(2)}) %collective-permute-start.29) | collective-permute-done | bytes 98336 | tf_op jit(solution)/shard_map/ppermute | solution.py:46
  280.0 3.6 %basis_grads.3 = f32[256,1792]{1,0:T(8,128)} custom-call(s32[2]{0:T(128)S(1)} %copy-done.17, bf16[128,384]{1,0:T(8,128)(2,1)S(1)} %get-tuple-element.107.refs_0_, bf16[128,384]{1,0:T(8,128)(2,1)S(1)} %get-tuple-element.105.refs_1_, bf16[128,384]{1,0:T(8,128)(2,1)S(1)} %collective-permute-done.32.refs_2_, ...), custom_call_target="tpu_custom_call" | custom-call | tf_op jit(solution)/shard_map/basis_grads/pallas_call | solution.py:192
  285.4 6.2 %all-to-all-done.4 = bf16[16,24,1920]{2,1,0:T(8,128)(2,1)} async-done(((bf16[16,24,1920]{2,1,0:T(8,128)(2,1)}), bf16[16,24,1920]{2,1,0:T(8,128)(2,1)}, u32[]{:S(2)}, u32[]{:S(2)}) %all-to-all-start.4) | async-done | bytes 1474592 | tf_op jit(solution)/shard_map/all_to_all | solution.py:574
  (209 shorter events, 100.3 us)
Async XLA Ops:
  6.8 74.7 %all-to-all-start = ((bf16[16,24,3712]{2,1,0:T(8,128)(2,1)}), bf16[16,24,3712]{2,1,0:T(8,128)(2,1)S(1)}, u32[]{:S(2)}, u32[]{:S(2)}) async-start(bf16[16,24,3712]{2,1,0:T(8,128)(2,1)} %bitcast.59), calls=%async_computation | async-start | bytes 5701632 | tf_op jit(solution)/shard_map/all_to_all | solution.py:467
  15.7 76.6 %collective-permute-start = (bf16[4,64,1792]{2,1,0:T(8,128)(2,1)}, bf16[4,64,1792]{2,1,0:T(8,128)(2,1)}, u32[]{:S(2)}, u32[]{:S(2)}) collective-permute-start(bf16[4,64,1792]{2,1,0:T(8,128)(2,1)} %refs_0_.2), channel_id=1, source_target_pairs={{0,1},{1,0},{2,3},{3,2},{4,5},{5,4},{6,7},{7,6},{8,9},{9,8},{10,11... | collective-permute-start | bytes 2752520 | tf_op jit(solution)/shard_map/ppermute | solution.py:30
  101.8 16.7 %all-to-all-start.1 = ((bf16[8,64,384]{2,1,0:T(8,128)(2,1)}), bf16[8,64,384]{2,1,0:T(8,128)(2,1)}, u32[]{:S(2)}, u32[]{:S(2)}) async-start(bf16[8,64,384]{2,1,0:T(8,128)(2,1)} %sum_for_groups.2), calls=%async_computation.1 | async-start | bytes 786432 | tf_op jit(solution)/shard_map/all_to_all | solution.py:521
  107.6 18.6 %collective-permute-start.1 = (bf16[128,384]{1,0:T(8,128)(2,1)}, bf16[128,384]{1,0:T(8,128)(2,1)S(1)}, u32[]{:S(2)}, u32[]{:S(2)}) collective-permute-start(bf16[128,384]{1,0:T(8,128)(2,1)} %get-tuple-element.46), channel_id=1, source_target_pairs={{0,8},{8,0},{16,24},{24,16},{1,9},{9,1},{17,25},{25,17},{2,10},{10... | collective-permute-start | bytes 294920 | tf_op jit(solution)/shard_map/ppermute | solution.py:46
  109.2 26.2 %collective-permute-start.2 = (bf16[128,384]{1,0:T(8,128)(2,1)}, bf16[128,384]{1,0:T(8,128)(2,1)S(1)}, u32[]{:S(2)}, u32[]{:S(2)}) collective-permute-start(bf16[128,384]{1,0:T(8,128)(2,1)} %get-tuple-element.47), channel_id=1, source_target_pairs={{0,16},{8,24},{16,0},{24,8},{1,17},{9,25},{17,1},{25,9},{2,18},{10... | collective-permute-start | bytes 294920 | tf_op jit(solution)/shard_map/ppermute | solution.py:46
  118.4 22.4 %collective-permute-start.9 = (bf16[8,64,384]{2,1,0:T(8,128)(2,1)}, bf16[8,64,384]{2,1,0:T(8,128)(2,1)S(1)}, u32[]{:S(2)}, u32[]{:S(2)}) collective-permute-start(bf16[8,64,384]{2,1,0:T(8,128)(2,1)} %all-to-all-done.1.refs_0_), channel_id=1, source_target_pairs={{0,8},{8,0},{16,24},{24,16},{1,9},{9,1},{17,25},{25,17},{2,10},{10... | collective-permute-start | bytes 1179656 | tf_op jit(solution)/shard_map/ppermute | solution.py:46
  120.0 21.2 %collective-permute-start.10 = (bf16[8,64,384]{2,1,0:T(8,128)(2,1)}, bf16[8,64,384]{2,1,0:T(8,128)(2,1)}, u32[]{:S(2)}, u32[]{:S(2)}) collective-permute-start(bf16[8,64,384]{2,1,0:T(8,128)(2,1)} %all-to-all-done.1.refs_0_), channel_id=1, source_target_pairs={{0,16},{8,24},{16,0},{24,8},{1,17},{9,25},{17,1},{25,9},{2,18},{10... | collective-permute-start | bytes 1179656 | tf_op jit(solution)/shard_map/ppermute | solution.py:46
  120.6 20.6 %collective-permute-start.11 = (bf16[8,64,384]{2,1,0:T(8,128)(2,1)}, bf16[8,64,384]{2,1,0:T(8,128)(2,1)}, u32[]{:S(2)}, u32[]{:S(2)}) collective-permute-start(bf16[8,64,384]{2,1,0:T(8,128)(2,1)} %all-to-all-done.1.refs_0_), channel_id=1, source_target_pairs={{0,24},{8,16},{16,8},{24,0},{1,25},{9,17},{17,9},{25,1},{2,26},{10... | collective-permute-start | bytes 1179656 | tf_op jit(solution)/shard_map/ppermute | solution.py:46
  126.2 14.7 %collective-permute-start.3 = (bf16[128,384]{1,0:T(8,128)(2,1)}, bf16[128,384]{1,0:T(8,128)(2,1)}, u32[]{:S(2)}, u32[]{:S(2)}) collective-permute-start(bf16[128,384]{1,0:T(8,128)(2,1)} %get-tuple-element.48), channel_id=1, source_target_pairs={{0,24},{8,16},{16,8},{24,0},{1,25},{9,17},{17,9},{25,1},{2,26},{10... | collective-permute-start | bytes 294920 | tf_op jit(solution)/shard_map/ppermute | solution.py:46
  142.9 11.7 %all-to-all-start.2 = ((bf16[8,32,384]{2,1,0:T(8,128)(2,1)}), bf16[8,32,384]{2,1,0:T(8,128)(2,1)S(1)}, u32[]{:S(2)}, u32[]{:S(2)}) async-start(bf16[8,32,384]{2,1,0:T(8,128)(2,1)} %sum_for_groups.3), calls=%async_computation.2 | async-start | bytes 393216 | tf_op jit(solution)/shard_map/all_to_all | solution.py:521
  154.5 19.8 %collective-permute-start.12 = (bf16[8,32,384]{2,1,0:T(8,128)(2,1)S(1)}, bf16[8,32,384]{2,1,0:T(8,128)(2,1)S(1)}, u32[]{:S(2)}, u32[]{:S(2)}) collective-permute-start(bf16[8,32,384]{2,1,0:T(8,128)(2,1)S(1)} %all-to-all-done.2.refs_0_), channel_id=1, source_target_pairs={{0,8},{8,0},{16,24},{24,16},{1,9},{9,1},{17,25},{25,17},{2,10},{10... | collective-permute-start | bytes 589832 | tf_op jit(solution)/shard_map/ppermute | solution.py:46
  155.1 20.7 %collective-permute-start.13 = (bf16[8,32,384]{2,1,0:T(8,128)(2,1)S(1)}, bf16[8,32,384]{2,1,0:T(8,128)(2,1)S(1)}, u32[]{:S(2)}, u32[]{:S(2)}) collective-permute-start(bf16[8,32,384]{2,1,0:T(8,128)(2,1)S(1)} %all-to-all-done.2.refs_0_), channel_id=1, source_target_pairs={{0,16},{8,24},{16,0},{24,8},{1,17},{9,25},{17,1},{25,9},{2,18},{10... | collective-permute-start | bytes 589832 | tf_op jit(solution)/shard_map/ppermute | solution.py:46
  156.5 19.3 %collective-permute-start.14 = (bf16[8,32,384]{2,1,0:T(8,128)(2,1)S(1)}, bf16[8,32,384]{2,1,0:T(8,128)(2,1)S(1)}, u32[]{:S(2)}, u32[]{:S(2)}) collective-permute-start(bf16[8,32,384]{2,1,0:T(8,128)(2,1)S(1)} %all-to-all-done.2.refs_0_), channel_id=1, source_target_pairs={{0,24},{8,16},{16,8},{24,0},{1,25},{9,17},{17,9},{25,1},{2,26},{10... | collective-permute-start | bytes 589832 | tf_op jit(solution)/shard_map/ppermute | solution.py:46
  172.2 18.6 %collective-permute-start.21 = (bf16[8,32,384]{2,1,0:T(8,128)(2,1)}, bf16[8,32,384]{2,1,0:T(8,128)(2,1)S(1)}, u32[]{:S(2)}, u32[]{:S(2)}) collective-permute-start(bf16[8,32,384]{2,1,0:T(8,128)(2,1)} %get-tuple-element.65), channel_id=1, source_target_pairs={{0,24},{8,16},{16,8},{24,0},{1,25},{9,17},{17,9},{25,1},{2,26},{10... | collective-permute-start | bytes 589832 | tf_op jit(solution)/shard_map/ppermute | solution.py:46
  173.7 18.6 %collective-permute-start.20 = (bf16[8,32,384]{2,1,0:T(8,128)(2,1)}, bf16[8,32,384]{2,1,0:T(8,128)(2,1)S(1)}, u32[]{:S(2)}, u32[]{:S(2)}) collective-permute-start(bf16[8,32,384]{2,1,0:T(8,128)(2,1)} %get-tuple-element.64), channel_id=1, source_target_pairs={{0,16},{8,24},{16,0},{24,8},{1,17},{9,25},{17,1},{25,9},{2,18},{10... | collective-permute-start | bytes 589832 | tf_op jit(solution)/shard_map/ppermute | solution.py:46
  174.4 18.0 %collective-permute-start.19 = (bf16[8,32,384]{2,1,0:T(8,128)(2,1)}, bf16[8,32,384]{2,1,0:T(8,128)(2,1)S(1)}, u32[]{:S(2)}, u32[]{:S(2)}) collective-permute-start(bf16[8,32,384]{2,1,0:T(8,128)(2,1)} %get-tuple-element.63), channel_id=1, source_target_pairs={{0,8},{8,0},{16,24},{24,16},{1,9},{9,1},{17,25},{25,17},{2,10},{10... | collective-permute-start | bytes 589832 | tf_op jit(solution)/shard_map/ppermute | solution.py:46
  188.8 13.2 %collective-permute-start.18 = (bf16[8,64,384]{2,1,0:T(8,128)(2,1)}, bf16[8,64,384]{2,1,0:T(8,128)(2,1)S(1)}, u32[]{:S(2)}, u32[]{:S(2)}) collective-permute-start(bf16[8,64,384]{2,1,0:T(8,128)(2,1)} %get-tuple-element.61), channel_id=1, source_target_pairs={{0,24},{8,16},{16,8},{24,0},{1,25},{9,17},{17,9},{25,1},{2,26},{10... | collective-permute-start | bytes 1179656 | tf_op jit(solution)/shard_map/ppermute | solution.py:46
  190.3 17.3 %collective-permute-start.17 = (bf16[8,64,384]{2,1,0:T(8,128)(2,1)}, bf16[8,64,384]{2,1,0:T(8,128)(2,1)S(1)}, u32[]{:S(2)}, u32[]{:S(2)}) collective-permute-start(bf16[8,64,384]{2,1,0:T(8,128)(2,1)} %get-tuple-element.60), channel_id=1, source_target_pairs={{0,16},{8,24},{16,0},{24,8},{1,17},{9,25},{17,1},{25,9},{2,18},{10... | collective-permute-start | bytes 1179656 | tf_op jit(solution)/shard_map/ppermute | solution.py:46
  190.9 16.7 %collective-permute-start.16 = (bf16[8,64,384]{2,1,0:T(8,128)(2,1)}, bf16[8,64,384]{2,1,0:T(8,128)(2,1)S(1)}, u32[]{:S(2)}, u32[]{:S(2)}) collective-permute-start(bf16[8,64,384]{2,1,0:T(8,128)(2,1)} %get-tuple-element.59), channel_id=1, source_target_pairs={{0,8},{8,0},{16,24},{24,16},{1,9},{9,1},{17,25},{25,17},{2,10},{10... | collective-permute-start | bytes 1179656 | tf_op jit(solution)/shard_map/ppermute | solution.py:46
  209.7 21.7 %all-to-all-start.3 = ((bf16[8,96,384]{2,1,0:T(8,128)(2,1)}), bf16[8,96,384]{2,1,0:T(8,128)(2,1)}, u32[]{:S(2)}, u32[]{:S(2)}) async-start(bf16[8,96,384]{2,1,0:T(8,128)(2,1)} %pad_maximum_fusion), calls=%async_computation.3 | async-start | bytes 1179648 | tf_op jit(solution)/shard_map/all_to_all | solution.py:521
  214.5 43.3 %collective-permute-start.28 = (bf16[384,3712]{1,0:T(8,128)(2,1)S(1)}, bf16[384,3712]{1,0:T(8,128)(2,1)}, u32[]{:S(2)}, u32[]{:S(2)}) collective-permute-start(bf16[384,3712]{1,0:T(8,128)(2,1)S(1)} %bitcast.55), channel_id=1, source_target_pairs={{0,1},{1,0},{2,3},{3,2},{4,5},{5,4},{6,7},{7,6},{8,9},{9,8},{10,11... | collective-permute-start | bytes 8552456 | tf_op jit(solution)/shard_map/ppermute | solution.py:30
  217.1 17.2 %collective-permute-start.25 = (bf16[4,384]{1,0:T(4,128)(2,1)S(1)}, bf16[4,384]{1,0:T(4,128)(2,1)S(1)}, u32[]{:S(2)}, u32[]{:S(2)}) collective-permute-start(bf16[4,384]{1,0:T(4,128)(2,1)S(1)} %select_bitcast_fusion.2), channel_id=1, source_target_pairs={{0,1},{1,0},{2,3},{3,2},{4,5},{5,4},{6,7},{7,6},{8,9},{9,8},{10,11... | collective-permute-start | bytes 9224 | tf_op jit(solution)/shard_map/ppermute | solution.py:30
  248.9 42.7 %all-to-all-start.4 = ((bf16[16,24,1920]{2,1,0:T(8,128)(2,1)}), bf16[16,24,1920]{2,1,0:T(8,128)(2,1)}, u32[]{:S(2)}, u32[]{:S(2)}) async-start(bf16[16,24,1920]{2,1,0:T(8,128)(2,1)} %bitcast.58), calls=%async_computation.4 | async-start | bytes 2949120 | tf_op jit(solution)/shard_map/all_to_all | solution.py:574
  264.3 11.1 %collective-permute-start.29 = (bf16[128,384]{1,0:T(8,128)(2,1)S(1)}, bf16[128,384]{1,0:T(8,128)(2,1)S(1)}, u32[]{:S(2)}, u32[]{:S(2)}) collective-permute-start(bf16[128,384]{1,0:T(8,128)(2,1)S(1)} %bitcast.68), channel_id=1, source_target_pairs={{0,16},{8,24},{16,0},{24,8},{1,17},{9,25},{17,1},{25,9},{2,18},{10... | collective-permute-start | bytes 294920 | tf_op jit(solution)/shard_map/ppermute | solution.py:46
  (49 other events, 379.7 us)

commit v8 on v4

--- a/solution.py
+++ b/solution.py
@@ -121,7 +121,38 @@
     return (got[:n_dp] if built else rows), got[-n_dp:]
 
 
-def basis_grads(keep, other, cols, other_cols, spot, shape, n_dp):
+def sum_for_groups(pieces, groups, clusters, count, firsts):
+    rows, half = pieces[0].shape
+    part = rows // (clusters * count)
+    n_ex = groups.shape[0]
+
+    def kernel(groups_ref, *refs):
+        got, out_ref, sum_ref = refs[: len(pieces)], refs[-2], refs[-1]
+        for b in range(count):
+            for c in range(clusters):
+                take = slice((c * count + b) * part, (c * count + b + 1) * part)
+                total = got[0][take, :].astype(FL)
+                for piece in got[1:]:
+                    total += piece[take, :].astype(FL)
+                sum_ref[c, b] = total.astype(BF)
+        for e in range(n_ex):
+            for b in range(count):
+                out_ref[e, b * part : (b + 1) * part, :] = sum_ref[groups_ref[e], b]
+
+    out = shaped((n_ex, count * part, half), BF)
+    return pl.pallas_call(
+        kernel,
+        out_shape=out,
+        in_specs=[SCALAR] + [whole(x) for x in pieces] + [ANYWHERE] * len(firsts),
+        out_specs=whole(out),
+        scratch_shapes=[pltpu.VMEM((clusters, count, part, half), BF)],
+        compiler_params=params(2 * half),
+        cost_estimate=FREE,
+        name="sum_for_groups",
+    )(groups, *pieces, *firsts)
+
+
+def basis_grads(keep, other, cols, other_cols, spot, shape, n_dp, first):
     clusters, rank_own, width = shape
     parts_core = n_dp // 2
     part = rank_own // parts_core
@@ -160,7 +191,8 @@
         out_shape=[out] * count,
         in_specs=[SCALAR]
         + [whole(x) for x in ins]
-        + [pl.BlockSpec((half, block), lambda j: (0, j), memory_space=VMEM)] * 2,
+        + [pl.BlockSpec((half, block), lambda j: (0, j), memory_space=VMEM)] * 2
+        + [ANYWHERE],
         out_specs=[
             pl.BlockSpec((clusters * rank_own, block), lambda j: (0, j), memory_space=VMEM)
         ]
@@ -169,7 +201,7 @@
         compiler_params=params(2 * half),
         cost_estimate=FREE,
         name="basis_grads",
-    )(spot, *ins, cols, other_cols)
+    )(spot, *ins, cols, other_cols, first)
     return [grad.reshape(shape) for grad in got]
 
 
@@ -336,7 +368,11 @@
         out_specs=[each(out) for out in outs] + [whole(chunk) for chunk in chunks],
         scratch_shapes=[pltpu.VMEM((1, rank, total), rows_kind(rows)), pltpu.VMEM((2, rank, total), FL)],
         compiler_params=params(total, True),
-        cost_estimate=FREE,
+        cost_estimate=pl.CostEstimate(
+            flops=local * slots * rank * (6 * total + 6 * hid),
+            bytes_accessed=32 << 20,
+            transcendentals=0,
+        ),
         name="backward",
     )(dp.reshape(1), *pieces, *ins)
     return got[:4], got[4:]
@@ -500,21 +536,23 @@
     def sum_parts(got):
         return sum(piece.astype(FL) for piece in got).astype(BF)
 
-    def to_group(mine):
-        mine = mine.reshape(clusters, -1, half)
-        send = mine.at[group_cluster].get(mode="promise_in_bounds")
-        return lax.all_to_all(send, ("ez", "core"), split_axis=0, concat_axis=0, tiled=True)
+    def spread(mine):
+        return lax.all_to_all(mine, ("ez", "core"), split_axis=0, concat_axis=0, tiled=True)
 
     rows_in, terms = project(
         x_half, chip_rows(own_in, other_in), own_in, other_in, spot, n_dp
     )
-    mine_in = sum_parts(trade(lambda k: terms[k], "dp"))
-    got_in = to_group(mine_in)
+    got_in = spread(
+        sum_for_groups(
+            trade(lambda k: terms[k], "dp"), group_cluster, clusters, 2, [dy_half, pick]
+        )
+    )
     _, terms_out = project(
         dy_half, chip_rows(own_out, other_out), own_out, other_out, spot, n_dp
     )
-    mine_out = sum_parts(trade(lambda k: terms_out[k], "dp"))
-    got_out = to_group(mine_out)
+    got_out = spread(
+        sum_for_groups(trade(lambda k: terms_out[k], "dp"), group_cluster, clusters, 1, [])
+    )
     h_pieces = trade(lambda k: got_in, "dp")
     hg, hu, hidden, mixed, act, lift = forward(
         h_pieces, pick, gate_factor, up_factor, down_factor, dp
@@ -531,24 +569,18 @@
         summed = jnp.sum(jnp.where(owner, got.astype(FL)[None], 0.0), axis=1)
         return summed.astype(BF).reshape(-1, half)
 
-    in_mine = sum_parts(trade(lambda k: in_chunks[k], "dp"))
-    mixed_chunks = mixed_sums(mixed, pick, weight_of, dp, got_out.shape, n_dp, in_mine)
+    in_got = trade(lambda k: in_chunks[k], "dp")
+    mixed_chunks = mixed_sums(mixed, pick, weight_of, dp, got_out.shape, n_dp, in_got[1])
     mixed_mine = sum_parts(trade(lambda k: mixed_chunks[k], "dp"))
-    got = lax.all_to_all(in_mine, ("ez", "core"), split_axis=0, concat_axis=0, tiled=True)
-    in_sum = after(by_cluster(got, group_cluster), mixed_mine)
+    in_mine = sum_parts(in_got)
+    grad_gate_factor, grad_up_factor, grad_down_factor = factor_grads(
+        hg, grad_gate, hu, grad_up, hidden, back, total, in_mine
+    )
+    mine = jnp.concatenate([in_mine, mixed_mine], axis=1)
+    got = spread(mine)
+    in_sum = after(by_cluster(got[:, : 2 * rank_part], group_cluster), grad_gate_factor)
+    mixed_sum = by_cluster(got[:, 2 * rank_part :], group_cluster)
     in_parts = trade(lambda k: in_sum, "dp")
-
-    mixed_mine = after(mixed_mine, in_parts[-1])
-    got = [lax.dynamic_index_in_dim(mixed_mine, me_e, 0, False)]
-    for k in range(1, n_ex):
-        piece = lax.dynamic_index_in_dim(mixed_mine, me_e ^ k, 0, False)
-        got.append(lax.ppermute(piece, ("ez", "core"), [(i, i ^ k) for i in range(n_ex)]))
-    partners = group_cluster[me_e ^ jnp.arange(n_ex, dtype=jnp.int32)]
-    mixed_sum = by_cluster(jnp.stack(got), partners)
-    mixed_parts = trade(lambda k: mixed_sum, "dp")
-    grad_gate_factor, grad_up_factor, grad_down_factor = factor_grads(
-        hg, grad_gate, hu, grad_up, hidden, back, total, in_parts[-1]
-    )
 
     placed = cell == jnp.arange(slots, dtype=jnp.int32)[None, :, None]
     scores = jnp.sum(jnp.where(placed, dots, 0.0), axis=1).reshape(local, 2, half)
@@ -560,11 +592,10 @@
     scores = jnp.pad(scores, ((0, 0), (0, lanes - 2 * local)))
 
     grad_x = sum(mm("rt,rf->tf", part, rows) for part, rows in zip(in_parts, rows_in))
-    rows = jnp.concatenate([grad_x.astype(BF), scores], axis=1)
-    rows = rows.reshape(n_dp * n_z, tok_rows, width + lanes)
+    leaving = jnp.concatenate([grad_x.astype(BF), scores], axis=1)
+    rows = leaving.reshape(n_dp * n_z, tok_rows, width + lanes)
     rows = lax.all_to_all(rows, ("dp", "ez"), split_axis=0, concat_axis=0, tiled=True)
     rows = rows.reshape(n_dp, n_z, tok_rows, width + lanes)
-
     x_other = core_swap(x_half)
     dy_other = core_swap(dy_half)
     same = core == dp // parts_core
@@ -577,15 +608,16 @@
 
     shape = (clusters, rank_own, width)
     grad_gate_basis, grad_up_basis = basis_grads(
-        *own_ranks(in_parts), x_half, x_other, spot, shape, n_dp
-    )
+        *own_ranks(in_parts), x_half, x_other, spot, shape, n_dp, leaving
+    )
+    mixed_sum = after(mixed_sum, grad_gate_basis)
+    mixed_parts = trade(lambda k: mixed_sum, "dp")
     (grad_down_basis,) = basis_grads(
-        *own_ranks(mixed_parts), dy_half, dy_other, spot, shape, n_dp
+        *own_ranks(mixed_parts), dy_half, dy_other, spot, shape, n_dp, leaving
     )
 
     grad_rows = jnp.sum(rows[..., :width].astype(FL), axis=1)
-    for part in (grad_gate_factor, grad_gate_basis, grad_down_basis):
-        grad_rows = after(grad_rows, part)
+    grad_rows = after(grad_rows, grad_down_basis)
     grad_tokens = grad_rows.astype(BF).transpose(1, 0, 2).reshape(tok_rows, model_width)
     by_expert = jnp.sum(rows[..., width : width + 2 * local].astype(FL), axis=0)
     by_expert = by_expert.transpose(1, 0, 2).reshape(tok_rows, 1, experts)

time: 324 us -> 276 us (0.85)
  starting transfers between devices: 70.8 us -> 51.5 us
  local copies, waits for them, and re-layouts: 38.2 us -> 19.3 us
  waiting for transfers between devices: 93.5 us -> 88.2 us
  other arithmetic: 19 us -> 14.9 us
    ppermute x7 -> x0, waiting for transfers between devices: 29.4 us -> none  [body(): lax.ppermute(piece, ('ez', 'core'), [(i, i ^ k) for i in range(n_ex)])]
    unnamed x97 -> x85, local copies, waits for them, and re-layouts: 21.4 us -> 9.92 us
    ppermute x7 -> x0, starting transfers between devices: 11.4 us -> none  [body(): lax.ppermute(piece, ('ez', 'core'), [(i, i ^ k) for i in range(n_ex)])]
    all_to_all x3, starting transfers between devices: 21 us -> 11.7 us  [spread(): lax.all_to_all(mine, ('ez', 'core'), split_axis=0, concat_axis=0, tiled=T...]
    all_to_all x1, waiting for transfers between devices: 0.01 us -> 7.63 us  [body(): lax.all_to_all(rows, ('dp', 'ez'), split_axis=0, concat_axis=0, tiled=True)]
    all_to_all x3, waiting for transfers between devices: 6.11 us -> 13.2 us  [spread(): lax.all_to_all(mine, ('ez', 'core'), split_axis=0, concat_axis=0, tiled=T...]
    convert_element_type x4 -> x2, other arithmetic: 4.27 us -> 0.32 us  [sum_parts(): return sum((piece.astype(FL) for piece in got)).astype(BF)]
    gather x3 -> x0, local copies, waits for them, and re-layouts: 3.84 us -> none  [the longest x2 2.6 us: to_group(): send = mine.at[group_cluster].get(mode='promise_in_bounds')]
  transfers between devices with their start and end apart: 47 -> 40, of which waited for: 21 -> 23; matrix products, arithmetic and copies ran while one was open for 12% -> 5% of each run, Pallas kernels for 11% -> 14%
where the time goes in v8:
time: 276 us; the launch traced here: 275 us
  waiting for transfers between devices  88.2 us (32%)
  starting transfers between devices  51.5 us (19%)
  Pallas kernels  50.1 us (18%)
  blocking collectives  44.7 us (16%)
  local copies, waits for them, and re-layouts  19.3 us (7%)
  other arithmetic  14.9 us (5%)
  between operations  4.05 us (1%)
    ppermute x24, waiting for transfers between devices, trade(): lax.ppermute(chunk_for(k), axis, [(i, i ^ k) for i in range(n)])  55.1 us
    all_to_all x1, blocking collectives, own_columns(): lax.all_to_all(rows, ('dp', 'ez'), split_axis=0, concat_axis=0, tiled=True)  44.7 us
    ppermute x24, starting transfers between devices, trade(): lax.ppermute(chunk_for(k), axis, [(i, i ^ k) for i in range(n)])  28 us
    all_to_all x3, waiting for transfers between devices, spread(): lax.all_to_all(mine, ('ez', 'core'), split_axis=0, concat_axis=0, tiled=T...  13.2 us
    pallas_call x1, Pallas kernels, backward(): pl.pallas_call(kernel, grid=(local,), out_shape=outs + chunks, in_specs=[...  12.3 us
    all_to_all x3, starting transfers between devices, spread(): lax.all_to_all(mine, ('ez', 'core'), split_axis=0, concat_axis=0, tiled=T...  11.7 us
    unnamed x85, local copies, waits for them, and re-layouts  9.92 us
    pallas_call x2, Pallas kernels, project(): pl.pallas_call(kernel, out_shape=outs, in_specs=[SCALAR] + [whole(x) for...  9.82 us
  transfers between devices with their start and end apart: 40, of which 23 were waited for; matrix products, arithmetic and copies ran while one was open for 5% of the time, Pallas kernels for 14%

profile of v8, /device:TPU:0, one launch (start us, length us, event | category | flops | bytes accessed | tf_op | source)
XLA Modules:
  0.0 275.0 jit_solution(8545644890748708196)
XLA Ops:
  3.7 44.7 %all_to_all.30 = bf16[16,24,1920]{2,1,0:T(8,128)(2,1)S(1)} all-to-all(bf16[16,24,1920]{2,1,0:T(8,128)(2,1)S(1)} %bitcast.64), channel_id=1, replica_groups=mesh['dp'=4,'ez'=4,'core'=2] {'dp','ez'}, dimensions={0} | all-to-all | bytes 2949120 | tf_op jit(solution)/shard_map/all_to_all | solution.py:486
  51.1 3.7 %all-to-all-start.1 = ((bf16[16,24,1792]{2,1,0:T(8,128)(2,1)}), bf16[16,24,1792]{2,1,0:T(8,128)(2,1)S(1)}, u32[]{:S(2)}, u32[]{:S(2)}) async-start(bf16[16,24,1792]{2,1,0:T(8,128)(2,1)} %bitcast.65), calls=%async_computation.1 | async-start | bytes 2752512 | tf_op jit(solution)/shard_map/all_to_all | solution.py:486
  59.1 5.5 %project.3 = (bf16[256,1792]{1,0:T(8,128)(2,1)}, bf16[256,1792]{1,0:T(8,128)(2,1)}, bf16[256,1792]{1,0:T(8,128)(2,1)}, bf16[256,1792]{1,0:T(8,128)(2,1)}, bf16[2...) custom-call(s32[2]{0:T(128)} %pad_add_fusion.spot_ref, ...), custom_call_target="tpu_custom_call" | custom-call | tf_op jit(solution)/shard_map/project/pallas_call | solution.py:112
  75.4 5.4 %collective-permute-done.12.refs_3_ = bf16[256,384]{1,0:T(8,128)(2,1)S(1)} collective-permute-done((bf16[256,384]{1,0:T(8,128)(2,1)}, bf16[256,384]{1,0:T(8,128)(2,1)S(1)}, u32[]{:S(2)}, u32[]{:S(2)}) %collective-permute-start.12) | collective-permute-done | bytes 196640 | tf_op jit(solution)/shard_map/ppermute | solution.py:46
  80.8 7.7 %all-to-all-done.1 = bf16[16,24,1792]{2,1,0:T(8,128)(2,1)S(1)} async-done(((bf16[16,24,1792]{2,1,0:T(8,128)(2,1)}), bf16[16,24,1792]{2,1,0:T(8,128)(2,1)S(1)}, u32[]{:S(2)}, u32[]{:S(2)}) %all-to-all-start.1) | async-done | bytes 1376288 | tf_op jit(solution)/shard_map/all_to_all | solution.py:486
  93.4 4.3 %project.2 = (bf16[128,1792]{1,0:T(8,128)(2,1)}, bf16[128,1792]{1,0:T(8,128)(2,1)}, bf16[128,1792]{1,0:T(8,128)(2,1)}, bf16[128,1792]{1,0:T(8,128)(2,1)}, bf16[1...) custom-call(s32[2]{0:T(128)} %pad_add_fusion.spot_ref, ...), custom_call_target="tpu_custom_call" | custom-call | tf_op jit(solution)/shard_map/project/pallas_call | solution.py:112
  101.2 4.6 %all-to-all-done.3.refs_0_ = bf16[8,64,384]{2,1,0:T(8,128)(2,1)S(1)} async-done(((bf16[8,64,384]{2,1,0:T(8,128)(2,1)}), bf16[8,64,384]{2,1,0:T(8,128)(2,1)S(1)}, u32[]{:S(2)}, u32[]{:S(2)}) %all-to-all-start.3) | async-done | bytes 393248 | tf_op jit(solution)/shard_map/all_to_all | solution.py:540
  108.2 3.9 %all-to-all-start.2 = ((bf16[8,32,384]{2,1,0:T(8,128)(2,1)}), bf16[8,32,384]{2,1,0:T(8,128)(2,1)S(1)}, u32[]{:S(2)}, u32[]{:S(2)}) async-start(bf16[8,32,384]{2,1,0:T(8,128)(2,1)} %sum_for_groups.2), calls=%async_computation.2 | async-start | bytes 393216 | tf_op jit(solution)/shard_map/all_to_all | solution.py:540
  115.3 5.1 %all-to-all-done.2.refs_0_ = bf16[8,32,384]{2,1,0:T(8,128)(2,1)S(1)} async-done(((bf16[8,32,384]{2,1,0:T(8,128)(2,1)}), bf16[8,32,384]{2,1,0:T(8,128)(2,1)S(1)}, u32[]{:S(2)}, u32[]{:S(2)}) %all-to-all-start.2) | async-done | bytes 196640 | tf_op jit(solution)/shard_map/all_to_all | solution.py:540
  123.9 12.7 %collective-permute-done.14.refs_2_ = bf16[8,64,384]{2,1,0:T(8,128)(2,1)S(1)} collective-permute-done((bf16[8,64,384]{2,1,0:T(8,128)(2,1)S(1)}, bf16[8,64,384]{2,1,0:T(8,128)(2,1)S(1)}, u32[]{:S(2)}, u32[]{:S(2)}) %collective-permute-start.14) | collective-permute-done | bytes 393248 | tf_op jit(solution)/shard_map/ppermute | solution.py:46
  138.1 8.9 %forward.1 = (bf16[4,224,512]{2,1,0:T(8,128)(2,1)}, bf16[4,224,512]{2,1,0:T(8,128)(2,1)}, bf16[4,224,512]{2,1,0:T(8,128)(2,1)}, bf16[4,224,512]{2,1,0:T(8,128)(2...) custom-call(s32[1]{0:T(128)} %bitcast.dp_ref, bf16[8,64,384]{2,1,0:T(8,128)(2,1)} %copy-done.17, ...), custom_call_target="tpu_custom_call" | custom-call | tf_op jit(solution)/shard_map/forward/pallas_call | solution.py:302
  147.9 12.3 %backward.1 = (bf16[4,224,512]{2,1,0:T(8,128)(2,1)}, bf16[4,224,512]{2,1,0:T(8,128)(2,1)}, bf16[4,224,512]{2,1,0:T(8,128)(2,1)}, f32[4,224,1]{2,1,0:T(8,128)}, b...) custom-call(s32[1]{0:T(128)} %bitcast.dp_ref, ...), custom_call_target="tpu_custom_call" | custom-call | flops 3523215360 | bytes 33554432 | tf_op jit(solution)/shard_map/backward/pallas_call | solution.py:363
  163.7 8.8 %collective-permute-done.16.refs_0_ = bf16[8,64,384]{2,1,0:T(8,128)(2,1)S(1)} collective-permute-done((bf16[8,64,384]{2,1,0:T(8,128)(2,1)}, bf16[8,64,384]{2,1,0:T(8,128)(2,1)S(1)}, u32[]{:S(2)}, u32[]{:S(2)}) %collective-permute-start.16) | collective-permute-done | bytes 393248 | tf_op jit(solution)/shard_map/ppermute | solution.py:46
  178.4 3.6 %collective-permute-done.18 = bf16[8,64,384]{2,1,0:T(8,128)(2,1)S(1)} collective-permute-done((bf16[8,64,384]{2,1,0:T(8,128)(2,1)}, bf16[8,64,384]{2,1,0:T(8,128)(2,1)S(1)}, u32[]{:S(2)}, u32[]{:S(2)}) %collective-permute-start.18) | collective-permute-done | bytes 393248 | tf_op jit(solution)/shard_map/ppermute | solution.py:46
  181.9 5.2 %collective-permute-done.17 = bf16[8,64,384]{2,1,0:T(8,128)(2,1)S(1)} collective-permute-done((bf16[8,64,384]{2,1,0:T(8,128)(2,1)}, bf16[8,64,384]{2,1,0:T(8,128)(2,1)S(1)}, u32[]{:S(2)}, u32[]{:S(2)}) %collective-permute-start.17) | collective-permute-done | bytes 393248 | tf_op jit(solution)/shard_map/ppermute | solution.py:46
  191.0 4.3 %all-to-all-start.4 = ((bf16[8,96,384]{2,1,0:T(8,128)(2,1)}), bf16[8,96,384]{2,1,0:T(8,128)(2,1)}, u32[]{:S(2)}, u32[]{:S(2)}) async-start(bf16[8,96,384]{2,1,0:T(8,128)(2,1)} %pad_maximum_fusion), calls=%async_computation.4 | async-start | bytes 1179648 | tf_op jit(solution)/shard_map/all_to_all | solution.py:540
  201.5 5.2 %factor_grads.1 = (f32[4,512,512]{2,1,0:T(8,128)}, f32[4,512,512]{2,1,0:T(8,128)}, f32[4,512,512]{2,1,0:T(8,128)}) custom-call(bf16[4,224,512]{2,1,0:T(8,128)(2,1)S(1)} %copy-done.7, bf16[4,224,512]{2,1,0:T(8,128)(2,1)S(1)} %copy-done.11, bf16[4,224,512]{2,1,0:T(8,128)(2,1)S(1)} %copy-done.8, bf16[4,224,512]{2,1,0:T(8,128)(2,1)S(1)} %copy-done.12, ...), custom_call_target="tpu_custom_call" | custom-call | tf_op jit(solution)/shard_map/factor_grads/pallas_call | solution.py:432
  208.7 3.5 %all-to-all-done.4 = bf16[8,96,384]{2,1,0:T(8,128)(2,1)} async-done(((bf16[8,96,384]{2,1,0:T(8,128)(2,1)}), bf16[8,96,384]{2,1,0:T(8,128)(2,1)}, u32[]{:S(2)}, u32[]{:S(2)}) %all-to-all-start.4) | async-done | bytes 589856 | tf_op jit(solution)/shard_map/all_to_all | solution.py:540
  217.5 5.0 %collective-permute-done.24 = bf16[256,384]{1,0:T(8,128)(2,1)S(1)} collective-permute-done((bf16[256,384]{1,0:T(8,128)(2,1)S(1)}, bf16[256,384]{1,0:T(8,128)(2,1)S(1)}, u32[]{:S(2)}, u32[]{:S(2)}) %collective-permute-start.24) | collective-permute-done | bytes 196640 | tf_op jit(solution)/shard_map/ppermute | solution.py:46
  228.9 4.9 %all-to-all-start.5 = ((bf16[16,24,1920]{2,1,0:T(8,128)(2,1)}), bf16[16,24,1920]{2,1,0:T(8,128)(2,1)}, u32[]{:S(2)}, u32[]{:S(2)}) async-start(bf16[16,24,1920]{2,1,0:T(8,128)(2,1)} %bitcast.19), calls=%async_computation.5 | async-start | bytes 2949120 | tf_op jit(solution)/shard_map/all_to_all | solution.py:597
  238.3 4.6 %basis_grads.2 = (f32[256,1792]{1,0:T(8,128)}, f32[256,1792]{1,0:T(8,128)}) custom-call(s32[2]{0:T(128)S(1)} %copy-done.16, bf16[256,384]{1,0:T(8,128)(2,1)S(1)} %get-tuple-element.103.refs_0_, bf16[256,384]{1,0:T(8,128)(2,1)S(1)} %get-tuple-element.101.refs_1_, bf16[256,384]{1,0:T(8,128)(2,1)S(1)} %collective-permute-done.26.refs_2_, ...), custom_call_target="tpu_custom_call" | custom-call | tf_op jit(solution)/shard_map/basis_grads/pallas_call | solution.py:188
  248.4 6.5 %collective-permute-done.29 = bf16[128,384]{1,0:T(8,128)(2,1)S(1)} collective-permute-done((bf16[128,384]{1,0:T(8,128)(2,1)S(1)}, bf16[128,384]{1,0:T(8,128)(2,1)S(1)}, u32[]{:S(2)}, u32[]{:S(2)}) %collective-permute-start.29) | collective-permute-done | bytes 98336 | tf_op jit(solution)/shard_map/ppermute | solution.py:46
  257.7 3.5 %basis_grads.3 = f32[256,1792]{1,0:T(8,128)} custom-call(s32[2]{0:T(128)S(1)} %copy-done.16, bf16[128,384]{1,0:T(8,128)(2,1)S(1)} %get-tuple-element.107.refs_0_, bf16[128,384]{1,0:T(8,128)(2,1)S(1)} %get-tuple-element.105.refs_1_, bf16[128,384]{1,0:T(8,128)(2,1)S(1)} %collective-permute-done.32.refs_2_, ...), custom_call_target="tpu_custom_call" | custom-call | tf_op jit(solution)/shard_map/basis_grads/pallas_call | solution.py:188
  263.0 7.6 %all-to-all-done.5 = bf16[16,24,1920]{2,1,0:T(8,128)(2,1)} async-done(((bf16[16,24,1920]{2,1,0:T(8,128)(2,1)}), bf16[16,24,1920]{2,1,0:T(8,128)(2,1)}, u32[]{:S(2)}, u32[]{:S(2)}) %all-to-all-start.5) | async-done | bytes 1474592 | tf_op jit(solution)/shard_map/all_to_all | solution.py:597
  (229 shorter events, 89.3 us)
Async XLA Ops:
  51.1 37.4 %all-to-all-start.1 = ((bf16[16,24,1792]{2,1,0:T(8,128)(2,1)}), bf16[16,24,1792]{2,1,0:T(8,128)(2,1)S(1)}, u32[]{:S(2)}, u32[]{:S(2)}) async-start(bf16[16,24,1792]{2,1,0:T(8,128)(2,1)} %bitcast.65), calls=%async_computation.1 | async-start | bytes 2752512 | tf_op jit(solution)/shard_map/all_to_all | solution.py:486
  55.4 38.0 %collective-permute-start = (bf16[4,64,1792]{2,1,0:T(8,128)(2,1)}, bf16[4,64,1792]{2,1,0:T(8,128)(2,1)}, u32[]{:S(2)}, u32[]{:S(2)}) collective-permute-start(bf16[4,64,1792]{2,1,0:T(8,128)(2,1)} %refs_0_.2), channel_id=1, source_target_pairs={{0,1},{1,0},{2,3},{3,2},{4,5},{5,4},{6,7},{7,6},{8,9},{9,8},{10,11... | collective-permute-start | bytes 2752520 | tf_op jit(solution)/shard_map/ppermute | solution.py:30
  55.9 12.3 %collective-permute-start.7 = (bf16[384,128]{1,0:T(8,128)(2,1)S(1)}, bf16[384,128]{1,0:T(8,128)(2,1)S(1)}, u32[]{:S(2)}, u32[]{:S(2)}) collective-permute-start(bf16[384,128]{1,0:T(8,128)(2,1)S(1)} %slice.59), channel_id=1, source_target_pairs={{0,1},{1,0},{2,3},{3,2},{4,5},{5,4},{6,7},{7,6},{8,9},{9,8},{10,11... | collective-permute-start | bytes 294920 | tf_op jit(solution)/shard_map/ppermute | solution.py:30
  64.7 10.7 %collective-permute-start.10 = (bf16[256,384]{1,0:T(8,128)(2,1)}, bf16[256,384]{1,0:T(8,128)(2,1)S(1)}, u32[]{:S(2)}, u32[]{:S(2)}) collective-permute-start(bf16[256,384]{1,0:T(8,128)(2,1)} %get-tuple-element.52), channel_id=1, source_target_pairs={{0,8},{8,0},{16,24},{24,16},{1,9},{9,1},{17,25},{25,17},{2,10},{10... | collective-permute-start | bytes 589832 | tf_op jit(solution)/shard_map/ppermute | solution.py:46
  67.9 12.8 %collective-permute-start.12 = (bf16[256,384]{1,0:T(8,128)(2,1)}, bf16[256,384]{1,0:T(8,128)(2,1)S(1)}, u32[]{:S(2)}, u32[]{:S(2)}) collective-permute-start(bf16[256,384]{1,0:T(8,128)(2,1)} %get-tuple-element.54), channel_id=1, source_target_pairs={{0,24},{8,16},{16,8},{24,0},{1,25},{9,17},{17,9},{25,1},{2,26},{10... | collective-permute-start | bytes 589832 | tf_op jit(solution)/shard_map/ppermute | solution.py:46
  89.9 15.9 %all-to-all-start.3 = ((bf16[8,64,384]{2,1,0:T(8,128)(2,1)}), bf16[8,64,384]{2,1,0:T(8,128)(2,1)S(1)}, u32[]{:S(2)}, u32[]{:S(2)}) async-start(bf16[8,64,384]{2,1,0:T(8,128)(2,1)} %sum_for_groups.3), calls=%async_computation.3 | async-start | bytes 786432 | tf_op jit(solution)/shard_map/all_to_all | solution.py:540
  105.9 17.2 %collective-permute-start.13 = (bf16[8,64,384]{2,1,0:T(8,128)(2,1)S(1)}, bf16[8,64,384]{2,1,0:T(8,128)(2,1)S(1)}, u32[]{:S(2)}, u32[]{:S(2)}) collective-permute-start(bf16[8,64,384]{2,1,0:T(8,128)(2,1)S(1)} %all-to-all-done.3.refs_0_), channel_id=1, source_target_pairs={{0,8},{8,0},{16,24},{24,16},{1,9},{9,1},{17,25},{25,17},{2,10},{10... | collective-permute-start | bytes 1179656 | tf_op jit(solution)/shard_map/ppermute | solution.py:46
  108.2 12.2 %all-to-all-start.2 = ((bf16[8,32,384]{2,1,0:T(8,128)(2,1)}), bf16[8,32,384]{2,1,0:T(8,128)(2,1)S(1)}, u32[]{:S(2)}, u32[]{:S(2)}) async-start(bf16[8,32,384]{2,1,0:T(8,128)(2,1)} %sum_for_groups.2), calls=%async_computation.2 | async-start | bytes 393216 | tf_op jit(solution)/shard_map/all_to_all | solution.py:540
  112.1 24.5 %collective-permute-start.14 = (bf16[8,64,384]{2,1,0:T(8,128)(2,1)S(1)}, bf16[8,64,384]{2,1,0:T(8,128)(2,1)S(1)}, u32[]{:S(2)}, u32[]{:S(2)}) collective-permute-start(bf16[8,64,384]{2,1,0:T(8,128)(2,1)S(1)} %all-to-all-done.3.refs_0_), channel_id=1, source_target_pairs={{0,16},{8,24},{16,0},{24,8},{1,17},{9,25},{17,1},{25,9},{2,18},{10... | collective-permute-start | bytes 1179656 | tf_op jit(solution)/shard_map/ppermute | solution.py:46
  113.5 23.1 %collective-permute-start.15 = (bf16[8,64,384]{2,1,0:T(8,128)(2,1)S(1)}, bf16[8,64,384]{2,1,0:T(8,128)(2,1)S(1)}, u32[]{:S(2)}, u32[]{:S(2)}) collective-permute-start(bf16[8,64,384]{2,1,0:T(8,128)(2,1)S(1)} %all-to-all-done.3.refs_0_), channel_id=1, source_target_pairs={{0,24},{8,16},{16,8},{24,0},{1,25},{9,17},{17,9},{25,1},{2,26},{10... | collective-permute-start | bytes 1179656 | tf_op jit(solution)/shard_map/ppermute | solution.py:46
  120.4 26.6 %collective-permute-start.4 = (bf16[8,32,384]{2,1,0:T(8,128)(2,1)S(1)}, bf16[8,32,384]{2,1,0:T(8,128)(2,1)S(1)}, u32[]{:S(2)}, u32[]{:S(2)}) collective-permute-start(bf16[8,32,384]{2,1,0:T(8,128)(2,1)S(1)} %all-to-all-done.2.refs_0_), channel_id=1, source_target_pairs={{0,8},{8,0},{16,24},{24,16},{1,9},{9,1},{17,25},{25,17},{2,10},{10... | collective-permute-start | bytes 589832 | tf_op jit(solution)/shard_map/ppermute | solution.py:46
  122.2 24.8 %collective-permute-start.5 = (bf16[8,32,384]{2,1,0:T(8,128)(2,1)S(1)}, bf16[8,32,384]{2,1,0:T(8,128)(2,1)S(1)}, u32[]{:S(2)}, u32[]{:S(2)}) collective-permute-start(bf16[8,32,384]{2,1,0:T(8,128)(2,1)S(1)} %all-to-all-done.2.refs_0_), channel_id=1, source_target_pairs={{0,16},{8,24},{16,0},{24,8},{1,17},{9,25},{17,1},{25,9},{2,18},{10... | collective-permute-start | bytes 589832 | tf_op jit(solution)/shard_map/ppermute | solution.py:46
  123.1 23.9 %collective-permute-start.6 = (bf16[8,32,384]{2,1,0:T(8,128)(2,1)S(1)}, bf16[8,32,384]{2,1,0:T(8,128)(2,1)S(1)}, u32[]{:S(2)}, u32[]{:S(2)}) collective-permute-start(bf16[8,32,384]{2,1,0:T(8,128)(2,1)S(1)} %all-to-all-done.2.refs_0_), channel_id=1, source_target_pairs={{0,24},{8,16},{16,8},{24,0},{1,25},{9,17},{17,9},{25,1},{2,26},{10... | collective-permute-start | bytes 589832 | tf_op jit(solution)/shard_map/ppermute | solution.py:46
  160.2 12.3 %collective-permute-start.16 = (bf16[8,64,384]{2,1,0:T(8,128)(2,1)}, bf16[8,64,384]{2,1,0:T(8,128)(2,1)S(1)}, u32[]{:S(2)}, u32[]{:S(2)}) collective-permute-start(bf16[8,64,384]{2,1,0:T(8,128)(2,1)} %get-tuple-element.59), channel_id=1, source_target_pairs={{0,8},{8,0},{16,24},{24,16},{1,9},{9,1},{17,25},{25,17},{2,10},{10... | collective-permute-start | bytes 1179656 | tf_op jit(solution)/shard_map/ppermute | solution.py:46
  162.1 19.9 %collective-permute-start.18 = (bf16[8,64,384]{2,1,0:T(8,128)(2,1)}, bf16[8,64,384]{2,1,0:T(8,128)(2,1)S(1)}, u32[]{:S(2)}, u32[]{:S(2)}) collective-permute-start(bf16[8,64,384]{2,1,0:T(8,128)(2,1)} %get-tuple-element.61), channel_id=1, source_target_pairs={{0,24},{8,16},{16,8},{24,0},{1,25},{9,17},{17,9},{25,1},{2,26},{10... | collective-permute-start | bytes 1179656 | tf_op jit(solution)/shard_map/ppermute | solution.py:46
  163.2 23.9 %collective-permute-start.17 = (bf16[8,64,384]{2,1,0:T(8,128)(2,1)}, bf16[8,64,384]{2,1,0:T(8,128)(2,1)S(1)}, u32[]{:S(2)}, u32[]{:S(2)}) collective-permute-start(bf16[8,64,384]{2,1,0:T(8,128)(2,1)} %get-tuple-element.60), channel_id=1, source_target_pairs={{0,16},{8,24},{16,0},{24,8},{1,17},{9,25},{17,1},{25,9},{2,18},{10... | collective-permute-start | bytes 1179656 | tf_op jit(solution)/shard_map/ppermute | solution.py:46
  174.8 12.6 %collective-permute-start.21 = (bf16[8,32,384]{2,1,0:T(8,128)(2,1)S(1)}, bf16[8,32,384]{2,1,0:T(8,128)(2,1)S(1)}, u32[]{:S(2)}, u32[]{:S(2)}) collective-permute-start(bf16[8,32,384]{2,1,0:T(8,128)(2,1)S(1)} %get-tuple-element.65), channel_id=1, source_target_pairs={{0,24},{8,16},{16,8},{24,0},{1,25},{9,17},{17,9},{25,1},{2,26},{10... | collective-permute-start | bytes 589832 | tf_op jit(solution)/shard_map/ppermute | solution.py:46
  177.0 13.1 %collective-permute-start.20 = (bf16[8,32,384]{2,1,0:T(8,128)(2,1)S(1)}, bf16[8,32,384]{2,1,0:T(8,128)(2,1)S(1)}, u32[]{:S(2)}, u32[]{:S(2)}) collective-permute-start(bf16[8,32,384]{2,1,0:T(8,128)(2,1)S(1)} %get-tuple-element.64), channel_id=1, source_target_pairs={{0,16},{8,24},{16,0},{24,8},{1,17},{9,25},{17,1},{25,9},{2,18},{10... | collective-permute-start | bytes 589832 | tf_op jit(solution)/shard_map/ppermute | solution.py:46
  178.1 11.9 %collective-permute-start.19 = (bf16[8,32,384]{2,1,0:T(8,128)(2,1)S(1)}, bf16[8,32,384]{2,1,0:T(8,128)(2,1)S(1)}, u32[]{:S(2)}, u32[]{:S(2)}) collective-permute-start(bf16[8,32,384]{2,1,0:T(8,128)(2,1)S(1)} %get-tuple-element.63), channel_id=1, source_target_pairs={{0,8},{8,0},{16,24},{24,16},{1,9},{9,1},{17,25},{25,17},{2,10},{10... | collective-permute-start | bytes 589832 | tf_op jit(solution)/shard_map/ppermute | solution.py:46
  191.0 21.2 %all-to-all-start.4 = ((bf16[8,96,384]{2,1,0:T(8,128)(2,1)}), bf16[8,96,384]{2,1,0:T(8,128)(2,1)}, u32[]{:S(2)}, u32[]{:S(2)}) async-start(bf16[8,96,384]{2,1,0:T(8,128)(2,1)} %pad_maximum_fusion), calls=%async_computation.4 | async-start | bytes 1179648 | tf_op jit(solution)/shard_map/all_to_all | solution.py:540
  197.4 18.2 %collective-permute-start.25 = (bf16[4,384]{1,0:T(4,128)(2,1)S(1)}, bf16[4,384]{1,0:T(4,128)(2,1)S(1)}, u32[]{:S(2)}, u32[]{:S(2)}) collective-permute-start(bf16[4,384]{1,0:T(4,128)(2,1)S(1)} %select_bitcast_fusion.2), channel_id=1, source_target_pairs={{0,1},{1,0},{2,3},{3,2},{4,5},{5,4},{6,7},{7,6},{8,9},{9,8},{10,11... | collective-permute-start | bytes 9224 | tf_op jit(solution)/shard_map/ppermute | solution.py:30
  228.9 41.7 %all-to-all-start.5 = ((bf16[16,24,1920]{2,1,0:T(8,128)(2,1)}), bf16[16,24,1920]{2,1,0:T(8,128)(2,1)}, u32[]{:S(2)}, u32[]{:S(2)}) async-start(bf16[16,24,1920]{2,1,0:T(8,128)(2,1)} %bitcast.19), calls=%async_computation.5 | async-start | bytes 2949120 | tf_op jit(solution)/shard_map/all_to_all | solution.py:597
  233.9 22.5 %collective-permute-start.34 = (bf16[384,1792]{1,0:T(8,128)(2,1)S(1)}, bf16[384,1792]{1,0:T(8,128)(2,1)}, u32[]{:S(2)}, u32[]{:S(2)}) collective-permute-start(bf16[384,1792]{1,0:T(8,128)(2,1)S(1)} %bitcast.56), channel_id=1, source_target_pairs={{0,1},{1,0},{2,3},{3,2},{4,5},{5,4},{6,7},{7,6},{8,9},{9,8},{10,11... | collective-permute-start | bytes 4128776 | tf_op jit(solution)/shard_map/ppermute | solution.py:30
  244.8 10.1 %collective-permute-start.29 = (bf16[128,384]{1,0:T(8,128)(2,1)S(1)}, bf16[128,384]{1,0:T(8,128)(2,1)S(1)}, u32[]{:S(2)}, u32[]{:S(2)}) collective-permute-start(bf16[128,384]{1,0:T(8,128)(2,1)S(1)} %bitcast.76), channel_id=1, source_target_pairs={{0,16},{8,24},{16,0},{24,8},{1,17},{9,25},{17,1},{25,9},{2,18},{10... | collective-permute-start | bytes 294920 | tf_op jit(solution)/shard_map/ppermute | solution.py:46
  (56 other events, 496.8 us)

commit v9 on v5

--- a/solution.py
+++ b/solution.py
@@ -119,6 +119,37 @@
         name="project",
     )(spot, *ins)
     return (got[:n_dp] if built else rows), got[-n_dp:]
+
+
+def sum_for_groups(pieces, groups, clusters, count, firsts):
+    rows, half = pieces[0].shape
+    part = rows // (clusters * count)
+    n_ex = groups.shape[0]
+
+    def kernel(groups_ref, *refs):
+        got, out_ref, sum_ref = refs[: len(pieces)], refs[-2], refs[-1]
+        for b in range(count):
+            for c in range(clusters):
+                take = slice((c * count + b) * part, (c * count + b + 1) * part)
+                total = got[0][take, :].astype(FL)
+                for piece in got[1:]:
+                    total += piece[take, :].astype(FL)
+                sum_ref[c, b] = total.astype(BF)
+        for e in range(n_ex):
+            for b in range(count):
+                out_ref[e, b * part : (b + 1) * part, :] = sum_ref[groups_ref[e], b]
+
+    out = shaped((n_ex, count * part, half), BF)
+    return pl.pallas_call(
+        kernel,
+        out_shape=out,
+        in_specs=[SCALAR] + [whole(x) for x in pieces] + [ANYWHERE] * len(firsts),
+        out_specs=whole(out),
+        scratch_shapes=[pltpu.VMEM((clusters, count, part, half), BF)],
+        compiler_params=params(2 * half),
+        cost_estimate=FREE,
+        name="sum_for_groups",
+    )(groups, *pieces, *firsts)
 
 
 def basis_grads(keep, other, cols, other_cols, spot, shape, n_dp, first):
@@ -480,24 +511,26 @@
     def sum_parts(got):
         return sum(piece.astype(FL) for piece in got).astype(BF)
 
-    def to_group(mine):
-        mine = mine.reshape(clusters, -1, half)
-        send = mine.at[group_cluster].get(mode="promise_in_bounds")
-        return lax.all_to_all(send, ("ez", "core"), split_axis=0, concat_axis=0, tiled=True)
+    def spread(mine):
+        return lax.all_to_all(mine, ("ez", "core"), split_axis=0, concat_axis=0, tiled=True)
 
     rows_in, terms = project(
         x_half, chip_rows(own_in, other_in), own_in, other_in, spot, n_dp
     )
-    mine_in = sum_parts(trade(lambda k: terms[k], "dp"))
-    got_in = to_group(mine_in)
+    got_in = spread(
+        sum_for_groups(
+            trade(lambda k: terms[k], "dp"), group_cluster, clusters, 2, [dy_half, pick]
+        )
+    )
     _, terms_out = project(
         dy_half, chip_rows(own_out, other_out), own_out, other_out, spot, n_dp
     )
-    mine_out = sum_parts(trade(lambda k: terms_out[k], "dp"))
     h_pieces = trade(lambda k: got_in, "dp")
-    for piece in h_pieces[1:]:
-        mine_out = after(mine_out, piece)
-    got_out = to_group(mine_out)
+    got_out = spread(
+        sum_for_groups(
+            trade(lambda k: terms_out[k], "dp"), group_cluster, clusters, 1, h_pieces[1:]
+        )
+    )
     (hg, hu, hidden, mixed, act, lift), mixed_chunks = forward(
         h_pieces, pick, weight_of, gate_factor, up_factor, down_factor, dp
     )
@@ -519,7 +552,7 @@
         hg, grad_gate, hu, grad_up, hidden, back, total, in_mine
     )
     mine = jnp.concatenate([in_mine, mixed_mine], axis=1)
-    got = lax.all_to_all(mine, ("ez", "core"), split_axis=0, concat_axis=0, tiled=True)
+    got = spread(mine)
     in_sum = after(by_cluster(got[:, : 2 * rank_part], group_cluster), grad_gate_factor)
     mixed_sum = by_cluster(got[:, 2 * rank_part :], group_cluster)
     in_parts = trade(lambda k: in_sum, "dp")

time: 292 us -> 284 us (0.973)
  blocking collectives: 0 us -> 70.7 us
  waiting for transfers between devices: 122 us -> 56.6 us
  starting transfers between devices: 61 us -> 46.5 us
    all_to_all x0 -> x3, blocking collectives: none -> 70.7 us  [the longest x1 44.7 us: own_columns(): lax.all_to_all(rows, ('dp', 'ez'), split_axis=0, concat_axis=0, tiled=True)]
    all_to_all x2 -> x1, waiting for transfers between devices: 57.9 us -> 2.44 us  [own_columns(): lax.all_to_all(rows, ('dp', 'ez'), split_axis=0, concat_axis=0, tiled=True)]
    all_to_all x3 -> x1, waiting for transfers between devices: 20.7 us -> 1.2 us  [spread(): lax.all_to_all(mine, ('ez', 'core'), split_axis=0, concat_axis=0, tiled=T...]
    ppermute x24, waiting for transfers between devices: 30.9 us -> 40.8 us  [trade(): lax.ppermute(chunk_for(k), axis, [(i, i ^ k) for i in range(n)])]
    all_to_all x2 -> x1, starting transfers between devices: 12 us -> 3.7 us  [own_columns(): lax.all_to_all(rows, ('dp', 'ez'), split_axis=0, concat_axis=0, tiled=True)]
    all_to_all x3 -> x1, starting transfers between devices: 11.2 us -> 3.97 us  [spread(): lax.all_to_all(mine, ('ez', 'core'), split_axis=0, concat_axis=0, tiled=T...]
    slice x7 -> x4, local copies, waits for them, and re-layouts: 8.33 us -> 4.13 us  [after(): lax.slice(first, (0,) * first.ndim, (1,) * first.ndim).reshape(())]
    unnamed x85 -> x83, local copies, waits for them, and re-layouts: 14.1 us -> 16.9 us
  transfers between devices with their start and end apart: 41 -> 38, of which waited for: 20 -> 17; matrix products, arithmetic and copies ran while one was open for 8% -> 10% of each run, Pallas kernels for 14% -> 17%
where the time goes in v9:
time: 284 us; the launch traced here: 283 us
  blocking collectives  70.7 us (25%)
  waiting for transfers between devices  56.6 us (20%)
  Pallas kernels  48.7 us (17%)
  starting transfers between devices  46.5 us (16%)
  local copies, waits for them, and re-layouts  30.6 us (11%)
  other arithmetic  19.8 us (7%)
  matrix products  5.68 us (2%)
  between operations  3.94 us (1%)
    all_to_all x1, blocking collectives, own_columns(): lax.all_to_all(rows, ('dp', 'ez'), split_axis=0, concat_axis=0, tiled=True)  44.7 us
    ppermute x24, waiting for transfers between devices, trade(): lax.ppermute(chunk_for(k), axis, [(i, i ^ k) for i in range(n)])  40.8 us
    ppermute x24, starting transfers between devices, trade(): lax.ppermute(chunk_for(k), axis, [(i, i ^ k) for i in range(n)])  29.9 us
    all_to_all x2, blocking collectives, spread(): lax.all_to_all(mine, ('ez', 'core'), split_axis=0, concat_axis=0, tiled=T...  26 us
    unnamed x83, local copies, waits for them, and re-layouts  16.9 us
    pallas_call x1, Pallas kernels, backward(): pl.pallas_call(kernel, grid=(local,), out_shape=outs + chunks, in_specs=[...  12.2 us
    pallas_call x1, Pallas kernels, forward(): pl.pallas_call(kernel, grid=(local,), out_shape=outs + chunks, in_specs=[...  10.9 us
    pallas_call x2, Pallas kernels, project(): pl.pallas_call(kernel, out_shape=outs, in_specs=[SCALAR] + [whole(x) for...  9.82 us
  transfers between devices with their start and end apart: 38, of which 17 were waited for; matrix products, arithmetic and copies ran while one was open for 10% of the time, Pallas kernels for 17%

profile of v9, /device:TPU:0, one launch (start us, length us, event | category | flops | bytes accessed | tf_op | source)
XLA Modules:
  0.0 282.5 jit_solution(7317930963768109889)
XLA Ops:
  3.7 44.7 %all_to_all.30 = bf16[16,24,1920]{2,1,0:T(8,128)(2,1)S(1)} all-to-all(bf16[16,24,1920]{2,1,0:T(8,128)(2,1)S(1)} %bitcast.64), channel_id=1, replica_groups=mesh['dp'=4,'ez'=4,'core'=2] {'dp','ez'}, dimensions={0} | all-to-all | bytes 2949120 | tf_op jit(solution)/shard_map/all_to_all | solution.py:461
  51.1 3.7 %all-to-all-start.1 = ((bf16[16,24,1792]{2,1,0:T(8,128)(2,1)}), bf16[16,24,1792]{2,1,0:T(8,128)(2,1)S(1)}, u32[]{:S(2)}, u32[]{:S(2)}) async-start(bf16[16,24,1792]{2,1,0:T(8,128)(2,1)} %bitcast.65), calls=%async_computation.1 | async-start | bytes 2752512 | tf_op jit(solution)/shard_map/all_to_all | solution.py:461
  59.1 5.5 %project.3 = (bf16[256,1792]{1,0:T(8,128)(2,1)}, bf16[256,1792]{1,0:T(8,128)(2,1)}, bf16[256,1792]{1,0:T(8,128)(2,1)}, bf16[256,1792]{1,0:T(8,128)(2,1)}, bf16[2...) custom-call(s32[2]{0:T(128)} %pad_add_fusion.spot_ref, ...), custom_call_target="tpu_custom_call" | custom-call | tf_op jit(solution)/shard_map/project/pallas_call | solution.py:112
  86.0 2.4 all-to-all-done.1
  91.4 14.9 %all_to_all.31.refs_0_ = bf16[8,64,384]{2,1,0:T(8,128)(2,1)S(1)} all-to-all(bf16[8,64,384]{2,1,0:T(8,128)(2,1)S(1)} %sum_for_groups.2), channel_id=1, replica_groups=mesh['dp'=4,'ez'=4,'core'=2] {'ez','core'}, dimensions={0} | all-to-all | bytes 786432 | tf_op jit(solution)/shard_map/all_to_all | solution.py:515
  109.9 4.3 %project.2 = (bf16[128,1792]{1,0:T(8,128)(2,1)}, bf16[128,1792]{1,0:T(8,128)(2,1)}, bf16[128,1792]{1,0:T(8,128)(2,1)}, bf16[128,1792]{1,0:T(8,128)(2,1)}, bf16[1...) custom-call(s32[2]{0:T(128)} %pad_add_fusion.spot_ref, ...), custom_call_target="tpu_custom_call" | custom-call | tf_op jit(solution)/shard_map/project/pallas_call | solution.py:112
  117.1 10.6 %collective-permute-done.1.refs_1_ = bf16[128,384]{1,0:T(8,128)(2,1)S(1)} collective-permute-done((bf16[128,384]{1,0:T(8,128)(2,1)}, bf16[128,384]{1,0:T(8,128)(2,1)S(1)}, u32[]{:S(2)}, u32[]{:S(2)}) %collective-permute-start.1) | collective-permute-done | bytes 98336 | tf_op jit(solution)/shard_map/ppermute | solution.py:46
  129.9 3.4 %collective-permute-done.3.refs_3_ = bf16[128,384]{1,0:T(8,128)(2,1)S(1)} collective-permute-done((bf16[128,384]{1,0:T(8,128)(2,1)}, bf16[128,384]{1,0:T(8,128)(2,1)S(1)}, u32[]{:S(2)}, u32[]{:S(2)}) %collective-permute-start.3) | collective-permute-done | bytes 98336 | tf_op jit(solution)/shard_map/ppermute | solution.py:46
  135.0 11.1 %all_to_all.32.refs_0_ = bf16[8,32,384]{2,1,0:T(8,128)(2,1)S(1)} all-to-all(bf16[8,32,384]{2,1,0:T(8,128)(2,1)S(1)} %sum_for_groups.3), channel_id=1, replica_groups=mesh['dp'=4,'ez'=4,'core'=2] {'ez','core'}, dimensions={0} | all-to-all | bytes 393216 | tf_op jit(solution)/shard_map/all_to_all | solution.py:515
  149.6 10.9 %forward.1 = (bf16[4,224,512]{2,1,0:T(8,128)(2,1)}, bf16[4,224,512]{2,1,0:T(8,128)(2,1)}, bf16[4,224,512]{2,1,0:T(8,128)(2,1)}, bf16[4,224,512]{2,1,0:T(8,128)(2...) custom-call(s32[1]{0:T(128)} %bitcast.dp_ref, ...), custom_call_target="tpu_custom_call" | custom-call | tf_op jit(solution)/shard_map/forward/pallas_call | solution.py:312
  160.6 2.3 collective-permute-start.21
  164.9 12.2 %backward.1 = (bf16[4,224,512]{2,1,0:T(8,128)(2,1)}, bf16[4,224,512]{2,1,0:T(8,128)(2,1)}, bf16[4,224,512]{2,1,0:T(8,128)(2,1)}, f32[4,224,1]{2,1,0:T(8,128)}, b...) custom-call(s32[1]{0:T(128)} %bitcast.dp_ref, ...), custom_call_target="tpu_custom_call" | custom-call | flops 3523215360 | bytes 33554432 | tf_op jit(solution)/shard_map/backward/pallas_call | solution.py:374
  177.1 2.3 collective-permute-start.18
  180.8 9.5 %collective-permute-done.18 = bf16[8,64,384]{2,1,0:T(8,128)(2,1)S(1)} collective-permute-done((bf16[8,64,384]{2,1,0:T(8,128)(2,1)}, bf16[8,64,384]{2,1,0:T(8,128)(2,1)S(1)}, u32[]{:S(2)}, u32[]{:S(2)}) %collective-permute-start.18) | collective-permute-done | bytes 393248 | tf_op jit(solution)/shard_map/ppermute | solution.py:46
  190.3 4.3 %collective-permute-done.17 = bf16[8,64,384]{2,1,0:T(8,128)(2,1)S(1)} collective-permute-done((bf16[8,64,384]{2,1,0:T(8,128)(2,1)}, bf16[8,64,384]{2,1,0:T(8,128)(2,1)S(1)}, u32[]{:S(2)}, u32[]{:S(2)}) %collective-permute-start.17) | collective-permute-done | bytes 393248 | tf_op jit(solution)/shard_map/ppermute | solution.py:46
  196.9 4.0 %all-to-all-start.4 = ((bf16[8,96,384]{2,1,0:T(8,128)(2,1)}), bf16[8,96,384]{2,1,0:T(8,128)(2,1)S(1)}, u32[]{:S(2)}, u32[]{:S(2)}) async-start(bf16[8,96,384]{2,1,0:T(8,128)(2,1)} %pad_maximum_fusion), calls=%async_computation.4 | async-start | bytes 1179648 | tf_op jit(solution)/shard_map/all_to_all | solution.py:515
  209.3 5.2 %factor_grads.1 = (f32[4,512,512]{2,1,0:T(8,128)}, f32[4,512,512]{2,1,0:T(8,128)}, f32[4,512,512]{2,1,0:T(8,128)}) custom-call(bf16[4,224,512]{2,1,0:T(8,128)(2,1)S(1)} %copy-done.9, bf16[4,224,512]{2,1,0:T(8,128)(2,1)S(1)} %copy-done.13, bf16[4,224,512]{2,1,0:T(8,128)(2,1)S(1)} %copy-done.10, bf16[4,224,512]{2,1,0:T(8,128)(2,1)S(1)} %copy-done.14, ...), custom_call_target="tpu_custom_call" | custom-call | tf_op jit(solution)/shard_map/factor_grads/pallas_call | solution.py:407
  221.9 5.0 %collective-permute-done.24 = bf16[256,384]{1,0:T(8,128)(2,1)S(1)} collective-permute-done((bf16[256,384]{1,0:T(8,128)(2,1)S(1)}, bf16[256,384]{1,0:T(8,128)(2,1)S(1)}, u32[]{:S(2)}, u32[]{:S(2)}) %collective-permute-start.24) | collective-permute-done | bytes 196640 | tf_op jit(solution)/shard_map/ppermute | solution.py:46
  235.6 5.7 %all-to-all-start.5 = ((bf16[16,24,1920]{2,1,0:T(8,128)(2,1)}), bf16[16,24,1920]{2,1,0:T(8,128)(2,1)}, u32[]{:S(2)}, u32[]{:S(2)}) async-start(bf16[16,24,1920]{2,1,0:T(8,128)(2,1)} %bitcast.19), calls=%async_computation.5 | async-start | bytes 2949120 | tf_op jit(solution)/shard_map/all_to_all | solution.py:572
  247.2 4.6 %basis_grads.2 = (f32[256,1792]{1,0:T(8,128)}, f32[256,1792]{1,0:T(8,128)}) custom-call(s32[2]{0:T(128)S(1)} %copy-done.19, bf16[256,384]{1,0:T(8,128)(2,1)S(1)} %get-tuple-element.103.refs_0_, bf16[256,384]{1,0:T(8,128)(2,1)S(1)} %get-tuple-element.101.refs_1_, bf16[256,384]{1,0:T(8,128)(2,1)S(1)} %collective-permute-done.26.refs_2_, ...), custom_call_target="tpu_custom_call" | custom-call | tf_op jit(solution)/shard_map/basis_grads/pallas_call | solution.py:188
  257.3 4.6 %collective-permute-done.29 = bf16[128,384]{1,0:T(8,128)(2,1)S(1)} collective-permute-done((bf16[128,384]{1,0:T(8,128)(2,1)S(1)}, bf16[128,384]{1,0:T(8,128)(2,1)S(1)}, u32[]{:S(2)}, u32[]{:S(2)}) %collective-permute-start.29) | collective-permute-done | bytes 98336 | tf_op jit(solution)/shard_map/ppermute | solution.py:46
  262.1 2.6 collective-permute-done.31
  266.4 3.5 %basis_grads.3 = f32[256,1792]{1,0:T(8,128)} custom-call(s32[2]{0:T(128)S(1)} %copy-done.19, bf16[128,384]{1,0:T(8,128)(2,1)S(1)} %get-tuple-element.107.refs_0_, bf16[128,384]{1,0:T(8,128)(2,1)S(1)} %get-tuple-element.105.refs_1_, bf16[128,384]{1,0:T(8,128)(2,1)S(1)} %collective-permute-done.32.refs_2_, ...), custom_call_target="tpu_custom_call" | custom-call | tf_op jit(solution)/shard_map/basis_grads/pallas_call | solution.py:188
  271.7 6.5 %all-to-all-done.5 = bf16[16,24,1920]{2,1,0:T(8,128)(2,1)} async-done(((bf16[16,24,1920]{2,1,0:T(8,128)(2,1)}), bf16[16,24,1920]{2,1,0:T(8,128)(2,1)}, u32[]{:S(2)}, u32[]{:S(2)}) %all-to-all-start.5) | async-done | bytes 1474592 | tf_op jit(solution)/shard_map/all_to_all | solution.py:572
  (224 shorter events, 94.4 us)
Async XLA Ops:
  51.1 37.4 %all-to-all-start.1 = ((bf16[16,24,1792]{2,1,0:T(8,128)(2,1)}), bf16[16,24,1792]{2,1,0:T(8,128)(2,1)S(1)}, u32[]{:S(2)}, u32[]{:S(2)}) async-start(bf16[16,24,1792]{2,1,0:T(8,128)(2,1)} %bitcast.65), calls=%async_computation.1 | async-start | bytes 2752512 | tf_op jit(solution)/shard_map/all_to_all | solution.py:461
  55.4 54.5 %collective-permute-start = (bf16[4,64,1792]{2,1,0:T(8,128)(2,1)}, bf16[4,64,1792]{2,1,0:T(8,128)(2,1)}, u32[]{:S(2)}, u32[]{:S(2)}) collective-permute-start(bf16[4,64,1792]{2,1,0:T(8,128)(2,1)} %refs_0_.2), channel_id=1, source_target_pairs={{0,1},{1,0},{2,3},{3,2},{4,5},{5,4},{6,7},{7,6},{8,9},{9,8},{10,11... | collective-permute-start | bytes 2752520 | tf_op jit(solution)/shard_map/ppermute | solution.py:30
  55.9 12.3 %collective-permute-start.9 = (bf16[384,128]{1,0:T(8,128)(2,1)S(1)}, bf16[384,128]{1,0:T(8,128)(2,1)S(1)}, u32[]{:S(2)}, u32[]{:S(2)}) collective-permute-start(bf16[384,128]{1,0:T(8,128)(2,1)S(1)} %slice.59), channel_id=1, source_target_pairs={{0,1},{1,0},{2,3},{3,2},{4,5},{5,4},{6,7},{7,6},{8,9},{9,8},{10,11... | collective-permute-start | bytes 294920 | tf_op jit(solution)/shard_map/ppermute | solution.py:30
  64.7 21.4 %collective-permute-start.6 = (bf16[256,384]{1,0:T(8,128)(2,1)}, bf16[256,384]{1,0:T(8,128)(2,1)S(1)}, u32[]{:S(2)}, u32[]{:S(2)}) collective-permute-start(bf16[256,384]{1,0:T(8,128)(2,1)} %get-tuple-element.50), channel_id=1, source_target_pairs={{0,8},{8,0},{16,24},{24,16},{1,9},{9,1},{17,25},{25,17},{2,10},{10... | collective-permute-start | bytes 589832 | tf_op jit(solution)/shard_map/ppermute | solution.py:46
  66.4 19.6 %collective-permute-start.7 = (bf16[256,384]{1,0:T(8,128)(2,1)}, bf16[256,384]{1,0:T(8,128)(2,1)S(1)}, u32[]{:S(2)}, u32[]{:S(2)}) collective-permute-start(bf16[256,384]{1,0:T(8,128)(2,1)} %get-tuple-element.51), channel_id=1, source_target_pairs={{0,16},{8,24},{16,0},{24,8},{1,17},{9,25},{17,1},{25,9},{2,18},{10... | collective-permute-start | bytes 589832 | tf_op jit(solution)/shard_map/ppermute | solution.py:46
  67.9 18.1 %collective-permute-start.8 = (bf16[256,384]{1,0:T(8,128)(2,1)}, bf16[256,384]{1,0:T(8,128)(2,1)}, u32[]{:S(2)}, u32[]{:S(2)}) collective-permute-start(bf16[256,384]{1,0:T(8,128)(2,1)} %get-tuple-element.52), channel_id=1, source_target_pairs={{0,24},{8,16},{16,8},{24,0},{1,25},{9,17},{17,9},{25,1},{2,26},{10... | collective-permute-start | bytes 589832 | tf_op jit(solution)/shard_map/ppermute | solution.py:46
  106.3 27.0 %collective-permute-start.10 = (bf16[8,64,384]{2,1,0:T(8,128)(2,1)S(1)}, bf16[8,64,384]{2,1,0:T(8,128)(2,1)S(1)}, u32[]{:S(2)}, u32[]{:S(2)}) collective-permute-start(bf16[8,64,384]{2,1,0:T(8,128)(2,1)S(1)} %all_to_all.31.refs_0_), channel_id=1, source_target_pairs={{0,8},{8,0},{16,24},{24,16},{1,9},{9,1},{17,25},{25,17},{2,10},{10... | collective-permute-start | bytes 1179656 | tf_op jit(solution)/shard_map/ppermute | solution.py:46
  107.7 25.7 %collective-permute-start.11 = (bf16[8,64,384]{2,1,0:T(8,128)(2,1)S(1)}, bf16[8,64,384]{2,1,0:T(8,128)(2,1)S(1)}, u32[]{:S(2)}, u32[]{:S(2)}) collective-permute-start(bf16[8,64,384]{2,1,0:T(8,128)(2,1)S(1)} %all_to_all.31.refs_0_), channel_id=1, source_target_pairs={{0,16},{8,24},{16,0},{24,8},{1,17},{9,25},{17,1},{25,9},{2,18},{10... | collective-permute-start | bytes 1179656 | tf_op jit(solution)/shard_map/ppermute | solution.py:46
  109.2 24.2 %collective-permute-start.12 = (bf16[8,64,384]{2,1,0:T(8,128)(2,1)S(1)}, bf16[8,64,384]{2,1,0:T(8,128)(2,1)S(1)}, u32[]{:S(2)}, u32[]{:S(2)}) collective-permute-start(bf16[8,64,384]{2,1,0:T(8,128)(2,1)S(1)} %all_to_all.31.refs_0_), channel_id=1, source_target_pairs={{0,24},{8,16},{16,8},{24,0},{1,25},{9,17},{17,9},{25,1},{2,26},{10... | collective-permute-start | bytes 1179656 | tf_op jit(solution)/shard_map/ppermute | solution.py:46
  114.2 13.4 %collective-permute-start.1 = (bf16[128,384]{1,0:T(8,128)(2,1)}, bf16[128,384]{1,0:T(8,128)(2,1)S(1)}, u32[]{:S(2)}, u32[]{:S(2)}) collective-permute-start(bf16[128,384]{1,0:T(8,128)(2,1)} %get-tuple-element.46), channel_id=1, source_target_pairs={{0,8},{8,0},{16,24},{24,16},{1,9},{9,1},{17,25},{25,17},{2,10},{10... | collective-permute-start | bytes 294920 | tf_op jit(solution)/shard_map/ppermute | solution.py:46
  115.5 14.4 %collective-permute-start.2 = (bf16[128,384]{1,0:T(8,128)(2,1)}, bf16[128,384]{1,0:T(8,128)(2,1)S(1)}, u32[]{:S(2)}, u32[]{:S(2)}) collective-permute-start(bf16[128,384]{1,0:T(8,128)(2,1)} %get-tuple-element.47), channel_id=1, source_target_pairs={{0,16},{8,24},{16,0},{24,8},{1,17},{9,25},{17,1},{25,9},{2,18},{10... | collective-permute-start | bytes 294920 | tf_op jit(solution)/shard_map/ppermute | solution.py:46
  146.1 17.3 %collective-permute-start.13 = (bf16[8,32,384]{2,1,0:T(8,128)(2,1)S(1)}, bf16[8,32,384]{2,1,0:T(8,128)(2,1)S(1)}, u32[]{:S(2)}, u32[]{:S(2)}) collective-permute-start(bf16[8,32,384]{2,1,0:T(8,128)(2,1)S(1)} %all_to_all.32.refs_0_), channel_id=1, source_target_pairs={{0,8},{8,0},{16,24},{24,16},{1,9},{9,1},{17,25},{25,17},{2,10},{10... | collective-permute-start | bytes 589832 | tf_op jit(solution)/shard_map/ppermute | solution.py:46
  147.5 16.7 %collective-permute-start.14 = (bf16[8,32,384]{2,1,0:T(8,128)(2,1)S(1)}, bf16[8,32,384]{2,1,0:T(8,128)(2,1)S(1)}, u32[]{:S(2)}, u32[]{:S(2)}) collective-permute-start(bf16[8,32,384]{2,1,0:T(8,128)(2,1)S(1)} %all_to_all.32.refs_0_), channel_id=1, source_target_pairs={{0,16},{8,24},{16,0},{24,8},{1,17},{9,25},{17,1},{25,9},{2,18},{10... | collective-permute-start | bytes 589832 | tf_op jit(solution)/shard_map/ppermute | solution.py:46
  149.0 15.2 %collective-permute-start.15 = (bf16[8,32,384]{2,1,0:T(8,128)(2,1)S(1)}, bf16[8,32,384]{2,1,0:T(8,128)(2,1)S(1)}, u32[]{:S(2)}, u32[]{:S(2)}) collective-permute-start(bf16[8,32,384]{2,1,0:T(8,128)(2,1)S(1)} %all_to_all.32.refs_0_), channel_id=1, source_target_pairs={{0,24},{8,16},{16,8},{24,0},{1,25},{9,17},{17,9},{25,1},{2,26},{10... | collective-permute-start | bytes 589832 | tf_op jit(solution)/shard_map/ppermute | solution.py:46
  160.6 19.4 %collective-permute-start.21 = (bf16[8,32,384]{2,1,0:T(8,128)(2,1)}, bf16[8,32,384]{2,1,0:T(8,128)(2,1)S(1)}, u32[]{:S(2)}, u32[]{:S(2)}) collective-permute-start(bf16[8,32,384]{2,1,0:T(8,128)(2,1)} %get-tuple-element.65), channel_id=1, source_target_pairs={{0,24},{8,16},{16,8},{24,0},{1,25},{9,17},{17,9},{25,1},{2,26},{10... | collective-permute-start | bytes 589832 | tf_op jit(solution)/shard_map/ppermute | solution.py:46
  162.9 17.7 %collective-permute-start.20 = (bf16[8,32,384]{2,1,0:T(8,128)(2,1)}, bf16[8,32,384]{2,1,0:T(8,128)(2,1)S(1)}, u32[]{:S(2)}, u32[]{:S(2)}) collective-permute-start(bf16[8,32,384]{2,1,0:T(8,128)(2,1)} %get-tuple-element.64), channel_id=1, source_target_pairs={{0,16},{8,24},{16,0},{24,8},{1,17},{9,25},{17,1},{25,9},{2,18},{10... | collective-permute-start | bytes 589832 | tf_op jit(solution)/shard_map/ppermute | solution.py:46
  163.4 17.2 %collective-permute-start.19 = (bf16[8,32,384]{2,1,0:T(8,128)(2,1)}, bf16[8,32,384]{2,1,0:T(8,128)(2,1)S(1)}, u32[]{:S(2)}, u32[]{:S(2)}) collective-permute-start(bf16[8,32,384]{2,1,0:T(8,128)(2,1)} %get-tuple-element.63), channel_id=1, source_target_pairs={{0,8},{8,0},{16,24},{24,16},{1,9},{9,1},{17,25},{25,17},{2,10},{10... | collective-permute-start | bytes 589832 | tf_op jit(solution)/shard_map/ppermute | solution.py:46
  177.1 13.2 %collective-permute-start.18 = (bf16[8,64,384]{2,1,0:T(8,128)(2,1)}, bf16[8,64,384]{2,1,0:T(8,128)(2,1)S(1)}, u32[]{:S(2)}, u32[]{:S(2)}) collective-permute-start(bf16[8,64,384]{2,1,0:T(8,128)(2,1)} %get-tuple-element.61), channel_id=1, source_target_pairs={{0,24},{8,16},{16,8},{24,0},{1,25},{9,17},{17,9},{25,1},{2,26},{10... | collective-permute-start | bytes 1179656 | tf_op jit(solution)/shard_map/ppermute | solution.py:46
  179.4 15.2 %collective-permute-start.17 = (bf16[8,64,384]{2,1,0:T(8,128)(2,1)}, bf16[8,64,384]{2,1,0:T(8,128)(2,1)S(1)}, u32[]{:S(2)}, u32[]{:S(2)}) collective-permute-start(bf16[8,64,384]{2,1,0:T(8,128)(2,1)} %get-tuple-element.60), channel_id=1, source_target_pairs={{0,16},{8,24},{16,0},{24,8},{1,17},{9,25},{17,1},{25,9},{2,18},{10... | collective-permute-start | bytes 1179656 | tf_op jit(solution)/shard_map/ppermute | solution.py:46
  179.9 14.7 %collective-permute-start.16 = (bf16[8,64,384]{2,1,0:T(8,128)(2,1)}, bf16[8,64,384]{2,1,0:T(8,128)(2,1)S(1)}, u32[]{:S(2)}, u32[]{:S(2)}) collective-permute-start(bf16[8,64,384]{2,1,0:T(8,128)(2,1)} %get-tuple-element.59), channel_id=1, source_target_pairs={{0,8},{8,0},{16,24},{24,16},{1,9},{9,1},{17,25},{25,17},{2,10},{10... | collective-permute-start | bytes 1179656 | tf_op jit(solution)/shard_map/ppermute | solution.py:46
  196.9 20.7 %all-to-all-start.4 = ((bf16[8,96,384]{2,1,0:T(8,128)(2,1)}), bf16[8,96,384]{2,1,0:T(8,128)(2,1)S(1)}, u32[]{:S(2)}, u32[]{:S(2)}) async-start(bf16[8,96,384]{2,1,0:T(8,128)(2,1)} %pad_maximum_fusion), calls=%async_computation.4 | async-start | bytes 1179648 | tf_op jit(solution)/shard_map/all_to_all | solution.py:515
  202.9 17.1 %collective-permute-start.25 = (bf16[4,384]{1,0:T(4,128)(2,1)S(1)}, bf16[4,384]{1,0:T(4,128)(2,1)S(1)}, u32[]{:S(2)}, u32[]{:S(2)}) collective-permute-start(bf16[4,384]{1,0:T(4,128)(2,1)S(1)} %select_bitcast_fusion.2), channel_id=1, source_target_pairs={{0,1},{1,0},{2,3},{3,2},{4,5},{5,4},{6,7},{7,6},{8,9},{9,8},{10,11... | collective-permute-start | bytes 9224 | tf_op jit(solution)/shard_map/ppermute | solution.py:30
  235.6 42.6 %all-to-all-start.5 = ((bf16[16,24,1920]{2,1,0:T(8,128)(2,1)}), bf16[16,24,1920]{2,1,0:T(8,128)(2,1)}, u32[]{:S(2)}, u32[]{:S(2)}) async-start(bf16[16,24,1920]{2,1,0:T(8,128)(2,1)} %bitcast.19), calls=%async_computation.5 | async-start | bytes 2949120 | tf_op jit(solution)/shard_map/all_to_all | solution.py:572
  241.5 23.7 %collective-permute-start.34 = (bf16[384,1792]{1,0:T(8,128)(2,1)S(1)}, bf16[384,1792]{1,0:T(8,128)(2,1)}, u32[]{:S(2)}, u32[]{:S(2)}) collective-permute-start(bf16[384,1792]{1,0:T(8,128)(2,1)S(1)} %bitcast.56), channel_id=1, source_target_pairs={{0,1},{1,0},{2,3},{3,2},{4,5},{5,4},{6,7},{7,6},{8,9},{9,8},{10,11... | collective-permute-start | bytes 4128776 | tf_op jit(solution)/shard_map/ppermute | solution.py:30
  (53 other events, 441.8 us)

commit v10 on v9

--- a/solution.py
+++ b/solution.py
@@ -150,6 +150,21 @@
         cost_estimate=FREE,
         name="sum_for_groups",
     )(groups, *pieces, *firsts)
+
+
+def hold(value, firsts):
+    def kernel(value_ref, *refs):
+        refs[-1][...] = value_ref[...]
+
+    return pl.pallas_call(
+        kernel,
+        out_shape=shaped(value.shape, value.dtype),
+        in_specs=[whole(value)] + [ANYWHERE] * len(firsts),
+        out_specs=whole(value),
+        compiler_params=params(2 * value.shape[-1]),
+        cost_estimate=FREE,
+        name="hold",
+    )(value, *firsts)
 
 
 def basis_grads(keep, other, cols, other_cols, spot, shape, n_dp, first):
@@ -528,13 +543,14 @@
     h_pieces = trade(lambda k: got_in, "dp")
     got_out = spread(
         sum_for_groups(
-            trade(lambda k: terms_out[k], "dp"), group_cluster, clusters, 1, h_pieces[1:]
+            trade(lambda k: terms_out[k], "dp"), group_cluster, clusters, 1, []
         )
     )
     (hg, hu, hidden, mixed, act, lift), mixed_chunks = forward(
         h_pieces, pick, weight_of, gate_factor, up_factor, down_factor, dp
     )
-    d_pieces = trade(lambda k: got_out, "dp")
+    held_out = hold(got_out, h_pieces[1:])
+    d_pieces = trade(lambda k: held_out, "dp")
     (back, grad_gate, grad_up, dots), in_chunks = backward(
         d_pieces, pick, slot_weight, mixed, act, lift, gate_factor, up_factor, down_factor, dp
     )

time: 284 us -> 267 us (0.940)
  blocking collectives: 70.7 us -> 55.4 us
  waiting for transfers between devices: 56.6 us -> 48.5 us
  other arithmetic: 19.8 us -> 23.5 us
    all_to_all x2 -> x1, blocking collectives: 26 us -> 10.7 us  [spread(): lax.all_to_all(mine, ('ez', 'core'), split_axis=0, concat_axis=0, tiled=T...]
    ppermute x24, waiting for transfers between devices: 40.8 us -> 31.8 us  [trade(): lax.ppermute(chunk_for(k), axis, [(i, i ^ k) for i in range(n)])]
    all_to_all x1 -> x2, waiting for transfers between devices: 1.2 us -> 5.92 us  [spread(): lax.all_to_all(mine, ('ez', 'core'), split_axis=0, concat_axis=0, tiled=T...]
    all_to_all x1 -> x2, starting transfers between devices: 3.97 us -> 8.37 us  [spread(): lax.all_to_all(mine, ('ez', 'core'), split_axis=0, concat_axis=0, tiled=T...]
  transfers between devices with their start and end apart: 38 -> 39, of which waited for: 17 -> 15; matrix products, arithmetic and copies ran while one was open for 10% -> 12% of each run, Pallas kernels for 17% -> 19%
where the time goes in v10:
time: 267 us; the launch traced here: 265 us
  blocking collectives  55.4 us (21%)
  Pallas kernels  49.5 us (19%)
  starting transfers between devices  49 us (18%)
  waiting for transfers between devices  48.5 us (18%)
  local copies, waits for them, and re-layouts  31.7 us (12%)
  other arithmetic  23.5 us (9%)
  between operations  3.9 us (1%)
  matrix products  3.58 us (1%)
    all_to_all x1, blocking collectives, own_columns(): lax.all_to_all(rows, ('dp', 'ez'), split_axis=0, concat_axis=0, tiled=True)  44.7 us
    ppermute x24, waiting for transfers between devices, trade(): lax.ppermute(chunk_for(k), axis, [(i, i ^ k) for i in range(n)])  31.8 us
    ppermute x24, starting transfers between devices, trade(): lax.ppermute(chunk_for(k), axis, [(i, i ^ k) for i in range(n)])  28.3 us
    unnamed x83, local copies, waits for them, and re-layouts  16.2 us
    pallas_call x1, Pallas kernels, backward(): pl.pallas_call(kernel, grid=(local,), out_shape=outs + chunks, in_specs=[...  12.2 us
    pallas_call x1, Pallas kernels, forward(): pl.pallas_call(kernel, grid=(local,), out_shape=outs + chunks, in_specs=[...  10.9 us
    all_to_all x1, blocking collectives, spread(): lax.all_to_all(mine, ('ez', 'core'), split_axis=0, concat_axis=0, tiled=T...  10.7 us
    pallas_call x2, Pallas kernels, project(): pl.pallas_call(kernel, out_shape=outs, in_specs=[SCALAR] + [whole(x) for...  9.82 us
  transfers between devices with their start and end apart: 39, of which 15 were waited for; matrix products, arithmetic and copies ran while one was open for 12% of the time, Pallas kernels for 19%

profile of v10, /device:TPU:0, one launch (start us, length us, event | category | flops | bytes accessed | tf_op | source)
XLA Modules:
  0.0 265.1 jit_solution(17280566282714404243)
XLA Ops:
  3.7 44.7 %all_to_all.30 = bf16[16,24,1920]{2,1,0:T(8,128)(2,1)S(1)} all-to-all(bf16[16,24,1920]{2,1,0:T(8,128)(2,1)S(1)} %bitcast.64), channel_id=1, replica_groups=mesh['dp'=4,'ez'=4,'core'=2] {'dp','ez'}, dimensions={0} | all-to-all | bytes 2949120 | tf_op jit(solution)/shard_map/all_to_all | solution.py:476
  51.1 3.7 %all-to-all-start.1 = ((bf16[16,24,1792]{2,1,0:T(8,128)(2,1)}), bf16[16,24,1792]{2,1,0:T(8,128)(2,1)S(1)}, u32[]{:S(2)}, u32[]{:S(2)}) async-start(bf16[16,24,1792]{2,1,0:T(8,128)(2,1)} %bitcast.65), calls=%async_computation.1 | async-start | bytes 2752512 | tf_op jit(solution)/shard_map/all_to_all | solution.py:476
  59.0 5.5 %project.3 = (bf16[256,1792]{1,0:T(8,128)(2,1)}, bf16[256,1792]{1,0:T(8,128)(2,1)}, bf16[256,1792]{1,0:T(8,128)(2,1)}, bf16[256,1792]{1,0:T(8,128)(2,1)}, bf16[2...) custom-call(s32[2]{0:T(128)} %pad_add_fusion.spot_ref, ...), custom_call_target="tpu_custom_call" | custom-call | tf_op jit(solution)/shard_map/project/pallas_call | solution.py:112
  75.9 3.0 %reduce_window_sum.11 = s32[4,32,24]{2,1,0:T(8,128)} reduce-window(s32[4,32,24]{2,1,0:T(8,128)} %copy.81, s32[]{:T(128)} %constant.40.clone.1), window={size=1x1x24 pad=0_0x0_0x23_0}, to_apply=%region_1.2 | reduce-window | flops 70656 | bytes 24580 | tf_op jit(solution)/shard_map/jit(cumsum)/reduce_window_sum | solution.py:518
  93.9 4.8 %all-to-all-start.3 = ((bf16[8,64,384]{2,1,0:T(8,128)(2,1)}), bf16[8,64,384]{2,1,0:T(8,128)(2,1)S(1)}, u32[]{:S(2)}, u32[]{:S(2)}) async-start(bf16[8,64,384]{2,1,0:T(8,128)(2,1)} %sum_for_groups.3), calls=%async_computation.3 | async-start | bytes 786432 | tf_op jit(solution)/shard_map/all_to_all | solution.py:530
  98.8 4.3 %project.2 = (bf16[128,1792]{1,0:T(8,128)(2,1)}, bf16[128,1792]{1,0:T(8,128)(2,1)}, bf16[128,1792]{1,0:T(8,128)(2,1)}, bf16[128,1792]{1,0:T(8,128)(2,1)}, bf16[1...) custom-call(s32[2]{0:T(128)} %pad_add_fusion.spot_ref, ...), custom_call_target="tpu_custom_call" | custom-call | tf_op jit(solution)/shard_map/project/pallas_call | solution.py:112
  106.6 4.7 %all-to-all-done.3.refs_0_ = bf16[8,64,384]{2,1,0:T(8,128)(2,1)S(1)} async-done(((bf16[8,64,384]{2,1,0:T(8,128)(2,1)}), bf16[8,64,384]{2,1,0:T(8,128)(2,1)S(1)}, u32[]{:S(2)}, u32[]{:S(2)}) %all-to-all-start.3) | async-done | bytes 393248 | tf_op jit(solution)/shard_map/all_to_all | solution.py:530
  116.3 10.7 %all_to_all.31.value_ref = bf16[8,32,384]{2,1,0:T(8,128)(2,1)S(1)} all-to-all(bf16[8,32,384]{2,1,0:T(8,128)(2,1)S(1)} %sum_for_groups.2), channel_id=1, replica_groups=mesh['dp'=4,'ez'=4,'core'=2] {'ez','core'}, dimensions={0} | all-to-all | bytes 393216 | tf_op jit(solution)/shard_map/all_to_all | solution.py:530
  127.1 4.5 %collective-permute-done.11.refs_1_.refs_2_ = bf16[8,64,384]{2,1,0:T(8,128)(2,1)S(1)} collective-permute-done((bf16[8,64,384]{2,1,0:T(8,128)(2,1)S(1)}, bf16[8,64,384]{2,1,0:T(8,128)(2,1)S(1)}, u32[]{:S(2)}, u32[]{:S(2)}) %collective-permute-start.11) | collective-permute-done | bytes 393248 | tf_op jit(solution)/shard_map/ppermute | solution.py:46
  135.2 10.9 %forward.1 = (bf16[4,224,512]{2,1,0:T(8,128)(2,1)}, bf16[4,224,512]{2,1,0:T(8,128)(2,1)}, bf16[4,224,512]{2,1,0:T(8,128)(2,1)}, bf16[4,224,512]{2,1,0:T(8,128)(2...) custom-call(s32[1]{0:T(128)} %bitcast.dp_ref, ...), custom_call_target="tpu_custom_call" | custom-call | tf_op jit(solution)/shard_map/forward/pallas_call | solution.py:327
  150.5 12.2 %backward.1 = (bf16[4,224,512]{2,1,0:T(8,128)(2,1)}, bf16[4,224,512]{2,1,0:T(8,128)(2,1)}, bf16[4,224,512]{2,1,0:T(8,128)(2,1)}, f32[4,224,1]{2,1,0:T(8,128)}, b...) custom-call(s32[1]{0:T(128)} %bitcast.dp_ref, ...), custom_call_target="tpu_custom_call" | custom-call | flops 3523215360 | bytes 33554432 | tf_op jit(solution)/shard_map/backward/pallas_call | solution.py:389
  166.4 9.5 %collective-permute-done.18 = bf16[8,64,384]{2,1,0:T(8,128)(2,1)S(1)} collective-permute-done((bf16[8,64,384]{2,1,0:T(8,128)(2,1)}, bf16[8,64,384]{2,1,0:T(8,128)(2,1)S(1)}, u32[]{:S(2)}, u32[]{:S(2)}) %collective-permute-start.18) | collective-permute-done | bytes 393248 | tf_op jit(solution)/shard_map/ppermute | solution.py:46
  175.9 4.2 %collective-permute-done.17 = bf16[8,64,384]{2,1,0:T(8,128)(2,1)S(1)} collective-permute-done((bf16[8,64,384]{2,1,0:T(8,128)(2,1)}, bf16[8,64,384]{2,1,0:T(8,128)(2,1)S(1)}, u32[]{:S(2)}, u32[]{:S(2)}) %collective-permute-start.17) | collective-permute-done | bytes 393248 | tf_op jit(solution)/shard_map/ppermute | solution.py:46
  182.3 3.5 %all-to-all-start.4 = ((bf16[8,96,384]{2,1,0:T(8,128)(2,1)}), bf16[8,96,384]{2,1,0:T(8,128)(2,1)S(1)}, u32[]{:S(2)}, u32[]{:S(2)}) async-start(bf16[8,96,384]{2,1,0:T(8,128)(2,1)} %pad_maximum_fusion), calls=%async_computation.4 | async-start | bytes 1179648 | tf_op jit(solution)/shard_map/all_to_all | solution.py:530
  194.3 5.2 %factor_grads.1 = (f32[4,512,512]{2,1,0:T(8,128)}, f32[4,512,512]{2,1,0:T(8,128)}, f32[4,512,512]{2,1,0:T(8,128)}) custom-call(bf16[4,224,512]{2,1,0:T(8,128)(2,1)S(1)} %copy-done.9, bf16[4,224,512]{2,1,0:T(8,128)(2,1)S(1)} %copy-done.13, bf16[4,224,512]{2,1,0:T(8,128)(2,1)S(1)} %copy-done.10, bf16[4,224,512]{2,1,0:T(8,128)(2,1)S(1)} %copy-done.14, ...), custom_call_target="tpu_custom_call" | custom-call | tf_op jit(solution)/shard_map/factor_grads/pallas_call | solution.py:422
  206.9 5.0 %collective-permute-done.24 = bf16[256,384]{1,0:T(8,128)(2,1)S(1)} collective-permute-done((bf16[256,384]{1,0:T(8,128)(2,1)S(1)}, bf16[256,384]{1,0:T(8,128)(2,1)S(1)}, u32[]{:S(2)}, u32[]{:S(2)}) %collective-permute-start.24) | collective-permute-done | bytes 196640 | tf_op jit(solution)/shard_map/ppermute | solution.py:46
  218.4 5.5 %all-to-all-start.5 = ((bf16[16,24,1920]{2,1,0:T(8,128)(2,1)}), bf16[16,24,1920]{2,1,0:T(8,128)(2,1)}, u32[]{:S(2)}, u32[]{:S(2)}) async-start(bf16[16,24,1920]{2,1,0:T(8,128)(2,1)} %bitcast.19), calls=%async_computation.5 | async-start | bytes 2949120 | tf_op jit(solution)/shard_map/all_to_all | solution.py:588
  227.8 2.0 collective-permute-done.27.refs_3_
  229.8 4.6 %basis_grads.2 = (f32[256,1792]{1,0:T(8,128)}, f32[256,1792]{1,0:T(8,128)}) custom-call(s32[2]{0:T(128)S(1)} %copy-done.20, bf16[256,384]{1,0:T(8,128)(2,1)S(1)} %get-tuple-element.103.refs_0_, bf16[256,384]{1,0:T(8,128)(2,1)S(1)} %get-tuple-element.101.refs_1_, bf16[256,384]{1,0:T(8,128)(2,1)S(1)} %collective-permute-done.26.refs_2_, ...), custom_call_target="tpu_custom_call" | custom-call | tf_op jit(solution)/shard_map/basis_grads/pallas_call | solution.py:203
  236.3 1.9 collective-permute-start.29
  239.9 4.6 %collective-permute-done.29 = bf16[128,384]{1,0:T(8,128)(2,1)S(1)} collective-permute-done((bf16[128,384]{1,0:T(8,128)(2,1)S(1)}, bf16[128,384]{1,0:T(8,128)(2,1)S(1)}, u32[]{:S(2)}, u32[]{:S(2)}) %collective-permute-start.29) | collective-permute-done | bytes 98336 | tf_op jit(solution)/shard_map/ppermute | solution.py:46
  244.7 2.6 collective-permute-done.31
  248.9 3.5 %basis_grads.3 = f32[256,1792]{1,0:T(8,128)} custom-call(s32[2]{0:T(128)S(1)} %copy-done.20, bf16[128,384]{1,0:T(8,128)(2,1)S(1)} %get-tuple-element.107.refs_0_, bf16[128,384]{1,0:T(8,128)(2,1)S(1)} %get-tuple-element.105.refs_1_, bf16[128,384]{1,0:T(8,128)(2,1)S(1)} %collective-permute-done.32.refs_2_, ...), custom_call_target="tpu_custom_call" | custom-call | tf_op jit(solution)/shard_map/basis_grads/pallas_call | solution.py:203
  254.3 6.5 %all-to-all-done.5 = bf16[16,24,1920]{2,1,0:T(8,128)(2,1)} async-done(((bf16[16,24,1920]{2,1,0:T(8,128)(2,1)}), bf16[16,24,1920]{2,1,0:T(8,128)(2,1)}, u32[]{:S(2)}, u32[]{:S(2)}) %all-to-all-start.5) | async-done | bytes 1474592 | tf_op jit(solution)/shard_map/all_to_all | solution.py:588
  (226 shorter events, 93.3 us)
Async XLA Ops:
  51.1 39.1 %all-to-all-start.1 = ((bf16[16,24,1792]{2,1,0:T(8,128)(2,1)}), bf16[16,24,1792]{2,1,0:T(8,128)(2,1)S(1)}, u32[]{:S(2)}, u32[]{:S(2)}) async-start(bf16[16,24,1792]{2,1,0:T(8,128)(2,1)} %bitcast.65), calls=%async_computation.1 | async-start | bytes 2752512 | tf_op jit(solution)/shard_map/all_to_all | solution.py:476
  55.4 43.4 %collective-permute-start = (bf16[4,64,1792]{2,1,0:T(8,128)(2,1)}, bf16[4,64,1792]{2,1,0:T(8,128)(2,1)}, u32[]{:S(2)}, u32[]{:S(2)}) collective-permute-start(bf16[4,64,1792]{2,1,0:T(8,128)(2,1)} %refs_0_.2), channel_id=1, source_target_pairs={{0,1},{1,0},{2,3},{3,2},{4,5},{5,4},{6,7},{7,6},{8,9},{9,8},{10,11... | collective-permute-start | bytes 2752520 | tf_op jit(solution)/shard_map/ppermute | solution.py:30
  57.0 11.0 %collective-permute-start.9 = (bf16[384,128]{1,0:T(8,128)(2,1)S(1)}, bf16[384,128]{1,0:T(8,128)(2,1)S(1)}, u32[]{:S(2)}, u32[]{:S(2)}) collective-permute-start(bf16[384,128]{1,0:T(8,128)(2,1)S(1)} %slice.59), channel_id=1, source_target_pairs={{0,1},{1,0},{2,3},{3,2},{4,5},{5,4},{6,7},{7,6},{8,9},{9,8},{10,11... | collective-permute-start | bytes 294920 | tf_op jit(solution)/shard_map/ppermute | solution.py:30
  64.5 25.7 %collective-permute-start.6 = (bf16[256,384]{1,0:T(8,128)(2,1)}, bf16[256,384]{1,0:T(8,128)(2,1)S(1)}, u32[]{:S(2)}, u32[]{:S(2)}) collective-permute-start(bf16[256,384]{1,0:T(8,128)(2,1)} %get-tuple-element.50), channel_id=1, source_target_pairs={{0,8},{8,0},{16,24},{24,16},{1,9},{9,1},{17,25},{25,17},{2,10},{10... | collective-permute-start | bytes 589832 | tf_op jit(solution)/shard_map/ppermute | solution.py:46
  66.3 24.0 %collective-permute-start.7 = (bf16[256,384]{1,0:T(8,128)(2,1)}, bf16[256,384]{1,0:T(8,128)(2,1)S(1)}, u32[]{:S(2)}, u32[]{:S(2)}) collective-permute-start(bf16[256,384]{1,0:T(8,128)(2,1)} %get-tuple-element.51), channel_id=1, source_target_pairs={{0,16},{8,24},{16,0},{24,8},{1,17},{9,25},{17,1},{25,9},{2,18},{10... | collective-permute-start | bytes 589832 | tf_op jit(solution)/shard_map/ppermute | solution.py:46
  67.8 22.4 %collective-permute-start.8 = (bf16[256,384]{1,0:T(8,128)(2,1)}, bf16[256,384]{1,0:T(8,128)(2,1)}, u32[]{:S(2)}, u32[]{:S(2)}) collective-permute-start(bf16[256,384]{1,0:T(8,128)(2,1)} %get-tuple-element.52), channel_id=1, source_target_pairs={{0,24},{8,16},{16,8},{24,0},{1,25},{9,17},{17,9},{25,1},{2,26},{10... | collective-permute-start | bytes 589832 | tf_op jit(solution)/shard_map/ppermute | solution.py:46
  93.9 17.4 %all-to-all-start.3 = ((bf16[8,64,384]{2,1,0:T(8,128)(2,1)}), bf16[8,64,384]{2,1,0:T(8,128)(2,1)S(1)}, u32[]{:S(2)}, u32[]{:S(2)}) async-start(bf16[8,64,384]{2,1,0:T(8,128)(2,1)} %sum_for_groups.3), calls=%async_computation.3 | async-start | bytes 786432 | tf_op jit(solution)/shard_map/all_to_all | solution.py:530
  103.1 11.2 %collective-permute-start.1 = (bf16[128,384]{1,0:T(8,128)(2,1)}, bf16[128,384]{1,0:T(8,128)(2,1)S(1)}, u32[]{:S(2)}, u32[]{:S(2)}) collective-permute-start(bf16[128,384]{1,0:T(8,128)(2,1)} %get-tuple-element.46), channel_id=1, source_target_pairs={{0,8},{8,0},{16,24},{24,16},{1,9},{9,1},{17,25},{25,17},{2,10},{10... | collective-permute-start | bytes 294920 | tf_op jit(solution)/shard_map/ppermute | solution.py:46
  111.3 15.7 %collective-permute-start.10 = (bf16[8,64,384]{2,1,0:T(8,128)(2,1)S(1)}, bf16[8,64,384]{2,1,0:T(8,128)(2,1)S(1)}, u32[]{:S(2)}, u32[]{:S(2)}) collective-permute-start(bf16[8,64,384]{2,1,0:T(8,128)(2,1)S(1)} %all-to-all-done.3.refs_0_), channel_id=1, source_target_pairs={{0,8},{8,0},{16,24},{24,16},{1,9},{9,1},{17,25},{25,17},{2,10},{10... | collective-permute-start | bytes 1179656 | tf_op jit(solution)/shard_map/ppermute | solution.py:46
  112.8 18.8 %collective-permute-start.11 = (bf16[8,64,384]{2,1,0:T(8,128)(2,1)S(1)}, bf16[8,64,384]{2,1,0:T(8,128)(2,1)S(1)}, u32[]{:S(2)}, u32[]{:S(2)}) collective-permute-start(bf16[8,64,384]{2,1,0:T(8,128)(2,1)S(1)} %all-to-all-done.3.refs_0_), channel_id=1, source_target_pairs={{0,16},{8,24},{16,0},{24,8},{1,17},{9,25},{17,1},{25,9},{2,18},{10... | collective-permute-start | bytes 1179656 | tf_op jit(solution)/shard_map/ppermute | solution.py:46
  114.3 17.3 %collective-permute-start.12 = (bf16[8,64,384]{2,1,0:T(8,128)(2,1)S(1)}, bf16[8,64,384]{2,1,0:T(8,128)(2,1)S(1)}, u32[]{:S(2)}, u32[]{:S(2)}) collective-permute-start(bf16[8,64,384]{2,1,0:T(8,128)(2,1)S(1)} %all-to-all-done.3.refs_0_), channel_id=1, source_target_pairs={{0,24},{8,16},{16,8},{24,0},{1,25},{9,17},{17,9},{25,1},{2,26},{10... | collective-permute-start | bytes 1179656 | tf_op jit(solution)/shard_map/ppermute | solution.py:46
  131.7 17.3 %collective-permute-start.13 = (bf16[8,32,384]{2,1,0:T(8,128)(2,1)S(1)}, bf16[8,32,384]{2,1,0:T(8,128)(2,1)S(1)}, u32[]{:S(2)}, u32[]{:S(2)}) collective-permute-start(bf16[8,32,384]{2,1,0:T(8,128)(2,1)S(1)} %hold.1.refs_0_), channel_id=1, source_target_pairs={{0,8},{8,0},{16,24},{24,16},{1,9},{9,1},{17,25},{25,17},{2,10},{10... | collective-permute-start | bytes 589832 | tf_op jit(solution)/shard_map/ppermute | solution.py:46
  133.0 16.8 %collective-permute-start.14 = (bf16[8,32,384]{2,1,0:T(8,128)(2,1)S(1)}, bf16[8,32,384]{2,1,0:T(8,128)(2,1)S(1)}, u32[]{:S(2)}, u32[]{:S(2)}) collective-permute-start(bf16[8,32,384]{2,1,0:T(8,128)(2,1)S(1)} %hold.1.refs_0_), channel_id=1, source_target_pairs={{0,16},{8,24},{16,0},{24,8},{1,17},{9,25},{17,1},{25,9},{2,18},{10... | collective-permute-start | bytes 589832 | tf_op jit(solution)/shard_map/ppermute | solution.py:46
  133.8 16.0 %collective-permute-start.15 = (bf16[8,32,384]{2,1,0:T(8,128)(2,1)S(1)}, bf16[8,32,384]{2,1,0:T(8,128)(2,1)S(1)}, u32[]{:S(2)}, u32[]{:S(2)}) collective-permute-start(bf16[8,32,384]{2,1,0:T(8,128)(2,1)S(1)} %hold.1.refs_0_), channel_id=1, source_target_pairs={{0,24},{8,16},{16,8},{24,0},{1,25},{9,17},{17,9},{25,1},{2,26},{10... | collective-permute-start | bytes 589832 | tf_op jit(solution)/shard_map/ppermute | solution.py:46
  146.2 19.3 %collective-permute-start.21 = (bf16[8,32,384]{2,1,0:T(8,128)(2,1)}, bf16[8,32,384]{2,1,0:T(8,128)(2,1)S(1)}, u32[]{:S(2)}, u32[]{:S(2)}) collective-permute-start(bf16[8,32,384]{2,1,0:T(8,128)(2,1)} %get-tuple-element.65), channel_id=1, source_target_pairs={{0,24},{8,16},{16,8},{24,0},{1,25},{9,17},{17,9},{25,1},{2,26},{10... | collective-permute-start | bytes 589832 | tf_op jit(solution)/shard_map/ppermute | solution.py:46
  147.8 18.5 %collective-permute-start.20 = (bf16[8,32,384]{2,1,0:T(8,128)(2,1)}, bf16[8,32,384]{2,1,0:T(8,128)(2,1)S(1)}, u32[]{:S(2)}, u32[]{:S(2)}) collective-permute-start(bf16[8,32,384]{2,1,0:T(8,128)(2,1)} %get-tuple-element.64), channel_id=1, source_target_pairs={{0,16},{8,24},{16,0},{24,8},{1,17},{9,25},{17,1},{25,9},{2,18},{10... | collective-permute-start | bytes 589832 | tf_op jit(solution)/shard_map/ppermute | solution.py:46
  149.0 17.3 %collective-permute-start.19 = (bf16[8,32,384]{2,1,0:T(8,128)(2,1)}, bf16[8,32,384]{2,1,0:T(8,128)(2,1)S(1)}, u32[]{:S(2)}, u32[]{:S(2)}) collective-permute-start(bf16[8,32,384]{2,1,0:T(8,128)(2,1)} %get-tuple-element.63), channel_id=1, source_target_pairs={{0,8},{8,0},{16,24},{24,16},{1,9},{9,1},{17,25},{25,17},{2,10},{10... | collective-permute-start | bytes 589832 | tf_op jit(solution)/shard_map/ppermute | solution.py:46
  162.7 13.2 %collective-permute-start.18 = (bf16[8,64,384]{2,1,0:T(8,128)(2,1)}, bf16[8,64,384]{2,1,0:T(8,128)(2,1)S(1)}, u32[]{:S(2)}, u32[]{:S(2)}) collective-permute-start(bf16[8,64,384]{2,1,0:T(8,128)(2,1)} %get-tuple-element.61), channel_id=1, source_target_pairs={{0,24},{8,16},{16,8},{24,0},{1,25},{9,17},{17,9},{25,1},{2,26},{10... | collective-permute-start | bytes 1179656 | tf_op jit(solution)/shard_map/ppermute | solution.py:46
  164.3 15.9 %collective-permute-start.17 = (bf16[8,64,384]{2,1,0:T(8,128)(2,1)}, bf16[8,64,384]{2,1,0:T(8,128)(2,1)S(1)}, u32[]{:S(2)}, u32[]{:S(2)}) collective-permute-start(bf16[8,64,384]{2,1,0:T(8,128)(2,1)} %get-tuple-element.60), channel_id=1, source_target_pairs={{0,16},{8,24},{16,0},{24,8},{1,17},{9,25},{17,1},{25,9},{2,18},{10... | collective-permute-start | bytes 1179656 | tf_op jit(solution)/shard_map/ppermute | solution.py:46
  165.5 14.7 %collective-permute-start.16 = (bf16[8,64,384]{2,1,0:T(8,128)(2,1)}, bf16[8,64,384]{2,1,0:T(8,128)(2,1)S(1)}, u32[]{:S(2)}, u32[]{:S(2)}) collective-permute-start(bf16[8,64,384]{2,1,0:T(8,128)(2,1)} %get-tuple-element.59), channel_id=1, source_target_pairs={{0,8},{8,0},{16,24},{24,16},{1,9},{9,1},{17,25},{25,17},{2,10},{10... | collective-permute-start | bytes 1179656 | tf_op jit(solution)/shard_map/ppermute | solution.py:46
  182.3 20.2 %all-to-all-start.4 = ((bf16[8,96,384]{2,1,0:T(8,128)(2,1)}), bf16[8,96,384]{2,1,0:T(8,128)(2,1)S(1)}, u32[]{:S(2)}, u32[]{:S(2)}) async-start(bf16[8,96,384]{2,1,0:T(8,128)(2,1)} %pad_maximum_fusion), calls=%async_computation.4 | async-start | bytes 1179648 | tf_op jit(solution)/shard_map/all_to_all | solution.py:530
  187.9 16.7 %collective-permute-start.25 = (bf16[4,384]{1,0:T(4,128)(2,1)S(1)}, bf16[4,384]{1,0:T(4,128)(2,1)S(1)}, u32[]{:S(2)}, u32[]{:S(2)}) collective-permute-start(bf16[4,384]{1,0:T(4,128)(2,1)S(1)} %select_bitcast_fusion.2), channel_id=1, source_target_pairs={{0,1},{1,0},{2,3},{3,2},{4,5},{5,4},{6,7},{7,6},{8,9},{9,8},{10,11... | collective-permute-start | bytes 9224 | tf_op jit(solution)/shard_map/ppermute | solution.py:30
  218.4 42.4 %all-to-all-start.5 = ((bf16[16,24,1920]{2,1,0:T(8,128)(2,1)}), bf16[16,24,1920]{2,1,0:T(8,128)(2,1)}, u32[]{:S(2)}, u32[]{:S(2)}) async-start(bf16[16,24,1920]{2,1,0:T(8,128)(2,1)} %bitcast.19), calls=%async_computation.5 | async-start | bytes 2949120 | tf_op jit(solution)/shard_map/all_to_all | solution.py:588
  224.0 23.7 %collective-permute-start.34 = (bf16[384,1792]{1,0:T(8,128)(2,1)S(1)}, bf16[384,1792]{1,0:T(8,128)(2,1)}, u32[]{:S(2)}, u32[]{:S(2)}) collective-permute-start(bf16[384,1792]{1,0:T(8,128)(2,1)S(1)} %bitcast.56), channel_id=1, source_target_pairs={{0,1},{1,0},{2,3},{3,2},{4,5},{5,4},{6,7},{7,6},{8,9},{9,8},{10,11... | collective-permute-start | bytes 4128776 | tf_op jit(solution)/shard_map/ppermute | solution.py:30
  (54 other events, 375.1 us)
